TPU v7x, 32 devices: a whole 2x2x4 slice. The times are simulated.
32 devices in a mesh: mat: 4 (over y, x), shard: 8 (over z, core).
Axes of the slice: x: 2, y: 2, z: 4, core: 2. Of those that a mesh axis runs over, the one named last changes fastest.
Arguments:
- iterate: bfloat16 [4, 2560, 2560], P('mat', 'shard')
Outputs:
- next_iterate: bfloat16 [4, 2560, 2560], P(None, 'shard')
All inputs are finite; a program needn't handle non-finite values.
Results may differ from a plain program's by a relative error of at most 0.0077.
Values may be sent and summed in bfloat16 or wider, within the bound.
No kernel may reach another device: no remote copies, remote signals or barrier semaphores. Data moves between devices by JAX's collectives and lax.ppermute only.
A program may use at most 128 MiB of HBM per device.

v0:
```python
import jax
import jax.numpy as jnp
from jax import lax
from jax.sharding import PartitionSpec as P

coef_a = 3.4445
coef_b = -4.775
coef_c = 2.0315


def shards(iterate):
    own_rows = iterate[0]
    gathered = lax.all_gather(own_rows, "shard", axis=0, tiled=True)
    full_gram = lax.dot_general(
        gathered, gathered, (((1,), (1,)), ((), ())), preferred_element_type=jnp.float32
    ).astype(jnp.bfloat16)
    row_start = lax.axis_index("shard") * own_rows.shape[0]
    gram_block = lax.dynamic_slice_in_dim(full_gram, row_start, own_rows.shape[0], 0)
    squared = jnp.dot(gram_block, full_gram, preferred_element_type=jnp.float32)
    polynomial = (coef_b * gram_block.astype(jnp.float32) + coef_c * squared).astype(jnp.bfloat16)
    product = jnp.dot(polynomial, gathered, preferred_element_type=jnp.float32)
    next_rows = (coef_a * own_rows.astype(jnp.float32) + product).astype(jnp.bfloat16)
    results = [next_rows]
    local_block = jnp.stack(results)
    return lax.all_gather(local_block, "mat", axis=0, tiled=True)


def solution(mesh):
    return jax.shard_map(
        shards,
        mesh=mesh,
        in_specs=(P("mat", "shard", None),),
        out_specs=P(None, "shard", None),
        check_vma=False,
    )
```

profile of v0, /device:TPU:0, one launch (start us, length us, event | category | flops | bytes accessed | tf_op | source)
XLA Modules:
  0.0 268.4 jit_solution(13898889958683041261)
XLA Ops:
  6.5 0.0 all-gather.5.cloned.1.call-start
  6.5 0.7 all-gather.5.cloned.1.call-update
  7.3 0.0 all-gather.7.cloned.1.call-start
  7.3 125.5 %all-gather.5.cloned.1.call-done = bf16[1,2560,2560]{2,1,0:T(8,128)(2,1)} async-done(((bf16[1,320,2560]{2,1,0:T(8,128)(2,1)}), bf16[1,2560,2560]{2,1,0:T(8,128)(2,1)}) %all-gather.5.cloned.1.call-update) | async-done | bytes 13107216 | tf_op jit(solution)/shard_map/all_gather | solution.py:13
  132.8 41.2 %convolution_convert_fusion = bf16[2560,2560]{1,0:T(8,128)(2,1)S(1)} fusion(bf16[1,2560,2560]{2,1,0:T(8,128)(2,1)} %all-gather.5.cloned.1.call-done), kind=kOutput, calls=%fused_computation | convolution fusion | flops 33560985600 | bytes 26214400 | tf_op jit(solution)/shard_map/dot_general | solution.py:14
  174.0 0.0 copy-start
  174.0 0.0 copy-start.1
  174.0 4.4 %fusion.10 = bf16[320,2560]{1,0:T(8,128)(2,1)S(1)} fusion(bf16[2560,2560]{1,0:T(8,128)(2,1)S(1)} %convolution_convert_fusion, s32[]{:T(128)S(6)} %select_n.3), kind=kOutput, calls=%fused_computation.8 | convolution fusion | flops 4198400000 | bytes 18023424 | tf_op jit(solution)/shard_map/dot_general | solution.py:19
  178.4 0.0 copy-done
  178.4 0.8 copy-done.1
  179.2 5.5 %fusion.7 = bf16[320,2560]{1,0:T(8,128)(2,1)} fusion(bf16[320,2560]{1,0:T(8,128)(2,1)S(1)} %fusion.10, bf16[1,2560,2560]{2,1,0:T(8,128)(2,1)S(1)} %copy-done.1, bf16[1,320,2560]{2,1,0:T(8,128)(2,1)S(1)} %copy-done), kind=kOutput, calls=%fused_computation.7 | convolution fusion | flops 4197580800 | bytes 18022400 | tf_op jit(solution)/shard_map/dot_general | solution.py:21
  184.7 0.0 all-gather.7.cloned.1.call-update
  184.7 70.7 %all-gather.7.cloned.1.call-done = bf16[1280,2560]{1,0:T(8,128)(2,1)} async-done(((bf16[320,2560]{1,0:T(8,128)(2,1)}), bf16[1280,2560]{1,0:T(8,128)(2,1)}) %all-gather.7.cloned.1.call-update) | async-done | bytes 6553616 | tf_op jit(solution)/shard_map/all_gather | solution.py:25
  255.4 6.1 %copy.3 = bf16[4,320,2560]{2,1,0:T(8,128)(2,1)} copy(bf16[4,320,2560]{2,1,0:T(8,128)(2,1)} %bitcast.14) | data formatting | bytes 13107200
Async XLA Ops:
  6.5 126.2 %all-gather.5.cloned.1.call-start = ((), (), s32[]{:S(2)}) async-start(), calls=%async_computation | async-start | bytes 14745600 | tf_op jit(solution)/shard_map/all_gather | solution.py:13
  7.3 248.2 %all-gather.7.cloned.1.call-start = ((), (), s32[]{:S(2)}) async-start(), calls=%async_computation.1 | async-start | bytes 8192000 | tf_op jit(solution)/shard_map/all_gather | solution.py:25
  174.0 4.5 %copy-start = (bf16[1,320,2560]{2,1,0:T(8,128)(2,1)S(1)}, bf16[1,320,2560]{2,1,0:T(8,128)(2,1)}, u32[]{:S(2)}) copy-start(bf16[1,320,2560]{2,1,0:T(8,128)(2,1)} %param.1) | copy-start | bytes 4915204
  174.0 5.2 %copy-start.1 = (bf16[1,2560,2560]{2,1,0:T(8,128)(2,1)S(1)}, bf16[1,2560,2560]{2,1,0:T(8,128)(2,1)}, u32[]{:S(2)}) copy-start(bf16[1,2560,2560]{2,1,0:T(8,128)(2,1)} %all-gather.5.cloned.1.call-done) | copy-start | bytes 39321604
Sparse Core Ops, SparseCore 0:
  9.0 123.7 all-gather.4
  184.8 70.5 all-gather.6
where the time goes:
time: 269 us; the launch traced here: 268 us
  waiting for transfers between devices  197 us (73%)
  matrix products  51.1 us (19%)
  between operations  13.4 us (5%)
  local copies, waits for them, and re-layouts  6.85 us (3%)
    all_gather x1, waiting for transfers between devices, shards(): gathered = lax.all_gather(own_rows, 'shard', axis=0, tiled=True)  125 us
    all_gather x1, waiting for transfers between devices, shards(): return lax.all_gather(local_block, 'mat', axis=0, tiled=True)  70.7 us
    dot_general x1, matrix products, shards(): lax.dot_general(gathered, gathered, (((1,), (1,)), ((), ())), preferred_e...  41.2 us
    unnamed x5, local copies, waits for them, and re-layouts  6.85 us
    dot_general x1, matrix products, shards(): product = jnp.dot(polynomial, gathered, preferred_element_type=jnp.float32)  5.5 us
  transfers between devices with their start and end apart: 2, of which 2 were waited for; matrix products, arithmetic and copies ran while one was open for 0% of the time, Pallas kernels for 0%

commit v1 on v0

v1 whole, which is shorter than its diff:
```python
import jax
import jax.numpy as jnp
from jax import lax
from jax.sharding import PartitionSpec as P

coef_a = 3.4445
coef_b = -4.775
coef_c = 2.0315


def dot_t(left, right):
    return lax.dot_general(
        left, right, (((1,), (1,)), ((), ())), preferred_element_type=jnp.float32
    )


def dot(left, right):
    return jnp.dot(left, right, preferred_element_type=jnp.float32)


def general_shards(iterate):
    own = iterate[0]
    gathered = lax.all_gather(own, "shard", axis=0, tiled=True)
    gram = dot_t(own, gathered).astype(jnp.bfloat16)
    cubic = dot(gram, gathered).astype(jnp.bfloat16)
    squared = dot_t(cubic, gathered)
    polynomial = (coef_b * gram.astype(jnp.float32) + coef_c * squared).astype(jnp.bfloat16)
    product = dot(polynomial, gathered)
    next_rows = (coef_a * own.astype(jnp.float32) + product).astype(jnp.bfloat16)
    return lax.all_gather(next_rows[None], "mat", axis=0, tiled=True)


def line_shards(iterate, row_cuts, column_cuts):
    own = iterate[0]
    rows, columns = own.shape
    place = lax.axis_index("shard") // 2
    outer = (place == 0) | (place == 3)
    mat = lax.axis_index("mat")

    other_core = [(d, d ^ 1) for d in range(8)]
    inwards = [(0, 2), (1, 3), (6, 4), (7, 5)]
    outwards = [(b, a) for a, b in inwards]
    middle = [(2, 4), (3, 5), (4, 2), (5, 3)]
    along_x = [(m, m ^ 1) for m in range(4)]
    along_y = [(m, m ^ 2) for m in range(4)]

    def send(value, axis, pairs):
        return lax.ppermute(value, axis, pairs)

    cut = rows // row_cuts
    own_cuts = [own[k * cut : (k + 1) * cut] for k in range(row_cuts)]
    from_outer = [send(part, "shard", inwards) for part in own_cuts]
    from_inner = [send(part, "shard", middle) for part in own_cuts]
    from_far = [send(part, "shard", middle) for part in from_outer]

    groups = []
    groups.append(own_cuts + [send(own, "shard", other_core)])
    for parts in (from_outer, from_inner, from_far):
        for part in parts:
            groups.append([part, send(part, "shard", other_core)])

    left = jnp.concatenate([own] + from_outer, axis=0)
    whole = jnp.zeros((8 * rows, columns), own.dtype)
    grams = []
    cubic = jnp.zeros(left.shape, jnp.float32)
    start = 0
    for group in groups:
        block = jnp.concatenate(group, axis=0)
        whole = lax.dynamic_update_slice_in_dim(whole, block, start, 0)
        start += block.shape[0]
        gram = dot_t(left, block).astype(jnp.bfloat16)
        cubic = cubic + dot(gram, block)
        grams.append(gram)
    gram = jnp.concatenate(grams, axis=1)
    cubic = cubic.astype(jnp.bfloat16)
    squared = dot_t(cubic, whole)
    polynomial = (coef_b * gram.astype(jnp.float32) + coef_c * squared).astype(jnp.bfloat16)

    width = columns // column_cuts

    def new_columns(first, k):
        part = lax.slice_in_dim(polynomial, first, first + rows, axis=0)
        base = lax.slice(left, (first, k * width), (first + rows, (k + 1) * width))
        product = dot(part, lax.slice_in_dim(whole, k * width, (k + 1) * width, axis=1))
        return (coef_a * base.astype(jnp.float32) + product).astype(jnp.bfloat16)

    for_outer = [new_columns(rows, k) for k in range(column_cuts)]
    returned = [send(part, "shard", outwards) for part in for_outer]
    result = jnp.zeros((4, rows, columns), jnp.bfloat16)

    def place_in(result, index, k, part):
        return lax.dynamic_update_slice(result, part[None], (index, 0, k * width))

    for k in range(column_cuts):
        mine = jnp.where(outer, returned[k], new_columns(0, k))
        by_x = send(mine, "mat", along_x)
        by_y = send(mine, "mat", along_y)
        if k % 2 == 0:
            across = send(by_x, "mat", along_y)
        else:
            across = send(by_y, "mat", along_x)
        result = place_in(result, mat, k, mine)
        result = place_in(result, mat ^ 1, k, by_x)
        result = place_in(result, mat ^ 2, k, by_y)
        result = place_in(result, mat ^ 3, k, across)
    return result


def solution(mesh):
    if (mesh.shape["mat"], mesh.shape["shard"]) == (4, 8):
        def shards(iterate):
            return line_shards(iterate, row_cuts=2, column_cuts=4)
    else:
        shards = general_shards
    return jax.shard_map(
        shards,
        mesh=mesh,
        in_specs=(P("mat", "shard", None),),
        out_specs=P(None, "shard", None),
        check_vma=False,
    )
```

time: 269 us -> 276 us (1.026)
  waiting for transfers between devices: 197 us -> 91.2 us
  matrix products: 51.1 us -> 107 us
  starting transfers between devices: 0.04 us -> 36.5 us
  local copies, waits for them, and re-layouts: 6.85 us -> 35.1 us
  between operations: 13.4 us -> 0.97 us
    all_gather x2 -> x0, waiting for transfers between devices: 196 us -> none  [the longest x1 125 us: shards(): gathered = lax.all_gather(own_rows, 'shard', axis=0, tiled=True)]
    ppermute x0 -> x29, waiting for transfers between devices: none -> 91.2 us  [send(): return lax.ppermute(value, axis, pairs)]
    dot_general x3 -> x22, matrix products: 51.1 us -> 107 us  [the longest x8 58.3 us: dot_t(): lax.dot_general(left, right, (((1,), (1,)), ((), ())), preferred_element_...]
    ppermute x0 -> x29, starting transfers between devices: none -> 36.5 us  [send(): return lax.ppermute(value, axis, pairs)]
    dynamic_update_slice x0 -> x19, local copies, waits for them, and re-layouts: none -> 16.7 us  [the longest x7 15.4 us: line_shards(): whole = lax.dynamic_update_slice_in_dim(whole, block, start, 0)]
    concatenate x0 -> x7, local copies, waits for them, and re-layouts: none -> 7.5 us  [the longest x6 5.33 us: line_shards(): block = jnp.concatenate(group, axis=0)]
    unnamed x5 -> x46, local copies, waits for them, and re-layouts: 6.85 us -> 8.76 us
  transfers between devices with their start and end apart: 2 -> 29, of which waited for: 2 -> 13; matrix products, arithmetic and copies ran while one was open for 0% -> 31% of each run, Pallas kernels for 0% -> 0%
where the time goes in v1:
time: 276 us; the launch traced here: 273 us
  matrix products  107 us (39%)
  waiting for transfers between devices  91.2 us (33%)
  starting transfers between devices  36.5 us (13%)
  local copies, waits for them, and re-layouts  35.1 us (13%)
    ppermute x29, waiting for transfers between devices, send(): return lax.ppermute(value, axis, pairs)  91.2 us
    dot_general x8, matrix products, dot_t(): lax.dot_general(left, right, (((1,), (1,)), ((), ())), preferred_element_...  58.3 us
    dot_general x14, matrix products, dot(): return jnp.dot(left, right, preferred_element_type=jnp.float32)  49 us
    ppermute x29, starting transfers between devices, send(): return lax.ppermute(value, axis, pairs)  36.5 us
    dynamic_update_slice x7, local copies, waits for them, and re-layouts, line_shards(): whole = lax.dynamic_update_slice_in_dim(whole, block, start, 0)  15.4 us
    unnamed x46, local copies, waits for them, and re-layouts  8.76 us
  transfers between devices with their start and end apart: 29, of which 13 were waited for; matrix products, arithmetic and copies ran while one was open for 31% of the time, Pallas kernels for 0%

profile of v1, /device:TPU:0, one launch (start us, length us, event | category | flops | bytes accessed | tf_op | source)
XLA Modules:
  0.0 272.9 jit_solution(10964154194439046772)
XLA Ops:
  1.6 5.9 %collective-permute-start = (bf16[160,2560]{1,0:T(8,128)(2,1)S(1)}, bf16[160,2560]{1,0:T(8,128)(2,1)}, u32[]{:S(2)}, u32[]{:S(2)}) collective-permute-start(bf16[160,2560]{1,0:T(8,128)(2,1)S(1)} %get-tuple-element.5), channel_id=1, source_target_pairs={{0,2},{1,3},{6,4},{7,5},{8,10},{9,11},{14,12},{15,13},{16,18},{17,... | collective-permute-start | bytes 2457608 | tf_op jit(solution)/shard_map/ppermute | solution.py:48
  12.9 12.4 %collective-permute-done = bf16[160,2560]{1,0:T(8,128)(2,1)} collective-permute-done((bf16[160,2560]{1,0:T(8,128)(2,1)S(1)}, bf16[160,2560]{1,0:T(8,128)(2,1)}, u32[]{:S(2)}, u32[]{:S(2)}) %collective-permute-start) | collective-permute-done | bytes 819232 | tf_op jit(solution)/shard_map/ppermute | solution.py:48
  26.6 15.0 %collective-permute-done.1 = bf16[160,2560]{1,0:T(8,128)(2,1)} collective-permute-done((bf16[160,2560]{1,0:T(8,128)(2,1)S(1)}, bf16[160,2560]{1,0:T(8,128)(2,1)}, u32[]{:S(2)}, u32[]{:S(2)}) %collective-permute-start.1) | collective-permute-done | bytes 819232 | tf_op jit(solution)/shard_map/ppermute | solution.py:48
  52.3 7.5 %dynamic_update_slice.69 = bf16[2560,2560]{1,0:T(8,128)(2,1)} pad(bf16[640,2560]{1,0:T(8,128)(2,1)} %pad_maximum_fusion.1, bf16[]{:T(256)} %constant.18.clone.1), padding=0_1920x0_0 | pad | bytes 16384002 | tf_op jit(solution)/shard_map/dynamic_update_slice | solution.py:69
  63.8 4.2 %constant_dynamic-update-slice_fusion.20 = (bf16[640,2560]{0,1:T(8,128)(2,1)S(1)}, bf16[640,640]{0,1:T(8,128)(2,1)S(1)}) fusion(bf16[320,2560]{1,0:T(8,128)(2,1)S(1)} %copy-done.11, bf16[160,2560]{1,0:T(8,128)(2,1)S(1)} %copy-done.6, bf16[160,2560]{1,0:T(8,128)(2,1)S(1)} %copy-done.4, bf16[160,2560]{1,0:T(8,128)(2,1)} %collective-permute-done.1, ...), kind=kOutput, calls=%fused_computation.94 | convolution fusion | flops 2117222400 | bytes 8192000 | tf_op jit(solution)/shard_map/dot_general | solution.py:12
  84.8 4.6 %fusion.130 = f32[640,2560]{1,0:T(8,128)} fusion(bf16[640,320]{0,1:T(8,128)(2,1)S(1)} %get-tuple-element.18, bf16[320,2560]{1,0:T(8,128)(2,1)S(1)} %constant_dynamic-update-slice_fusion.8), kind=kOutput, calls=%fused_computation.105 | convolution fusion | flops 1048576000 | bytes 8601600 | tf_op jit(solution)/shard_map/dot_general | solution.py:18
  89.4 4.6 %fusion.129 = f32[640,2560]{1,0:T(8,128)} fusion(bf16[640,320]{0,1:T(8,128)(2,1)S(1)} %get-tuple-element.16, bf16[320,2560]{1,0:T(8,128)(2,1)S(1)} %constant_dynamic-update-slice_fusion.6), kind=kOutput, calls=%fused_computation.104 | convolution fusion | flops 1048576000 | bytes 8601600 | tf_op jit(solution)/shard_map/dot_general | solution.py:18
  95.3 4.6 %fusion.128 = f32[640,2560]{1,0:T(8,128)} fusion(bf16[640,320]{0,1:T(8,128)(2,1)S(1)} %get-tuple-element.14, bf16[320,2560]{1,0:T(8,128)(2,1)S(1)} %constant_dynamic-update-slice_fusion.4), kind=kOutput, calls=%fused_computation.103 | convolution fusion | flops 1048576000 | bytes 8601600 | tf_op jit(solution)/shard_map/dot_general | solution.py:18
  102.9 4.6 %fusion.127 = f32[640,2560]{1,0:T(8,128)} fusion(bf16[640,320]{0,1:T(8,128)(2,1)S(1)} %get-tuple-element.12, bf16[320,2560]{1,0:T(8,128)(2,1)S(1)} %constant_dynamic-update-slice_fusion.2), kind=kOutput, calls=%fused_computation.102 | convolution fusion | flops 1048576000 | bytes 8601600 | tf_op jit(solution)/shard_map/dot_general | solution.py:18
  107.6 4.9 %fusion.126 = f32[640,2560]{1,0:T(8,128)} fusion(bf16[640,640]{0,1:T(8,128)(2,1)S(1)} %get-tuple-element.10, bf16[320,2560]{1,0:T(8,128)(2,1)S(1)} %copy-done.11, bf16[160,2560]{1,0:T(8,128)(2,1)S(1)} %copy-done.6, bf16[160,2560]{1,0:T(8,128)(2,1)S(1)} %copy-done.4), kind=kOutput, calls=%fused_computation.101 | convolution fusion | flops 2106982400 | bytes 10649600 | tf_op jit(solution)/shard_map/dot_general | solution.py:18
  116.8 4.7 %fusion.131 = f32[640,2560]{1,0:T(8,128)} fusion(bf16[640,320]{0,1:T(8,128)(2,1)S(1)} %get-tuple-element.20, bf16[320,2560]{1,0:T(8,128)(2,1)S(1)} %constant_dynamic-update-slice_fusion.10), kind=kOutput, calls=%fused_computation.106 | convolution fusion | flops 1048576000 | bytes 8601600 | tf_op jit(solution)/shard_map/dot_general | solution.py:18
  122.9 3.7 %constant_dynamic-update-slice_fusion.14 = (bf16[640,2560]{0,1:T(8,128)(2,1)S(1)}, bf16[640,320]{0,1:T(8,128)(2,1)}) fusion(bf16[640,2560]{0,1:T(8,128)(2,1)S(1)} %get-tuple-element.19, bf16[320,2560]{1,0:T(8,128)(2,1)S(1)} %constant_dynamic-update-slice_fusion.12, bf16[160,2560]{1,0:T(8,128)(2,1)} %collective-permute-done.1, ...), kind=kOutput, calls=%fused_computation.88 | convolution fusion | flops 1058611200 | bytes 5734400 | tf_op jit(solution)/shard_map/dot_general | solution.py:12
  128.2 35.7 %add_convert_fusion = bf16[640,2560]{0,1:T(8,128)(2,1)} fusion(bf16[640,2560]{0,1:T(8,128)(2,1)} %copy-done.15, bf16[2560,2560]{1,0:T(8,128)(2,1)} %constant_dynamic-update-slice_fusion.21, f32[640,2560]{1,0:T(8,128)} %fusion.131, f32[640,2560]{1,0:T(8,128)} %fusion.130, f32[640,2560]{1,0:T(8,128)} %fusion.129, f32[640,2560]{1,0:T(8,128)} %fusion.128, ...), kind=kOutput, calls=%fused_computation | convolution fusion | flops 9456844800 | bytes 61030400 | tf_op jit(solution)/shard_map/dot_general | solution.py:12
  163.9 4.6 %fusion.81 = bf16[320,640]{1,0:T(8,128)(2,1)S(1)} fusion(bf16[2560,2560]{1,0:T(8,128)(2,1)} %constant_dynamic-update-slice_fusion.21, bf16[640,2560]{0,1:T(8,128)(2,1)} %add_convert_fusion, bf16[320,2560]{1,0:T(8,128)(2,1)S(1)} %copy-done.13), kind=kOutput, calls=%fused_computation.41 | convolution fusion | flops 1049395200 | bytes 6062080 | tf_op jit(solution)/shard_map/dot_general | solution.py:18
  170.1 17.2 %collective-permute-done.13 = bf16[320,640]{1,0:T(8,128)(2,1)S(1)} collective-permute-done((bf16[320,640]{1,0:T(8,128)(2,1)S(1)}, bf16[320,640]{1,0:T(8,128)(2,1)S(1)}, u32[]{:S(2)}, u32[]{:S(2)}) %collective-permute-start.13) | collective-permute-done | bytes 409632 | tf_op jit(solution)/shard_map/ppermute | solution.py:48
  187.9 3.6 %bitcast_dynamic-update-slice_fusion.15 = (bf16[4,320,2560]{2,1,0:T(8,128)(2,1)S(1)}, bf16[320,640]{1,0:T(8,128)(2,1)S(1)}) fusion(bf16[4,320,2560]{2,1,0:T(8,128)(2,1)S(1)} %broadcast_in_dim.52, s32[]{:T(128)S(6)} %select_n.52, bf16[320,640]{1,0:T(8,128)(2,1)S(1)} %collective-permute-done.13, bf16[2560,2560]{1,0:T(8,128)(2,1)} %constant_dynamic-update-slice_fusion.21, ...), kind=kOutput, calls=%fused_computation.69 | convolution fusion | flops 1049600000 | bytes 6881285 | tf_op jit(solution)/shard_map/dot_general | solution.py:18
  194.6 4.0 %fusion.76 = bf16[320,640]{1,0:T(8,128)(2,1)S(1)} fusion(bf16[2560,2560]{1,0:T(8,128)(2,1)} %constant_dynamic-update-slice_fusion.21, bf16[640,2560]{0,1:T(8,128)(2,1)S(1)} %copy-done.14, bf16[320,2560]{1,0:T(8,128)(2,1)S(1)} %copy-done.13), kind=kOutput, calls=%fused_computation.40 | convolution fusion | flops 1049395200 | bytes 6062080 | tf_op jit(solution)/shard_map/dot_general | solution.py:18
  204.1 8.3 %collective-permute-done.16 = bf16[320,640]{1,0:T(8,128)(2,1)S(1)} collective-permute-done((bf16[320,640]{1,0:T(8,128)(2,1)S(1)}, bf16[320,640]{1,0:T(8,128)(2,1)S(1)}, u32[]{:S(2)}, u32[]{:S(2)}) %collective-permute-start.16) | collective-permute-done | bytes 409632 | tf_op jit(solution)/shard_map/ppermute | solution.py:48
  220.5 3.8 %collective-permute-done.19 = bf16[320,640]{1,0:T(8,128)(2,1)S(1)} collective-permute-done((bf16[320,640]{1,0:T(8,128)(2,1)S(1)}, bf16[320,640]{1,0:T(8,128)(2,1)S(1)}, u32[]{:S(2)}, u32[]{:S(2)}) %collective-permute-start.19) | collective-permute-done | bytes 409632 | tf_op jit(solution)/shard_map/ppermute | solution.py:48
  225.1 7.3 %collective-permute-done.20 = bf16[320,640]{1,0:T(8,128)(2,1)S(1)} collective-permute-done((bf16[320,640]{1,0:T(8,128)(2,1)S(1)}, bf16[320,640]{1,0:T(8,128)(2,1)S(1)}, u32[]{:S(2)}, u32[]{:S(2)}) %collective-permute-start.20) | collective-permute-done | bytes 409632 | tf_op jit(solution)/shard_map/ppermute | solution.py:48
  247.0 4.7 %collective-permute-done.24 = bf16[320,640]{1,0:T(8,128)(2,1)S(1)} collective-permute-done((bf16[320,640]{1,0:T(8,128)(2,1)S(1)}, bf16[320,640]{1,0:T(8,128)(2,1)S(1)}, u32[]{:S(2)}, u32[]{:S(2)}) %collective-permute-start.24) | collective-permute-done | bytes 409632 | tf_op jit(solution)/shard_map/ppermute | solution.py:48
  255.9 5.4 %collective-permute-done.27 = bf16[320,640]{1,0:T(8,128)(2,1)S(1)} collective-permute-done((bf16[320,640]{1,0:T(8,128)(2,1)S(1)}, bf16[320,640]{1,0:T(8,128)(2,1)S(1)}, u32[]{:S(2)}, u32[]{:S(2)}) %collective-permute-start.27) | collective-permute-done | bytes 409632 | tf_op jit(solution)/shard_map/ppermute | solution.py:48
  262.5 4.4 %collective-permute-done.26 = bf16[320,640]{1,0:T(8,128)(2,1)S(1)} collective-permute-done((bf16[320,640]{1,0:T(8,128)(2,1)S(1)}, bf16[320,640]{1,0:T(8,128)(2,1)S(1)}, u32[]{:S(2)}, u32[]{:S(2)}) %collective-permute-start.26) | collective-permute-done | bytes 409632 | tf_op jit(solution)/shard_map/ppermute | solution.py:48
  266.9 4.7 %collective-permute-done.28 = bf16[320,640]{1,0:T(8,128)(2,1)S(1)} collective-permute-done((bf16[320,640]{1,0:T(8,128)(2,1)S(1)}, bf16[320,640]{1,0:T(8,128)(2,1)S(1)}, u32[]{:S(2)}, u32[]{:S(2)}) %collective-permute-start.28) | collective-permute-done | bytes 409632 | tf_op jit(solution)/shard_map/ppermute | solution.py:48
  (132 shorter events, 91.5 us)
Async XLA Ops:
  1.6 23.6 %collective-permute-start = (bf16[160,2560]{1,0:T(8,128)(2,1)S(1)}, bf16[160,2560]{1,0:T(8,128)(2,1)}, u32[]{:S(2)}, u32[]{:S(2)}) collective-permute-start(bf16[160,2560]{1,0:T(8,128)(2,1)S(1)} %get-tuple-element.5), channel_id=1, source_target_pairs={{0,2},{1,3},{6,4},{7,5},{8,10},{9,11},{14,12},{15,13},{16,18},{17,... | collective-permute-start | bytes 2457608 | tf_op jit(solution)/shard_map/ppermute | solution.py:48
  7.5 34.1 %collective-permute-start.1 = (bf16[160,2560]{1,0:T(8,128)(2,1)S(1)}, bf16[160,2560]{1,0:T(8,128)(2,1)}, u32[]{:S(2)}, u32[]{:S(2)}) collective-permute-start(bf16[160,2560]{1,0:T(8,128)(2,1)S(1)} %get-tuple-element.6), channel_id=1, source_target_pairs={{0,2},{1,3},{6,4},{7,5},{8,10},{9,11},{14,12},{15,13},{16,18},{17,... | collective-permute-start | bytes 2457608 | tf_op jit(solution)/shard_map/ppermute | solution.py:48
  9.7 31.9 %collective-permute-start.5 = (bf16[160,2560]{1,0:T(8,128)(2,1)S(1)}, bf16[160,2560]{1,0:T(8,128)(2,1)}, u32[]{:S(2)}, u32[]{:S(2)}) collective-permute-start(bf16[160,2560]{1,0:T(8,128)(2,1)S(1)} %get-tuple-element.5), channel_id=1, source_target_pairs={{2,4},{3,5},{4,2},{5,3},{10,12},{11,13},{12,10},{13,11},{18,20},{1... | collective-permute-start | bytes 2457608 | tf_op jit(solution)/shard_map/ppermute | solution.py:48
  11.3 30.9 %collective-permute-start.7 = (bf16[160,2560]{1,0:T(8,128)(2,1)S(1)}, bf16[160,2560]{1,0:T(8,128)(2,1)}, u32[]{:S(2)}, u32[]{:S(2)}) collective-permute-start(bf16[160,2560]{1,0:T(8,128)(2,1)S(1)} %get-tuple-element.6), channel_id=1, source_target_pairs={{2,4},{3,5},{4,2},{5,3},{10,12},{11,13},{12,10},{13,11},{18,20},{1... | collective-permute-start | bytes 2457608 | tf_op jit(solution)/shard_map/ppermute | solution.py:48
  12.8 34.8 %collective-permute-start.2 = (bf16[320,2560]{1,0:T(8,128)(2,1)S(1)}, bf16[320,2560]{1,0:T(8,128)(2,1)S(1)}, u32[]{:S(2)}, u32[]{:S(2)}) collective-permute-start(bf16[320,2560]{1,0:T(8,128)(2,1)S(1)} %bitcast.59), channel_id=1, source_target_pairs={{0,1},{1,0},{2,3},{3,2},{4,5},{5,4},{6,7},{7,6},{8,9},{9,8},{10,11... | collective-permute-start | bytes 4915208 | tf_op jit(solution)/shard_map/ppermute | solution.py:48
  26.5 33.3 %collective-permute-start.3 = (bf16[160,2560]{1,0:T(8,128)(2,1)}, bf16[160,2560]{1,0:T(8,128)(2,1)}, u32[]{:S(2)}, u32[]{:S(2)}) collective-permute-start(bf16[160,2560]{1,0:T(8,128)(2,1)} %collective-permute-done), channel_id=1, source_target_pairs={{0,1},{1,0},{2,3},{3,2},{4,5},{5,4},{6,7},{7,6},{8,9},{9,8},{10,11... | collective-permute-start | bytes 2457608 | tf_op jit(solution)/shard_map/ppermute | solution.py:48
  41.6 26.5 %collective-permute-start.4 = (bf16[160,2560]{1,0:T(8,128)(2,1)}, bf16[160,2560]{1,0:T(8,128)(2,1)}, u32[]{:S(2)}, u32[]{:S(2)}) collective-permute-start(bf16[160,2560]{1,0:T(8,128)(2,1)} %collective-permute-done.1), channel_id=1, source_target_pairs={{0,1},{1,0},{2,3},{3,2},{4,5},{5,4},{6,7},{7,6},{8,9},{9,8},{10,11... | collective-permute-start | bytes 2457608 | tf_op jit(solution)/shard_map/ppermute | solution.py:48
  41.6 32.0 %collective-permute-start.6 = (bf16[160,2560]{1,0:T(8,128)(2,1)}, bf16[160,2560]{1,0:T(8,128)(2,1)}, u32[]{:S(2)}, u32[]{:S(2)}) collective-permute-start(bf16[160,2560]{1,0:T(8,128)(2,1)} %collective-permute-done.5), channel_id=1, source_target_pairs={{0,1},{1,0},{2,3},{3,2},{4,5},{5,4},{6,7},{7,6},{8,9},{9,8},{10,11... | collective-permute-start | bytes 2457608 | tf_op jit(solution)/shard_map/ppermute | solution.py:48
  42.1 35.6 %collective-permute-start.8 = (bf16[160,2560]{1,0:T(8,128)(2,1)}, bf16[160,2560]{1,0:T(8,128)(2,1)}, u32[]{:S(2)}, u32[]{:S(2)}) collective-permute-start(bf16[160,2560]{1,0:T(8,128)(2,1)} %collective-permute-done.7), channel_id=1, source_target_pairs={{0,1},{1,0},{2,3},{3,2},{4,5},{5,4},{6,7},{7,6},{8,9},{9,8},{10,11... | collective-permute-start | bytes 2457608 | tf_op jit(solution)/shard_map/ppermute | solution.py:48
  48.9 51.1 %collective-permute-start.9 = (bf16[160,2560]{1,0:T(8,128)(2,1)}, bf16[160,2560]{1,0:T(8,128)(2,1)}, u32[]{:S(2)}, u32[]{:S(2)}) collective-permute-start(bf16[160,2560]{1,0:T(8,128)(2,1)} %collective-permute-done), channel_id=1, source_target_pairs={{2,4},{3,5},{4,2},{5,3},{10,12},{11,13},{12,10},{13,11},{18,20},{1... | collective-permute-start | bytes 2457608 | tf_op jit(solution)/shard_map/ppermute | solution.py:48
  59.8 47.7 %collective-permute-start.11 = (bf16[160,2560]{1,0:T(8,128)(2,1)}, bf16[160,2560]{1,0:T(8,128)(2,1)S(1)}, u32[]{:S(2)}, u32[]{:S(2)}) collective-permute-start(bf16[160,2560]{1,0:T(8,128)(2,1)} %collective-permute-done.1), channel_id=1, source_target_pairs={{2,4},{3,5},{4,2},{5,3},{10,12},{11,13},{12,10},{13,11},{18,20},{1... | collective-permute-start | bytes 2457608 | tf_op jit(solution)/shard_map/ppermute | solution.py:48
  101.1 11.4 %collective-permute-start.10 = (bf16[160,2560]{1,0:T(8,128)(2,1)}, bf16[160,2560]{1,0:T(8,128)(2,1)S(1)}, u32[]{:S(2)}, u32[]{:S(2)}) collective-permute-start(bf16[160,2560]{1,0:T(8,128)(2,1)} %collective-permute-done.9), channel_id=1, source_target_pairs={{0,1},{1,0},{2,3},{3,2},{4,5},{5,4},{6,7},{7,6},{8,9},{9,8},{10,11... | collective-permute-start | bytes 2457608 | tf_op jit(solution)/shard_map/ppermute | solution.py:48
  107.5 14.0 %collective-permute-start.12 = (bf16[160,2560]{1,0:T(8,128)(2,1)S(1)}, bf16[160,2560]{1,0:T(8,128)(2,1)S(1)}, u32[]{:S(2)}, u32[]{:S(2)}) collective-permute-start(bf16[160,2560]{1,0:T(8,128)(2,1)S(1)} %collective-permute-done.11), channel_id=1, source_target_pairs={{0,1},{1,0},{2,3},{3,2},{4,5},{5,4},{6,7},{7,6},{8,9},{9,8},{10,11... | collective-permute-start | bytes 2457608 | tf_op jit(solution)/shard_map/ppermute | solution.py:48
  168.5 18.8 %collective-permute-start.13 = (bf16[320,640]{1,0:T(8,128)(2,1)S(1)}, bf16[320,640]{1,0:T(8,128)(2,1)S(1)}, u32[]{:S(2)}, u32[]{:S(2)}) collective-permute-start(bf16[320,640]{1,0:T(8,128)(2,1)S(1)} %fusion.81), channel_id=1, source_target_pairs={{2,0},{3,1},{4,6},{5,7},{10,8},{11,9},{12,14},{13,15},{18,16},{19,... | collective-permute-start | bytes 1228808 | tf_op jit(solution)/shard_map/ppermute | solution.py:48
  191.5 10.9 %collective-permute-start.14 = (bf16[320,640]{1,0:T(8,128)(2,1)S(1)}, bf16[320,640]{1,0:T(8,128)(2,1)S(1)}, u32[]{:S(2)}, u32[]{:S(2)}) collective-permute-start(bf16[320,640]{1,0:T(8,128)(2,1)S(1)} %get-tuple-element.24), channel_id=1, source_target_pairs={{0,8},{8,0},{16,24},{24,16},{1,9},{9,1},{17,25},{25,17},{2,10},{10... | collective-permute-start | bytes 1228808 | tf_op jit(solution)/shard_map/ppermute | solution.py:48
  193.0 10.9 %collective-permute-start.15 = (bf16[320,640]{1,0:T(8,128)(2,1)S(1)}, bf16[320,640]{1,0:T(8,128)(2,1)S(1)}, u32[]{:S(2)}, u32[]{:S(2)}) collective-permute-start(bf16[320,640]{1,0:T(8,128)(2,1)S(1)} %get-tuple-element.24), channel_id=1, source_target_pairs={{0,16},{8,24},{16,0},{24,8},{1,17},{9,25},{17,1},{25,9},{2,18},{10... | collective-permute-start | bytes 1228808 | tf_op jit(solution)/shard_map/ppermute | solution.py:48
  198.6 13.9 %collective-permute-start.17 = (bf16[320,640]{1,0:T(8,128)(2,1)S(1)}, bf16[320,640]{1,0:T(8,128)(2,1)S(1)}, u32[]{:S(2)}, u32[]{:S(2)}) collective-permute-start(bf16[320,640]{1,0:T(8,128)(2,1)S(1)} %fusion.76), channel_id=1, source_target_pairs={{2,0},{3,1},{4,6},{5,7},{10,8},{11,9},{12,14},{13,15},{18,16},{19,... | collective-permute-start | bytes 1228808 | tf_op jit(solution)/shard_map/ppermute | solution.py:48
  202.4 10.0 %collective-permute-start.16 = (bf16[320,640]{1,0:T(8,128)(2,1)S(1)}, bf16[320,640]{1,0:T(8,128)(2,1)S(1)}, u32[]{:S(2)}, u32[]{:S(2)}) collective-permute-start(bf16[320,640]{1,0:T(8,128)(2,1)S(1)} %collective-permute-done.14), channel_id=1, source_target_pairs={{0,16},{8,24},{16,0},{24,8},{1,17},{9,25},{17,1},{25,9},{2,18},{10... | collective-permute-start | bytes 1228808 | tf_op jit(solution)/shard_map/ppermute | solution.py:48
  214.1 10.9 %collective-permute-start.18 = (bf16[320,640]{1,0:T(8,128)(2,1)S(1)}, bf16[320,640]{1,0:T(8,128)(2,1)S(1)}, u32[]{:S(2)}, u32[]{:S(2)}) collective-permute-start(bf16[320,640]{1,0:T(8,128)(2,1)S(1)} %get-tuple-element.26), channel_id=1, source_target_pairs={{0,8},{8,0},{16,24},{24,16},{1,9},{9,1},{17,25},{25,17},{2,10},{10... | collective-permute-start | bytes 1228808 | tf_op jit(solution)/shard_map/ppermute | solution.py:48
  219.2 13.2 %collective-permute-start.21 = (bf16[320,640]{1,0:T(8,128)(2,1)S(1)}, bf16[320,640]{1,0:T(8,128)(2,1)S(1)}, u32[]{:S(2)}, u32[]{:S(2)}) collective-permute-start(bf16[320,640]{1,0:T(8,128)(2,1)S(1)} %fusion.71), channel_id=1, source_target_pairs={{2,0},{3,1},{4,6},{5,7},{10,8},{11,9},{12,14},{13,15},{18,16},{19,... | collective-permute-start | bytes 1228808 | tf_op jit(solution)/shard_map/ppermute | solution.py:48
  235.0 11.9 %collective-permute-start.23 = (bf16[320,640]{1,0:T(8,128)(2,1)S(1)}, bf16[320,640]{1,0:T(8,128)(2,1)S(1)}, u32[]{:S(2)}, u32[]{:S(2)}) collective-permute-start(bf16[320,640]{1,0:T(8,128)(2,1)S(1)} %get-tuple-element.28), channel_id=1, source_target_pairs={{0,16},{8,24},{16,0},{24,8},{1,17},{9,25},{17,1},{25,9},{2,18},{10... | collective-permute-start | bytes 1228808 | tf_op jit(solution)/shard_map/ppermute | solution.py:48
  238.6 13.2 %collective-permute-start.25 = (bf16[320,640]{1,0:T(8,128)(2,1)S(1)}, bf16[320,640]{1,0:T(8,128)(2,1)S(1)}, u32[]{:S(2)}, u32[]{:S(2)}) collective-permute-start(bf16[320,640]{1,0:T(8,128)(2,1)S(1)} %fusion.66), channel_id=1, source_target_pairs={{2,0},{3,1},{4,6},{5,7},{10,8},{11,9},{12,14},{13,15},{18,16},{19,... | collective-permute-start | bytes 1228808 | tf_op jit(solution)/shard_map/ppermute | solution.py:48
  254.9 11.9 %collective-permute-start.26 = (bf16[320,640]{1,0:T(8,128)(2,1)S(1)}, bf16[320,640]{1,0:T(8,128)(2,1)S(1)}, u32[]{:S(2)}, u32[]{:S(2)}) collective-permute-start(bf16[320,640]{1,0:T(8,128)(2,1)S(1)} %get-tuple-element.30), channel_id=1, source_target_pairs={{0,8},{8,0},{16,24},{24,16},{1,9},{9,1},{17,25},{25,17},{2,10},{10... | collective-permute-start | bytes 1228808 | tf_op jit(solution)/shard_map/ppermute | solution.py:48
  261.4 10.3 %collective-permute-start.28 = (bf16[320,640]{1,0:T(8,128)(2,1)S(1)}, bf16[320,640]{1,0:T(8,128)(2,1)S(1)}, u32[]{:S(2)}, u32[]{:S(2)}) collective-permute-start(bf16[320,640]{1,0:T(8,128)(2,1)S(1)} %collective-permute-done.27), channel_id=1, source_target_pairs={{0,8},{8,0},{16,24},{24,16},{1,9},{9,1},{17,25},{25,17},{2,10},{10... | collective-permute-start | bytes 1228808 | tf_op jit(solution)/shard_map/ppermute | solution.py:48
  (25 other events, 352.1 us)

commit v2 on v0

v2 whole, which is shorter than its diff:
```python
import functools

import jax
import jax.numpy as jnp
from jax import lax
from jax.experimental import pallas as pl
from jax.experimental.pallas import tpu as pltpu
from jax.sharding import PartitionSpec as P

coef_a = 3.4445
coef_b = -4.775
coef_c = 2.0315

TILE = 256
VMEM_LIMIT = 48 * 1024 * 1024


def dot_t(left, right):
    return lax.dot_general(
        left, right, (((1,), (1,)), ((), ())), preferred_element_type=jnp.float32
    )


def dot(left, right):
    return jnp.dot(left, right, preferred_element_type=jnp.float32)


def general_shards(iterate):
    own = iterate[0]
    gathered = lax.all_gather(own, "shard", axis=0, tiled=True)
    gram = dot_t(own, gathered).astype(jnp.bfloat16)
    cubic = dot(gram, gathered).astype(jnp.bfloat16)
    squared = dot_t(cubic, gathered)
    polynomial = (coef_b * gram.astype(jnp.float32) + coef_c * squared).astype(jnp.bfloat16)
    product = dot(polynomial, gathered)
    next_rows = (coef_a * own.astype(jnp.float32) + product).astype(jnp.bfloat16)
    return lax.all_gather(next_rows[None], "mat", axis=0, tiled=True)


def tiles(total):
    return [(s, min(TILE, total - s)) for s in range(0, total, TILE)]


def early_kernel(count, *refs):
    blocks, (gram, cubic, whole, sems) = refs[:count], refs[count:]
    rows = blocks[0].shape[0]
    copies = []
    for k, block in enumerate(blocks):
        copy = pltpu.make_async_copy(block, whole.at[pl.ds(k * rows, rows), :], sems.at[k])
        copy.start()
        copies.append(copy)
    for copy in copies:
        copy.wait()

    def gram_tile(start, width):
        gram[:, pl.ds(start, width)] = dot_t(
            whole[: 2 * rows, :], whole[pl.ds(start, width), :]
        ).astype(jnp.bfloat16)

    full = (count * rows) // TILE

    @pl.loop(0, full)
    def _(n):
        gram_tile(pl.multiple_of(n * TILE, TILE), TILE)

    if full * TILE < count * rows:
        gram_tile(full * TILE, count * rows - full * TILE)

    @pl.loop(0, whole.shape[1] // TILE)
    def _(n):
        at = pl.ds(pl.multiple_of(n * TILE, TILE), TILE)
        cubic[:, at] = dot(gram[...], whole[:, at])


def early_products(blocks):
    count = len(blocks)
    rows, columns = blocks[0].shape
    known = count * rows
    return pl.pallas_call(
        functools.partial(early_kernel, count),
        out_shape=(
            jax.ShapeDtypeStruct((2 * rows, known), jnp.bfloat16),
            jax.ShapeDtypeStruct((2 * rows, columns), jnp.float32),
        ),
        in_specs=[pl.BlockSpec(memory_space=pl.ANY)] * count,
        out_specs=(pl.BlockSpec(memory_space=pltpu.VMEM),) * 2,
        scratch_shapes=[
            pltpu.VMEM((known, columns), jnp.bfloat16),
            pltpu.SemaphoreType.DMA((count,)),
        ],
        compiler_params=pltpu.CompilerParams(vmem_limit_bytes=VMEM_LIMIT),
        cost_estimate=pl.CostEstimate(
            flops=8 * rows * known * columns, bytes_accessed=2 * known * columns, transcendentals=0
        ),
    )(*blocks)


def late_kernel(count, first, widths, *refs):
    blocks, gram_in, cubic_in = refs[:count], refs[count], refs[count + 1]
    outs = refs[count + 2 : count + 2 + len(widths)]
    whole, gram, cubic_sum, cubic, poly, sems = refs[count + 2 + len(widths) :]
    rows, columns = blocks[0].shape
    known = (count - 2) * rows
    mine = pl.ds(first * rows, rows)

    copies = {}

    def fetch(name, source, target):
        copies[name] = pltpu.make_async_copy(source, target, sems.at[len(copies)])
        copies[name].start()

    def fetch_block(k):
        if k not in copies:
            fetch(k, blocks[k], whole.at[pl.ds(k * rows, rows), :])

    fetch_block(count - 2)
    fetch_block(count - 1)
    fetch_block(first)
    fetch("gram", gram_in.at[mine, :], gram.at[:, pl.ds(0, known)])
    fetch("cubic", cubic_in.at[mine, :], cubic_sum)
    for k in range(count):
        fetch_block(k)

    for name in (count - 2, count - 1, first, "gram"):
        copies[name].wait()
    late = dot_t(whole[mine, :], whole[known:, :]).astype(jnp.bfloat16)
    gram[:, pl.ds(known, 2 * rows)] = late
    copies["cubic"].wait()

    @pl.loop(0, columns // TILE)
    def _(n):
        at = pl.ds(pl.multiple_of(n * TILE, TILE), TILE)
        add = dot(gram[:, pl.ds(known, 2 * rows)], whole[pl.ds(known, 2 * rows), at])
        cubic[:, at] = (cubic_sum[:, at] + add).astype(jnp.bfloat16)

    for k in range(count - 2):
        if k != first:
            copies[k].wait()

    @pl.loop(0, count * rows // TILE)
    def _(n):
        at = pl.ds(pl.multiple_of(n * TILE, TILE), TILE)
        squared = dot_t(cubic[...], whole[at, :])
        poly[:, at] = (coef_b * gram[:, at].astype(jnp.float32) + coef_c * squared).astype(
            jnp.bfloat16
        )

    begin = 0
    for out, width in zip(outs, widths):

        @pl.loop(0, width // TILE)
        def _(n, out=out, begin=begin):
            local = pl.ds(pl.multiple_of(n * TILE, TILE), TILE)
            at = pl.ds(pl.multiple_of(begin + n * TILE, TILE), TILE)
            product = dot(poly[...], whole[:, at])
            base = whole[mine, at].astype(jnp.float32)
            out[:, local] = (coef_a * base + product).astype(jnp.bfloat16)

        begin += width


def late_products(blocks, gram, cubic, first, widths):
    count = len(blocks)
    rows, columns = blocks[0].shape
    total = count * rows
    return pl.pallas_call(
        functools.partial(late_kernel, count, first, widths),
        out_shape=tuple(jax.ShapeDtypeStruct((rows, w), jnp.bfloat16) for w in widths),
        in_specs=[pl.BlockSpec(memory_space=pl.ANY)] * (count + 2),
        out_specs=tuple(pl.BlockSpec(memory_space=pltpu.VMEM) for _ in widths),
        scratch_shapes=[
            pltpu.VMEM((total, columns), jnp.bfloat16),
            pltpu.VMEM((rows, total), jnp.bfloat16),
            pltpu.VMEM((rows, columns), jnp.float32),
            pltpu.VMEM((rows, columns), jnp.bfloat16),
            pltpu.VMEM((rows, total), jnp.bfloat16),
            pltpu.SemaphoreType.DMA((count + 2,)),
        ],
        compiler_params=pltpu.CompilerParams(vmem_limit_bytes=VMEM_LIMIT),
        cost_estimate=pl.CostEstimate(
            flops=5 * rows * total * columns, bytes_accessed=2 * total * columns, transcendentals=0
        ),
    )(*blocks, gram, cubic)


def line_shards(iterate, widths):
    own = iterate[0]
    rows, columns = own.shape
    place = lax.axis_index("shard") // 2
    outer = (place == 0) | (place == 3)
    mat = lax.axis_index("mat")

    other_core = [(d, d ^ 1) for d in range(8)]
    inwards = [(0, 2), (1, 3), (6, 4), (7, 5)]
    outwards = [(b, a) for a, b in inwards]
    middle = [(2, 4), (3, 5), (4, 2), (5, 3)]
    along_x = [(m, m ^ 1) for m in range(4)]
    along_y = [(m, m ^ 2) for m in range(4)]

    from_outer = lax.ppermute(own, "shard", inwards)
    from_inner = lax.ppermute(own, "shard", middle)
    from_far = lax.ppermute(from_outer, "shard", middle)

    def swap(block):
        return lax.ppermute(block, "shard", other_core)

    early = [from_outer, own, swap(from_outer), swap(own), from_inner, swap(from_inner)]
    gram, cubic = early_products(early)
    blocks = early + [from_far, swap(from_far)]
    for_outer = late_products(blocks, gram, cubic, 0, widths)
    for_own = late_products(blocks, gram, cubic, 1, widths)

    result = jnp.zeros((4, rows, columns), jnp.bfloat16)
    begin = 0
    onward, onward_axis, onward_at = None, None, None

    def place(result, flip, at, part):
        return lax.dynamic_update_slice(result, part[None], (mat ^ flip, 0, at))

    for k, width in enumerate(widths):
        returned = lax.ppermute(for_outer[k], "shard", outwards)
        mine = jnp.where(outer, returned, for_own[k])
        if onward is not None:
            mine, onward = lax.optimization_barrier((mine, onward))
        by_x = lax.ppermute(mine, "mat", along_x)
        by_y = lax.ppermute(mine, "mat", along_y)
        if onward is not None:
            across = lax.ppermute(onward, "mat", onward_axis)
            result = place(result, 3, onward_at, across)
        for flip, part in enumerate((mine, by_x, by_y)):
            result = place(result, flip, begin, part)
        onward, onward_axis = (by_x, along_y) if k % 2 == 0 else (by_y, along_x)
        onward_at = begin
        begin += width
    across = lax.ppermute(onward, "mat", onward_axis)
    result = place(result, 3, onward_at, across)
    return result


def solution(mesh):
    if (mesh.shape["mat"], mesh.shape["shard"]) == (4, 8):
        def shards(iterate):
            return line_shards(iterate, widths=(512, 512, 768, 768))
    else:
        shards = general_shards
    return jax.shard_map(
        shards,
        mesh=mesh,
        in_specs=(P("mat", "shard", None),),
        out_specs=P(None, "shard", None),
        check_vma=False,
    )
```

time: 269 us -> 218 us (0.81)
  waiting for transfers between devices: 197 us -> 124 us
  Pallas kernels: 0 us -> 60.8 us
  matrix products: 51.1 us -> 0 us
  starting transfers between devices: 0.04 us -> 29.2 us
  between operations: 13.4 us -> 0.29 us
  local copies, waits for them, and re-layouts: 6.85 us -> 3.43 us
    all_gather x2 -> x0, waiting for transfers between devices: 196 us -> none  [the longest x1 125 us: shards(): gathered = lax.all_gather(own_rows, 'shard', axis=0, tiled=True)]
    ppermute x0 -> x23, waiting for transfers between devices: none -> 124 us  [the longest x4 41 us: line_shards(): returned = lax.ppermute(for_outer[k], 'shard', outwards)]
    pallas_call x0 -> x3, Pallas kernels: none -> 60.8 us  [the longest x2 38.2 us: late_products(): pl.pallas_call(functools.partial(late_kernel, count, first, widths), out_...]
    dot_general x3 -> x0, matrix products: 51.1 us -> none  [the longest x1 41.2 us: shards(): lax.dot_general(gathered, gathered, (((1,), (1,)), ((), ())), preferred_e...]
    ppermute x0 -> x23, starting transfers between devices: none -> 29.2 us  [the longest x4 6.14 us: line_shards(): by_y = lax.ppermute(mine, 'mat', along_y)]
    unnamed x5 -> x6, local copies, waits for them, and re-layouts: 6.85 us -> 1.66 us
  transfers between devices with their start and end apart: 2 -> 23, of which waited for: 2 -> 12; matrix products, arithmetic and copies ran while one was open for 0% -> 1% of each run, Pallas kernels for 0% -> 19%
where the time goes in v2:
time: 218 us
  waiting for transfers between devices  124 us (57%)
  Pallas kernels  60.8 us (28%)
  starting transfers between devices  29.2 us (13%)
  local copies, waits for them, and re-layouts  3.43 us (2%)
    ppermute x4, waiting for transfers between devices, line_shards(): returned = lax.ppermute(for_outer[k], 'shard', outwards)  41 us
    pallas_call x2, Pallas kernels, late_products(): pl.pallas_call(functools.partial(late_kernel, count, first, widths), out_...  38.2 us
    ppermute x1, waiting for transfers between devices, line_shards(): from_outer = lax.ppermute(own, 'shard', inwards)  33.4 us
    ppermute x4, waiting for transfers between devices, line_shards(): across = lax.ppermute(onward, 'mat', onward_axis)  22.6 us
    pallas_call x1, Pallas kernels, early_products(): pl.pallas_call(functools.partial(early_kernel, count), out_shape=(jax.Sha...  22.6 us
    ppermute x4, waiting for transfers between devices, line_shards(): by_y = lax.ppermute(mine, 'mat', along_y)  19 us
    ppermute x4, waiting for transfers between devices, swap(): return lax.ppermute(block, 'shard', other_core)  7.5 us
    ppermute x4, starting transfers between devices, line_shards(): by_y = lax.ppermute(mine, 'mat', along_y)  6.14 us
  transfers between devices with their start and end apart: 23, of which 12 were waited for; matrix products, arithmetic and copies ran while one was open for 1% of the time, Pallas kernels for 19%

profile of v2, /device:TPU:0, one launch (start us, length us, event | category | flops | bytes accessed | tf_op | source)
XLA Modules:
  0.0 217.6 jit_solution(8214604339385841970)
XLA Ops:
  0.0 5.0 %collective-permute-start = (bf16[320,2560]{1,0:T(8,128)(2,1)}, bf16[320,2560]{1,0:T(8,128)(2,1)S(1)}, u32[]{:S(2)}, u32[]{:S(2)}) collective-permute-start(bf16[320,2560]{1,0:T(8,128)(2,1)} %bitcast.33), channel_id=1, source_target_pairs={{0,2},{1,3},{6,4},{7,5},{8,10},{9,11},{14,12},{15,13},{16,18},{17,... | collective-permute-start | bytes 4915208 | tf_op jit(solution)/shard_map/ppermute | solution.py:200
  5.0 1.8 collective-permute-start.3
  6.9 33.4 %collective-permute-done.refs_0_ = bf16[320,2560]{1,0:T(8,128)(2,1)S(1)} collective-permute-done((bf16[320,2560]{1,0:T(8,128)(2,1)}, bf16[320,2560]{1,0:T(8,128)(2,1)S(1)}, u32[]{:S(2)}, u32[]{:S(2)}) %collective-permute-start) | collective-permute-done | bytes 1638432 | tf_op jit(solution)/shard_map/ppermute | solution.py:200
  40.3 1.8 collective-permute-start.5
  43.1 5.1 %collective-permute-done.2.refs_3_ = bf16[320,2560]{1,0:T(8,128)(2,1)} collective-permute-done((bf16[320,2560]{1,0:T(8,128)(2,1)}, bf16[320,2560]{1,0:T(8,128)(2,1)}, u32[]{:S(2)}, u32[]{:S(2)}) %collective-permute-start.2) | collective-permute-done | bytes 1638432 | tf_op jit(solution)/shard_map/ppermute | solution.py:205
  48.3 1.7 collective-permute-done.1.refs_2_
  52.1 22.6 %shard_map.17 = (bf16[640,1920]{1,0:T(8,128)(2,1)}, f32[640,2560]{1,0:T(8,128)}) custom-call(bf16[320,2560]{1,0:T(8,128)(2,1)S(1)} %collective-permute-done.refs_0_, bf16[320,2560]{1,0:T(8,128)(2,1)S(1)} %bitcast.36, bf16[320,2560]{1,0:T(8,128)(2,1)S(1)} %collective-permute-done.1.refs_2_, bf16[320,2560]{1,0:T(8,128)(2,1)} %collective-permute-done.2.refs_3_, ...), custom_call_target="tpu_custom_call" | custom-call | flops 12582912000 | bytes 9830400 | tf_op jit(solution)/shard_map/pallas_call | solution.py:79
  74.7 19.1 %shard_map.18 = (bf16[320,512]{1,0:T(8,128)(2,1)S(1)}, bf16[320,512]{1,0:T(8,128)(2,1)S(1)}, bf16[320,768]{1,0:T(8,128)(2,1)S(1)}, bf16[320,768]{1,0:T(8,128)(2,1)S(1)}) custom-call(bf16[320,2560]{1,0:T(8,128)(2,1)S(1)} %collective-permute-done.refs_0_, bf16[320,2560]{1,0:T(8,128)(2,1)S(1)} %bitcast.37, bf16[320,2560]{1,0:T(8,128)(2,1)} %copy-done.1, ...), custom_call_target="tpu_custom_call" | custom-call | flops 10485760000 | bytes 13107200 | tf_op jit(solution)/shard_map/pallas_call | solution.py:166
  99.0 19.1 %shard_map.19 = (bf16[320,512]{1,0:T(8,128)(2,1)S(1)}, bf16[320,512]{1,0:T(8,128)(2,1)S(1)}, bf16[320,768]{1,0:T(8,128)(2,1)S(1)}, bf16[320,768]{1,0:T(8,128)(2,1)S(1)}) custom-call(bf16[320,2560]{1,0:T(8,128)(2,1)S(1)} %collective-permute-done.refs_0_, bf16[320,2560]{1,0:T(8,128)(2,1)S(1)} %bitcast.38, bf16[320,2560]{1,0:T(8,128)(2,1)} %copy-done.1, ...), custom_call_target="tpu_custom_call" | custom-call | flops 10485760000 | bytes 13107200 | tf_op jit(solution)/shard_map/pallas_call | solution.py:166
  118.1 34.5 %collective-permute-done.7 = bf16[320,512]{1,0:T(8,128)(2,1)S(1)} collective-permute-done((bf16[320,512]{1,0:T(8,128)(2,1)S(1)}, bf16[320,512]{1,0:T(8,128)(2,1)S(1)}, u32[]{:S(2)}, u32[]{:S(2)}) %collective-permute-start.7) | collective-permute-done | bytes 327712 | tf_op jit(solution)/shard_map/ppermute | solution.py:221
  153.2 1.6 collective-permute-start.8
  154.8 1.5 collective-permute-start.9
  156.4 6.5 %collective-permute-done.18 = bf16[320,768]{1,0:T(8,128)(2,1)S(1)} collective-permute-done((bf16[320,768]{1,0:T(8,128)(2,1)S(1)}, bf16[320,768]{1,0:T(8,128)(2,1)S(1)}, u32[]{:S(2)}, u32[]{:S(2)}) %collective-permute-start.18) | collective-permute-done | bytes 491552 | tf_op jit(solution)/shard_map/ppermute | solution.py:221
  163.0 1.6 collective-permute-start.13
  166.7 7.0 %collective-permute-done.13 = bf16[320,512]{1,0:T(8,128)(2,1)S(1)} collective-permute-done((bf16[320,512]{1,0:T(8,128)(2,1)S(1)}, bf16[320,512]{1,0:T(8,128)(2,1)S(1)}, u32[]{:S(2)}, u32[]{:S(2)}) %collective-permute-start.13) | collective-permute-done | bytes 327712 | tf_op jit(solution)/shard_map/ppermute | solution.py:226
  173.7 1.5 collective-permute-start.16
  175.2 1.5 collective-permute-start.17
  177.2 3.5 %collective-permute-done.11 = bf16[320,512]{1,0:T(8,128)(2,1)S(1)} collective-permute-done((bf16[320,512]{1,0:T(8,128)(2,1)S(1)}, bf16[320,512]{1,0:T(8,128)(2,1)S(1)}, u32[]{:S(2)}, u32[]{:S(2)}) %collective-permute-start.11) | collective-permute-done | bytes 327712 | tf_op jit(solution)/shard_map/ppermute | solution.py:228
  180.9 11.1 %collective-permute-done.15 = bf16[320,512]{1,0:T(8,128)(2,1)S(1)} collective-permute-done((bf16[320,512]{1,0:T(8,128)(2,1)S(1)}, bf16[320,512]{1,0:T(8,128)(2,1)S(1)}, u32[]{:S(2)}, u32[]{:S(2)}) %collective-permute-start.15) | collective-permute-done | bytes 327712 | tf_op jit(solution)/shard_map/ppermute | solution.py:228
  192.0 1.6 collective-permute-start.20
  193.6 1.5 collective-permute-start.21
  195.7 12.0 %collective-permute-done.21 = bf16[320,768]{1,0:T(8,128)(2,1)S(1)} collective-permute-done((bf16[320,768]{1,0:T(8,128)(2,1)S(1)}, bf16[320,768]{1,0:T(8,128)(2,1)S(1)}, u32[]{:S(2)}, u32[]{:S(2)}) %collective-permute-start.21) | collective-permute-done | bytes 491552 | tf_op jit(solution)/shard_map/ppermute | solution.py:226
  208.3 5.5 %collective-permute-done.19 = bf16[320,768]{1,0:T(8,128)(2,1)S(1)} collective-permute-done((bf16[320,768]{1,0:T(8,128)(2,1)S(1)}, bf16[320,768]{1,0:T(8,128)(2,1)S(1)}, u32[]{:S(2)}, u32[]{:S(2)}) %collective-permute-start.19) | collective-permute-done | bytes 491552 | tf_op jit(solution)/shard_map/ppermute | solution.py:228
  214.0 2.6 %collective-permute-done.22 = bf16[320,768]{1,0:T(8,128)(2,1)S(1)} collective-permute-done((bf16[320,768]{1,0:T(8,128)(2,1)S(1)}, bf16[320,768]{1,0:T(8,128)(2,1)S(1)}, u32[]{:S(2)}, u32[]{:S(2)}) %collective-permute-start.22) | collective-permute-done | bytes 491552 | tf_op jit(solution)/shard_map/ppermute | solution.py:235
  (51 shorter events, 14.2 us)
Async XLA Ops:
  0.0 40.3 %collective-permute-start = (bf16[320,2560]{1,0:T(8,128)(2,1)}, bf16[320,2560]{1,0:T(8,128)(2,1)S(1)}, u32[]{:S(2)}, u32[]{:S(2)}) collective-permute-start(bf16[320,2560]{1,0:T(8,128)(2,1)} %bitcast.33), channel_id=1, source_target_pairs={{0,2},{1,3},{6,4},{7,5},{8,10},{9,11},{14,12},{15,13},{16,18},{17,... | collective-permute-start | bytes 4915208 | tf_op jit(solution)/shard_map/ppermute | solution.py:200
  5.0 37.6 %collective-permute-start.3 = (bf16[320,2560]{1,0:T(8,128)(2,1)}, bf16[320,2560]{1,0:T(8,128)(2,1)}, u32[]{:S(2)}, u32[]{:S(2)}) collective-permute-start(bf16[320,2560]{1,0:T(8,128)(2,1)} %bitcast.34), channel_id=1, source_target_pairs={{2,4},{3,5},{4,2},{5,3},{10,12},{11,13},{12,10},{13,11},{18,20},{1... | collective-permute-start | bytes 4915208 | tf_op jit(solution)/shard_map/ppermute | solution.py:201
  40.3 2.4 %collective-permute-start.5 = (bf16[320,2560]{1,0:T(8,128)(2,1)S(1)}, bf16[320,2560]{1,0:T(8,128)(2,1)}, u32[]{:S(2)}, u32[]{:S(2)}) collective-permute-start(bf16[320,2560]{1,0:T(8,128)(2,1)S(1)} %collective-permute-done.refs_0_), channel_id=1, source_target_pairs={{2,4},{3,5},{4,2},{5,3},{10,12},{11,13},{12,10},{13,11},{18,20},{1... | collective-permute-start | bytes 4915208 | tf_op jit(solution)/shard_map/ppermute | solution.py:202
  42.1 6.2 %collective-permute-start.2 = (bf16[320,2560]{1,0:T(8,128)(2,1)}, bf16[320,2560]{1,0:T(8,128)(2,1)}, u32[]{:S(2)}, u32[]{:S(2)}) collective-permute-start(bf16[320,2560]{1,0:T(8,128)(2,1)} %bitcast.35), channel_id=1, source_target_pairs={{0,1},{1,0},{2,3},{3,2},{4,5},{5,4},{6,7},{7,6},{8,9},{9,8},{10,11... | collective-permute-start | bytes 4915208 | tf_op jit(solution)/shard_map/ppermute | solution.py:205
  42.1 7.8 %collective-permute-start.1 = (bf16[320,2560]{1,0:T(8,128)(2,1)S(1)}, bf16[320,2560]{1,0:T(8,128)(2,1)S(1)}, u32[]{:S(2)}, u32[]{:S(2)}) collective-permute-start(bf16[320,2560]{1,0:T(8,128)(2,1)S(1)} %collective-permute-done.refs_0_), channel_id=1, source_target_pairs={{0,1},{1,0},{2,3},{3,2},{4,5},{5,4},{6,7},{7,6},{8,9},{9,8},{10,11... | collective-permute-start | bytes 4915208 | tf_op jit(solution)/shard_map/ppermute | solution.py:205
  42.6 8.0 %collective-permute-start.4 = (bf16[320,2560]{1,0:T(8,128)(2,1)}, bf16[320,2560]{1,0:T(8,128)(2,1)}, u32[]{:S(2)}, u32[]{:S(2)}) collective-permute-start(bf16[320,2560]{1,0:T(8,128)(2,1)} %collective-permute-done.3.refs_4_), channel_id=1, source_target_pairs={{0,1},{1,0},{2,3},{3,2},{4,5},{5,4},{6,7},{7,6},{8,9},{9,8},{10,11... | collective-permute-start | bytes 4915208 | tf_op jit(solution)/shard_map/ppermute | solution.py:205
  42.6 32.1 %collective-permute-start.6 = (bf16[320,2560]{1,0:T(8,128)(2,1)}, bf16[320,2560]{1,0:T(8,128)(2,1)}, u32[]{:S(2)}, u32[]{:S(2)}) collective-permute-start(bf16[320,2560]{1,0:T(8,128)(2,1)} %collective-permute-done.5.refs_6_), channel_id=1, source_target_pairs={{0,1},{1,0},{2,3},{3,2},{4,5},{5,4},{6,7},{7,6},{8,9},{9,8},{10,11... | collective-permute-start | bytes 4915208 | tf_op jit(solution)/shard_map/ppermute | solution.py:205
  49.9 24.8 %copy-start.1 = (bf16[320,2560]{1,0:T(8,128)(2,1)}, bf16[320,2560]{1,0:T(8,128)(2,1)S(1)}, u32[]{:S(2)}) copy-start(bf16[320,2560]{1,0:T(8,128)(2,1)S(1)} %collective-permute-done.1.refs_2_) | copy-start | bytes 4915204
  93.8 62.5 %collective-permute-start.14 = (bf16[320,768]{1,0:T(8,128)(2,1)S(1)}, bf16[320,768]{1,0:T(8,128)(2,1)S(1)}, u32[]{:S(2)}, u32[]{:S(2)}) collective-permute-start(bf16[320,768]{1,0:T(8,128)(2,1)S(1)} %get-tuple-element.29), channel_id=1, source_target_pairs={{2,0},{3,1},{4,6},{5,7},{10,8},{11,9},{12,14},{13,15},{18,16},{19,... | collective-permute-start | bytes 1474568 | tf_op jit(solution)/shard_map/ppermute | solution.py:221
  95.1 61.2 %collective-permute-start.10 = (bf16[320,512]{1,0:T(8,128)(2,1)S(1)}, bf16[320,512]{1,0:T(8,128)(2,1)S(1)}, u32[]{:S(2)}, u32[]{:S(2)}) collective-permute-start(bf16[320,512]{1,0:T(8,128)(2,1)S(1)} %get-tuple-element.25), channel_id=1, source_target_pairs={{2,0},{3,1},{4,6},{5,7},{10,8},{11,9},{12,14},{13,15},{18,16},{19,... | collective-permute-start | bytes 983048 | tf_op jit(solution)/shard_map/ppermute | solution.py:221
  96.4 56.2 %collective-permute-start.7 = (bf16[320,512]{1,0:T(8,128)(2,1)S(1)}, bf16[320,512]{1,0:T(8,128)(2,1)S(1)}, u32[]{:S(2)}, u32[]{:S(2)}) collective-permute-start(bf16[320,512]{1,0:T(8,128)(2,1)S(1)} %get-tuple-element.23), channel_id=1, source_target_pairs={{2,0},{3,1},{4,6},{5,7},{10,8},{11,9},{12,14},{13,15},{18,16},{19,... | collective-permute-start | bytes 983048 | tf_op jit(solution)/shard_map/ppermute | solution.py:221
  97.7 65.2 %collective-permute-start.18 = (bf16[320,768]{1,0:T(8,128)(2,1)S(1)}, bf16[320,768]{1,0:T(8,128)(2,1)S(1)}, u32[]{:S(2)}, u32[]{:S(2)}) collective-permute-start(bf16[320,768]{1,0:T(8,128)(2,1)S(1)} %get-tuple-element.33), channel_id=1, source_target_pairs={{2,0},{3,1},{4,6},{5,7},{10,8},{11,9},{12,14},{13,15},{18,16},{19,... | collective-permute-start | bytes 1474568 | tf_op jit(solution)/shard_map/ppermute | solution.py:221
  153.2 9.8 %collective-permute-start.8 = (bf16[320,512]{1,0:T(8,128)(2,1)S(1)}, bf16[320,512]{1,0:T(8,128)(2,1)S(1)}, u32[]{:S(2)}, u32[]{:S(2)}) collective-permute-start(bf16[320,512]{1,0:T(8,128)(2,1)S(1)} %get-tuple-element.38), channel_id=1, source_target_pairs={{0,8},{8,0},{16,24},{24,16},{1,9},{9,1},{17,25},{25,17},{2,10},{10... | collective-permute-start | bytes 983048 | tf_op jit(solution)/shard_map/ppermute | solution.py:225
  154.8 11.8 %collective-permute-start.9 = (bf16[320,512]{1,0:T(8,128)(2,1)S(1)}, bf16[320,512]{1,0:T(8,128)(2,1)S(1)}, u32[]{:S(2)}, u32[]{:S(2)}) collective-permute-start(bf16[320,512]{1,0:T(8,128)(2,1)S(1)} %get-tuple-element.38), channel_id=1, source_target_pairs={{0,16},{8,24},{16,0},{24,8},{1,17},{9,25},{17,1},{25,9},{2,18},{10... | collective-permute-start | bytes 983048 | tf_op jit(solution)/shard_map/ppermute | solution.py:226
  163.0 10.7 %collective-permute-start.13 = (bf16[320,512]{1,0:T(8,128)(2,1)S(1)}, bf16[320,512]{1,0:T(8,128)(2,1)S(1)}, u32[]{:S(2)}, u32[]{:S(2)}) collective-permute-start(bf16[320,512]{1,0:T(8,128)(2,1)S(1)} %broadcast_select_fusion.2), channel_id=1, source_target_pairs={{0,16},{8,24},{16,0},{24,8},{1,17},{9,25},{17,1},{25,9},{2,18},{10... | collective-permute-start | bytes 983048 | tf_op jit(solution)/shard_map/ppermute | solution.py:226
  164.6 16.1 %collective-permute-start.12 = (bf16[320,512]{1,0:T(8,128)(2,1)S(1)}, bf16[320,512]{1,0:T(8,128)(2,1)S(1)}, u32[]{:S(2)}, u32[]{:S(2)}) collective-permute-start(bf16[320,512]{1,0:T(8,128)(2,1)S(1)} %broadcast_select_fusion.2), channel_id=1, source_target_pairs={{0,8},{8,0},{16,24},{24,16},{1,9},{9,1},{17,25},{25,17},{2,10},{10... | collective-permute-start | bytes 983048 | tf_op jit(solution)/shard_map/ppermute | solution.py:225
  166.1 14.6 %collective-permute-start.11 = (bf16[320,512]{1,0:T(8,128)(2,1)S(1)}, bf16[320,512]{1,0:T(8,128)(2,1)S(1)}, u32[]{:S(2)}, u32[]{:S(2)}) collective-permute-start(bf16[320,512]{1,0:T(8,128)(2,1)S(1)} %collective-permute-done.8), channel_id=1, source_target_pairs={{0,16},{8,24},{16,0},{24,8},{1,17},{9,25},{17,1},{25,9},{2,18},{10... | collective-permute-start | bytes 983048 | tf_op jit(solution)/shard_map/ppermute | solution.py:228
  173.7 18.3 %collective-permute-start.16 = (bf16[320,768]{1,0:T(8,128)(2,1)S(1)}, bf16[320,768]{1,0:T(8,128)(2,1)S(1)}, u32[]{:S(2)}, u32[]{:S(2)}) collective-permute-start(bf16[320,768]{1,0:T(8,128)(2,1)S(1)} %broadcast_select_fusion.1), channel_id=1, source_target_pairs={{0,8},{8,0},{16,24},{24,16},{1,9},{9,1},{17,25},{25,17},{2,10},{10... | collective-permute-start | bytes 1474568 | tf_op jit(solution)/shard_map/ppermute | solution.py:225
  175.2 20.5 %collective-permute-start.17 = (bf16[320,768]{1,0:T(8,128)(2,1)S(1)}, bf16[320,768]{1,0:T(8,128)(2,1)S(1)}, u32[]{:S(2)}, u32[]{:S(2)}) collective-permute-start(bf16[320,768]{1,0:T(8,128)(2,1)S(1)} %broadcast_select_fusion.1), channel_id=1, source_target_pairs={{0,16},{8,24},{16,0},{24,8},{1,17},{9,25},{17,1},{25,9},{2,18},{10... | collective-permute-start | bytes 1474568 | tf_op jit(solution)/shard_map/ppermute | solution.py:226
  176.7 15.2 %collective-permute-start.15 = (bf16[320,512]{1,0:T(8,128)(2,1)S(1)}, bf16[320,512]{1,0:T(8,128)(2,1)S(1)}, u32[]{:S(2)}, u32[]{:S(2)}) collective-permute-start(bf16[320,512]{1,0:T(8,128)(2,1)S(1)} %collective-permute-done.13), channel_id=1, source_target_pairs={{0,8},{8,0},{16,24},{24,16},{1,9},{9,1},{17,25},{25,17},{2,10},{10... | collective-permute-start | bytes 983048 | tf_op jit(solution)/shard_map/ppermute | solution.py:228
  192.0 21.9 %collective-permute-start.20 = (bf16[320,768]{1,0:T(8,128)(2,1)S(1)}, bf16[320,768]{1,0:T(8,128)(2,1)S(1)}, u32[]{:S(2)}, u32[]{:S(2)}) collective-permute-start(bf16[320,768]{1,0:T(8,128)(2,1)S(1)} %broadcast_select_fusion), channel_id=1, source_target_pairs={{0,8},{8,0},{16,24},{24,16},{1,9},{9,1},{17,25},{25,17},{2,10},{10... | collective-permute-start | bytes 1474568 | tf_op jit(solution)/shard_map/ppermute | solution.py:225
  193.6 14.2 %collective-permute-start.21 = (bf16[320,768]{1,0:T(8,128)(2,1)S(1)}, bf16[320,768]{1,0:T(8,128)(2,1)S(1)}, u32[]{:S(2)}, u32[]{:S(2)}) collective-permute-start(bf16[320,768]{1,0:T(8,128)(2,1)S(1)} %broadcast_select_fusion), channel_id=1, source_target_pairs={{0,16},{8,24},{16,0},{24,8},{1,17},{9,25},{17,1},{25,9},{2,18},{10... | collective-permute-start | bytes 1474568 | tf_op jit(solution)/shard_map/ppermute | solution.py:226
  195.1 18.7 %collective-permute-start.19 = (bf16[320,768]{1,0:T(8,128)(2,1)S(1)}, bf16[320,768]{1,0:T(8,128)(2,1)S(1)}, u32[]{:S(2)}, u32[]{:S(2)}) collective-permute-start(bf16[320,768]{1,0:T(8,128)(2,1)S(1)} %collective-permute-done.16), channel_id=1, source_target_pairs={{0,16},{8,24},{16,0},{24,8},{1,17},{9,25},{17,1},{25,9},{2,18},{10... | collective-permute-start | bytes 1474568 | tf_op jit(solution)/shard_map/ppermute | solution.py:228
  207.7 8.8 %collective-permute-start.22 = (bf16[320,768]{1,0:T(8,128)(2,1)S(1)}, bf16[320,768]{1,0:T(8,128)(2,1)S(1)}, u32[]{:S(2)}, u32[]{:S(2)}) collective-permute-start(bf16[320,768]{1,0:T(8,128)(2,1)S(1)} %collective-permute-done.21), channel_id=1, source_target_pairs={{0,8},{8,0},{16,24},{24,16},{1,9},{9,1},{17,25},{25,17},{2,10},{10... | collective-permute-start | bytes 1474568 | tf_op jit(solution)/shard_map/ppermute | solution.py:235
  (2 other events, 4.2 us)

commit v3 on v2

v3 whole, which is shorter than its diff:
```python
import functools

import jax
import jax.numpy as jnp
from jax import lax
from jax.experimental import pallas as pl
from jax.experimental.pallas import tpu as pltpu
from jax.sharding import PartitionSpec as P

coef_a = 3.4445
coef_b = -4.775
coef_c = 2.0315

TILE = 1280
VMEM_LIMIT = 48 * 1024 * 1024


def dot_t(left, right):
    return lax.dot_general(
        left, right, (((1,), (1,)), ((), ())), preferred_element_type=jnp.float32
    )


def dot(left, right):
    return jnp.dot(left, right, preferred_element_type=jnp.float32)


def general_shards(iterate):
    own = iterate[0]
    gathered = lax.all_gather(own, "shard", axis=0, tiled=True)
    gram = dot_t(own, gathered).astype(jnp.bfloat16)
    cubic = dot(gram, gathered).astype(jnp.bfloat16)
    squared = dot_t(cubic, gathered)
    polynomial = (coef_b * gram.astype(jnp.float32) + coef_c * squared).astype(jnp.bfloat16)
    product = dot(polynomial, gathered)
    next_rows = (coef_a * own.astype(jnp.float32) + product).astype(jnp.bfloat16)
    return lax.all_gather(next_rows[None], "mat", axis=0, tiled=True)


def tiles(start, stop):
    return [pl.ds(at, min(TILE, stop - at)) for at in range(start, stop, TILE)]


def early_kernel(count, *refs):
    inner, blocks, (gram, cubic, whole, sems) = refs[0], refs[1 : count + 1], refs[count + 1 :]
    rows, columns = blocks[0].shape

    @pl.when(inner[0] != 0)
    def _():
        copies = []
        for k, block in enumerate(blocks):
            target = whole.at[pl.ds(k * rows, rows), :]
            copy = pltpu.make_async_copy(block, target, sems.at[k])
            copy.start()
            copies.append(copy)
        for copy in copies:
            copy.wait()
        for at in tiles(0, count * rows):
            gram[:, at] = dot_t(whole[: 2 * rows, :], whole[at, :]).astype(jnp.bfloat16)
        for at in tiles(0, columns):
            cubic[:, at] = dot(gram[...], whole[:, at])


def early_products(inner, blocks):
    count = len(blocks)
    rows, columns = blocks[0].shape
    known = count * rows
    return pl.pallas_call(
        functools.partial(early_kernel, count),
        out_shape=(
            jax.ShapeDtypeStruct((2 * rows, known), jnp.bfloat16),
            jax.ShapeDtypeStruct((2 * rows, columns), jnp.float32),
        ),
        in_specs=[pl.BlockSpec(memory_space=pltpu.SMEM)]
        + [pl.BlockSpec(memory_space=pl.ANY)] * count,
        out_specs=(pl.BlockSpec(memory_space=pltpu.VMEM),) * 2,
        scratch_shapes=[
            pltpu.VMEM((known, columns), jnp.bfloat16),
            pltpu.SemaphoreType.DMA((count,)),
        ],
        compiler_params=pltpu.CompilerParams(vmem_limit_bytes=VMEM_LIMIT),
        cost_estimate=pl.CostEstimate(
            flops=8 * rows * known * columns, bytes_accessed=2 * known * columns, transcendentals=0
        ),
    )(inner, *blocks)


def late_kernel(count, first, widths, *refs):
    inner, refs = refs[0], refs[1:]
    blocks, gram_in, cubic_in = refs[:count], refs[count], refs[count + 1]
    outs = refs[count + 2 : count + 2 + len(widths)]
    whole, gram, cubic_sum, cubic, poly, sems = refs[count + 2 + len(widths) :]
    rows, columns = blocks[0].shape
    known = (count - 2) * rows
    mine = pl.ds(first * rows, rows)
    late = pl.ds(known, 2 * rows)

    @pl.when(inner[0] != 0)
    def _():
        copies = {}

        def fetch(name, source, target):
            copies[name] = pltpu.make_async_copy(source, target, sems.at[len(copies)])
            copies[name].start()

        def fetch_block(k):
            if k not in copies:
                fetch(k, blocks[k], whole.at[pl.ds(k * rows, rows), :])

        fetch_block(count - 2)
        fetch_block(count - 1)
        fetch_block(first)
        fetch("gram", gram_in.at[mine, :], gram.at[:, pl.ds(0, known)])
        fetch("cubic", cubic_in.at[mine, :], cubic_sum)
        for k in range(count):
            fetch_block(k)

        for name in (count - 2, count - 1, first, "gram"):
            copies[name].wait()
        gram[:, late] = dot_t(whole[mine, :], whole[late, :]).astype(jnp.bfloat16)
        copies["cubic"].wait()
        for at in tiles(0, columns):
            add = dot(gram[:, late], whole[late, at])
            cubic[:, at] = (cubic_sum[:, at] + add).astype(jnp.bfloat16)

        for k in range(count - 2):
            if k != first:
                copies[k].wait()
        for at in tiles(0, count * rows):
            squared = dot_t(cubic[...], whole[at, :])
            poly[:, at] = (coef_b * gram[:, at].astype(jnp.float32) + coef_c * squared).astype(
                jnp.bfloat16
            )

        begin = 0
        for out, width in zip(outs, widths):
            at = pl.ds(begin, width)
            product = dot(poly[...], whole[:, at])
            base = whole[mine, at].astype(jnp.float32)
            out[...] = (coef_a * base + product).astype(jnp.bfloat16)
            begin += width


def late_products(inner, blocks, gram, cubic, first, widths):
    count = len(blocks)
    rows, columns = blocks[0].shape
    total = count * rows
    return pl.pallas_call(
        functools.partial(late_kernel, count, first, widths),
        out_shape=tuple(jax.ShapeDtypeStruct((rows, w), jnp.bfloat16) for w in widths),
        in_specs=[pl.BlockSpec(memory_space=pltpu.SMEM)]
        + [pl.BlockSpec(memory_space=pl.ANY)] * (count + 2),
        out_specs=tuple(pl.BlockSpec(memory_space=pltpu.VMEM) for _ in widths),
        scratch_shapes=[
            pltpu.VMEM((total, columns), jnp.bfloat16),
            pltpu.VMEM((rows, total), jnp.bfloat16),
            pltpu.VMEM((rows, columns), jnp.float32),
            pltpu.VMEM((rows, columns), jnp.bfloat16),
            pltpu.VMEM((rows, total), jnp.bfloat16),
            pltpu.SemaphoreType.DMA((count + 2,)),
        ],
        compiler_params=pltpu.CompilerParams(vmem_limit_bytes=VMEM_LIMIT),
        cost_estimate=pl.CostEstimate(
            flops=5 * rows * total * columns, bytes_accessed=2 * total * columns, transcendentals=0
        ),
    )(inner, *blocks, gram, cubic)


def line_shards(iterate, widths):
    own = iterate[0]
    rows, columns = own.shape
    place = lax.axis_index("shard") // 2
    outer = (place == 0) | (place == 3)
    mat = lax.axis_index("mat")

    inner = jnp.where(outer, 0, 1).astype(jnp.int32)[None]
    tie = lax.optimization_barrier

    other_core = [(2, 3), (3, 2), (4, 5), (5, 4)]
    inwards = [(0, 2), (1, 3), (6, 4), (7, 5)]
    outwards = [(b, a) for a, b in inwards]
    middle = [(2, 4), (3, 5), (4, 2), (5, 3)]
    along_x = [(m, m ^ 1) for m in range(4)]
    along_y = [(m, m ^ 2) for m in range(4)]

    from_outer = lax.ppermute(own, "shard", inwards)
    from_inner = lax.ppermute(own, "shard", middle)
    from_far = lax.ppermute(from_outer, "shard", middle)

    def swap(block):
        return lax.ppermute(block, "shard", other_core)

    early = [from_outer, own, swap(from_outer), swap(own), from_inner, swap(from_inner)]
    gram, cubic = early_products(inner, early)
    from_far, gram, cubic = tie((from_far, gram, cubic))
    blocks = early + [from_far, swap(from_far)]
    for_outer = list(late_products(inner, blocks, gram, cubic, 0, widths))
    for_own = list(late_products(inner, blocks, gram, cubic, 1, widths))
    for_outer[2], for_outer[3], for_own[0] = tie((for_outer[2], for_outer[3], for_own[0]))

    result = jnp.zeros((4, rows, columns), jnp.bfloat16)

    def place_in(result, flip, at, part):
        return lax.dynamic_update_slice(result, part[None], (mat ^ flip, 0, at))

    begins = [sum(widths[:k]) for k in range(len(widths))]
    first_hop = []

    def send_corner(k):
        by_x, by_y = first_hop[k]
        return lax.ppermute(*((by_x, "mat", along_y) if k % 2 == 0 else (by_y, "mat", along_x)))

    for k in range(len(widths)):
        returned = lax.ppermute(for_outer[k], "shard", outwards)
        here, returned = tie((outer, returned))
        mine = jnp.where(here, returned, for_own[k])
        if k >= 2:
            by_x, by_y = first_hop[k - 2]
            if k % 2 == 0:
                mine, by_x = tie((mine, by_x))
            else:
                mine, by_y = tie((mine, by_y))
            first_hop[k - 2] = (by_x, by_y)
        first_hop.append((lax.ppermute(mine, "mat", along_x), lax.ppermute(mine, "mat", along_y)))
        result = place_in(result, 0, begins[k], mine)
    corners = [send_corner(k) for k in range(len(widths))]
    for k in range(len(widths)):
        by_x, by_y = first_hop[k]
        for flip, part in ((1, by_x), (2, by_y), (3, corners[k])):
            result = place_in(result, flip, begins[k], part)
    return result


def solution(mesh):
    if (mesh.shape["mat"], mesh.shape["shard"]) == (4, 8):
        def shards(iterate):
            return line_shards(iterate, widths=(512, 512, 768, 768))
    else:
        shards = general_shards
    return jax.shard_map(
        shards,
        mesh=mesh,
        in_specs=(P("mat", "shard", None),),
        out_specs=P(None, "shard", None),
        check_vma=False,
    )
```

time: 218 us -> 196 us (0.90)
  Pallas kernels: 60.8 us -> 4.06 us
  waiting for transfers between devices: 124 us -> 148 us
  starting transfers between devices: 29.2 us -> 34.3 us
  local copies, waits for them, and re-layouts: 3.43 us -> 8.47 us
    ppermute x4, waiting for transfers between devices: 41 us -> 81.9 us  [line_shards(): returned = lax.ppermute(for_outer[k], 'shard', outwards)]
    pallas_call x2, Pallas kernels: 38.2 us -> 0.41 us  [late_products(): pl.pallas_call(functools.partial(late_kernel, count, first, widths), out_...]
    pallas_call x1, Pallas kernels: 22.6 us -> 3.65 us  [early_products(): pl.pallas_call(functools.partial(early_kernel, count), out_shape=(jax.Sha...]
    ppermute x4, waiting for transfers between devices: 7.5 us -> 0.01 us  [swap(): return lax.ppermute(block, 'shard', other_core)]
    ppermute x12, waiting for transfers between devices: 41.7 us -> 34.8 us  [the longest x4 32.8 us: send_corner(): lax.ppermute(*((by_x, 'mat', along_y) if k % 2 == 0 else (by_y, 'mat', al...]
    ppermute x4, starting transfers between devices: 1.02 us -> 6.38 us  [swap(): return lax.ppermute(block, 'shard', other_core)]
    unnamed x6 -> x10, local copies, waits for them, and re-layouts: 1.66 us -> 6.74 us
  transfers between devices with their start and end apart: 23 -> 23, of which waited for: 12 -> 10; matrix products, arithmetic and copies ran while one was open for 1% -> 1% of each run, Pallas kernels for 19% -> 2%
where the time goes in v3:
time: 196 us
  waiting for transfers between devices  148 us (76%)
  starting transfers between devices  34.3 us (17%)
  local copies, waits for them, and re-layouts  8.47 us (4%)
  Pallas kernels  4.06 us (2%)
    ppermute x4, waiting for transfers between devices, line_shards(): returned = lax.ppermute(for_outer[k], 'shard', outwards)  81.9 us
    ppermute x4, waiting for transfers between devices, send_corner(): lax.ppermute(*((by_x, 'mat', along_y) if k % 2 == 0 else (by_y, 'mat', al...  32.8 us
    ppermute x1, waiting for transfers between devices, line_shards(): from_outer = lax.ppermute(own, 'shard', inwards)  31.6 us
    unnamed x10, local copies, waits for them, and re-layouts  6.74 us
    ppermute x4, starting transfers between devices, swap(): return lax.ppermute(block, 'shard', other_core)  6.38 us
    ppermute x4, starting transfers between devices, line_shards(): lax.ppermute(mine, 'mat', along_y)  6.16 us
    ppermute x4, starting transfers between devices, line_shards(): lax.ppermute(mine, 'mat', along_x)  5.21 us
    ppermute x4, starting transfers between devices, line_shards(): returned = lax.ppermute(for_outer[k], 'shard', outwards)  5.17 us
  transfers between devices with their start and end apart: 23, of which 10 were waited for; matrix products, arithmetic and copies ran while one was open for 1% of the time, Pallas kernels for 2%

profile of v3, /device:TPU:0, one launch (start us, length us, event | category | flops | bytes accessed | tf_op | source)
XLA Modules:
  0.0 195.7 jit_solution(16316085211177569433)
XLA Ops:
  0.0 5.0 %collective-permute-start = (bf16[320,2560]{1,0:T(8,128)(2,1)}, bf16[320,2560]{1,0:T(8,128)(2,1)S(1)}, u32[]{:S(2)}, u32[]{:S(2)}) collective-permute-start(bf16[320,2560]{1,0:T(8,128)(2,1)} %bitcast.34), channel_id=1, source_target_pairs={{0,2},{1,3},{6,4},{7,5},{8,10},{9,11},{14,12},{15,13},{16,18},{17,... | collective-permute-start | bytes 4915208 | tf_op jit(solution)/shard_map/ppermute | solution.py:186
  5.0 1.8 collective-permute-start.3
  6.9 1.8 collective-permute-start.2
  8.7 31.6 %collective-permute-done.refs_1_ = bf16[320,2560]{1,0:T(8,128)(2,1)S(1)} collective-permute-done((bf16[320,2560]{1,0:T(8,128)(2,1)}, bf16[320,2560]{1,0:T(8,128)(2,1)S(1)}, u32[]{:S(2)}, u32[]{:S(2)}) %collective-permute-start) | collective-permute-done | bytes 1638432 | tf_op jit(solution)/shard_map/ppermute | solution.py:186
  41.1 1.9 collective-permute-start.4
  43.0 1.8 collective-permute-start.5
  48.8 3.7 %shard_map.17 = (bf16[640,1920]{1,0:T(8,128)(2,1)}, f32[640,2560]{1,0:T(8,128)}) custom-call(s32[1]{0:T(128)} %bitcast.refs_0_, bf16[320,2560]{1,0:T(8,128)(2,1)S(1)} %collective-permute-done.refs_1_, bf16[320,2560]{1,0:T(8,128)(2,1)S(1)} %bitcast.37, bf16[320,2560]{1,0:T(8,128)(2,1)S(1)} %copy-done.3, bf16[320,2560]{1,0:T(8,128)(2,1)} %collective-permute-done.2.refs_4_, ...), custom_call_target="tpu_custom_call" | custom-call | flops 12582912000 | bytes 9830400 | tf_op jit(solution)/shard_map/pallas_call | solution.py:68
  52.5 1.9 collective-permute-start.6
  60.0 57.3 %collective-permute-done.7 = bf16[320,512]{1,0:T(8,128)(2,1)S(1)} collective-permute-done((bf16[320,512]{1,0:T(8,128)(2,1)S(1)}, bf16[320,512]{1,0:T(8,128)(2,1)S(1)}, u32[]{:S(2)}, u32[]{:S(2)}) %collective-permute-start.7) | collective-permute-done | bytes 327712 | tf_op jit(solution)/shard_map/ppermute | solution.py:214
  117.9 1.6 collective-permute-start.10
  119.5 1.5 collective-permute-start.13
  121.0 2.9 %collective-permute-done.8 = bf16[320,512]{1,0:T(8,128)(2,1)S(1)} collective-permute-done((bf16[320,512]{1,0:T(8,128)(2,1)S(1)}, bf16[320,512]{1,0:T(8,128)(2,1)S(1)}, u32[]{:S(2)}, u32[]{:S(2)}) %collective-permute-start.8) | collective-permute-done | bytes 327712 | tf_op jit(solution)/shard_map/ppermute | solution.py:214
  123.9 1.6 collective-permute-start.12
  125.5 13.2 %collective-permute-done.11 = bf16[320,768]{1,0:T(8,128)(2,1)S(1)} collective-permute-done((bf16[320,768]{1,0:T(8,128)(2,1)S(1)}, bf16[320,768]{1,0:T(8,128)(2,1)S(1)}, u32[]{:S(2)}, u32[]{:S(2)}) %collective-permute-start.11) | collective-permute-done | bytes 491552 | tf_op jit(solution)/shard_map/ppermute | solution.py:214
  140.3 8.5 %collective-permute-done.9 = bf16[320,768]{1,0:T(8,128)(2,1)S(1)} collective-permute-done((bf16[320,768]{1,0:T(8,128)(2,1)S(1)}, bf16[320,768]{1,0:T(8,128)(2,1)S(1)}, u32[]{:S(2)}, u32[]{:S(2)}) %collective-permute-start.9) | collective-permute-done | bytes 491552 | tf_op jit(solution)/shard_map/ppermute | solution.py:214
  148.8 1.5 collective-permute-start.17
  150.4 1.5 collective-permute-start.18
  153.2 16.6 %collective-permute-done.14 = bf16[320,512]{1,0:T(8,128)(2,1)S(1)} collective-permute-done((bf16[320,512]{1,0:T(8,128)(2,1)S(1)}, bf16[320,512]{1,0:T(8,128)(2,1)S(1)}, u32[]{:S(2)}, u32[]{:S(2)}) %collective-permute-start.14) | collective-permute-done | bytes 327712 | tf_op jit(solution)/shard_map/ppermute | solution.py:211
  169.9 1.5 collective-permute-start.21
  172.1 7.1 %collective-permute-done.16 = bf16[320,512]{1,0:T(8,128)(2,1)S(1)} collective-permute-done((bf16[320,512]{1,0:T(8,128)(2,1)S(1)}, bf16[320,512]{1,0:T(8,128)(2,1)S(1)}, u32[]{:S(2)}, u32[]{:S(2)}) %collective-permute-start.16) | collective-permute-done | bytes 327712 | tf_op jit(solution)/shard_map/ppermute | solution.py:211
  179.3 1.5 collective-permute-start.19
  180.8 2.0 %collective-permute-done.21 = bf16[320,768]{1,0:T(8,128)(2,1)S(1)} collective-permute-done((bf16[320,768]{1,0:T(8,128)(2,1)S(1)}, bf16[320,768]{1,0:T(8,128)(2,1)S(1)}, u32[]{:S(2)}, u32[]{:S(2)}) %collective-permute-start.21) | collective-permute-done | bytes 491552 | tf_op jit(solution)/shard_map/ppermute | solution.py:224
  182.9 9.0 %collective-permute-done.19 = bf16[320,768]{1,0:T(8,128)(2,1)S(1)} collective-permute-done((bf16[320,768]{1,0:T(8,128)(2,1)S(1)}, bf16[320,768]{1,0:T(8,128)(2,1)S(1)}, u32[]{:S(2)}, u32[]{:S(2)}) %collective-permute-start.19) | collective-permute-done | bytes 491552 | tf_op jit(solution)/shard_map/ppermute | solution.py:211
  192.1 2.7 %copy-done.4 = bf16[4,320,2560]{2,1,0:T(8,128)(2,1)} copy-done((bf16[4,320,2560]{2,1,0:T(8,128)(2,1)}, bf16[4,320,2560]{2,1,0:T(8,128)(2,1)S(1)}, u32[]{:S(2)}) %copy-start.4) | copy-done | bytes 6553624
  (54 shorter events, 15.8 us)
Async XLA Ops:
  0.0 40.3 %collective-permute-start = (bf16[320,2560]{1,0:T(8,128)(2,1)}, bf16[320,2560]{1,0:T(8,128)(2,1)S(1)}, u32[]{:S(2)}, u32[]{:S(2)}) collective-permute-start(bf16[320,2560]{1,0:T(8,128)(2,1)} %bitcast.34), channel_id=1, source_target_pairs={{0,2},{1,3},{6,4},{7,5},{8,10},{9,11},{14,12},{15,13},{16,18},{17,... | collective-permute-start | bytes 4915208 | tf_op jit(solution)/shard_map/ppermute | solution.py:186
  5.0 36.0 %collective-permute-start.3 = (bf16[320,2560]{1,0:T(8,128)(2,1)}, bf16[320,2560]{1,0:T(8,128)(2,1)}, u32[]{:S(2)}, u32[]{:S(2)}) collective-permute-start(bf16[320,2560]{1,0:T(8,128)(2,1)} %bitcast.35), channel_id=1, source_target_pairs={{2,4},{3,5},{4,2},{5,3},{10,12},{11,13},{12,10},{13,11},{18,20},{1... | collective-permute-start | bytes 4915208 | tf_op jit(solution)/shard_map/ppermute | solution.py:187
  6.9 37.9 %collective-permute-start.2 = (bf16[320,2560]{1,0:T(8,128)(2,1)}, bf16[320,2560]{1,0:T(8,128)(2,1)}, u32[]{:S(2)}, u32[]{:S(2)}) collective-permute-start(bf16[320,2560]{1,0:T(8,128)(2,1)} %bitcast.36), channel_id=1, source_target_pairs={{2,3},{3,2},{4,5},{5,4},{10,11},{11,10},{12,13},{13,12},{18,19},{1... | collective-permute-start | bytes 4915208 | tf_op jit(solution)/shard_map/ppermute | solution.py:191
  40.3 4.5 %collective-permute-start.1 = (bf16[320,2560]{1,0:T(8,128)(2,1)S(1)}, bf16[320,2560]{1,0:T(8,128)(2,1)S(1)}, u32[]{:S(2)}, u32[]{:S(2)}) collective-permute-start(bf16[320,2560]{1,0:T(8,128)(2,1)S(1)} %collective-permute-done.refs_1_), channel_id=1, source_target_pairs={{2,3},{3,2},{4,5},{5,4},{10,11},{11,10},{12,13},{13,12},{18,19},{1... | collective-permute-start | bytes 4915208 | tf_op jit(solution)/shard_map/ppermute | solution.py:191
  41.1 4.9 %collective-permute-start.4 = (bf16[320,2560]{1,0:T(8,128)(2,1)}, bf16[320,2560]{1,0:T(8,128)(2,1)}, u32[]{:S(2)}, u32[]{:S(2)}) collective-permute-start(bf16[320,2560]{1,0:T(8,128)(2,1)} %collective-permute-done.3.refs_5_), channel_id=1, source_target_pairs={{2,3},{3,2},{4,5},{5,4},{10,11},{11,10},{12,13},{13,12},{18,19},{1... | collective-permute-start | bytes 4915208 | tf_op jit(solution)/shard_map/ppermute | solution.py:191
  43.0 9.5 %collective-permute-start.5 = (bf16[320,2560]{1,0:T(8,128)(2,1)S(1)}, bf16[320,2560]{1,0:T(8,128)(2,1)}, u32[]{:S(2)}, u32[]{:S(2)}) collective-permute-start(bf16[320,2560]{1,0:T(8,128)(2,1)S(1)} %collective-permute-done.refs_1_), channel_id=1, source_target_pairs={{2,4},{3,5},{4,2},{5,3},{10,12},{11,13},{12,10},{13,11},{18,20},{1... | collective-permute-start | bytes 4915208 | tf_op jit(solution)/shard_map/ppermute | solution.py:188
  48.8 5.5 %copy-start.1 = (bf16[1,320,2560]{2,1,0:T(8,128)(2,1)S(1)}, bf16[1,320,2560]{2,1,0:T(8,128)(2,1)}, u32[]{:S(2)}) copy-start(bf16[1,320,2560]{2,1,0:T(8,128)(2,1)} %param.1) | copy-start | bytes 4915204
  52.5 1.9 collective-permute-start.6
  54.5 62.8 %collective-permute-start.7 = (bf16[320,512]{1,0:T(8,128)(2,1)S(1)}, bf16[320,512]{1,0:T(8,128)(2,1)S(1)}, u32[]{:S(2)}, u32[]{:S(2)}) collective-permute-start(bf16[320,512]{1,0:T(8,128)(2,1)S(1)} %get-tuple-element.38), channel_id=1, source_target_pairs={{2,0},{3,1},{4,6},{5,7},{10,8},{11,9},{12,14},{13,15},{18,16},{19,... | collective-permute-start | bytes 983048 | tf_op jit(solution)/shard_map/ppermute | solution.py:214
  55.8 68.0 %collective-permute-start.8 = (bf16[320,512]{1,0:T(8,128)(2,1)S(1)}, bf16[320,512]{1,0:T(8,128)(2,1)S(1)}, u32[]{:S(2)}, u32[]{:S(2)}) collective-permute-start(bf16[320,512]{1,0:T(8,128)(2,1)S(1)} %get-tuple-element.45), channel_id=1, source_target_pairs={{2,0},{3,1},{4,6},{5,7},{10,8},{11,9},{12,14},{13,15},{18,16},{19,... | collective-permute-start | bytes 983048 | tf_op jit(solution)/shard_map/ppermute | solution.py:214
  57.4 81.3 %collective-permute-start.11 = (bf16[320,768]{1,0:T(8,128)(2,1)S(1)}, bf16[320,768]{1,0:T(8,128)(2,1)S(1)}, u32[]{:S(2)}, u32[]{:S(2)}) collective-permute-start(bf16[320,768]{1,0:T(8,128)(2,1)S(1)} %get-tuple-element.54), channel_id=1, source_target_pairs={{2,0},{3,1},{4,6},{5,7},{10,8},{11,9},{12,14},{13,15},{18,16},{19,... | collective-permute-start | bytes 1474568 | tf_op jit(solution)/shard_map/ppermute | solution.py:214
  58.7 90.1 %collective-permute-start.9 = (bf16[320,768]{1,0:T(8,128)(2,1)S(1)}, bf16[320,768]{1,0:T(8,128)(2,1)S(1)}, u32[]{:S(2)}, u32[]{:S(2)}) collective-permute-start(bf16[320,768]{1,0:T(8,128)(2,1)S(1)} %get-tuple-element.49), channel_id=1, source_target_pairs={{2,0},{3,1},{4,6},{5,7},{10,8},{11,9},{12,14},{13,15},{18,16},{19,... | collective-permute-start | bytes 1474568 | tf_op jit(solution)/shard_map/ppermute | solution.py:214
  117.9 30.9 %collective-permute-start.10 = (bf16[320,512]{1,0:T(8,128)(2,1)S(1)}, bf16[320,512]{1,0:T(8,128)(2,1)S(1)}, u32[]{:S(2)}, u32[]{:S(2)}) collective-permute-start(bf16[320,512]{1,0:T(8,128)(2,1)S(1)} %get-tuple-element.64), channel_id=1, source_target_pairs={{0,8},{8,0},{16,24},{24,16},{1,9},{9,1},{17,25},{25,17},{2,10},{10... | collective-permute-start | bytes 983048 | tf_op jit(solution)/shard_map/ppermute | solution.py:224
  119.5 33.1 %collective-permute-start.13 = (bf16[320,512]{1,0:T(8,128)(2,1)S(1)}, bf16[320,512]{1,0:T(8,128)(2,1)S(1)}, u32[]{:S(2)}, u32[]{:S(2)}) collective-permute-start(bf16[320,512]{1,0:T(8,128)(2,1)S(1)} %get-tuple-element.64), channel_id=1, source_target_pairs={{0,16},{8,24},{16,0},{24,8},{1,17},{9,25},{17,1},{25,9},{2,18},{10... | collective-permute-start | bytes 983048 | tf_op jit(solution)/shard_map/ppermute | solution.py:224
  123.9 28.0 %collective-permute-start.12 = (bf16[320,512]{1,0:T(8,128)(2,1)S(1)}, bf16[320,512]{1,0:T(8,128)(2,1)S(1)}, u32[]{:S(2)}, u32[]{:S(2)}) collective-permute-start(bf16[320,512]{1,0:T(8,128)(2,1)S(1)} %get-tuple-element.62), channel_id=1, source_target_pairs={{0,16},{8,24},{16,0},{24,8},{1,17},{9,25},{17,1},{25,9},{2,18},{10... | collective-permute-start | bytes 983048 | tf_op jit(solution)/shard_map/ppermute | solution.py:224
  138.7 32.7 %collective-permute-start.15 = (bf16[320,512]{1,0:T(8,128)(2,1)S(1)}, bf16[320,512]{1,0:T(8,128)(2,1)S(1)}, u32[]{:S(2)}, u32[]{:S(2)}) collective-permute-start(bf16[320,512]{1,0:T(8,128)(2,1)S(1)} %get-tuple-element.62), channel_id=1, source_target_pairs={{0,8},{8,0},{16,24},{24,16},{1,9},{9,1},{17,25},{25,17},{2,10},{10... | collective-permute-start | bytes 983048 | tf_op jit(solution)/shard_map/ppermute | solution.py:224
  148.8 30.5 %collective-permute-start.17 = (bf16[320,768]{1,0:T(8,128)(2,1)S(1)}, bf16[320,768]{1,0:T(8,128)(2,1)S(1)}, u32[]{:S(2)}, u32[]{:S(2)}) collective-permute-start(bf16[320,768]{1,0:T(8,128)(2,1)S(1)} %broadcast_select_fusion.1), channel_id=1, source_target_pairs={{0,8},{8,0},{16,24},{24,16},{1,9},{9,1},{17,25},{25,17},{2,10},{10... | collective-permute-start | bytes 1474568 | tf_op jit(solution)/shard_map/ppermute | solution.py:224
  150.4 32.5 %collective-permute-start.18 = (bf16[320,768]{1,0:T(8,128)(2,1)S(1)}, bf16[320,768]{1,0:T(8,128)(2,1)S(1)}, u32[]{:S(2)}, u32[]{:S(2)}) collective-permute-start(bf16[320,768]{1,0:T(8,128)(2,1)S(1)} %broadcast_select_fusion.1), channel_id=1, source_target_pairs={{0,16},{8,24},{16,0},{24,8},{1,17},{9,25},{17,1},{25,9},{2,18},{10... | collective-permute-start | bytes 1474568 | tf_op jit(solution)/shard_map/ppermute | solution.py:224
  152.0 17.9 %collective-permute-start.14 = (bf16[320,512]{1,0:T(8,128)(2,1)S(1)}, bf16[320,512]{1,0:T(8,128)(2,1)S(1)}, u32[]{:S(2)}, u32[]{:S(2)}) collective-permute-start(bf16[320,512]{1,0:T(8,128)(2,1)S(1)} %collective-permute-done.10), channel_id=1, source_target_pairs={{0,16},{8,24},{16,0},{24,8},{1,17},{9,25},{17,1},{25,9},{2,18},{10... | collective-permute-start | bytes 983048 | tf_op jit(solution)/shard_map/ppermute | solution.py:211
  152.6 39.4 %collective-permute-start.20 = (bf16[320,768]{1,0:T(8,128)(2,1)S(1)}, bf16[320,768]{1,0:T(8,128)(2,1)S(1)}, u32[]{:S(2)}, u32[]{:S(2)}) collective-permute-start(bf16[320,768]{1,0:T(8,128)(2,1)S(1)} %broadcast_select_fusion), channel_id=1, source_target_pairs={{0,8},{8,0},{16,24},{24,16},{1,9},{9,1},{17,25},{25,17},{2,10},{10... | collective-permute-start | bytes 1474568 | tf_op jit(solution)/shard_map/ppermute | solution.py:224
  169.9 13.0 %collective-permute-start.21 = (bf16[320,768]{1,0:T(8,128)(2,1)S(1)}, bf16[320,768]{1,0:T(8,128)(2,1)S(1)}, u32[]{:S(2)}, u32[]{:S(2)}) collective-permute-start(bf16[320,768]{1,0:T(8,128)(2,1)S(1)} %broadcast_select_fusion), channel_id=1, source_target_pairs={{0,16},{8,24},{16,0},{24,8},{1,17},{9,25},{17,1},{25,9},{2,18},{10... | collective-permute-start | bytes 1474568 | tf_op jit(solution)/shard_map/ppermute | solution.py:224
  171.4 7.8 %collective-permute-start.16 = (bf16[320,512]{1,0:T(8,128)(2,1)S(1)}, bf16[320,512]{1,0:T(8,128)(2,1)S(1)}, u32[]{:S(2)}, u32[]{:S(2)}) collective-permute-start(bf16[320,512]{1,0:T(8,128)(2,1)S(1)} %collective-permute-done.12), channel_id=1, source_target_pairs={{0,8},{8,0},{16,24},{24,16},{1,9},{9,1},{17,25},{25,17},{2,10},{10... | collective-permute-start | bytes 983048 | tf_op jit(solution)/shard_map/ppermute | solution.py:211
  179.3 12.6 %collective-permute-start.19 = (bf16[320,768]{1,0:T(8,128)(2,1)S(1)}, bf16[320,768]{1,0:T(8,128)(2,1)S(1)}, u32[]{:S(2)}, u32[]{:S(2)}) collective-permute-start(bf16[320,768]{1,0:T(8,128)(2,1)S(1)} %collective-permute-done.17), channel_id=1, source_target_pairs={{0,16},{8,24},{16,0},{24,8},{1,17},{9,25},{17,1},{25,9},{2,18},{10... | collective-permute-start | bytes 1474568 | tf_op jit(solution)/shard_map/ppermute | solution.py:211
  182.8 9.3 %collective-permute-start.22 = (bf16[320,768]{1,0:T(8,128)(2,1)S(1)}, bf16[320,768]{1,0:T(8,128)(2,1)S(1)}, u32[]{:S(2)}, u32[]{:S(2)}) collective-permute-start(bf16[320,768]{1,0:T(8,128)(2,1)S(1)} %collective-permute-done.21), channel_id=1, source_target_pairs={{0,8},{8,0},{16,24},{24,16},{1,9},{9,1},{17,25},{25,17},{2,10},{10... | collective-permute-start | bytes 1474568 | tf_op jit(solution)/shard_map/ppermute | solution.py:211
  (4 other events, 6.8 us)

commit v4 on v3

--- a/solution.py
+++ b/solution.py
@@ -80,7 +80,7 @@
         ],
         compiler_params=pltpu.CompilerParams(vmem_limit_bytes=VMEM_LIMIT),
         cost_estimate=pl.CostEstimate(
-            flops=8 * rows * known * columns, bytes_accessed=2 * known * columns, transcendentals=0
+            flops=rows * known, bytes_accessed=2 * rows, transcendentals=0
         ),
     )(inner, *blocks)
 
@@ -166,6 +166,36 @@
     )(inner, *blocks, gram, cubic)
 
 
+def put_kernel(places, aliased, *refs):
+    matrices, parts = refs[0], refs[1 : 1 + len(places)]
+    out, sems = refs[1 + len(places) + aliased :]
+    copies = []
+    for k, ((flip, at), part) in enumerate(zip(places, parts)):
+        target = out.at[matrices[flip], :, pl.ds(at, part.shape[1])]
+        copies.append(pltpu.make_async_copy(part, target, sems.at[k]))
+        copies[k].start()
+    for copy in copies:
+        copy.wait()
+
+
+def put(result, matrices, stage, shape):
+    places = [(flip, at) for flip, at, _ in stage]
+    parts = [part for _, _, part in stage]
+    aliased = result is not None
+    return pl.pallas_call(
+        functools.partial(put_kernel, places, aliased),
+        out_shape=jax.ShapeDtypeStruct(shape, parts[0].dtype),
+        in_specs=[pl.BlockSpec(memory_space=pltpu.SMEM)]
+        + [pl.BlockSpec(memory_space=pl.ANY)] * len(parts)
+        + [pl.BlockSpec(memory_space=pltpu.HBM)] * aliased,
+        out_specs=pl.BlockSpec(memory_space=pltpu.HBM),
+        scratch_shapes=[pltpu.SemaphoreType.DMA((len(parts),))],
+        input_output_aliases={1 + len(parts): 0} if aliased else {},
+        compiler_params=pltpu.CompilerParams(vmem_limit_bytes=1024 * 1024),
+        cost_estimate=pl.CostEstimate(flops=0, bytes_accessed=1024, transcendentals=0),
+    )(matrices, *parts, *([result] if aliased else []))
+
+
 def line_shards(iterate, widths):
     own = iterate[0]
     rows, columns = own.shape
@@ -196,45 +226,32 @@
     blocks = early + [from_far, swap(from_far)]
     for_outer = list(late_products(inner, blocks, gram, cubic, 0, widths))
     for_own = list(late_products(inner, blocks, gram, cubic, 1, widths))
-    for_outer[2], for_outer[3], for_own[0] = tie((for_outer[2], for_outer[3], for_own[0]))
-
-    result = jnp.zeros((4, rows, columns), jnp.bfloat16)
-
-    def place_in(result, flip, at, part):
-        return lax.dynamic_update_slice(result, part[None], (mat ^ flip, 0, at))
-
-    begins = [sum(widths[:k]) for k in range(len(widths))]
-    first_hop = []
-
-    def send_corner(k):
-        by_x, by_y = first_hop[k]
-        return lax.ppermute(*((by_x, "mat", along_y) if k % 2 == 0 else (by_y, "mat", along_x)))
-
-    for k in range(len(widths)):
+    result = None
+    begin = 0
+    stages = []
+    for k, width in enumerate(widths):
+        half = width // 2
         returned = lax.ppermute(for_outer[k], "shard", outwards)
-        here, returned = tie((outer, returned))
-        mine = jnp.where(here, returned, for_own[k])
-        if k >= 2:
-            by_x, by_y = first_hop[k - 2]
-            if k % 2 == 0:
-                mine, by_x = tie((mine, by_x))
-            else:
-                mine, by_y = tie((mine, by_y))
-            first_hop[k - 2] = (by_x, by_y)
-        first_hop.append((lax.ppermute(mine, "mat", along_x), lax.ppermute(mine, "mat", along_y)))
-        result = place_in(result, 0, begins[k], mine)
-    corners = [send_corner(k) for k in range(len(widths))]
-    for k in range(len(widths)):
-        by_x, by_y = first_hop[k]
-        for flip, part in ((1, by_x), (2, by_y), (3, corners[k])):
-            result = place_in(result, flip, begins[k], part)
+        mine = tie(jnp.where(outer, returned, for_own[k]))
+        by_x = lax.ppermute(mine, "mat", along_x)
+        by_y = lax.ppermute(mine, "mat", along_y)
+        by_x, by_y = tie((by_x, by_y))
+        left_half = lax.ppermute(by_x[:, :half], "mat", along_y)
+        right_half = lax.ppermute(by_y[:, half:], "mat", along_x)
+        stages.append([(0, begin, mine), (1, begin, by_x), (2, begin, by_y)])
+        stages.append([(3, begin, left_half), (3, begin + half, right_half)])
+        begin += width
+    matrices = mat[None] ^ jnp.arange(4, dtype=jnp.int32)
+    order = stages[:1] + [stages[1] + stages[2]] + stages[3:] if len(stages) == 4 else stages
+    for stage in order:
+        result = put(result, matrices, stage, (4, rows, columns))
     return result
 
 
 def solution(mesh):
     if (mesh.shape["mat"], mesh.shape["shard"]) == (4, 8):
         def shards(iterate):
-            return line_shards(iterate, widths=(512, 512, 768, 768))
+            return line_shards(iterate, widths=(1280, 1280))
     else:
         shards = general_shards
     return jax.shard_map(

time: 196 us -> 238 us (1.21)
  Pallas kernels: 4.06 us -> 59.1 us
  starting transfers between devices: 34.3 us -> 28.5 us
  waiting for transfers between devices: 148 us -> 143 us
    pallas_call x0 -> x3, Pallas kernels: none -> 55 us  [put(): pl.pallas_call(functools.partial(put_kernel, places, aliased), out_shape=...]
    ppermute x12 -> x8, waiting for transfers between devices: 34.8 us -> 24.5 us  [the longest x2 15.4 us: line_shards(): by_y = lax.ppermute(mine, 'mat', along_y)]
    ppermute x4 -> x2, waiting for transfers between devices: 81.9 us -> 87.2 us  [line_shards(): returned = lax.ppermute(for_outer[k], 'shard', outwards)]
    ppermute x12 -> x8, starting transfers between devices: 14.1 us -> 10.2 us  [the longest x2 3.19 us: line_shards(): by_y = lax.ppermute(mine, 'mat', along_y)]
    unnamed x10 -> x14, local copies, waits for them, and re-layouts: 6.74 us -> 3.21 us
    slice x0 -> x4, local copies, waits for them, and re-layouts: none -> 3.22 us  [the longest x2 1.64 us: line_shards(): left_half = lax.ppermute(by_x[:, :half], 'mat', along_y)]
    ppermute x4 -> x2, starting transfers between devices: 5.17 us -> 2.58 us  [line_shards(): returned = lax.ppermute(for_outer[k], 'shard', outwards)]
  transfers between devices with their start and end apart: 23 -> 17, of which waited for: 10 -> 8; matrix products, arithmetic and copies ran while one was open for 1% -> 1% of each run, Pallas kernels for 2% -> 14%
where the time goes in v4:
time: 238 us; the launch traced here: 237 us
  waiting for transfers between devices  143 us (60%)
  Pallas kernels  59.1 us (25%)
  starting transfers between devices  28.5 us (12%)
  local copies, waits for them, and re-layouts  6.43 us (3%)
    ppermute x2, waiting for transfers between devices, line_shards(): returned = lax.ppermute(for_outer[k], 'shard', outwards)  87.2 us
    pallas_call x3, Pallas kernels, put(): pl.pallas_call(functools.partial(put_kernel, places, aliased), out_shape=...  55 us
    ppermute x1, waiting for transfers between devices, line_shards(): from_outer = lax.ppermute(own, 'shard', inwards)  31.2 us
    ppermute x2, waiting for transfers between devices, line_shards(): by_y = lax.ppermute(mine, 'mat', along_y)  15.4 us
    ppermute x1, starting transfers between devices, line_shards(): from_outer = lax.ppermute(own, 'shard', inwards)  6.68 us
    ppermute x2, waiting for transfers between devices, line_shards(): right_half = lax.ppermute(by_y[:, half:], 'mat', along_x)  5.85 us
    ppermute x4, starting transfers between devices, swap(): return lax.ppermute(block, 'shard', other_core)  5.29 us
  transfers between devices with their start and end apart: 17, of which 8 were waited for; matrix products, arithmetic and copies ran while one was open for 1% of the time, Pallas kernels for 14%

profile of v4, /device:TPU:0, one launch (start us, length us, event | category | flops | bytes accessed | tf_op | source)
XLA Modules:
  0.0 237.4 jit_solution(14030571229085096917)
XLA Ops:
  0.0 1.8 collective-permute-start.3
  1.8 6.7 %collective-permute-start = (bf16[320,2560]{1,0:T(8,128)(2,1)}, bf16[320,2560]{1,0:T(8,128)(2,1)S(1)}, u32[]{:S(2)}, u32[]{:S(2)}) collective-permute-start(bf16[320,2560]{1,0:T(8,128)(2,1)} %bitcast.3), channel_id=1, source_target_pairs={{0,2},{1,3},{6,4},{7,5},{8,10},{9,11},{14,12},{15,13},{16,18},{17,... | collective-permute-start | bytes 4915208 | tf_op jit(solution)/shard_map/ppermute | solution.py:216
  8.5 1.9 collective-permute-start.2
  10.4 1.9 collective-permute-start.4
  12.3 31.2 %collective-permute-done.refs_1_ = bf16[320,2560]{1,0:T(8,128)(2,1)S(1)} collective-permute-done((bf16[320,2560]{1,0:T(8,128)(2,1)}, bf16[320,2560]{1,0:T(8,128)(2,1)S(1)}, u32[]{:S(2)}, u32[]{:S(2)}) %collective-permute-start) | collective-permute-done | bytes 1638432 | tf_op jit(solution)/shard_map/ppermute | solution.py:216
  44.3 1.9 collective-permute-start.5
  46.1 2.0 copy-done.4
  48.2 3.7 %shard_map.17 = (bf16[640,1920]{1,0:T(8,128)(2,1)}, f32[640,2560]{1,0:T(8,128)}) custom-call(s32[1]{0:T(128)} %bitcast.refs_0_, bf16[320,2560]{1,0:T(8,128)(2,1)S(1)} %collective-permute-done.refs_1_, bf16[320,2560]{1,0:T(8,128)(2,1)S(1)} %bitcast.5, bf16[320,2560]{1,0:T(8,128)(2,1)S(1)} %collective-permute-done.1.refs_3_, ...), custom_call_target="tpu_custom_call" | custom-call | flops 614400 | bytes 640 | tf_op jit(solution)/shard_map/pallas_call | solution.py:68
  53.9 1.3 collective-permute-start.7
  55.2 1.3 collective-permute-start.12
  56.8 73.3 %collective-permute-done.7 = bf16[320,1280]{1,0:T(8,128)(2,1)S(1)} collective-permute-done((bf16[320,1280]{1,0:T(8,128)(2,1)S(1)}, bf16[320,1280]{1,0:T(8,128)(2,1)S(1)}, u32[]{:S(2)}, u32[]{:S(2)}) %collective-permute-start.7) | collective-permute-done | bytes 819232 | tf_op jit(solution)/shard_map/ppermute | solution.py:234
  130.2 1.6 collective-permute-start.9
  131.8 1.5 collective-permute-start.8
  133.3 13.9 %collective-permute-done.12 = bf16[320,1280]{1,0:T(8,128)(2,1)S(1)} collective-permute-done((bf16[320,1280]{1,0:T(8,128)(2,1)S(1)}, bf16[320,1280]{1,0:T(8,128)(2,1)S(1)}, u32[]{:S(2)}, u32[]{:S(2)}) %collective-permute-start.12) | collective-permute-done | bytes 819232 | tf_op jit(solution)/shard_map/ppermute | solution.py:234
  147.3 1.6 collective-permute-start.14
  148.9 1.5 collective-permute-start.13
  151.7 15.4 %collective-permute-done.14.refs_3_ = bf16[320,1280]{1,0:T(8,128)(2,1)S(1)} collective-permute-done((bf16[320,1280]{1,0:T(8,128)(2,1)S(1)}, bf16[320,1280]{1,0:T(8,128)(2,1)S(1)}, u32[]{:S(2)}, u32[]{:S(2)}) %collective-permute-start.14) | collective-permute-done | bytes 819232 | tf_op jit(solution)/shard_map/ppermute | solution.py:237
  170.0 1.5 collective-permute-start.16
  173.3 1.5 collective-permute-start.10
  174.8 2.0 shard_map.20.refs_6_
  176.8 5.9 %collective-permute-done.16.refs_2_ = bf16[320,640]{1,0:T(8,128)(2,1)} collective-permute-done((bf16[320,640]{1,0:T(8,128)(2,1)}, bf16[320,640]{1,0:T(8,128)(2,1)}, u32[]{:S(2)}, u32[]{:S(2)}) %collective-permute-start.16) | collective-permute-done | bytes 409632 | tf_op jit(solution)/shard_map/ppermute | solution.py:240
  182.7 1.5 collective-permute-done.15.refs_1_
  184.2 26.5 %shard_map.21.refs_3_ = bf16[4,320,2560]{2,1,0:T(8,128)(2,1)} custom-call(s32[4]{0:T(128)S(1)} %iota_xor_fusion.refs_0_, bf16[320,640]{1,0:T(8,128)(2,1)} %collective-permute-done.15.refs_1_, bf16[320,640]{1,0:T(8,128)(2,1)} %collective-permute-done.16.refs_2_, bf16[320,1280]{1,0:T(8,128)(2,1)S(1)} %broadcast_select_fusion.1.refs_3_, ...), custom_call_target="tpu_custom_call", output_to_operand_aliasing={{}: (6, {})} | custom-call | bytes 1024 | tf_op jit(solution)/shard_map/pallas_call | solution.py:185
  210.7 26.5 %shard_map.22 = bf16[4,320,2560]{2,1,0:T(8,128)(2,1)} custom-call(s32[4]{0:T(128)S(1)} %iota_xor_fusion.refs_0_, bf16[320,640]{1,0:T(8,128)(2,1)} %collective-permute-done.10.refs_1_, bf16[320,640]{1,0:T(8,128)(2,1)} %collective-permute-done.11.refs_2_, bf16[4,320,2560]{2,1,0:T(8,128)(2,1)} %shard_map.21.refs_3_), custom_call_target="tpu_custom_call", output_to_operand_aliasing={{}: (3, {})} | custom-call | bytes 1024 | tf_op jit(solution)/shard_map/pallas_call | solution.py:185
  (37 shorter events, 9.3 us)
Async XLA Ops:
  0.0 10.4 %collective-permute-start.3 = (bf16[320,2560]{1,0:T(8,128)(2,1)}, bf16[320,2560]{1,0:T(8,128)(2,1)}, u32[]{:S(2)}, u32[]{:S(2)}) collective-permute-start(bf16[320,2560]{1,0:T(8,128)(2,1)} %bitcast.2), channel_id=1, source_target_pairs={{2,4},{3,5},{4,2},{5,3},{10,12},{11,13},{12,10},{13,11},{18,20},{1... | collective-permute-start | bytes 4915208 | tf_op jit(solution)/shard_map/ppermute | solution.py:217
  1.8 41.7 %collective-permute-start = (bf16[320,2560]{1,0:T(8,128)(2,1)}, bf16[320,2560]{1,0:T(8,128)(2,1)S(1)}, u32[]{:S(2)}, u32[]{:S(2)}) collective-permute-start(bf16[320,2560]{1,0:T(8,128)(2,1)} %bitcast.3), channel_id=1, source_target_pairs={{0,2},{1,3},{6,4},{7,5},{8,10},{9,11},{14,12},{15,13},{16,18},{17,... | collective-permute-start | bytes 4915208 | tf_op jit(solution)/shard_map/ppermute | solution.py:216
  8.5 37.6 %collective-permute-start.2 = (bf16[320,2560]{1,0:T(8,128)(2,1)}, bf16[320,2560]{1,0:T(8,128)(2,1)}, u32[]{:S(2)}, u32[]{:S(2)}) collective-permute-start(bf16[320,2560]{1,0:T(8,128)(2,1)} %bitcast.4), channel_id=1, source_target_pairs={{2,3},{3,2},{4,5},{5,4},{10,11},{11,10},{12,13},{13,12},{18,19},{1... | collective-permute-start | bytes 4915208 | tf_op jit(solution)/shard_map/ppermute | solution.py:221
  10.4 35.7 %collective-permute-start.4 = (bf16[320,2560]{1,0:T(8,128)(2,1)}, bf16[320,2560]{1,0:T(8,128)(2,1)}, u32[]{:S(2)}, u32[]{:S(2)}) collective-permute-start(bf16[320,2560]{1,0:T(8,128)(2,1)} %collective-permute-done.3.refs_5_), channel_id=1, source_target_pairs={{2,3},{3,2},{4,5},{5,4},{10,11},{11,10},{12,13},{13,12},{18,19},{1... | collective-permute-start | bytes 4915208 | tf_op jit(solution)/shard_map/ppermute | solution.py:221
  43.5 2.6 %collective-permute-start.1 = (bf16[320,2560]{1,0:T(8,128)(2,1)S(1)}, bf16[320,2560]{1,0:T(8,128)(2,1)S(1)}, u32[]{:S(2)}, u32[]{:S(2)}) collective-permute-start(bf16[320,2560]{1,0:T(8,128)(2,1)S(1)} %collective-permute-done.refs_1_), channel_id=1, source_target_pairs={{2,3},{3,2},{4,5},{5,4},{10,11},{11,10},{12,13},{13,12},{18,19},{1... | collective-permute-start | bytes 4915208 | tf_op jit(solution)/shard_map/ppermute | solution.py:221
  44.3 7.6 %collective-permute-start.5 = (bf16[320,2560]{1,0:T(8,128)(2,1)S(1)}, bf16[320,2560]{1,0:T(8,128)(2,1)}, u32[]{:S(2)}, u32[]{:S(2)}) collective-permute-start(bf16[320,2560]{1,0:T(8,128)(2,1)S(1)} %collective-permute-done.refs_1_), channel_id=1, source_target_pairs={{2,4},{3,5},{4,2},{5,3},{10,12},{11,13},{12,10},{13,11},{18,20},{1... | collective-permute-start | bytes 4915208 | tf_op jit(solution)/shard_map/ppermute | solution.py:218
  46.1 5.7 %copy-start.5 = (bf16[320,2560]{1,0:T(8,128)(2,1)}, bf16[320,2560]{1,0:T(8,128)(2,1)S(1)}, u32[]{:S(2)}) copy-start(bf16[320,2560]{1,0:T(8,128)(2,1)S(1)} %collective-permute-done.1.refs_3_) | copy-start | bytes 4915204
  46.1 2.0 copy-start.4
  51.8 0.8 collective-permute-start.6
  52.6 1.2 copy-start.6
  53.9 76.2 %collective-permute-start.7 = (bf16[320,1280]{1,0:T(8,128)(2,1)S(1)}, bf16[320,1280]{1,0:T(8,128)(2,1)S(1)}, u32[]{:S(2)}, u32[]{:S(2)}) collective-permute-start(bf16[320,1280]{1,0:T(8,128)(2,1)S(1)} %get-tuple-element.23), channel_id=1, source_target_pairs={{2,0},{3,1},{4,6},{5,7},{10,8},{11,9},{12,14},{13,15},{18,16},{19,... | collective-permute-start | bytes 2457608 | tf_op jit(solution)/shard_map/ppermute | solution.py:234
  55.2 92.0 %collective-permute-start.12 = (bf16[320,1280]{1,0:T(8,128)(2,1)S(1)}, bf16[320,1280]{1,0:T(8,128)(2,1)S(1)}, u32[]{:S(2)}, u32[]{:S(2)}) collective-permute-start(bf16[320,1280]{1,0:T(8,128)(2,1)S(1)} %get-tuple-element.27), channel_id=1, source_target_pairs={{2,0},{3,1},{4,6},{5,7},{10,8},{11,9},{12,14},{13,15},{18,16},{19,... | collective-permute-start | bytes 2457608 | tf_op jit(solution)/shard_map/ppermute | solution.py:234
  130.2 20.2 %collective-permute-start.9 = (bf16[320,1280]{1,0:T(8,128)(2,1)S(1)}, bf16[320,1280]{1,0:T(8,128)(2,1)S(1)}, u32[]{:S(2)}, u32[]{:S(2)}) collective-permute-start(bf16[320,1280]{1,0:T(8,128)(2,1)S(1)} %broadcast_select_fusion.1.refs_3_), channel_id=1, source_target_pairs={{0,16},{8,24},{16,0},{24,8},{1,17},{9,25},{17,1},{25,9},{2,18},{10... | collective-permute-start | bytes 2457608 | tf_op jit(solution)/shard_map/ppermute | solution.py:237
  131.8 19.0 %collective-permute-start.8 = (bf16[320,1280]{1,0:T(8,128)(2,1)S(1)}, bf16[320,1280]{1,0:T(8,128)(2,1)S(1)}, u32[]{:S(2)}, u32[]{:S(2)}) collective-permute-start(bf16[320,1280]{1,0:T(8,128)(2,1)S(1)} %broadcast_select_fusion.1.refs_3_), channel_id=1, source_target_pairs={{0,8},{8,0},{16,24},{24,16},{1,9},{9,1},{17,25},{25,17},{2,10},{10... | collective-permute-start | bytes 2457608 | tf_op jit(solution)/shard_map/ppermute | solution.py:236
  147.3 19.8 %collective-permute-start.14 = (bf16[320,1280]{1,0:T(8,128)(2,1)S(1)}, bf16[320,1280]{1,0:T(8,128)(2,1)S(1)}, u32[]{:S(2)}, u32[]{:S(2)}) collective-permute-start(bf16[320,1280]{1,0:T(8,128)(2,1)S(1)} %broadcast_select_fusion.refs_1_), channel_id=1, source_target_pairs={{0,16},{8,24},{16,0},{24,8},{1,17},{9,25},{17,1},{25,9},{2,18},{10... | collective-permute-start | bytes 2457608 | tf_op jit(solution)/shard_map/ppermute | solution.py:237
  148.9 19.5 %collective-permute-start.13 = (bf16[320,1280]{1,0:T(8,128)(2,1)S(1)}, bf16[320,1280]{1,0:T(8,128)(2,1)S(1)}, u32[]{:S(2)}, u32[]{:S(2)}) collective-permute-start(bf16[320,1280]{1,0:T(8,128)(2,1)S(1)} %broadcast_select_fusion.refs_1_), channel_id=1, source_target_pairs={{0,8},{8,0},{16,24},{24,16},{1,9},{9,1},{17,25},{25,17},{2,10},{10... | collective-permute-start | bytes 2457608 | tf_op jit(solution)/shard_map/ppermute | solution.py:236
  150.4 21.6 %copy-start = (bf16[320,1280]{1,0:T(8,128)(2,1)}, bf16[320,1280]{1,0:T(8,128)(2,1)S(1)}, u32[]{:S(2)}) copy-start(bf16[320,1280]{1,0:T(8,128)(2,1)S(1)} %collective-permute-done.9.refs_5_) | copy-start | bytes 2457604
  150.8 21.9 %copy-start.2 = (bf16[320,1280]{1,0:T(8,128)(2,1)}, bf16[320,1280]{1,0:T(8,128)(2,1)S(1)}, u32[]{:S(2)}) copy-start(bf16[320,1280]{1,0:T(8,128)(2,1)S(1)} %collective-permute-done.8.refs_4_) | copy-start | bytes 2457604
  170.0 12.7 %collective-permute-start.16 = (bf16[320,640]{1,0:T(8,128)(2,1)}, bf16[320,640]{1,0:T(8,128)(2,1)}, u32[]{:S(2)}, u32[]{:S(2)}) collective-permute-start(bf16[320,640]{1,0:T(8,128)(2,1)} %slice.15), channel_id=1, source_target_pairs={{0,8},{8,0},{16,24},{24,16},{1,9},{9,1},{17,25},{25,17},{2,10},{10... | collective-permute-start | bytes 1228808 | tf_op jit(solution)/shard_map/ppermute | solution.py:240
  171.4 12.7 %collective-permute-start.15 = (bf16[320,640]{1,0:T(8,128)(2,1)}, bf16[320,640]{1,0:T(8,128)(2,1)}, u32[]{:S(2)}, u32[]{:S(2)}) collective-permute-start(bf16[320,640]{1,0:T(8,128)(2,1)} %slice.14), channel_id=1, source_target_pairs={{0,16},{8,24},{16,0},{24,8},{1,17},{9,25},{17,1},{25,9},{2,18},{10... | collective-permute-start | bytes 1228808 | tf_op jit(solution)/shard_map/ppermute | solution.py:239
  172.7 37.9 %collective-permute-start.11 = (bf16[320,640]{1,0:T(8,128)(2,1)}, bf16[320,640]{1,0:T(8,128)(2,1)}, u32[]{:S(2)}, u32[]{:S(2)}) collective-permute-start(bf16[320,640]{1,0:T(8,128)(2,1)} %slice.13), channel_id=1, source_target_pairs={{0,8},{8,0},{16,24},{24,16},{1,9},{9,1},{17,25},{25,17},{2,10},{10... | collective-permute-start | bytes 1228808 | tf_op jit(solution)/shard_map/ppermute | solution.py:240
  173.3 37.4 %collective-permute-start.10 = (bf16[320,640]{1,0:T(8,128)(2,1)}, bf16[320,640]{1,0:T(8,128)(2,1)}, u32[]{:S(2)}, u32[]{:S(2)}) collective-permute-start(bf16[320,640]{1,0:T(8,128)(2,1)} %slice.12), channel_id=1, source_target_pairs={{0,16},{8,24},{16,0},{24,8},{1,17},{9,25},{17,1},{25,9},{2,18},{10... | collective-permute-start | bytes 1228808 | tf_op jit(solution)/shard_map/ppermute | solution.py:239
  174.8 9.3 %copy-start.1 = (bf16[320,1280]{1,0:T(8,128)(2,1)S(1)}, bf16[320,1280]{1,0:T(8,128)(2,1)}, u32[]{:S(2)}) copy-start(bf16[320,1280]{1,0:T(8,128)(2,1)} %copy-done) | copy-start | bytes 2457604
  174.8 9.3 %copy-start.3 = (bf16[320,1280]{1,0:T(8,128)(2,1)S(1)}, bf16[320,1280]{1,0:T(8,128)(2,1)}, u32[]{:S(2)}) copy-start(bf16[320,1280]{1,0:T(8,128)(2,1)} %copy-done.2) | copy-start | bytes 2457604

commit v5 on v3

v5 whole, which is shorter than its diff:
```python
import functools

import jax
import jax.numpy as jnp
from jax import lax
from jax.experimental import pallas as pl
from jax.experimental.pallas import tpu as pltpu
from jax.sharding import PartitionSpec as P

coef_a = 3.4445
coef_b = -4.775
coef_c = 2.0315

TILE = 1280
LANES = 128
VMEM_LIMIT = 48 * 1024 * 1024


def dot_t(left, right):
    return lax.dot_general(
        left, right, (((1,), (1,)), ((), ())), preferred_element_type=jnp.float32
    )


def dot(left, right):
    return jnp.dot(left, right, preferred_element_type=jnp.float32)


def general_shards(iterate):
    own = iterate[0]
    gathered = lax.all_gather(own, "shard", axis=0, tiled=True)
    gram = dot_t(own, gathered).astype(jnp.bfloat16)
    cubic = dot(gram, gathered).astype(jnp.bfloat16)
    squared = dot_t(cubic, gathered)
    polynomial = (coef_b * gram.astype(jnp.float32) + coef_c * squared).astype(jnp.bfloat16)
    product = dot(polynomial, gathered)
    next_rows = (coef_a * own.astype(jnp.float32) + product).astype(jnp.bfloat16)
    return lax.all_gather(next_rows[None], "mat", axis=0, tiled=True)


def tiles(start, stop):
    return [pl.ds(at, min(TILE, stop - at)) for at in range(start, stop, TILE)]


def starts(blocks):
    return [sum(b.shape[0] for b in blocks[:k]) for k in range(len(blocks) + 1)]


def early_kernel(rows, first, count, *refs):
    inner, blocks, refs = refs[0], refs[1 : count + 1], refs[count + 1 :]
    *cubic_in, gram, cubic, whole, sems = refs
    columns = blocks[0].shape[1]
    begin = starts(blocks)
    base = begin[first]

    @pl.when(inner[0] != 0)
    def _():
        copies = []
        for k, block in enumerate(blocks):
            target = whole.at[pl.ds(begin[k], block.shape[0]), :]
            copies.append(pltpu.make_async_copy(block, target, sems.at[k]))
        if cubic_in:
            copies.append(pltpu.make_async_copy(cubic_in[0], cubic, sems.at[count]))
        for copy in copies:
            copy.start()
        for copy in copies:
            copy.wait()
        for at in tiles(base, begin[-1]):
            out = pl.ds(at.start - base, at.size)
            gram[:, out] = dot_t(whole[: 2 * rows, :], whole[at, :]).astype(jnp.bfloat16)
        for at in tiles(0, columns):
            add = dot(gram[:, : begin[-1] - base], whole[pl.ds(base, begin[-1] - base), at])
            cubic[:, at] = (cubic[:, at] + add) if cubic_in else add


def early_products(inner, rows, left, blocks, cubic=None):
    blocks, first = left + blocks, len(left)
    count = len(blocks)
    columns = blocks[0].shape[1]
    begin = starts(blocks)
    known = begin[-1] - begin[first]
    more = [] if cubic is None else [cubic]
    return pl.pallas_call(
        functools.partial(early_kernel, rows, first, count),
        out_shape=(
            jax.ShapeDtypeStruct((2 * rows, pl.cdiv(known, LANES) * LANES), jnp.bfloat16),
            jax.ShapeDtypeStruct((2 * rows, columns), jnp.float32),
        ),
        in_specs=[pl.BlockSpec(memory_space=pltpu.SMEM)]
        + [pl.BlockSpec(memory_space=pl.ANY)] * (count + len(more)),
        out_specs=(pl.BlockSpec(memory_space=pltpu.VMEM),) * 2,
        scratch_shapes=[
            pltpu.VMEM((begin[-1], columns), jnp.bfloat16),
            pltpu.SemaphoreType.DMA((count + len(more),)),
        ],
        compiler_params=pltpu.CompilerParams(vmem_limit_bytes=VMEM_LIMIT),
        cost_estimate=pl.CostEstimate(
            flops=8 * rows * known * columns, bytes_accessed=4 * known * columns, transcendentals=0
        ),
    )(inner, *blocks, *more)


def late_kernel(first, early_count, count, gram_count, widths, *refs):
    inner, refs = refs[0], refs[1:]
    blocks, grams_in = refs[:count], refs[count : count + gram_count]
    cubic_in, refs = refs[count + gram_count], refs[count + gram_count + 1 :]
    outs = refs[: len(widths)]
    whole, gram, cubic_sum, cubic, poly, sems = refs[len(widths) :]
    rows, total = gram.shape
    columns = blocks[0].shape[1]
    begin = starts(blocks)
    known = begin[early_count]
    mine = pl.ds(first, rows)
    late = pl.ds(known, total - known)

    @pl.when(inner[0] != 0)
    def _():
        copies = {}

        def fetch(name, source, target):
            copies[name] = pltpu.make_async_copy(source, target, sems.at[len(copies)])
            copies[name].start()

        def fetch_block(k):
            fetch(k, blocks[k], whole.at[pl.ds(begin[k], blocks[k].shape[0]), :])

        own = [k for k in range(early_count) if first <= begin[k] < first + rows]
        others = [k for k in range(early_count) if k not in own]
        for k in own + list(range(early_count, count)):
            fetch_block(k)
        at = 0
        for k, gram_in in enumerate(grams_in):
            width = gram_in.shape[1]
            fetch("gram%d" % k, gram_in.at[mine, :], gram.at[:, pl.ds(at, width)])
            at += width
        fetch("cubic", cubic_in.at[mine, :], cubic_sum)
        for k in others:
            fetch_block(k)

        for k in own + list(range(early_count, count)):
            copies[k].wait()
        for k in range(gram_count):
            copies["gram%d" % k].wait()
        gram[:, late] = dot_t(whole[mine, :], whole[late, :]).astype(jnp.bfloat16)
        copies["cubic"].wait()
        for at in tiles(0, columns):
            add = dot(gram[:, late], whole[late, at])
            cubic[:, at] = (cubic_sum[:, at] + add).astype(jnp.bfloat16)

        for k in others:
            copies[k].wait()
        for at in tiles(0, total):
            squared = dot_t(cubic[...], whole[at, :])
            poly[:, at] = (coef_b * gram[:, at].astype(jnp.float32) + coef_c * squared).astype(
                jnp.bfloat16
            )

        left = 0
        for out, width in zip(outs, widths):
            at = pl.ds(left, width)
            product = dot(poly[...], whole[:, at])
            base = whole[mine, at].astype(jnp.float32)
            out[...] = (coef_a * base + product).astype(jnp.bfloat16)
            left += width


def late_products(inner, first, rows, early, late, grams, cubic, widths):
    blocks = early + late
    count = len(blocks)
    columns = blocks[0].shape[1]
    total = starts(blocks)[-1]
    return pl.pallas_call(
        functools.partial(late_kernel, first, len(early), count, len(grams), widths),
        out_shape=tuple(jax.ShapeDtypeStruct((rows, w), jnp.bfloat16) for w in widths),
        in_specs=[pl.BlockSpec(memory_space=pltpu.SMEM)]
        + [pl.BlockSpec(memory_space=pl.ANY)] * (count + len(grams) + 1),
        out_specs=tuple(pl.BlockSpec(memory_space=pltpu.VMEM) for _ in widths),
        scratch_shapes=[
            pltpu.VMEM((total, columns), jnp.bfloat16),
            pltpu.VMEM((rows, total), jnp.bfloat16),
            pltpu.VMEM((rows, columns), jnp.float32),
            pltpu.VMEM((rows, columns), jnp.bfloat16),
            pltpu.VMEM((rows, total), jnp.bfloat16),
            pltpu.SemaphoreType.DMA((count + len(grams) + 1,)),
        ],
        compiler_params=pltpu.CompilerParams(vmem_limit_bytes=VMEM_LIMIT),
        cost_estimate=pl.CostEstimate(
            flops=5 * rows * total * columns, bytes_accessed=2 * total * columns, transcendentals=0
        ),
    )(inner, *blocks, *grams, cubic)


def line_shards(iterate, widths):
    own = iterate[0]
    rows, columns = own.shape
    place = lax.axis_index("shard") // 2
    outer = (place == 0) | (place == 3)
    mat = lax.axis_index("mat")

    inner = jnp.where(outer, 0, 1).astype(jnp.int32)[None]
    tie = lax.optimization_barrier

    other_core = [(2, 3), (3, 2), (4, 5), (5, 4)]
    inwards = [(0, 2), (1, 3), (6, 4), (7, 5)]
    outwards = [(b, a) for a, b in inwards]
    middle = [(2, 4), (3, 5), (4, 2), (5, 3)]
    along_x = [(m, m ^ 1) for m in range(4)]
    along_y = [(m, m ^ 2) for m in range(4)]

    def swap(block):
        return lax.ppermute(block, "shard", other_core)

    from_outer = lax.ppermute(own, "shard", inwards)
    from_inner = lax.ppermute(own, "shard", middle)
    from_far = lax.ppermute(from_outer, "shard", middle)

    left = [from_outer, own]
    first = left + [swap(own), from_inner]
    first_gram, cubic = early_products(inner, rows, [], first)
    from_far, first_gram, cubic = tie((from_far, first_gram, cubic))
    then = [swap(from_outer), swap(from_inner), from_far]
    then_gram, cubic = early_products(inner, rows, left, then, cubic)
    early, grams, late = first + then, [first_gram, then_gram], [swap(from_far)]
    for_outer = late_products(inner, 0, rows, early, late, grams, cubic, widths)
    for_own = late_products(inner, rows, rows, early, late, grams, cubic, widths)

    result = jnp.zeros((4, rows, columns), jnp.bfloat16)

    def place_in(result, flip, at, part):
        return lax.dynamic_update_slice(result, part[None], (mat ^ flip, 0, at))

    begin = 0
    for k, width in enumerate(widths):
        returned = lax.ppermute(for_outer[k], "shard", outwards)
        mine = tie(jnp.where(outer, returned, for_own[k]))
        by_x = lax.ppermute(mine, "mat", along_x)
        by_y = lax.ppermute(mine, "mat", along_y)
        by_x, by_y = tie((by_x, by_y))
        if k % 2 == 0:
            across = lax.ppermute(by_x, "mat", along_y)
        else:
            across = lax.ppermute(by_y, "mat", along_x)
        for flip, part in enumerate((mine, by_x, by_y, across)):
            result = place_in(result, flip, begin, part)
        begin += width
    return result


def solution(mesh):
    if (mesh.shape["mat"], mesh.shape["shard"]) == (4, 8):
        def shards(iterate):
            return line_shards(iterate, widths=(1280, 1280))
    else:
        shards = general_shards
    return jax.shard_map(
        shards,
        mesh=mesh,
        in_specs=(P("mat", "shard", None),),
        out_specs=P(None, "shard", None),
        check_vma=False,
    )
```

time: 196 us -> 199 us (1.015)
  starting transfers between devices: 34.3 us -> 22.5 us
  waiting for transfers between devices: 148 us -> 158 us
  local copies, waits for them, and re-layouts: 8.47 us -> 11.7 us
    ppermute x4 -> x2, waiting for transfers between devices: 81.9 us -> 91.9 us  [line_shards(): returned = lax.ppermute(for_outer[k], 'shard', outwards)]
    ppermute x12 -> x6, starting transfers between devices: 14.1 us -> 8.2 us  [the longest x2 3.11 us: line_shards(): by_x = lax.ppermute(mine, 'mat', along_x)]
    ppermute x4 -> x2, starting transfers between devices: 5.17 us -> 2.58 us  [line_shards(): returned = lax.ppermute(for_outer[k], 'shard', outwards)]
    dynamic_update_slice x14 -> x8, local copies, waits for them, and re-layouts: 1.23 us -> 3.69 us  [place_in(): return lax.dynamic_update_slice(result, part[None], (mat ^ flip, 0, at))]
    ppermute x4, starting transfers between devices: 6.38 us -> 4.15 us  [swap(): return lax.ppermute(block, 'shard', other_core)]
    pallas_call x3 -> x4, Pallas kernels: 4.06 us -> 6.02 us  [the longest x2 5.59 us: early_products(): pl.pallas_call(functools.partial(early_kernel, rows, first, count), out_s...]
    ppermute x12 -> x6, waiting for transfers between devices: 34.8 us -> 33.1 us  [the longest x2 16.5 us: line_shards(): by_x = lax.ppermute(mine, 'mat', along_x)]
    unnamed x10 -> x14, local copies, waits for them, and re-layouts: 6.74 us -> 7.51 us
  transfers between devices with their start and end apart: 23 -> 15, of which waited for: 10 -> 8; matrix products, arithmetic and copies ran while one was open for 1% -> 2% of each run, Pallas kernels for 2% -> 3%
where the time goes in v5:
time: 199 us; the launch traced here: 198 us
  waiting for transfers between devices  158 us (79%)
  starting transfers between devices  22.5 us (11%)
  local copies, waits for them, and re-layouts  11.7 us (6%)
  Pallas kernels  6.02 us (3%)
    ppermute x2, waiting for transfers between devices, line_shards(): returned = lax.ppermute(for_outer[k], 'shard', outwards)  91.9 us
    ppermute x1, waiting for transfers between devices, line_shards(): from_outer = lax.ppermute(own, 'shard', inwards)  32.6 us
    ppermute x2, waiting for transfers between devices, line_shards(): by_x = lax.ppermute(mine, 'mat', along_x)  16.5 us
    ppermute x1, waiting for transfers between devices, line_shards(): across = lax.ppermute(by_x, 'mat', along_y)  14.6 us
    unnamed x14, local copies, waits for them, and re-layouts  7.51 us
    pallas_call x2, Pallas kernels, early_products(): pl.pallas_call(functools.partial(early_kernel, rows, first, count), out_s...  5.59 us
    ppermute x1, starting transfers between devices, line_shards(): from_outer = lax.ppermute(own, 'shard', inwards)  5.02 us
    ppermute x4, starting transfers between devices, swap(): return lax.ppermute(block, 'shard', other_core)  4.15 us
  transfers between devices with their start and end apart: 15, of which 8 were waited for; matrix products, arithmetic and copies ran while one was open for 2% of the time, Pallas kernels for 3%

profile of v5, /device:TPU:0, one launch (start us, length us, event | category | flops | bytes accessed | tf_op | source)
XLA Modules:
  0.0 198.3 jit_solution(7365825671567801130)
XLA Ops:
  0.0 5.0 %collective-permute-start = (bf16[320,2560]{1,0:T(8,128)(2,1)}, bf16[320,2560]{1,0:T(8,128)(2,1)S(1)}, u32[]{:S(2)}, u32[]{:S(2)}) collective-permute-start(bf16[320,2560]{1,0:T(8,128)(2,1)} %bitcast.18), channel_id=1, source_target_pairs={{0,2},{1,3},{6,4},{7,5},{8,10},{9,11},{14,12},{15,13},{16,18},{17,... | collective-permute-start | bytes 4915208 | tf_op jit(solution)/shard_map/ppermute | solution.py:213
  5.8 1.9 collective-permute-start.1
  7.7 32.6 %collective-permute-done.refs_1_ = bf16[320,2560]{1,0:T(8,128)(2,1)S(1)} collective-permute-done((bf16[320,2560]{1,0:T(8,128)(2,1)}, bf16[320,2560]{1,0:T(8,128)(2,1)S(1)}, u32[]{:S(2)}, u32[]{:S(2)}) %collective-permute-start) | collective-permute-done | bytes 1638432 | tf_op jit(solution)/shard_map/ppermute | solution.py:213
  40.3 1.8 collective-permute-start.5
  44.1 1.4 copy-done
  45.5 2.8 %shard_map.17 = (bf16[640,1280]{1,0:T(8,128)(2,1)S(1)}, f32[640,2560]{1,0:T(8,128)}) custom-call(s32[1]{0:T(128)} %bitcast.refs_0_, bf16[320,2560]{1,0:T(8,128)(2,1)S(1)} %collective-permute-done.refs_1_, bf16[320,2560]{1,0:T(8,128)(2,1)S(1)} %bitcast.23, bf16[320,2560]{1,0:T(8,128)(2,1)} %collective-permute-done.1.refs_3_, bf16[320,2560]{1,0:T(8,128)(2,1)} %copy-done.3), custom_call_target="tpu_custom_call" | custom-call | flops 8388608000 | bytes 13107200 | tf_op jit(solution)/shard_map/pallas_call | solution.py:83
  50.3 1.3 copy-done.5
  51.6 2.8 %shard_map.18 = (bf16[640,1024]{1,0:T(8,128)(2,1)S(1)}, f32[640,2560]{1,0:T(8,128)}) custom-call(s32[1]{0:T(128)} %bitcast.refs_0_, bf16[320,2560]{1,0:T(8,128)(2,1)S(1)} %collective-permute-done.refs_1_, bf16[320,2560]{1,0:T(8,128)(2,1)S(1)} %bitcast.24, bf16[320,2560]{1,0:T(8,128)(2,1)} %copy-done.4, bf16[320,2560]{1,0:T(8,128)(2,1)} %copy-done.5, ...), custom_call_target="tpu_custom_call" | custom-call | flops 6291456000 | bytes 9830400 | tf_op jit(solution)/shard_map/pallas_call | solution.py:83
  54.4 1.2 copy-done.6
  55.7 1.3 collective-permute-start.11
  57.0 1.3 collective-permute-start.7
  58.6 77.7 %collective-permute-done.11 = bf16[320,1280]{1,0:T(8,128)(2,1)S(1)} collective-permute-done((bf16[320,1280]{1,0:T(8,128)(2,1)S(1)}, bf16[320,1280]{1,0:T(8,128)(2,1)S(1)}, u32[]{:S(2)}, u32[]{:S(2)}) %collective-permute-start.11) | collective-permute-done | bytes 819232 | tf_op jit(solution)/shard_map/ppermute | solution.py:234
  136.4 1.6 collective-permute-start.12
  137.9 1.5 collective-permute-start.13
  139.4 14.2 %collective-permute-done.7 = bf16[320,1280]{1,0:T(8,128)(2,1)S(1)} collective-permute-done((bf16[320,1280]{1,0:T(8,128)(2,1)S(1)}, bf16[320,1280]{1,0:T(8,128)(2,1)S(1)}, u32[]{:S(2)}, u32[]{:S(2)}) %collective-permute-start.7) | collective-permute-done | bytes 819232 | tf_op jit(solution)/shard_map/ppermute | solution.py:234
  153.7 1.6 collective-permute-start.8
  155.3 1.5 collective-permute-start.9
  157.5 16.5 %collective-permute-done.8 = bf16[320,1280]{1,0:T(8,128)(2,1)} collective-permute-done((bf16[320,1280]{1,0:T(8,128)(2,1)S(1)}, bf16[320,1280]{1,0:T(8,128)(2,1)}, u32[]{:S(2)}, u32[]{:S(2)}) %collective-permute-start.8) | collective-permute-done | bytes 819232 | tf_op jit(solution)/shard_map/ppermute | solution.py:236
  174.0 1.2 collective-permute-done.9
  175.2 1.5 collective-permute-start.10
  177.2 1.2 bitcast_dynamic-update-slice_fusion.6
  178.4 1.2 bitcast_dynamic-update-slice_fusion.5
  179.7 14.6 %collective-permute-done.10 = bf16[320,1280]{1,0:T(8,128)(2,1)S(1)} collective-permute-done((bf16[320,1280]{1,0:T(8,128)(2,1)}, bf16[320,1280]{1,0:T(8,128)(2,1)S(1)}, u32[]{:S(2)}, u32[]{:S(2)}) %collective-permute-start.10) | collective-permute-done | bytes 819232 | tf_op jit(solution)/shard_map/ppermute | solution.py:240
  195.3 2.1 %copy-done.2 = bf16[4,320,2560]{2,1,0:T(8,128)(2,1)} copy-done((bf16[4,320,2560]{2,1,0:T(8,128)(2,1)}, bf16[4,320,2560]{2,1,0:T(8,128)(2,1)S(1)}, u32[]{:S(2)}) %copy-start.2) | copy-done | bytes 6553624
  (35 shorter events, 8.4 us)
Async XLA Ops:
  0.0 40.3 %collective-permute-start = (bf16[320,2560]{1,0:T(8,128)(2,1)}, bf16[320,2560]{1,0:T(8,128)(2,1)S(1)}, u32[]{:S(2)}, u32[]{:S(2)}) collective-permute-start(bf16[320,2560]{1,0:T(8,128)(2,1)} %bitcast.18), channel_id=1, source_target_pairs={{0,2},{1,3},{6,4},{7,5},{8,10},{9,11},{14,12},{15,13},{16,18},{17,... | collective-permute-start | bytes 4915208 | tf_op jit(solution)/shard_map/ppermute | solution.py:213
  5.0 37.8 %collective-permute-start.2 = (bf16[320,2560]{1,0:T(8,128)(2,1)}, bf16[320,2560]{1,0:T(8,128)(2,1)S(1)}, u32[]{:S(2)}, u32[]{:S(2)}) collective-permute-start(bf16[320,2560]{1,0:T(8,128)(2,1)} %bitcast.19), channel_id=1, source_target_pairs={{2,4},{3,5},{4,2},{5,3},{10,12},{11,13},{12,10},{13,11},{18,20},{1... | collective-permute-start | bytes 4915208 | tf_op jit(solution)/shard_map/ppermute | solution.py:214
  5.8 37.9 %collective-permute-start.1 = (bf16[320,2560]{1,0:T(8,128)(2,1)}, bf16[320,2560]{1,0:T(8,128)(2,1)}, u32[]{:S(2)}, u32[]{:S(2)}) collective-permute-start(bf16[320,2560]{1,0:T(8,128)(2,1)} %bitcast.20), channel_id=1, source_target_pairs={{2,3},{3,2},{4,5},{5,4},{10,11},{11,10},{12,13},{13,12},{18,19},{1... | collective-permute-start | bytes 4915208 | tf_op jit(solution)/shard_map/ppermute | solution.py:211
  40.3 8.1 %collective-permute-start.5 = (bf16[320,2560]{1,0:T(8,128)(2,1)S(1)}, bf16[320,2560]{1,0:T(8,128)(2,1)}, u32[]{:S(2)}, u32[]{:S(2)}) collective-permute-start(bf16[320,2560]{1,0:T(8,128)(2,1)S(1)} %collective-permute-done.refs_1_), channel_id=1, source_target_pairs={{2,4},{3,5},{4,2},{5,3},{10,12},{11,13},{12,10},{13,11},{18,20},{1... | collective-permute-start | bytes 4915208 | tf_op jit(solution)/shard_map/ppermute | solution.py:215
  42.1 7.1 %collective-permute-start.3 = (bf16[320,2560]{1,0:T(8,128)(2,1)S(1)}, bf16[320,2560]{1,0:T(8,128)(2,1)S(1)}, u32[]{:S(2)}, u32[]{:S(2)}) collective-permute-start(bf16[320,2560]{1,0:T(8,128)(2,1)S(1)} %collective-permute-done.refs_1_), channel_id=1, source_target_pairs={{2,3},{3,2},{4,5},{5,4},{10,11},{11,10},{12,13},{13,12},{18,19},{1... | collective-permute-start | bytes 4915208 | tf_op jit(solution)/shard_map/ppermute | solution.py:211
  42.9 1.2 copy-start.3
  42.9 6.3 %collective-permute-start.4 = (bf16[320,2560]{1,0:T(8,128)(2,1)S(1)}, bf16[320,2560]{1,0:T(8,128)(2,1)S(1)}, u32[]{:S(2)}, u32[]{:S(2)}) collective-permute-start(bf16[320,2560]{1,0:T(8,128)(2,1)S(1)} %collective-permute-done.2.refs_4_), channel_id=1, source_target_pairs={{2,3},{3,2},{4,5},{5,4},{10,11},{11,10},{12,13},{13,12},{18,19},{1... | collective-permute-start | bytes 4915208 | tf_op jit(solution)/shard_map/ppermute | solution.py:211
  44.1 1.4 copy-start
  48.4 6.0 %copy-start.1 = (bf16[640,1280]{1,0:T(8,128)(2,1)}, bf16[640,1280]{1,0:T(8,128)(2,1)S(1)}, u32[]{:S(2)}) copy-start(bf16[640,1280]{1,0:T(8,128)(2,1)S(1)} %get-tuple-element.23.refs_9_) | copy-start | bytes 4915204
  48.4 6.0 %collective-permute-start.6 = (bf16[320,2560]{1,0:T(8,128)(2,1)}, bf16[320,2560]{1,0:T(8,128)(2,1)S(1)}, u32[]{:S(2)}, u32[]{:S(2)}) collective-permute-start(bf16[320,2560]{1,0:T(8,128)(2,1)} %collective-permute-done.5.refs_5_.refs_7_), channel_id=1, source_target_pairs={{2,3},{3,2},{4,5},{5,4},{10,11},{11,10},{12,13},{13,12},{18,19},{1... | collective-permute-start | bytes 4915208 | tf_op jit(solution)/shard_map/ppermute | solution.py:211
  49.2 1.2 copy-start.4
  50.3 1.3 copy-start.5
  54.4 1.2 copy-start.6
  55.7 80.6 %collective-permute-start.11 = (bf16[320,1280]{1,0:T(8,128)(2,1)S(1)}, bf16[320,1280]{1,0:T(8,128)(2,1)S(1)}, u32[]{:S(2)}, u32[]{:S(2)}) collective-permute-start(bf16[320,1280]{1,0:T(8,128)(2,1)S(1)} %get-tuple-element.31), channel_id=1, source_target_pairs={{2,0},{3,1},{4,6},{5,7},{10,8},{11,9},{12,14},{13,15},{18,16},{19,... | collective-permute-start | bytes 2457608 | tf_op jit(solution)/shard_map/ppermute | solution.py:234
  57.0 96.7 %collective-permute-start.7 = (bf16[320,1280]{1,0:T(8,128)(2,1)S(1)}, bf16[320,1280]{1,0:T(8,128)(2,1)S(1)}, u32[]{:S(2)}, u32[]{:S(2)}) collective-permute-start(bf16[320,1280]{1,0:T(8,128)(2,1)S(1)} %get-tuple-element.27), channel_id=1, source_target_pairs={{2,0},{3,1},{4,6},{5,7},{10,8},{11,9},{12,14},{13,15},{18,16},{19,... | collective-permute-start | bytes 2457608 | tf_op jit(solution)/shard_map/ppermute | solution.py:234
  136.4 21.0 %collective-permute-start.12 = (bf16[320,1280]{1,0:T(8,128)(2,1)S(1)}, bf16[320,1280]{1,0:T(8,128)(2,1)S(1)}, u32[]{:S(2)}, u32[]{:S(2)}) collective-permute-start(bf16[320,1280]{1,0:T(8,128)(2,1)S(1)} %broadcast_select_fusion), channel_id=1, source_target_pairs={{0,8},{8,0},{16,24},{24,16},{1,9},{9,1},{17,25},{25,17},{2,10},{10... | collective-permute-start | bytes 2457608 | tf_op jit(solution)/shard_map/ppermute | solution.py:236
  137.9 19.6 %collective-permute-start.13 = (bf16[320,1280]{1,0:T(8,128)(2,1)S(1)}, bf16[320,1280]{1,0:T(8,128)(2,1)S(1)}, u32[]{:S(2)}, u32[]{:S(2)}) collective-permute-start(bf16[320,1280]{1,0:T(8,128)(2,1)S(1)} %broadcast_select_fusion), channel_id=1, source_target_pairs={{0,16},{8,24},{16,0},{24,8},{1,17},{9,25},{17,1},{25,9},{2,18},{10... | collective-permute-start | bytes 2457608 | tf_op jit(solution)/shard_map/ppermute | solution.py:237
  153.7 20.2 %collective-permute-start.8 = (bf16[320,1280]{1,0:T(8,128)(2,1)S(1)}, bf16[320,1280]{1,0:T(8,128)(2,1)}, u32[]{:S(2)}, u32[]{:S(2)}) collective-permute-start(bf16[320,1280]{1,0:T(8,128)(2,1)S(1)} %broadcast_select_fusion.1), channel_id=1, source_target_pairs={{0,8},{8,0},{16,24},{24,16},{1,9},{9,1},{17,25},{25,17},{2,10},{10... | collective-permute-start | bytes 2457608 | tf_op jit(solution)/shard_map/ppermute | solution.py:236
  155.3 19.9 %collective-permute-start.9 = (bf16[320,1280]{1,0:T(8,128)(2,1)S(1)}, bf16[320,1280]{1,0:T(8,128)(2,1)}, u32[]{:S(2)}, u32[]{:S(2)}) collective-permute-start(bf16[320,1280]{1,0:T(8,128)(2,1)S(1)} %broadcast_select_fusion.1), channel_id=1, source_target_pairs={{0,16},{8,24},{16,0},{24,8},{1,17},{9,25},{17,1},{25,9},{2,18},{10... | collective-permute-start | bytes 2457608 | tf_op jit(solution)/shard_map/ppermute | solution.py:237
  175.2 19.1 %collective-permute-start.10 = (bf16[320,1280]{1,0:T(8,128)(2,1)}, bf16[320,1280]{1,0:T(8,128)(2,1)S(1)}, u32[]{:S(2)}, u32[]{:S(2)}) collective-permute-start(bf16[320,1280]{1,0:T(8,128)(2,1)} %collective-permute-done.8), channel_id=1, source_target_pairs={{0,16},{8,24},{16,0},{24,8},{1,17},{9,25},{17,1},{25,9},{2,18},{10... | collective-permute-start | bytes 2457608 | tf_op jit(solution)/shard_map/ppermute | solution.py:240
  176.7 18.6 %collective-permute-start.14 = (bf16[320,1280]{1,0:T(8,128)(2,1)S(1)}, bf16[320,1280]{1,0:T(8,128)(2,1)S(1)}, u32[]{:S(2)}, u32[]{:S(2)}) collective-permute-start(bf16[320,1280]{1,0:T(8,128)(2,1)S(1)} %collective-permute-done.13), channel_id=1, source_target_pairs={{0,8},{8,0},{16,24},{24,16},{1,9},{9,1},{17,25},{25,17},{2,10},{10... | collective-permute-start | bytes 2457608 | tf_op jit(solution)/shard_map/ppermute | solution.py:242
  194.6 2.8 %copy-start.2 = (bf16[4,320,2560]{2,1,0:T(8,128)(2,1)}, bf16[4,320,2560]{2,1,0:T(8,128)(2,1)S(1)}, u32[]{:S(2)}) copy-start(bf16[4,320,2560]{2,1,0:T(8,128)(2,1)S(1)} %bitcast_dynamic-update-slice_fusion.1) | copy-start | bytes 19660804

commit v6 on v5

--- a/solution.py
+++ b/solution.py
@@ -12,7 +12,6 @@
 coef_c = 2.0315
 
 TILE = 1280
-LANES = 128
 VMEM_LIMIT = 48 * 1024 * 1024
 
 
@@ -46,58 +45,80 @@
     return [sum(b.shape[0] for b in blocks[:k]) for k in range(len(blocks) + 1)]
 
 
-def early_kernel(rows, first, count, *refs):
-    inner, blocks, refs = refs[0], refs[1 : count + 1], refs[count + 1 :]
-    *cubic_in, gram, cubic, whole, sems = refs
-    columns = blocks[0].shape[1]
-    begin = starts(blocks)
-    base = begin[first]
+def fetch_blocks(blocks, whole, sems):
+    copies = []
+    for k, (block, at) in enumerate(zip(blocks, starts(blocks))):
+        target = whole.at[pl.ds(at, block.shape[0]), :]
+        copies.append(pltpu.make_async_copy(block, target, sems.at[k]))
+        copies[k].start()
+    return copies
+
+
+def gram_kernel(count, *refs):
+    inner, blocks, (gram, whole, sems) = refs[0], refs[1 : count + 1], refs[count + 1 :]
+    left = pl.ds(0, gram.shape[0])
 
     @pl.when(inner[0] != 0)
     def _():
-        copies = []
-        for k, block in enumerate(blocks):
-            target = whole.at[pl.ds(begin[k], block.shape[0]), :]
-            copies.append(pltpu.make_async_copy(block, target, sems.at[k]))
-        if cubic_in:
-            copies.append(pltpu.make_async_copy(cubic_in[0], cubic, sems.at[count]))
-        for copy in copies:
-            copy.start()
+        for copy in fetch_blocks(blocks, whole, sems):
+            copy.wait()
+        for at in tiles(0, whole.shape[0]):
+            gram[:, at] = dot_t(whole[left, :], whole[at, :]).astype(jnp.bfloat16)
+
+
+def cubic_kernel(count, *refs):
+    inner, blocks, refs = refs[0], refs[1 : count + 1], refs[count + 1 :]
+    gram_in, gram, cubic, whole, sems = refs
+    left = pl.ds(0, gram.shape[0])
+    known = gram_in.shape[1]
+
+    @pl.when(inner[0] != 0)
+    def _():
+        copies = fetch_blocks(blocks, whole, sems)
+        copies.append(
+            pltpu.make_async_copy(gram_in, gram.at[:, pl.ds(0, known)], sems.at[count])
+        )
+        copies[count].start()
         for copy in copies:
             copy.wait()
-        for at in tiles(base, begin[-1]):
-            out = pl.ds(at.start - base, at.size)
-            gram[:, out] = dot_t(whole[: 2 * rows, :], whole[at, :]).astype(jnp.bfloat16)
-        for at in tiles(0, columns):
-            add = dot(gram[:, : begin[-1] - base], whole[pl.ds(base, begin[-1] - base), at])
-            cubic[:, at] = (cubic[:, at] + add) if cubic_in else add
-
-
-def early_products(inner, rows, left, blocks, cubic=None):
-    blocks, first = left + blocks, len(left)
+        for at in tiles(known, whole.shape[0]):
+            gram[:, at] = dot_t(whole[left, :], whole[at, :]).astype(jnp.bfloat16)
+        for at in tiles(0, whole.shape[1]):
+            cubic[:, at] = dot(gram[...], whole[:, at])
+
+
+def early_products(kernel, inner, blocks, more, out_shape, flops):
     count = len(blocks)
-    columns = blocks[0].shape[1]
-    begin = starts(blocks)
-    known = begin[-1] - begin[first]
-    more = [] if cubic is None else [cubic]
     return pl.pallas_call(
-        functools.partial(early_kernel, rows, first, count),
-        out_shape=(
-            jax.ShapeDtypeStruct((2 * rows, pl.cdiv(known, LANES) * LANES), jnp.bfloat16),
-            jax.ShapeDtypeStruct((2 * rows, columns), jnp.float32),
-        ),
+        functools.partial(kernel, count),
+        out_shape=out_shape,
         in_specs=[pl.BlockSpec(memory_space=pltpu.SMEM)]
         + [pl.BlockSpec(memory_space=pl.ANY)] * (count + len(more)),
-        out_specs=(pl.BlockSpec(memory_space=pltpu.VMEM),) * 2,
+        out_specs=tuple(pl.BlockSpec(memory_space=pltpu.VMEM) for _ in out_shape),
         scratch_shapes=[
-            pltpu.VMEM((begin[-1], columns), jnp.bfloat16),
+            pltpu.VMEM((starts(blocks)[-1], blocks[0].shape[1]), jnp.bfloat16),
             pltpu.SemaphoreType.DMA((count + len(more),)),
         ],
         compiler_params=pltpu.CompilerParams(vmem_limit_bytes=VMEM_LIMIT),
-        cost_estimate=pl.CostEstimate(
-            flops=8 * rows * known * columns, bytes_accessed=4 * known * columns, transcendentals=0
-        ),
+        cost_estimate=pl.CostEstimate(flops=flops, bytes_accessed=flops // 1024, transcendentals=0),
     )(inner, *blocks, *more)
+
+
+def first_grams(inner, blocks, rows):
+    columns = blocks[0].shape[1]
+    known = starts(blocks)[-1]
+    shape = (jax.ShapeDtypeStruct((2 * rows, known), jnp.bfloat16),)
+    return early_products(gram_kernel, inner, blocks, [], shape, 4 * rows * known * columns)[0]
+
+
+def early_cubic(inner, blocks, rows, gram):
+    columns = blocks[0].shape[1]
+    known = starts(blocks)[-1]
+    shape = (
+        jax.ShapeDtypeStruct((2 * rows, known), jnp.bfloat16),
+        jax.ShapeDtypeStruct((2 * rows, columns), jnp.float32),
+    )
+    return early_products(cubic_kernel, inner, blocks, [gram], shape, 6 * rows * known * columns)
 
 
 def late_kernel(first, early_count, count, gram_count, widths, *refs):
@@ -207,22 +228,30 @@
     along_x = [(m, m ^ 1) for m in range(4)]
     along_y = [(m, m ^ 2) for m in range(4)]
 
-    def swap(block):
-        return lax.ppermute(block, "shard", other_core)
-
-    from_outer = lax.ppermute(own, "shard", inwards)
-    from_inner = lax.ppermute(own, "shard", middle)
-    from_far = lax.ppermute(from_outer, "shard", middle)
-
-    left = [from_outer, own]
-    first = left + [swap(own), from_inner]
-    first_gram, cubic = early_products(inner, rows, [], first)
-    from_far, first_gram, cubic = tie((from_far, first_gram, cubic))
-    then = [swap(from_outer), swap(from_inner), from_far]
-    then_gram, cubic = early_products(inner, rows, left, then, cubic)
-    early, grams, late = first + then, [first_gram, then_gram], [swap(from_far)]
-    for_outer = late_products(inner, 0, rows, early, late, grams, cubic, widths)
-    for_own = late_products(inner, rows, rows, early, late, grams, cubic, widths)
+    def move(name, block, axis, pairs):
+        with jax.named_scope(name):
+            return lax.ppermute(block, axis, pairs)
+
+    def swap(name, block):
+        return move("swap_" + name, block, "shard", other_core)
+
+    cut = rows // 2
+    halves = [own[:cut], own[cut:]]
+    outer_rows = [move("rows_in", half, "shard", inwards) for half in halves]
+    inner_rows = move("middle_own", own, "shard", middle)
+    far_rows = [move("middle_far", half, "shard", middle) for half in outer_rows]
+
+    inner_rows, _ = tie((inner_rows, outer_rows[1]))
+    first = outer_rows + [own, swap("own", own), inner_rows]
+    gram = first_grams(inner, first, rows)
+    far_rows[0], gram = tie((far_rows[0], gram))
+    then = [swap("outer", half) for half in outer_rows] + [swap("inner", inner_rows)]
+    early = first + then
+    gram, cubic = early_cubic(inner, early, rows, gram)
+    far_rows[1], gram, cubic = tie((far_rows[1], gram, cubic))
+    late = far_rows + [swap("far", half) for half in far_rows]
+    for_outer = late_products(inner, 0, rows, early, late, [gram], cubic, widths)
+    for_own = late_products(inner, rows, rows, early, late, [gram], cubic, widths)
 
     result = jnp.zeros((4, rows, columns), jnp.bfloat16)
 
@@ -231,15 +260,15 @@
 
     begin = 0
     for k, width in enumerate(widths):
-        returned = lax.ppermute(for_outer[k], "shard", outwards)
+        returned = move("rows_out", for_outer[k], "shard", outwards)
         mine = tie(jnp.where(outer, returned, for_own[k]))
-        by_x = lax.ppermute(mine, "mat", along_x)
-        by_y = lax.ppermute(mine, "mat", along_y)
+        by_x = move("along_x", mine, "mat", along_x)
+        by_y = move("along_y", mine, "mat", along_y)
         by_x, by_y = tie((by_x, by_y))
         if k % 2 == 0:
-            across = lax.ppermute(by_x, "mat", along_y)
+            across = move("across_y", by_x, "mat", along_y)
         else:
-            across = lax.ppermute(by_y, "mat", along_x)
+            across = move("across_x", by_y, "mat", along_x)
         for flip, part in enumerate((mine, by_x, by_y, across)):
             result = place_in(result, flip, begin, part)
         begin += width

time: 199 us -> 193 us (0.970)
  waiting for transfers between devices: 158 us -> 146 us
  starting transfers between devices: 22.5 us -> 29.4 us
    ppermute x15 -> x19, waiting for transfers between devices: 158 us -> 146 us  [move(): return lax.ppermute(block, axis, pairs)]
    ppermute x15 -> x19, starting transfers between devices: 22.5 us -> 29.4 us  [move(): return lax.ppermute(block, axis, pairs)]
    unnamed x14 -> x12, local copies, waits for them, and re-layouts: 7.51 us -> 6.61 us
  transfers between devices with their start and end apart: 15 -> 19, of which waited for: 8 -> 8; matrix products, arithmetic and copies ran while one was open for 2% -> 3% of each run, Pallas kernels for 3% -> 2%
where the time goes in v6:
time: 193 us
  waiting for transfers between devices  146 us (76%)
  starting transfers between devices  29.4 us (15%)
  local copies, waits for them, and re-layouts  12.3 us (6%)
  Pallas kernels  4.22 us (2%)
    ppermute x19, waiting for transfers between devices, move(): return lax.ppermute(block, axis, pairs)  146 us
    ppermute x19, starting transfers between devices, move(): return lax.ppermute(block, axis, pairs)  29.4 us
    unnamed x12, local copies, waits for them, and re-layouts  6.61 us
  transfers between devices with their start and end apart: 19, of which 8 were waited for; matrix products, arithmetic and copies ran while one was open for 3% of the time, Pallas kernels for 2%

profile of v6, /device:TPU:0, one launch (start us, length us, event | category | flops | bytes accessed | tf_op | source)
XLA Modules:
  0.0 192.9 jit_solution(17933753372930256118)
XLA Ops:
  0.0 1.9 collective-permute-start.3
  1.9 1.5 slice_bitcast_fusion
  3.4 6.6 %collective-permute-start.1 = (bf16[160,2560]{1,0:T(8,128)(2,1)S(1)}, bf16[160,2560]{1,0:T(8,128)(2,1)S(1)}, u32[]{:S(2)}, u32[]{:S(2)}) collective-permute-start(bf16[160,2560]{1,0:T(8,128)(2,1)S(1)} %get-tuple-element.37), channel_id=1, source_target_pairs={{0,2},{1,3},{6,4},{7,5},{8,10},{9,11},{14,12},{15,13},{16,18},{17,... | collective-permute-start | bytes 2457608 | tf_op jit(solution)/shard_map/rows_in/ppermute | solution.py:233
  10.0 1.8 collective-permute-start.2
  11.8 1.4 collective-permute-start
  13.2 15.4 %collective-permute-done.1.refs_2_ = bf16[160,2560]{1,0:T(8,128)(2,1)S(1)} collective-permute-done((bf16[160,2560]{1,0:T(8,128)(2,1)S(1)}, bf16[160,2560]{1,0:T(8,128)(2,1)S(1)}, u32[]{:S(2)}, u32[]{:S(2)}) %collective-permute-start.1) | collective-permute-done | bytes 819232 | tf_op jit(solution)/shard_map/rows_in/ppermute | solution.py:233
  28.6 1.8 collective-permute-start.6
  30.4 14.3 %collective-permute-done.refs_1_ = bf16[160,2560]{1,0:T(8,128)(2,1)S(1)} collective-permute-done((bf16[160,2560]{1,0:T(8,128)(2,1)S(1)}, bf16[160,2560]{1,0:T(8,128)(2,1)S(1)}, u32[]{:S(2)}, u32[]{:S(2)}) %collective-permute-start) | collective-permute-done | bytes 819232 | tf_op jit(solution)/shard_map/rows_in/ppermute | solution.py:233
  46.1 1.6 collective-permute-start.4
  48.4 1.4 copy-done
  51.9 3.7 %shard_map.18 = (bf16[640,1920]{1,0:T(8,128)(2,1)}, f32[640,2560]{1,0:T(8,128)}) custom-call(s32[1]{0:T(128)} %bitcast.refs_0_, bf16[160,2560]{1,0:T(8,128)(2,1)S(1)} %collective-permute-done.refs_1_, bf16[160,2560]{1,0:T(8,128)(2,1)S(1)} %collective-permute-done.1.refs_2_, bf16[320,2560]{1,0:T(8,128)(2,1)S(1)} %bitcast.27, ...), custom_call_target="tpu_custom_call" | custom-call | flops 9437184000 | bytes 9216000 | tf_op jit(solution)/shard_map/pallas_call | solution.py:92
  58.4 1.3 collective-permute-start.15
  59.7 1.3 collective-permute-start.11
  61.3 69.9 %collective-permute-done.15 = bf16[320,1280]{1,0:T(8,128)(2,1)S(1)} collective-permute-done((bf16[320,1280]{1,0:T(8,128)(2,1)S(1)}, bf16[320,1280]{1,0:T(8,128)(2,1)S(1)}, u32[]{:S(2)}, u32[]{:S(2)}) %collective-permute-start.15) | collective-permute-done | bytes 819232 | tf_op jit(solution)/shard_map/rows_out/ppermute | solution.py:233
  131.3 1.5 collective-permute-start.16
  132.9 1.5 collective-permute-start.17
  134.4 14.1 %collective-permute-done.11 = bf16[320,1280]{1,0:T(8,128)(2,1)S(1)} collective-permute-done((bf16[320,1280]{1,0:T(8,128)(2,1)S(1)}, bf16[320,1280]{1,0:T(8,128)(2,1)S(1)}, u32[]{:S(2)}, u32[]{:S(2)}) %collective-permute-start.11) | collective-permute-done | bytes 819232 | tf_op jit(solution)/shard_map/rows_out/ppermute | solution.py:233
  148.5 1.6 collective-permute-start.12
  150.1 1.5 collective-permute-start.13
  152.2 16.4 %collective-permute-done.12 = bf16[320,1280]{1,0:T(8,128)(2,1)} collective-permute-done((bf16[320,1280]{1,0:T(8,128)(2,1)S(1)}, bf16[320,1280]{1,0:T(8,128)(2,1)}, u32[]{:S(2)}, u32[]{:S(2)}) %collective-permute-start.12) | collective-permute-done | bytes 819232 | tf_op jit(solution)/shard_map/along_x/ppermute | solution.py:233
  168.6 1.2 collective-permute-done.13
  169.9 1.5 collective-permute-start.14
  174.3 14.5 %collective-permute-done.14 = bf16[320,1280]{1,0:T(8,128)(2,1)S(1)} collective-permute-done((bf16[320,1280]{1,0:T(8,128)(2,1)}, bf16[320,1280]{1,0:T(8,128)(2,1)S(1)}, u32[]{:S(2)}, u32[]{:S(2)}) %collective-permute-start.14) | collective-permute-done | bytes 819232 | tf_op jit(solution)/shard_map/across_y/ppermute | solution.py:233
  189.9 2.0 %copy-done.2 = bf16[4,320,2560]{2,1,0:T(8,128)(2,1)} copy-done((bf16[4,320,2560]{2,1,0:T(8,128)(2,1)}, bf16[4,320,2560]{2,1,0:T(8,128)(2,1)S(1)}, u32[]{:S(2)}) %copy-start.2) | copy-done | bytes 6553624
  (42 shorter events, 12.8 us)
Async XLA Ops:
  0.0 28.6 %collective-permute-start.3 = (bf16[320,2560]{1,0:T(8,128)(2,1)}, bf16[320,2560]{1,0:T(8,128)(2,1)}, u32[]{:S(2)}, u32[]{:S(2)}) collective-permute-start(bf16[320,2560]{1,0:T(8,128)(2,1)} %bitcast.22), channel_id=1, source_target_pairs={{2,4},{3,5},{4,2},{5,3},{10,12},{11,13},{12,10},{13,11},{18,20},{1... | collective-permute-start | bytes 4915208 | tf_op jit(solution)/shard_map/middle_own/ppermute | solution.py:233
  3.4 25.2 %collective-permute-start.1 = (bf16[160,2560]{1,0:T(8,128)(2,1)S(1)}, bf16[160,2560]{1,0:T(8,128)(2,1)S(1)}, u32[]{:S(2)}, u32[]{:S(2)}) collective-permute-start(bf16[160,2560]{1,0:T(8,128)(2,1)S(1)} %get-tuple-element.37), channel_id=1, source_target_pairs={{0,2},{1,3},{6,4},{7,5},{8,10},{9,11},{14,12},{15,13},{16,18},{17,... | collective-permute-start | bytes 2457608 | tf_op jit(solution)/shard_map/rows_in/ppermute | solution.py:233
  10.0 37.7 %collective-permute-start.2 = (bf16[320,2560]{1,0:T(8,128)(2,1)}, bf16[320,2560]{1,0:T(8,128)(2,1)}, u32[]{:S(2)}, u32[]{:S(2)}) collective-permute-start(bf16[320,2560]{1,0:T(8,128)(2,1)} %bitcast.23), channel_id=1, source_target_pairs={{2,3},{3,2},{4,5},{5,4},{10,11},{11,10},{12,13},{13,12},{18,19},{1... | collective-permute-start | bytes 4915208 | tf_op jit(solution)/shard_map/swap_own/ppermute | solution.py:233
  11.8 32.9 %collective-permute-start = (bf16[160,2560]{1,0:T(8,128)(2,1)S(1)}, bf16[160,2560]{1,0:T(8,128)(2,1)S(1)}, u32[]{:S(2)}, u32[]{:S(2)}) collective-permute-start(bf16[160,2560]{1,0:T(8,128)(2,1)S(1)} %get-tuple-element.38), channel_id=1, source_target_pairs={{0,2},{1,3},{6,4},{7,5},{8,10},{9,11},{14,12},{15,13},{16,18},{17,... | collective-permute-start | bytes 2457608 | tf_op jit(solution)/shard_map/rows_in/ppermute | solution.py:233
  28.6 23.3 %collective-permute-start.6 = (bf16[320,2560]{1,0:T(8,128)(2,1)}, bf16[320,2560]{1,0:T(8,128)(2,1)}, u32[]{:S(2)}, u32[]{:S(2)}) collective-permute-start(bf16[320,2560]{1,0:T(8,128)(2,1)} %collective-permute-done.3.refs_5_), channel_id=1, source_target_pairs={{2,3},{3,2},{4,5},{5,4},{10,11},{11,10},{12,13},{13,12},{18,19},{1... | collective-permute-start | bytes 4915208 | tf_op jit(solution)/shard_map/swap_inner/ppermute | solution.py:233
  44.7 6.4 %collective-permute-start.7 = (bf16[160,2560]{1,0:T(8,128)(2,1)S(1)}, bf16[160,2560]{1,0:T(8,128)(2,1)S(1)}, u32[]{:S(2)}, u32[]{:S(2)}) collective-permute-start(bf16[160,2560]{1,0:T(8,128)(2,1)S(1)} %collective-permute-done.refs_1_), channel_id=1, source_target_pairs={{2,4},{3,5},{4,2},{5,3},{10,12},{11,13},{12,10},{13,11},{18,20},{1... | collective-permute-start | bytes 2457608 | tf_op jit(solution)/shard_map/middle_far/ppermute | solution.py:233
  45.4 6.4 %collective-permute-start.5 = (bf16[160,2560]{1,0:T(8,128)(2,1)S(1)}, bf16[160,2560]{1,0:T(8,128)(2,1)S(1)}, u32[]{:S(2)}, u32[]{:S(2)}) collective-permute-start(bf16[160,2560]{1,0:T(8,128)(2,1)S(1)} %collective-permute-done.1.refs_2_), channel_id=1, source_target_pairs={{2,3},{3,2},{4,5},{5,4},{10,11},{11,10},{12,13},{13,12},{18,19},{1... | collective-permute-start | bytes 2457608 | tf_op jit(solution)/shard_map/swap_outer/ppermute | solution.py:233
  46.1 5.7 %collective-permute-start.4 = (bf16[160,2560]{1,0:T(8,128)(2,1)S(1)}, bf16[160,2560]{1,0:T(8,128)(2,1)}, u32[]{:S(2)}, u32[]{:S(2)}) collective-permute-start(bf16[160,2560]{1,0:T(8,128)(2,1)S(1)} %collective-permute-done.refs_1_), channel_id=1, source_target_pairs={{2,3},{3,2},{4,5},{5,4},{10,11},{11,10},{12,13},{13,12},{18,19},{1... | collective-permute-start | bytes 2457608 | tf_op jit(solution)/shard_map/swap_outer/ppermute | solution.py:233
  47.7 7.9 %collective-permute-start.8 = (bf16[160,2560]{1,0:T(8,128)(2,1)S(1)}, bf16[160,2560]{1,0:T(8,128)(2,1)S(1)}, u32[]{:S(2)}, u32[]{:S(2)}) collective-permute-start(bf16[160,2560]{1,0:T(8,128)(2,1)S(1)} %collective-permute-done.1.refs_2_), channel_id=1, source_target_pairs={{2,4},{3,5},{4,2},{5,3},{10,12},{11,13},{12,10},{13,11},{18,20},{1... | collective-permute-start | bytes 2457608 | tf_op jit(solution)/shard_map/middle_far/ppermute | solution.py:233
  48.4 1.4 copy-start
  49.9 1.3 copy-start.1
  51.1 5.2 %collective-permute-start.9 = (bf16[160,2560]{1,0:T(8,128)(2,1)S(1)}, bf16[160,2560]{1,0:T(8,128)(2,1)S(1)}, u32[]{:S(2)}, u32[]{:S(2)}) collective-permute-start(bf16[160,2560]{1,0:T(8,128)(2,1)S(1)} %collective-permute-done.7.refs_9_), channel_id=1, source_target_pairs={{2,3},{3,2},{4,5},{5,4},{10,11},{11,10},{12,13},{13,12},{18,19},{1... | collective-permute-start | bytes 2457608 | tf_op jit(solution)/shard_map/swap_far/ppermute | solution.py:233
  55.6 1.0 copy-start.3
  55.6 0.7 collective-permute-start.10
  56.3 1.0 copy-start.4
  58.4 72.9 %collective-permute-start.15 = (bf16[320,1280]{1,0:T(8,128)(2,1)S(1)}, bf16[320,1280]{1,0:T(8,128)(2,1)S(1)}, u32[]{:S(2)}, u32[]{:S(2)}) collective-permute-start(bf16[320,1280]{1,0:T(8,128)(2,1)S(1)} %get-tuple-element.33), channel_id=1, source_target_pairs={{2,0},{3,1},{4,6},{5,7},{10,8},{11,9},{12,14},{13,15},{18,16},{19,... | collective-permute-start | bytes 2457608 | tf_op jit(solution)/shard_map/rows_out/ppermute | solution.py:233
  59.7 88.8 %collective-permute-start.11 = (bf16[320,1280]{1,0:T(8,128)(2,1)S(1)}, bf16[320,1280]{1,0:T(8,128)(2,1)S(1)}, u32[]{:S(2)}, u32[]{:S(2)}) collective-permute-start(bf16[320,1280]{1,0:T(8,128)(2,1)S(1)} %get-tuple-element.29), channel_id=1, source_target_pairs={{2,0},{3,1},{4,6},{5,7},{10,8},{11,9},{12,14},{13,15},{18,16},{19,... | collective-permute-start | bytes 2457608 | tf_op jit(solution)/shard_map/rows_out/ppermute | solution.py:233
  131.3 20.9 %collective-permute-start.16 = (bf16[320,1280]{1,0:T(8,128)(2,1)S(1)}, bf16[320,1280]{1,0:T(8,128)(2,1)S(1)}, u32[]{:S(2)}, u32[]{:S(2)}) collective-permute-start(bf16[320,1280]{1,0:T(8,128)(2,1)S(1)} %broadcast_select_fusion), channel_id=1, source_target_pairs={{0,8},{8,0},{16,24},{24,16},{1,9},{9,1},{17,25},{25,17},{2,10},{10... | collective-permute-start | bytes 2457608 | tf_op jit(solution)/shard_map/along_x/ppermute | solution.py:233
  132.9 19.4 %collective-permute-start.17 = (bf16[320,1280]{1,0:T(8,128)(2,1)S(1)}, bf16[320,1280]{1,0:T(8,128)(2,1)S(1)}, u32[]{:S(2)}, u32[]{:S(2)}) collective-permute-start(bf16[320,1280]{1,0:T(8,128)(2,1)S(1)} %broadcast_select_fusion), channel_id=1, source_target_pairs={{0,16},{8,24},{16,0},{24,8},{1,17},{9,25},{17,1},{25,9},{2,18},{10... | collective-permute-start | bytes 2457608 | tf_op jit(solution)/shard_map/along_y/ppermute | solution.py:233
  148.5 20.1 %collective-permute-start.12 = (bf16[320,1280]{1,0:T(8,128)(2,1)S(1)}, bf16[320,1280]{1,0:T(8,128)(2,1)}, u32[]{:S(2)}, u32[]{:S(2)}) collective-permute-start(bf16[320,1280]{1,0:T(8,128)(2,1)S(1)} %broadcast_select_fusion.1), channel_id=1, source_target_pairs={{0,8},{8,0},{16,24},{24,16},{1,9},{9,1},{17,25},{25,17},{2,10},{10... | collective-permute-start | bytes 2457608 | tf_op jit(solution)/shard_map/along_x/ppermute | solution.py:233
  150.1 19.8 %collective-permute-start.13 = (bf16[320,1280]{1,0:T(8,128)(2,1)S(1)}, bf16[320,1280]{1,0:T(8,128)(2,1)}, u32[]{:S(2)}, u32[]{:S(2)}) collective-permute-start(bf16[320,1280]{1,0:T(8,128)(2,1)S(1)} %broadcast_select_fusion.1), channel_id=1, source_target_pairs={{0,16},{8,24},{16,0},{24,8},{1,17},{9,25},{17,1},{25,9},{2,18},{10... | collective-permute-start | bytes 2457608 | tf_op jit(solution)/shard_map/along_y/ppermute | solution.py:233
  169.9 19.0 %collective-permute-start.14 = (bf16[320,1280]{1,0:T(8,128)(2,1)}, bf16[320,1280]{1,0:T(8,128)(2,1)S(1)}, u32[]{:S(2)}, u32[]{:S(2)}) collective-permute-start(bf16[320,1280]{1,0:T(8,128)(2,1)} %collective-permute-done.12), channel_id=1, source_target_pairs={{0,16},{8,24},{16,0},{24,8},{1,17},{9,25},{17,1},{25,9},{2,18},{10... | collective-permute-start | bytes 2457608 | tf_op jit(solution)/shard_map/across_y/ppermute | solution.py:233
  171.4 18.5 %collective-permute-start.18 = (bf16[320,1280]{1,0:T(8,128)(2,1)S(1)}, bf16[320,1280]{1,0:T(8,128)(2,1)S(1)}, u32[]{:S(2)}, u32[]{:S(2)}) collective-permute-start(bf16[320,1280]{1,0:T(8,128)(2,1)S(1)} %collective-permute-done.17), channel_id=1, source_target_pairs={{0,8},{8,0},{16,24},{24,16},{1,9},{9,1},{17,25},{25,17},{2,10},{10... | collective-permute-start | bytes 2457608 | tf_op jit(solution)/shard_map/across_x/ppermute | solution.py:233
  189.1 2.8 %copy-start.2 = (bf16[4,320,2560]{2,1,0:T(8,128)(2,1)}, bf16[4,320,2560]{2,1,0:T(8,128)(2,1)S(1)}, u32[]{:S(2)}) copy-start(bf16[4,320,2560]{2,1,0:T(8,128)(2,1)S(1)} %bitcast_dynamic-update-slice_fusion.1) | copy-start | bytes 19660804
  (1 other events, 0.9 us)

commit v7 on v6

--- a/solution.py
+++ b/solution.py
@@ -11,8 +11,8 @@
 coef_b = -4.775
 coef_c = 2.0315
 
-TILE = 1280
-VMEM_LIMIT = 48 * 1024 * 1024
+TILE = 1024
+VMEM_LIMIT = 30 * 1024 * 1024
 
 
 def dot_t(left, right):
@@ -93,7 +93,8 @@
         functools.partial(kernel, count),
         out_shape=out_shape,
         in_specs=[pl.BlockSpec(memory_space=pltpu.SMEM)]
-        + [pl.BlockSpec(memory_space=pl.ANY)] * (count + len(more)),
+        + [pl.BlockSpec(memory_space=pltpu.HBM)] * count
+        + [pl.BlockSpec(memory_space=pl.ANY)] * len(more),
         out_specs=tuple(pl.BlockSpec(memory_space=pltpu.VMEM) for _ in out_shape),
         scratch_shapes=[
             pltpu.VMEM((starts(blocks)[-1], blocks[0].shape[1]), jnp.bfloat16),
@@ -176,13 +177,16 @@
                 jnp.bfloat16
             )
 
-        left = 0
-        for out, width in zip(outs, widths):
-            at = pl.ds(left, width)
+        for at in tiles(0, columns):
             product = dot(poly[...], whole[:, at])
             base = whole[mine, at].astype(jnp.float32)
-            out[...] = (coef_a * base + product).astype(jnp.bfloat16)
-            left += width
+            new = (coef_a * base + product).astype(jnp.bfloat16)
+            left = 0
+            for out, width in zip(outs, widths):
+                low, high = max(at.start, left), min(at.start + at.size, left + width)
+                if low < high:
+                    out[:, low - left : high - left] = new[:, low - at.start : high - at.start]
+                left += width
 
 
 def late_products(inner, first, rows, early, late, grams, cubic, widths):
@@ -194,7 +198,8 @@
         functools.partial(late_kernel, first, len(early), count, len(grams), widths),
         out_shape=tuple(jax.ShapeDtypeStruct((rows, w), jnp.bfloat16) for w in widths),
         in_specs=[pl.BlockSpec(memory_space=pltpu.SMEM)]
-        + [pl.BlockSpec(memory_space=pl.ANY)] * (count + len(grams) + 1),
+        + [pl.BlockSpec(memory_space=pltpu.HBM)] * count
+        + [pl.BlockSpec(memory_space=pl.ANY)] * (len(grams) + 1),
         out_specs=tuple(pl.BlockSpec(memory_space=pltpu.VMEM) for _ in widths),
         scratch_shapes=[
             pltpu.VMEM((total, columns), jnp.bfloat16),

time: 193 us -> 188 us (0.974)
  Pallas kernels: 4.22 us -> 0.82 us
  local copies, waits for them, and re-layouts: 12.3 us -> 9.17 us
  starting transfers between devices: 29.4 us -> 32 us
    pallas_call x2, Pallas kernels: 3.73 us -> 0.14 us  [early_products(): pl.pallas_call(functools.partial(kernel, count), out_shape=out_shape, in_...]
    unnamed x12 -> x4, local copies, waits for them, and re-layouts: 6.61 us -> 3.48 us
    ppermute x19, starting transfers between devices: 29.4 us -> 32 us  [move(): return lax.ppermute(block, axis, pairs)]
  transfers between devices with their start and end apart: 19 -> 19, of which waited for: 8 -> 8; matrix products, arithmetic and copies ran while one was open for 3% -> 3% of each run, Pallas kernels for 2% -> 0%
where the time goes in v7:
time: 188 us; the launch traced here: 187 us
  waiting for transfers between devices  145 us (77%)
  starting transfers between devices  32 us (17%)
  local copies, waits for them, and re-layouts  9.17 us (5%)
    ppermute x19, waiting for transfers between devices, move(): return lax.ppermute(block, axis, pairs)  145 us
    ppermute x19, starting transfers between devices, move(): return lax.ppermute(block, axis, pairs)  32 us
  transfers between devices with their start and end apart: 19, of which 8 were waited for; matrix products, arithmetic and copies ran while one was open for 3% of the time, Pallas kernels for 0%

profile of v7, /device:TPU:0, one launch (start us, length us, event | category | flops | bytes accessed | tf_op | source)
XLA Modules:
  0.0 187.2 jit_solution(16785288822517285715)
XLA Ops:
  0.8 1.5 slice_bitcast_fusion
  2.3 8.6 %collective-permute-start.1 = (bf16[160,2560]{1,0:T(8,128)(2,1)S(1)}, bf16[160,2560]{1,0:T(8,128)(2,1)}, u32[]{:S(2)}, u32[]{:S(2)}) collective-permute-start(bf16[160,2560]{1,0:T(8,128)(2,1)S(1)} %get-tuple-element.37), channel_id=1, source_target_pairs={{0,2},{1,3},{6,4},{7,5},{8,10},{9,11},{14,12},{15,13},{16,18},{17,... | collective-permute-start | bytes 2457608 | tf_op jit(solution)/shard_map/rows_in/ppermute | solution.py:238
  11.6 2.5 %collective-permute-start = (bf16[160,2560]{1,0:T(8,128)(2,1)S(1)}, bf16[160,2560]{1,0:T(8,128)(2,1)}, u32[]{:S(2)}, u32[]{:S(2)}) collective-permute-start(bf16[160,2560]{1,0:T(8,128)(2,1)S(1)} %get-tuple-element.38), channel_id=1, source_target_pairs={{0,2},{1,3},{6,4},{7,5},{8,10},{9,11},{14,12},{15,13},{16,18},{17,... | collective-permute-start | bytes 2457608 | tf_op jit(solution)/shard_map/rows_in/ppermute | solution.py:238
  14.1 14.5 %collective-permute-done.1.refs_2_ = bf16[160,2560]{1,0:T(8,128)(2,1)} collective-permute-done((bf16[160,2560]{1,0:T(8,128)(2,1)S(1)}, bf16[160,2560]{1,0:T(8,128)(2,1)}, u32[]{:S(2)}, u32[]{:S(2)}) %collective-permute-start.1) | collective-permute-done | bytes 819232 | tf_op jit(solution)/shard_map/rows_in/ppermute | solution.py:238
  28.6 1.9 collective-permute-start.6
  30.4 14.2 %collective-permute-done.refs_1_ = bf16[160,2560]{1,0:T(8,128)(2,1)} collective-permute-done((bf16[160,2560]{1,0:T(8,128)(2,1)S(1)}, bf16[160,2560]{1,0:T(8,128)(2,1)}, u32[]{:S(2)}, u32[]{:S(2)}) %collective-permute-start) | collective-permute-done | bytes 819232 | tf_op jit(solution)/shard_map/rows_in/ppermute | solution.py:238
  44.7 1.6 collective-permute-start.7
  46.3 1.6 collective-permute-start.5
  47.8 1.6 collective-permute-start.4
  50.1 1.4 copy-done
  53.5 1.3 collective-permute-start.15
  54.8 1.3 collective-permute-start.11
  56.5 69.1 %collective-permute-done.15 = bf16[320,1280]{1,0:T(8,128)(2,1)S(1)} collective-permute-done((bf16[320,1280]{1,0:T(8,128)(2,1)S(1)}, bf16[320,1280]{1,0:T(8,128)(2,1)S(1)}, u32[]{:S(2)}, u32[]{:S(2)}) %collective-permute-start.15) | collective-permute-done | bytes 819232 | tf_op jit(solution)/shard_map/rows_out/ppermute | solution.py:238
  125.7 1.6 collective-permute-start.16
  127.2 1.5 collective-permute-start.17
  128.8 14.1 %collective-permute-done.11 = bf16[320,1280]{1,0:T(8,128)(2,1)S(1)} collective-permute-done((bf16[320,1280]{1,0:T(8,128)(2,1)S(1)}, bf16[320,1280]{1,0:T(8,128)(2,1)S(1)}, u32[]{:S(2)}, u32[]{:S(2)}) %collective-permute-start.11) | collective-permute-done | bytes 819232 | tf_op jit(solution)/shard_map/rows_out/ppermute | solution.py:238
  142.9 1.5 collective-permute-start.12
  144.5 1.5 collective-permute-start.13
  146.6 16.5 %collective-permute-done.12 = bf16[320,1280]{1,0:T(8,128)(2,1)} collective-permute-done((bf16[320,1280]{1,0:T(8,128)(2,1)S(1)}, bf16[320,1280]{1,0:T(8,128)(2,1)}, u32[]{:S(2)}, u32[]{:S(2)}) %collective-permute-start.12) | collective-permute-done | bytes 819232 | tf_op jit(solution)/shard_map/along_x/ppermute | solution.py:238
  164.2 1.5 collective-permute-start.14
  166.3 1.2 bitcast_dynamic-update-slice_fusion.6
  167.5 1.2 bitcast_dynamic-update-slice_fusion.5
  168.7 14.4 %collective-permute-done.14 = bf16[320,1280]{1,0:T(8,128)(2,1)S(1)} collective-permute-done((bf16[320,1280]{1,0:T(8,128)(2,1)}, bf16[320,1280]{1,0:T(8,128)(2,1)S(1)}, u32[]{:S(2)}, u32[]{:S(2)}) %collective-permute-start.14) | collective-permute-done | bytes 819232 | tf_op jit(solution)/shard_map/across_y/ppermute | solution.py:238
  184.2 2.1 %copy-done.1 = bf16[4,320,2560]{2,1,0:T(8,128)(2,1)} copy-done((bf16[4,320,2560]{2,1,0:T(8,128)(2,1)}, bf16[4,320,2560]{2,1,0:T(8,128)(2,1)S(1)}, u32[]{:S(2)}) %copy-start.1) | copy-done | bytes 6553624
  (34 shorter events, 8.9 us)
Async XLA Ops:
  0.0 28.6 %collective-permute-start.3 = (bf16[320,2560]{1,0:T(8,128)(2,1)}, bf16[320,2560]{1,0:T(8,128)(2,1)S(1)}, u32[]{:S(2)}, u32[]{:S(2)}) collective-permute-start(bf16[320,2560]{1,0:T(8,128)(2,1)} %bitcast.22), channel_id=1, source_target_pairs={{2,4},{3,5},{4,2},{5,3},{10,12},{11,13},{12,10},{13,11},{18,20},{1... | collective-permute-start | bytes 4915208 | tf_op jit(solution)/shard_map/middle_own/ppermute | solution.py:238
  2.3 26.3 %collective-permute-start.1 = (bf16[160,2560]{1,0:T(8,128)(2,1)S(1)}, bf16[160,2560]{1,0:T(8,128)(2,1)}, u32[]{:S(2)}, u32[]{:S(2)}) collective-permute-start(bf16[160,2560]{1,0:T(8,128)(2,1)S(1)} %get-tuple-element.37), channel_id=1, source_target_pairs={{0,2},{1,3},{6,4},{7,5},{8,10},{9,11},{14,12},{15,13},{16,18},{17,... | collective-permute-start | bytes 2457608 | tf_op jit(solution)/shard_map/rows_in/ppermute | solution.py:238
  10.8 38.6 %collective-permute-start.2 = (bf16[320,2560]{1,0:T(8,128)(2,1)}, bf16[320,2560]{1,0:T(8,128)(2,1)S(1)}, u32[]{:S(2)}, u32[]{:S(2)}) collective-permute-start(bf16[320,2560]{1,0:T(8,128)(2,1)} %bitcast.23), channel_id=1, source_target_pairs={{2,3},{3,2},{4,5},{5,4},{10,11},{11,10},{12,13},{13,12},{18,19},{1... | collective-permute-start | bytes 4915208 | tf_op jit(solution)/shard_map/swap_own/ppermute | solution.py:238
  11.6 33.1 %collective-permute-start = (bf16[160,2560]{1,0:T(8,128)(2,1)S(1)}, bf16[160,2560]{1,0:T(8,128)(2,1)}, u32[]{:S(2)}, u32[]{:S(2)}) collective-permute-start(bf16[160,2560]{1,0:T(8,128)(2,1)S(1)} %get-tuple-element.38), channel_id=1, source_target_pairs={{0,2},{1,3},{6,4},{7,5},{8,10},{9,11},{14,12},{15,13},{16,18},{17,... | collective-permute-start | bytes 2457608 | tf_op jit(solution)/shard_map/rows_in/ppermute | solution.py:238
  28.6 23.7 %collective-permute-start.6 = (bf16[320,2560]{1,0:T(8,128)(2,1)S(1)}, bf16[320,2560]{1,0:T(8,128)(2,1)}, u32[]{:S(2)}, u32[]{:S(2)}) collective-permute-start(bf16[320,2560]{1,0:T(8,128)(2,1)S(1)} %collective-permute-done.3.refs_5_), channel_id=1, source_target_pairs={{2,3},{3,2},{4,5},{5,4},{10,11},{11,10},{12,13},{13,12},{18,19},{1... | collective-permute-start | bytes 4915208 | tf_op jit(solution)/shard_map/swap_inner/ppermute | solution.py:238
  44.7 6.9 %collective-permute-start.7 = (bf16[160,2560]{1,0:T(8,128)(2,1)}, bf16[160,2560]{1,0:T(8,128)(2,1)}, u32[]{:S(2)}, u32[]{:S(2)}) collective-permute-start(bf16[160,2560]{1,0:T(8,128)(2,1)} %collective-permute-done.refs_1_), channel_id=1, source_target_pairs={{2,4},{3,5},{4,2},{5,3},{10,12},{11,13},{12,10},{13,11},{18,20},{1... | collective-permute-start | bytes 2457608 | tf_op jit(solution)/shard_map/middle_far/ppermute | solution.py:238
  46.3 6.1 %collective-permute-start.5 = (bf16[160,2560]{1,0:T(8,128)(2,1)}, bf16[160,2560]{1,0:T(8,128)(2,1)}, u32[]{:S(2)}, u32[]{:S(2)}) collective-permute-start(bf16[160,2560]{1,0:T(8,128)(2,1)} %collective-permute-done.1.refs_2_), channel_id=1, source_target_pairs={{2,3},{3,2},{4,5},{5,4},{10,11},{11,10},{12,13},{13,12},{18,19},{1... | collective-permute-start | bytes 2457608 | tf_op jit(solution)/shard_map/swap_outer/ppermute | solution.py:238
  47.8 4.5 %collective-permute-start.4 = (bf16[160,2560]{1,0:T(8,128)(2,1)}, bf16[160,2560]{1,0:T(8,128)(2,1)}, u32[]{:S(2)}, u32[]{:S(2)}) collective-permute-start(bf16[160,2560]{1,0:T(8,128)(2,1)} %collective-permute-done.refs_1_), channel_id=1, source_target_pairs={{2,3},{3,2},{4,5},{5,4},{10,11},{11,10},{12,13},{13,12},{18,19},{1... | collective-permute-start | bytes 2457608 | tf_op jit(solution)/shard_map/swap_outer/ppermute | solution.py:238
  49.4 3.1 %collective-permute-start.8 = (bf16[160,2560]{1,0:T(8,128)(2,1)}, bf16[160,2560]{1,0:T(8,128)(2,1)S(1)}, u32[]{:S(2)}, u32[]{:S(2)}) collective-permute-start(bf16[160,2560]{1,0:T(8,128)(2,1)} %collective-permute-done.1.refs_2_), channel_id=1, source_target_pairs={{2,4},{3,5},{4,2},{5,3},{10,12},{11,13},{12,10},{13,11},{18,20},{1... | collective-permute-start | bytes 2457608 | tf_op jit(solution)/shard_map/middle_far/ppermute | solution.py:238
  50.1 1.4 copy-start
  51.6 1.6 collective-permute-start.9
  52.5 0.7 collective-permute-start.10
  53.5 72.0 %collective-permute-start.15 = (bf16[320,1280]{1,0:T(8,128)(2,1)S(1)}, bf16[320,1280]{1,0:T(8,128)(2,1)S(1)}, u32[]{:S(2)}, u32[]{:S(2)}) collective-permute-start(bf16[320,1280]{1,0:T(8,128)(2,1)S(1)} %get-tuple-element.33), channel_id=1, source_target_pairs={{2,0},{3,1},{4,6},{5,7},{10,8},{11,9},{12,14},{13,15},{18,16},{19,... | collective-permute-start | bytes 2457608 | tf_op jit(solution)/shard_map/rows_out/ppermute | solution.py:238
  54.8 88.0 %collective-permute-start.11 = (bf16[320,1280]{1,0:T(8,128)(2,1)S(1)}, bf16[320,1280]{1,0:T(8,128)(2,1)S(1)}, u32[]{:S(2)}, u32[]{:S(2)}) collective-permute-start(bf16[320,1280]{1,0:T(8,128)(2,1)S(1)} %get-tuple-element.29), channel_id=1, source_target_pairs={{2,0},{3,1},{4,6},{5,7},{10,8},{11,9},{12,14},{13,15},{18,16},{19,... | collective-permute-start | bytes 2457608 | tf_op jit(solution)/shard_map/rows_out/ppermute | solution.py:238
  125.7 20.9 %collective-permute-start.16 = (bf16[320,1280]{1,0:T(8,128)(2,1)S(1)}, bf16[320,1280]{1,0:T(8,128)(2,1)S(1)}, u32[]{:S(2)}, u32[]{:S(2)}) collective-permute-start(bf16[320,1280]{1,0:T(8,128)(2,1)S(1)} %broadcast_select_fusion), channel_id=1, source_target_pairs={{0,8},{8,0},{16,24},{24,16},{1,9},{9,1},{17,25},{25,17},{2,10},{10... | collective-permute-start | bytes 2457608 | tf_op jit(solution)/shard_map/along_x/ppermute | solution.py:238
  127.2 19.3 %collective-permute-start.17 = (bf16[320,1280]{1,0:T(8,128)(2,1)S(1)}, bf16[320,1280]{1,0:T(8,128)(2,1)S(1)}, u32[]{:S(2)}, u32[]{:S(2)}) collective-permute-start(bf16[320,1280]{1,0:T(8,128)(2,1)S(1)} %broadcast_select_fusion), channel_id=1, source_target_pairs={{0,16},{8,24},{16,0},{24,8},{1,17},{9,25},{17,1},{25,9},{2,18},{10... | collective-permute-start | bytes 2457608 | tf_op jit(solution)/shard_map/along_y/ppermute | solution.py:238
  142.9 20.1 %collective-permute-start.12 = (bf16[320,1280]{1,0:T(8,128)(2,1)S(1)}, bf16[320,1280]{1,0:T(8,128)(2,1)}, u32[]{:S(2)}, u32[]{:S(2)}) collective-permute-start(bf16[320,1280]{1,0:T(8,128)(2,1)S(1)} %broadcast_select_fusion.1), channel_id=1, source_target_pairs={{0,8},{8,0},{16,24},{24,16},{1,9},{9,1},{17,25},{25,17},{2,10},{10... | collective-permute-start | bytes 2457608 | tf_op jit(solution)/shard_map/along_x/ppermute | solution.py:238
  144.5 19.8 %collective-permute-start.13 = (bf16[320,1280]{1,0:T(8,128)(2,1)S(1)}, bf16[320,1280]{1,0:T(8,128)(2,1)}, u32[]{:S(2)}, u32[]{:S(2)}) collective-permute-start(bf16[320,1280]{1,0:T(8,128)(2,1)S(1)} %broadcast_select_fusion.1), channel_id=1, source_target_pairs={{0,16},{8,24},{16,0},{24,8},{1,17},{9,25},{17,1},{25,9},{2,18},{10... | collective-permute-start | bytes 2457608 | tf_op jit(solution)/shard_map/along_y/ppermute | solution.py:238
  164.2 18.9 %collective-permute-start.14 = (bf16[320,1280]{1,0:T(8,128)(2,1)}, bf16[320,1280]{1,0:T(8,128)(2,1)S(1)}, u32[]{:S(2)}, u32[]{:S(2)}) collective-permute-start(bf16[320,1280]{1,0:T(8,128)(2,1)} %collective-permute-done.12), channel_id=1, source_target_pairs={{0,16},{8,24},{16,0},{24,8},{1,17},{9,25},{17,1},{25,9},{2,18},{10... | collective-permute-start | bytes 2457608 | tf_op jit(solution)/shard_map/across_y/ppermute | solution.py:238
  165.7 18.4 %collective-permute-start.18 = (bf16[320,1280]{1,0:T(8,128)(2,1)S(1)}, bf16[320,1280]{1,0:T(8,128)(2,1)S(1)}, u32[]{:S(2)}, u32[]{:S(2)}) collective-permute-start(bf16[320,1280]{1,0:T(8,128)(2,1)S(1)} %collective-permute-done.17), channel_id=1, source_target_pairs={{0,8},{8,0},{16,24},{24,16},{1,9},{9,1},{17,25},{25,17},{2,10},{10... | collective-permute-start | bytes 2457608 | tf_op jit(solution)/shard_map/across_x/ppermute | solution.py:238
  183.4 2.8 %copy-start.1 = (bf16[4,320,2560]{2,1,0:T(8,128)(2,1)}, bf16[4,320,2560]{2,1,0:T(8,128)(2,1)S(1)}, u32[]{:S(2)}) copy-start(bf16[4,320,2560]{2,1,0:T(8,128)(2,1)S(1)} %bitcast_dynamic-update-slice_fusion.1) | copy-start | bytes 19660804

commit v8 on v7

--- a/solution.py
+++ b/solution.py
@@ -54,8 +54,8 @@
     return copies
 
 
-def gram_kernel(count, *refs):
-    inner, blocks, (gram, whole, sems) = refs[0], refs[1 : count + 1], refs[count + 1 :]
+def early_kernel(count, *refs):
+    inner, blocks, (gram, cubic, whole, sems) = refs[0], refs[1 : count + 1], refs[count + 1 :]
     left = pl.ds(0, gram.shape[0])
 
     @pl.when(inner[0] != 0)
@@ -64,62 +64,32 @@
             copy.wait()
         for at in tiles(0, whole.shape[0]):
             gram[:, at] = dot_t(whole[left, :], whole[at, :]).astype(jnp.bfloat16)
-
-
-def cubic_kernel(count, *refs):
-    inner, blocks, refs = refs[0], refs[1 : count + 1], refs[count + 1 :]
-    gram_in, gram, cubic, whole, sems = refs
-    left = pl.ds(0, gram.shape[0])
-    known = gram_in.shape[1]
-
-    @pl.when(inner[0] != 0)
-    def _():
-        copies = fetch_blocks(blocks, whole, sems)
-        copies.append(
-            pltpu.make_async_copy(gram_in, gram.at[:, pl.ds(0, known)], sems.at[count])
-        )
-        copies[count].start()
-        for copy in copies:
-            copy.wait()
-        for at in tiles(known, whole.shape[0]):
-            gram[:, at] = dot_t(whole[left, :], whole[at, :]).astype(jnp.bfloat16)
         for at in tiles(0, whole.shape[1]):
             cubic[:, at] = dot(gram[...], whole[:, at])
 
 
-def early_products(kernel, inner, blocks, more, out_shape, flops):
+def early_products(inner, rows, blocks):
     count = len(blocks)
+    columns = blocks[0].shape[1]
+    known = starts(blocks)[-1]
     return pl.pallas_call(
-        functools.partial(kernel, count),
-        out_shape=out_shape,
+        functools.partial(early_kernel, count),
+        out_shape=(
+            jax.ShapeDtypeStruct((2 * rows, known), jnp.bfloat16),
+            jax.ShapeDtypeStruct((2 * rows, columns), jnp.float32),
+        ),
         in_specs=[pl.BlockSpec(memory_space=pltpu.SMEM)]
-        + [pl.BlockSpec(memory_space=pltpu.HBM)] * count
-        + [pl.BlockSpec(memory_space=pl.ANY)] * len(more),
-        out_specs=tuple(pl.BlockSpec(memory_space=pltpu.VMEM) for _ in out_shape),
+        + [pl.BlockSpec(memory_space=pltpu.HBM)] * count,
+        out_specs=(pl.BlockSpec(memory_space=pltpu.VMEM),) * 2,
         scratch_shapes=[
-            pltpu.VMEM((starts(blocks)[-1], blocks[0].shape[1]), jnp.bfloat16),
-            pltpu.SemaphoreType.DMA((count + len(more),)),
+            pltpu.VMEM((known, columns), jnp.bfloat16),
+            pltpu.SemaphoreType.DMA((count,)),
         ],
         compiler_params=pltpu.CompilerParams(vmem_limit_bytes=VMEM_LIMIT),
-        cost_estimate=pl.CostEstimate(flops=flops, bytes_accessed=flops // 1024, transcendentals=0),
-    )(inner, *blocks, *more)
-
-
-def first_grams(inner, blocks, rows):
-    columns = blocks[0].shape[1]
-    known = starts(blocks)[-1]
-    shape = (jax.ShapeDtypeStruct((2 * rows, known), jnp.bfloat16),)
-    return early_products(gram_kernel, inner, blocks, [], shape, 4 * rows * known * columns)[0]
-
-
-def early_cubic(inner, blocks, rows, gram):
-    columns = blocks[0].shape[1]
-    known = starts(blocks)[-1]
-    shape = (
-        jax.ShapeDtypeStruct((2 * rows, known), jnp.bfloat16),
-        jax.ShapeDtypeStruct((2 * rows, columns), jnp.float32),
-    )
-    return early_products(cubic_kernel, inner, blocks, [gram], shape, 6 * rows * known * columns)
+        cost_estimate=pl.CostEstimate(
+            flops=rows * known, bytes_accessed=2 * rows, transcendentals=0
+        ),
+    )(inner, *blocks)
 
 
 def late_kernel(first, early_count, count, gram_count, widths, *refs):
@@ -230,6 +200,7 @@
     inwards = [(0, 2), (1, 3), (6, 4), (7, 5)]
     outwards = [(b, a) for a, b in inwards]
     middle = [(2, 4), (3, 5), (4, 2), (5, 3)]
+    across_middle = [(0, 4), (1, 5), (6, 2), (7, 3)]
     along_x = [(m, m ^ 1) for m in range(4)]
     along_y = [(m, m ^ 2) for m in range(4)]
 
@@ -242,19 +213,17 @@
 
     cut = rows // 2
     halves = [own[:cut], own[cut:]]
-    outer_rows = [move("rows_in", half, "shard", inwards) for half in halves]
-    inner_rows = move("middle_own", own, "shard", middle)
-    far_rows = [move("middle_far", half, "shard", middle) for half in outer_rows]
-
-    inner_rows, _ = tie((inner_rows, outer_rows[1]))
-    first = outer_rows + [own, swap("own", own), inner_rows]
-    gram = first_grams(inner, first, rows)
-    far_rows[0], gram = tie((far_rows[0], gram))
-    then = [swap("outer", half) for half in outer_rows] + [swap("inner", inner_rows)]
-    early = first + then
-    gram, cubic = early_cubic(inner, early, rows, gram)
-    far_rows[1], gram, cubic = tie((far_rows[1], gram, cubic))
-    late = far_rows + [swap("far", half) for half in far_rows]
+    first_rows = move("rows_in", halves[0], "shard", inwards)
+    second_half, first_rows = tie((halves[1], first_rows))
+    outer_rows = [first_rows, move("rows_in", second_half, "shard", inwards)]
+    inner_rows = [move("middle", half, "shard", middle) for half in halves]
+    far_rows = move("rows_far", own, "shard", across_middle)
+
+    early = outer_rows + [own, swap("own", own)] + inner_rows
+    early += [swap("rows", half) for half in outer_rows + inner_rows]
+    gram, cubic = early_products(inner, rows, early)
+    far_rows, gram, cubic = tie((far_rows, gram, cubic))
+    late = [far_rows, swap("far", far_rows)]
     for_outer = late_products(inner, 0, rows, early, late, [gram], cubic, widths)
     for_own = late_products(inner, rows, rows, early, late, [gram], cubic, widths)
 

time: 188 us -> 186 us (0.989)
  waiting for transfers between devices: 145 us -> 136 us
  local copies, waits for them, and re-layouts: 9.17 us -> 13.4 us
  starting transfers between devices: 32 us -> 34.9 us
    ppermute x19, waiting for transfers between devices: 145 us -> 136 us  [move(): return lax.ppermute(block, axis, pairs)]
    unnamed x4 -> x16, local copies, waits for them, and re-layouts: 3.48 us -> 7.64 us
    ppermute x19, starting transfers between devices: 32 us -> 34.9 us  [move(): return lax.ppermute(block, axis, pairs)]
  transfers between devices with their start and end apart: 19 -> 19, of which waited for: 8 -> 9; matrix products, arithmetic and copies ran while one was open for 3% -> 2% of each run, Pallas kernels for 0% -> 0%
where the time goes in v8:
time: 186 us; the launch traced here: 185 us
  waiting for transfers between devices  136 us (73%)
  starting transfers between devices  34.9 us (19%)
  local copies, waits for them, and re-layouts  13.4 us (7%)
    ppermute x19, waiting for transfers between devices, move(): return lax.ppermute(block, axis, pairs)  136 us
    ppermute x19, starting transfers between devices, move(): return lax.ppermute(block, axis, pairs)  34.9 us
    unnamed x16, local copies, waits for them, and re-layouts  7.64 us
  transfers between devices with their start and end apart: 19, of which 9 were waited for; matrix products, arithmetic and copies ran while one was open for 2% of the time, Pallas kernels for 0%

profile of v8, /device:TPU:0, one launch (start us, length us, event | category | flops | bytes accessed | tf_op | source)
XLA Modules:
  0.0 185.5 jit_solution(10909226158344015016)
XLA Ops:
  0.0 1.6 slice_bitcast_fusion
  1.6 5.0 %collective-permute-start = (bf16[160,2560]{1,0:T(8,128)(2,1)S(1)}, bf16[160,2560]{1,0:T(8,128)(2,1)S(1)}, u32[]{:S(2)}, u32[]{:S(2)}) collective-permute-start(bf16[160,2560]{1,0:T(8,128)(2,1)S(1)} %get-tuple-element.35), channel_id=1, source_target_pairs={{0,2},{1,3},{6,4},{7,5},{8,10},{9,11},{14,12},{15,13},{16,18},{17,... | collective-permute-start | bytes 2457608 | tf_op jit(solution)/shard_map/rows_in/ppermute | solution.py:209
  6.6 1.6 collective-permute-start.3
  8.2 1.5 collective-permute-start.4
  10.5 13.6 %collective-permute-done.refs_1_ = bf16[160,2560]{1,0:T(8,128)(2,1)S(1)} collective-permute-done((bf16[160,2560]{1,0:T(8,128)(2,1)S(1)}, bf16[160,2560]{1,0:T(8,128)(2,1)S(1)}, u32[]{:S(2)}, u32[]{:S(2)}) %collective-permute-start) | collective-permute-done | bytes 819232 | tf_op jit(solution)/shard_map/rows_in/ppermute | solution.py:209
  24.0 5.3 %collective-permute-start.1 = (bf16[160,2560]{1,0:T(8,128)(2,1)S(1)}, bf16[160,2560]{1,0:T(8,128)(2,1)}, u32[]{:S(2)}, u32[]{:S(2)}) collective-permute-start(bf16[160,2560]{1,0:T(8,128)(2,1)S(1)} %get-tuple-element.21), channel_id=1, source_target_pairs={{0,2},{1,3},{6,4},{7,5},{8,10},{9,11},{14,12},{15,13},{16,18},{17,... | collective-permute-start | bytes 2457608 | tf_op jit(solution)/shard_map/rows_in/ppermute | solution.py:209
  30.9 3.8 %collective-permute-start.9 = (bf16[320,2560]{1,0:T(8,128)(2,1)}, bf16[320,2560]{1,0:T(8,128)(2,1)}, u32[]{:S(2)}, u32[]{:S(2)}) collective-permute-start(bf16[320,2560]{1,0:T(8,128)(2,1)} %bitcast.23), channel_id=1, source_target_pairs={{0,4},{1,5},{6,2},{7,3},{8,12},{9,13},{14,10},{15,11},{16,20},{17,... | collective-permute-start | bytes 4915208 | tf_op jit(solution)/shard_map/rows_far/ppermute | solution.py:209
  34.8 1.5 collective-permute-start.7
  36.3 10.8 %collective-permute-done.1.refs_2_ = bf16[160,2560]{1,0:T(8,128)(2,1)} collective-permute-done((bf16[160,2560]{1,0:T(8,128)(2,1)S(1)}, bf16[160,2560]{1,0:T(8,128)(2,1)}, u32[]{:S(2)}, u32[]{:S(2)}) %collective-permute-start.1) | collective-permute-done | bytes 819232 | tf_op jit(solution)/shard_map/rows_in/ppermute | solution.py:209
  47.1 1.6 collective-permute-start.8
  49.6 1.5 collective-permute-start.6
  51.2 1.4 copy-done
  55.0 25.4 %collective-permute-done.9.refs_11_ = bf16[320,2560]{1,0:T(8,128)(2,1)} collective-permute-done((bf16[320,2560]{1,0:T(8,128)(2,1)}, bf16[320,2560]{1,0:T(8,128)(2,1)}, u32[]{:S(2)}, u32[]{:S(2)}) %collective-permute-start.9) | collective-permute-done | bytes 1638432 | tf_op jit(solution)/shard_map/rows_far/ppermute | solution.py:209
  81.5 1.3 collective-permute-start.15
  84.5 39.9 %collective-permute-done.15 = bf16[320,1280]{1,0:T(8,128)(2,1)S(1)} collective-permute-done((bf16[320,1280]{1,0:T(8,128)(2,1)S(1)}, bf16[320,1280]{1,0:T(8,128)(2,1)S(1)}, u32[]{:S(2)}, u32[]{:S(2)}) %collective-permute-start.15) | collective-permute-done | bytes 819232 | tf_op jit(solution)/shard_map/rows_out/ppermute | solution.py:209
  124.4 1.6 collective-permute-start.16
  126.0 1.5 collective-permute-start.17
  127.5 13.9 %collective-permute-done.11 = bf16[320,1280]{1,0:T(8,128)(2,1)S(1)} collective-permute-done((bf16[320,1280]{1,0:T(8,128)(2,1)S(1)}, bf16[320,1280]{1,0:T(8,128)(2,1)S(1)}, u32[]{:S(2)}, u32[]{:S(2)}) %collective-permute-start.11) | collective-permute-done | bytes 819232 | tf_op jit(solution)/shard_map/rows_out/ppermute | solution.py:209
  141.5 1.6 collective-permute-start.12
  143.1 1.5 collective-permute-start.13
  145.2 16.3 %collective-permute-done.12 = bf16[320,1280]{1,0:T(8,128)(2,1)} collective-permute-done((bf16[320,1280]{1,0:T(8,128)(2,1)S(1)}, bf16[320,1280]{1,0:T(8,128)(2,1)}, u32[]{:S(2)}, u32[]{:S(2)}) %collective-permute-start.12) | collective-permute-done | bytes 819232 | tf_op jit(solution)/shard_map/along_x/ppermute | solution.py:209
  162.7 1.5 collective-permute-start.14
  167.1 14.3 %collective-permute-done.14 = bf16[320,1280]{1,0:T(8,128)(2,1)S(1)} collective-permute-done((bf16[320,1280]{1,0:T(8,128)(2,1)}, bf16[320,1280]{1,0:T(8,128)(2,1)S(1)}, u32[]{:S(2)}, u32[]{:S(2)}) %collective-permute-start.14) | collective-permute-done | bytes 819232 | tf_op jit(solution)/shard_map/across_y/ppermute | solution.py:209
  182.4 2.1 %copy-done.7 = bf16[4,320,2560]{2,1,0:T(8,128)(2,1)} copy-done((bf16[4,320,2560]{2,1,0:T(8,128)(2,1)}, bf16[4,320,2560]{2,1,0:T(8,128)(2,1)S(1)}, u32[]{:S(2)}) %copy-start.7) | copy-done | bytes 6553624
  (45 shorter events, 15.2 us)
Async XLA Ops:
  0.0 81.1 %copy-start.1 = (bf16[1,320,2560]{2,1,0:T(8,128)(2,1)S(1)}, bf16[1,320,2560]{2,1,0:T(8,128)(2,1)}, u32[]{:S(2)}) copy-start(bf16[1,320,2560]{2,1,0:T(8,128)(2,1)} %param.1) | copy-start | bytes 4915204
  1.6 22.4 %collective-permute-start = (bf16[160,2560]{1,0:T(8,128)(2,1)S(1)}, bf16[160,2560]{1,0:T(8,128)(2,1)S(1)}, u32[]{:S(2)}, u32[]{:S(2)}) collective-permute-start(bf16[160,2560]{1,0:T(8,128)(2,1)S(1)} %get-tuple-element.35), channel_id=1, source_target_pairs={{0,2},{1,3},{6,4},{7,5},{8,10},{9,11},{14,12},{15,13},{16,18},{17,... | collective-permute-start | bytes 2457608 | tf_op jit(solution)/shard_map/rows_in/ppermute | solution.py:209
  6.6 24.3 %collective-permute-start.3 = (bf16[160,2560]{1,0:T(8,128)(2,1)S(1)}, bf16[160,2560]{1,0:T(8,128)(2,1)}, u32[]{:S(2)}, u32[]{:S(2)}) collective-permute-start(bf16[160,2560]{1,0:T(8,128)(2,1)S(1)} %get-tuple-element.35), channel_id=1, source_target_pairs={{2,4},{3,5},{4,2},{5,3},{10,12},{11,13},{12,10},{13,11},{18,20},{1... | collective-permute-start | bytes 2457608 | tf_op jit(solution)/shard_map/middle/ppermute | solution.py:209
  8.2 26.6 %collective-permute-start.4 = (bf16[160,2560]{1,0:T(8,128)(2,1)S(1)}, bf16[160,2560]{1,0:T(8,128)(2,1)}, u32[]{:S(2)}, u32[]{:S(2)}) collective-permute-start(bf16[160,2560]{1,0:T(8,128)(2,1)S(1)} %get-tuple-element.21), channel_id=1, source_target_pairs={{2,4},{3,5},{4,2},{5,3},{10,12},{11,13},{12,10},{13,11},{18,20},{1... | collective-permute-start | bytes 2457608 | tf_op jit(solution)/shard_map/middle/ppermute | solution.py:209
  9.7 41.4 %collective-permute-start.2 = (bf16[320,2560]{1,0:T(8,128)(2,1)}, bf16[320,2560]{1,0:T(8,128)(2,1)S(1)}, u32[]{:S(2)}, u32[]{:S(2)}) collective-permute-start(bf16[320,2560]{1,0:T(8,128)(2,1)} %bitcast.22), channel_id=1, source_target_pairs={{2,3},{3,2},{4,5},{5,4},{10,11},{11,10},{12,13},{13,12},{18,19},{1... | collective-permute-start | bytes 4915208 | tf_op jit(solution)/shard_map/swap_own/ppermute | solution.py:209
  24.0 23.1 %collective-permute-start.1 = (bf16[160,2560]{1,0:T(8,128)(2,1)S(1)}, bf16[160,2560]{1,0:T(8,128)(2,1)}, u32[]{:S(2)}, u32[]{:S(2)}) collective-permute-start(bf16[160,2560]{1,0:T(8,128)(2,1)S(1)} %get-tuple-element.21), channel_id=1, source_target_pairs={{0,2},{1,3},{6,4},{7,5},{8,10},{9,11},{14,12},{15,13},{16,18},{17,... | collective-permute-start | bytes 2457608 | tf_op jit(solution)/shard_map/rows_in/ppermute | solution.py:209
  29.3 19.4 %collective-permute-start.5 = (bf16[160,2560]{1,0:T(8,128)(2,1)S(1)}, bf16[160,2560]{1,0:T(8,128)(2,1)S(1)}, u32[]{:S(2)}, u32[]{:S(2)}) collective-permute-start(bf16[160,2560]{1,0:T(8,128)(2,1)S(1)} %collective-permute-done.refs_1_), channel_id=1, source_target_pairs={{2,3},{3,2},{4,5},{5,4},{10,11},{11,10},{12,13},{13,12},{18,19},{1... | collective-permute-start | bytes 2457608 | tf_op jit(solution)/shard_map/swap_rows/ppermute | solution.py:209
  30.9 49.4 %collective-permute-start.9 = (bf16[320,2560]{1,0:T(8,128)(2,1)}, bf16[320,2560]{1,0:T(8,128)(2,1)}, u32[]{:S(2)}, u32[]{:S(2)}) collective-permute-start(bf16[320,2560]{1,0:T(8,128)(2,1)} %bitcast.23), channel_id=1, source_target_pairs={{0,4},{1,5},{6,2},{7,3},{8,12},{9,13},{14,10},{15,11},{16,20},{17,... | collective-permute-start | bytes 4915208 | tf_op jit(solution)/shard_map/rows_far/ppermute | solution.py:209
  34.8 16.4 %collective-permute-start.7 = (bf16[160,2560]{1,0:T(8,128)(2,1)}, bf16[160,2560]{1,0:T(8,128)(2,1)}, u32[]{:S(2)}, u32[]{:S(2)}) collective-permute-start(bf16[160,2560]{1,0:T(8,128)(2,1)} %collective-permute-done.3.refs_5_), channel_id=1, source_target_pairs={{2,3},{3,2},{4,5},{5,4},{10,11},{11,10},{12,13},{13,12},{18,19},{1... | collective-permute-start | bytes 2457608 | tf_op jit(solution)/shard_map/swap_rows/ppermute | solution.py:209
  47.1 4.0 %collective-permute-start.8 = (bf16[160,2560]{1,0:T(8,128)(2,1)}, bf16[160,2560]{1,0:T(8,128)(2,1)}, u32[]{:S(2)}, u32[]{:S(2)}) collective-permute-start(bf16[160,2560]{1,0:T(8,128)(2,1)} %collective-permute-done.4.refs_6_), channel_id=1, source_target_pairs={{2,3},{3,2},{4,5},{5,4},{10,11},{11,10},{12,13},{13,12},{18,19},{1... | collective-permute-start | bytes 2457608 | tf_op jit(solution)/shard_map/swap_rows/ppermute | solution.py:209
  49.6 1.6 collective-permute-start.6
  51.2 1.4 copy-start
  52.6 1.1 copy-start.3
  54.9 26.2 %copy-start.4 = (bf16[160,2560]{1,0:T(8,128)(2,1)S(1)}, bf16[160,2560]{1,0:T(8,128)(2,1)}, u32[]{:S(2)}) copy-start(bf16[160,2560]{1,0:T(8,128)(2,1)} %copy-done.2) | copy-start | bytes 2457604
  80.4 0.8 collective-permute-start.10
  81.5 42.8 %collective-permute-start.15 = (bf16[320,1280]{1,0:T(8,128)(2,1)S(1)}, bf16[320,1280]{1,0:T(8,128)(2,1)S(1)}, u32[]{:S(2)}, u32[]{:S(2)}) collective-permute-start(bf16[320,1280]{1,0:T(8,128)(2,1)S(1)} %get-tuple-element.31), channel_id=1, source_target_pairs={{2,0},{3,1},{4,6},{5,7},{10,8},{11,9},{12,14},{13,15},{18,16},{19,... | collective-permute-start | bytes 2457608 | tf_op jit(solution)/shard_map/rows_out/ppermute | solution.py:209
  82.8 58.6 %collective-permute-start.11 = (bf16[320,1280]{1,0:T(8,128)(2,1)S(1)}, bf16[320,1280]{1,0:T(8,128)(2,1)S(1)}, u32[]{:S(2)}, u32[]{:S(2)}) collective-permute-start(bf16[320,1280]{1,0:T(8,128)(2,1)S(1)} %get-tuple-element.27), channel_id=1, source_target_pairs={{2,0},{3,1},{4,6},{5,7},{10,8},{11,9},{12,14},{13,15},{18,16},{19,... | collective-permute-start | bytes 2457608 | tf_op jit(solution)/shard_map/rows_out/ppermute | solution.py:209
  124.4 20.7 %collective-permute-start.16 = (bf16[320,1280]{1,0:T(8,128)(2,1)S(1)}, bf16[320,1280]{1,0:T(8,128)(2,1)S(1)}, u32[]{:S(2)}, u32[]{:S(2)}) collective-permute-start(bf16[320,1280]{1,0:T(8,128)(2,1)S(1)} %broadcast_select_fusion), channel_id=1, source_target_pairs={{0,8},{8,0},{16,24},{24,16},{1,9},{9,1},{17,25},{25,17},{2,10},{10... | collective-permute-start | bytes 2457608 | tf_op jit(solution)/shard_map/along_x/ppermute | solution.py:209
  126.0 19.2 %collective-permute-start.17 = (bf16[320,1280]{1,0:T(8,128)(2,1)S(1)}, bf16[320,1280]{1,0:T(8,128)(2,1)S(1)}, u32[]{:S(2)}, u32[]{:S(2)}) collective-permute-start(bf16[320,1280]{1,0:T(8,128)(2,1)S(1)} %broadcast_select_fusion), channel_id=1, source_target_pairs={{0,16},{8,24},{16,0},{24,8},{1,17},{9,25},{17,1},{25,9},{2,18},{10... | collective-permute-start | bytes 2457608 | tf_op jit(solution)/shard_map/along_y/ppermute | solution.py:209
  141.5 20.0 %collective-permute-start.12 = (bf16[320,1280]{1,0:T(8,128)(2,1)S(1)}, bf16[320,1280]{1,0:T(8,128)(2,1)}, u32[]{:S(2)}, u32[]{:S(2)}) collective-permute-start(bf16[320,1280]{1,0:T(8,128)(2,1)S(1)} %broadcast_select_fusion.1), channel_id=1, source_target_pairs={{0,8},{8,0},{16,24},{24,16},{1,9},{9,1},{17,25},{25,17},{2,10},{10... | collective-permute-start | bytes 2457608 | tf_op jit(solution)/shard_map/along_x/ppermute | solution.py:209
  143.1 19.6 %collective-permute-start.13 = (bf16[320,1280]{1,0:T(8,128)(2,1)S(1)}, bf16[320,1280]{1,0:T(8,128)(2,1)}, u32[]{:S(2)}, u32[]{:S(2)}) collective-permute-start(bf16[320,1280]{1,0:T(8,128)(2,1)S(1)} %broadcast_select_fusion.1), channel_id=1, source_target_pairs={{0,16},{8,24},{16,0},{24,8},{1,17},{9,25},{17,1},{25,9},{2,18},{10... | collective-permute-start | bytes 2457608 | tf_op jit(solution)/shard_map/along_y/ppermute | solution.py:209
  162.7 18.8 %collective-permute-start.14 = (bf16[320,1280]{1,0:T(8,128)(2,1)}, bf16[320,1280]{1,0:T(8,128)(2,1)S(1)}, u32[]{:S(2)}, u32[]{:S(2)}) collective-permute-start(bf16[320,1280]{1,0:T(8,128)(2,1)} %collective-permute-done.12), channel_id=1, source_target_pairs={{0,16},{8,24},{16,0},{24,8},{1,17},{9,25},{17,1},{25,9},{2,18},{10... | collective-permute-start | bytes 2457608 | tf_op jit(solution)/shard_map/across_y/ppermute | solution.py:209
  164.1 18.3 %collective-permute-start.18 = (bf16[320,1280]{1,0:T(8,128)(2,1)S(1)}, bf16[320,1280]{1,0:T(8,128)(2,1)S(1)}, u32[]{:S(2)}, u32[]{:S(2)}) collective-permute-start(bf16[320,1280]{1,0:T(8,128)(2,1)S(1)} %collective-permute-done.17), channel_id=1, source_target_pairs={{0,8},{8,0},{16,24},{24,16},{1,9},{9,1},{17,25},{25,17},{2,10},{10... | collective-permute-start | bytes 2457608 | tf_op jit(solution)/shard_map/across_x/ppermute | solution.py:209
  181.8 2.8 %copy-start.7 = (bf16[4,320,2560]{2,1,0:T(8,128)(2,1)}, bf16[4,320,2560]{2,1,0:T(8,128)(2,1)S(1)}, u32[]{:S(2)}) copy-start(bf16[4,320,2560]{2,1,0:T(8,128)(2,1)S(1)} %bitcast_dynamic-update-slice_fusion.1) | copy-start | bytes 19660804
  (3 other events, 2.9 us)

commit v9 on v8

--- a/solution.py
+++ b/solution.py
@@ -12,7 +12,7 @@
 coef_c = 2.0315
 
 TILE = 1024
-VMEM_LIMIT = 30 * 1024 * 1024
+VMEM_LIMIT = 40 * 1024 * 1024
 
 
 def dot_t(left, right):
@@ -213,13 +213,14 @@
 
     cut = rows // 2
     halves = [own[:cut], own[cut:]]
-    first_rows = move("rows_in", halves[0], "shard", inwards)
+    outer_rows = [move("rows_in", half, "shard", inwards) for half in halves]
+    first_rows = move("middle", halves[0], "shard", middle)
     second_half, first_rows = tie((halves[1], first_rows))
-    outer_rows = [first_rows, move("rows_in", second_half, "shard", inwards)]
-    inner_rows = [move("middle", half, "shard", middle) for half in halves]
+    inner_rows = [first_rows, move("middle", second_half, "shard", middle)]
+    outer_rows[1], inner_rows[1] = tie((outer_rows[1], inner_rows[1]))
     far_rows = move("rows_far", own, "shard", across_middle)
 
-    early = outer_rows + [own, swap("own", own)] + inner_rows
+    early = outer_rows + halves + [swap("own", own)] + inner_rows
     early += [swap("rows", half) for half in outer_rows + inner_rows]
     gram, cubic = early_products(inner, rows, early)
     far_rows, gram, cubic = tie((far_rows, gram, cubic))
@@ -232,7 +233,7 @@
     def place_in(result, flip, at, part):
         return lax.dynamic_update_slice(result, part[None], (mat ^ flip, 0, at))
 
-    begin = 0
+    begin, corner = 0, []
     for k, width in enumerate(widths):
         returned = move("rows_out", for_outer[k], "shard", outwards)
         mine = tie(jnp.where(outer, returned, for_own[k]))
@@ -240,12 +241,13 @@
         by_y = move("along_y", mine, "mat", along_y)
         by_x, by_y = tie((by_x, by_y))
         if k % 2 == 0:
-            across = move("across_y", by_x, "mat", along_y)
+            corner.append(move("across_y", by_x, "mat", along_y))
         else:
-            across = move("across_x", by_y, "mat", along_x)
-        for flip, part in enumerate((mine, by_x, by_y, across)):
+            corner.append(move("across_x", by_y, "mat", along_x))
+        for flip, part in enumerate((mine, by_x, by_y)):
             result = place_in(result, flip, begin, part)
         begin += width
+    result = place_in(result, 3, 0, jnp.concatenate(corner, axis=1))
     return result
 
 

time: 186 us -> 219 us (1.18)
  waiting for transfers between devices: 136 us -> 161 us
  starting transfers between devices: 34.9 us -> 40.4 us
  Pallas kernels: 0.77 us -> 3.39 us
    ppermute x19, waiting for transfers between devices: 136 us -> 161 us  [move(): return lax.ppermute(block, axis, pairs)]
    ppermute x19, starting transfers between devices: 34.9 us -> 40.4 us  [move(): return lax.ppermute(block, axis, pairs)]
    pallas_call x1, Pallas kernels: 0.09 us -> 2.89 us  [early_products(): pl.pallas_call(functools.partial(early_kernel, count), out_shape=(jax.Sha...]
    unnamed x16 -> x14, local copies, waits for them, and re-layouts: 7.64 us -> 6.71 us
  transfers between devices with their start and end apart: 19 -> 19, of which waited for: 9 -> 8; matrix products, arithmetic and copies ran while one was open for 2% -> 2% of each run, Pallas kernels for 0% -> 1%
where the time goes in v9:
time: 219 us; the launch traced here: 218 us
  waiting for transfers between devices  161 us (74%)
  starting transfers between devices  40.4 us (18%)
  local copies, waits for them, and re-layouts  11.4 us (5%)
  Pallas kernels  3.39 us (2%)
    ppermute x19, waiting for transfers between devices, move(): return lax.ppermute(block, axis, pairs)  161 us
    ppermute x19, starting transfers between devices, move(): return lax.ppermute(block, axis, pairs)  40.4 us
    unnamed x14, local copies, waits for them, and re-layouts  6.71 us
  transfers between devices with their start and end apart: 19, of which 8 were waited for; matrix products, arithmetic and copies ran while one was open for 2% of the time, Pallas kernels for 1%

profile of v9, /device:TPU:0, one launch (start us, length us, event | category | flops | bytes accessed | tf_op | source)
XLA Modules:
  0.0 218.4 jit_solution(6628640832198086396)
XLA Ops:
  0.0 1.5 slice_bitcast_fusion
  2.2 8.6 %collective-permute-start.1 = (bf16[160,2560]{1,0:T(8,128)(2,1)S(1)}, bf16[160,2560]{1,0:T(8,128)(2,1)}, u32[]{:S(2)}, u32[]{:S(2)}) collective-permute-start(bf16[160,2560]{1,0:T(8,128)(2,1)S(1)} %get-tuple-element.22.refs_4_), channel_id=1, source_target_pairs={{0,2},{1,3},{6,4},{7,5},{8,10},{9,11},{14,12},{15,13},{16,18},{17,... | collective-permute-start | bytes 2457608 | tf_op jit(solution)/shard_map/rows_in/ppermute | solution.py:209
  10.8 2.2 collective-permute-start
  13.0 1.6 collective-permute-start.3
  17.0 11.6 %collective-permute-done.1.refs_2_ = bf16[160,2560]{1,0:T(8,128)(2,1)} collective-permute-done((bf16[160,2560]{1,0:T(8,128)(2,1)S(1)}, bf16[160,2560]{1,0:T(8,128)(2,1)}, u32[]{:S(2)}, u32[]{:S(2)}) %collective-permute-start.1) | collective-permute-done | bytes 819232 | tf_op jit(solution)/shard_map/rows_in/ppermute | solution.py:209
  28.6 9.5 %collective-permute-start.9 = (bf16[320,2560]{1,0:T(8,128)(2,1)}, bf16[320,2560]{1,0:T(8,128)(2,1)}, u32[]{:S(2)}, u32[]{:S(2)}) collective-permute-start(bf16[320,2560]{1,0:T(8,128)(2,1)} %bitcast.23), channel_id=1, source_target_pairs={{0,4},{1,5},{6,2},{7,3},{8,12},{9,13},{14,10},{15,11},{16,20},{17,... | collective-permute-start | bytes 4915208 | tf_op jit(solution)/shard_map/rows_far/ppermute | solution.py:209
  38.1 8.1 %collective-permute-done.refs_1_ = bf16[160,2560]{1,0:T(8,128)(2,1)} collective-permute-done((bf16[160,2560]{1,0:T(8,128)(2,1)S(1)}, bf16[160,2560]{1,0:T(8,128)(2,1)}, u32[]{:S(2)}, u32[]{:S(2)}) %collective-permute-start) | collective-permute-done | bytes 819232 | tf_op jit(solution)/shard_map/rows_in/ppermute | solution.py:209
  46.2 1.6 collective-permute-start.5
  47.8 1.5 collective-permute-start.6
  50.2 1.6 collective-permute-start.8
  54.1 2.9 %shard_map.17 = (bf16[640,1920]{1,0:T(8,128)(2,1)S(1)}, f32[640,2560]{1,0:T(8,128)}) custom-call(s32[1]{0:T(128)} %bitcast.refs_0_, bf16[160,2560]{1,0:T(8,128)(2,1)} %collective-permute-done.refs_1_, bf16[160,2560]{1,0:T(8,128)(2,1)} %collective-permute-done.1.refs_2_, bf16[160,2560]{1,0:T(8,128)(2,1)S(1)} %get-tuple-element.40.refs_3_, ...), custom_call_target="tpu_custom_call" | custom-call | flops 614400 | bytes 640 | tf_op jit(solution)/shard_map/pallas_call | solution.py:75
  57.0 1.4 copy-done.4
  58.5 21.5 %collective-permute-done.9.refs_12_ = bf16[320,2560]{1,0:T(8,128)(2,1)} collective-permute-done((bf16[320,2560]{1,0:T(8,128)(2,1)}, bf16[320,2560]{1,0:T(8,128)(2,1)}, u32[]{:S(2)}, u32[]{:S(2)}) %collective-permute-start.9) | collective-permute-done | bytes 1638432 | tf_op jit(solution)/shard_map/rows_far/ppermute | solution.py:209
  82.1 1.3 collective-permute-start.14
  83.4 1.3 collective-permute-start.11
  85.0 70.8 %collective-permute-done.14 = bf16[320,1280]{1,0:T(8,128)(2,1)S(1)} collective-permute-done((bf16[320,1280]{1,0:T(8,128)(2,1)S(1)}, bf16[320,1280]{1,0:T(8,128)(2,1)S(1)}, u32[]{:S(2)}, u32[]{:S(2)}) %collective-permute-start.14) | collective-permute-done | bytes 819232 | tf_op jit(solution)/shard_map/rows_out/ppermute | solution.py:209
  155.9 1.5 collective-permute-start.15
  157.4 1.5 collective-permute-start.16
  159.0 14.1 %collective-permute-done.11 = bf16[320,1280]{1,0:T(8,128)(2,1)S(1)} collective-permute-done((bf16[320,1280]{1,0:T(8,128)(2,1)S(1)}, bf16[320,1280]{1,0:T(8,128)(2,1)S(1)}, u32[]{:S(2)}, u32[]{:S(2)}) %collective-permute-start.11) | collective-permute-done | bytes 819232 | tf_op jit(solution)/shard_map/rows_out/ppermute | solution.py:209
  173.1 1.5 collective-permute-start.12
  174.7 1.5 collective-permute-start.13
  176.8 16.4 %collective-permute-done.12 = bf16[320,1280]{1,0:T(8,128)(2,1)} collective-permute-done((bf16[320,1280]{1,0:T(8,128)(2,1)S(1)}, bf16[320,1280]{1,0:T(8,128)(2,1)}, u32[]{:S(2)}, u32[]{:S(2)}) %collective-permute-start.12) | collective-permute-done | bytes 819232 | tf_op jit(solution)/shard_map/along_x/ppermute | solution.py:209
  194.4 1.6 collective-permute-start.17
  199.3 17.8 %collective-permute-done.18 = bf16[320,1280]{1,0:T(8,128)(2,1)S(1)} collective-permute-done((bf16[320,1280]{1,0:T(8,128)(2,1)S(1)}, bf16[320,1280]{1,0:T(8,128)(2,1)S(1)}, u32[]{:S(2)}, u32[]{:S(2)}) %collective-permute-start.18) | collective-permute-done | bytes 819232 | tf_op jit(solution)/shard_map/across_x/ppermute | solution.py:209
  (42 shorter events, 15.2 us)
Async XLA Ops:
  1.5 11.5 %collective-permute-start.2 = (bf16[160,2560]{1,0:T(8,128)(2,1)S(1)}, bf16[160,2560]{1,0:T(8,128)(2,1)S(1)}, u32[]{:S(2)}, u32[]{:S(2)}) collective-permute-start(bf16[160,2560]{1,0:T(8,128)(2,1)S(1)} %get-tuple-element.40.refs_3_), channel_id=1, source_target_pairs={{2,4},{3,5},{4,2},{5,3},{10,12},{11,13},{12,10},{13,11},{18,20},{1... | collective-permute-start | bytes 2457608 | tf_op jit(solution)/shard_map/middle/ppermute | solution.py:209
  2.2 26.4 %collective-permute-start.1 = (bf16[160,2560]{1,0:T(8,128)(2,1)S(1)}, bf16[160,2560]{1,0:T(8,128)(2,1)}, u32[]{:S(2)}, u32[]{:S(2)}) collective-permute-start(bf16[160,2560]{1,0:T(8,128)(2,1)S(1)} %get-tuple-element.22.refs_4_), channel_id=1, source_target_pairs={{0,2},{1,3},{6,4},{7,5},{8,10},{9,11},{14,12},{15,13},{16,18},{17,... | collective-permute-start | bytes 2457608 | tf_op jit(solution)/shard_map/rows_in/ppermute | solution.py:209
  10.8 35.3 %collective-permute-start = (bf16[160,2560]{1,0:T(8,128)(2,1)S(1)}, bf16[160,2560]{1,0:T(8,128)(2,1)}, u32[]{:S(2)}, u32[]{:S(2)}) collective-permute-start(bf16[160,2560]{1,0:T(8,128)(2,1)S(1)} %get-tuple-element.40.refs_3_), channel_id=1, source_target_pairs={{0,2},{1,3},{6,4},{7,5},{8,10},{9,11},{14,12},{15,13},{16,18},{17,... | collective-permute-start | bytes 2457608 | tf_op jit(solution)/shard_map/rows_in/ppermute | solution.py:209
  13.0 34.8 %collective-permute-start.3 = (bf16[160,2560]{1,0:T(8,128)(2,1)S(1)}, bf16[160,2560]{1,0:T(8,128)(2,1)}, u32[]{:S(2)}, u32[]{:S(2)}) collective-permute-start(bf16[160,2560]{1,0:T(8,128)(2,1)S(1)} %get-tuple-element.22.refs_4_), channel_id=1, source_target_pairs={{2,4},{3,5},{4,2},{5,3},{10,12},{11,13},{12,10},{13,11},{18,20},{1... | collective-permute-start | bytes 2457608 | tf_op jit(solution)/shard_map/middle/ppermute | solution.py:209
  14.6 37.2 %collective-permute-start.4 = (bf16[320,2560]{1,0:T(8,128)(2,1)}, bf16[320,2560]{1,0:T(8,128)(2,1)S(1)}, u32[]{:S(2)}, u32[]{:S(2)}) collective-permute-start(bf16[320,2560]{1,0:T(8,128)(2,1)} %bitcast.22), channel_id=1, source_target_pairs={{2,3},{3,2},{4,5},{5,4},{10,11},{11,10},{12,13},{13,12},{18,19},{1... | collective-permute-start | bytes 4915208 | tf_op jit(solution)/shard_map/swap_own/ppermute | solution.py:209
  15.4 34.0 %collective-permute-start.7 = (bf16[160,2560]{1,0:T(8,128)(2,1)S(1)}, bf16[160,2560]{1,0:T(8,128)(2,1)S(1)}, u32[]{:S(2)}, u32[]{:S(2)}) collective-permute-start(bf16[160,2560]{1,0:T(8,128)(2,1)S(1)} %collective-permute-done.2.refs_6_), channel_id=1, source_target_pairs={{2,3},{3,2},{4,5},{5,4},{10,11},{11,10},{12,13},{13,12},{18,19},{1... | collective-permute-start | bytes 2457608 | tf_op jit(solution)/shard_map/swap_rows/ppermute | solution.py:209
  28.6 51.4 %collective-permute-start.9 = (bf16[320,2560]{1,0:T(8,128)(2,1)}, bf16[320,2560]{1,0:T(8,128)(2,1)}, u32[]{:S(2)}, u32[]{:S(2)}) collective-permute-start(bf16[320,2560]{1,0:T(8,128)(2,1)} %bitcast.23), channel_id=1, source_target_pairs={{0,4},{1,5},{6,2},{7,3},{8,12},{9,13},{14,10},{15,11},{16,20},{17,... | collective-permute-start | bytes 4915208 | tf_op jit(solution)/shard_map/rows_far/ppermute | solution.py:209
  46.2 5.7 %collective-permute-start.5 = (bf16[160,2560]{1,0:T(8,128)(2,1)}, bf16[160,2560]{1,0:T(8,128)(2,1)}, u32[]{:S(2)}, u32[]{:S(2)}) collective-permute-start(bf16[160,2560]{1,0:T(8,128)(2,1)} %collective-permute-done.refs_1_), channel_id=1, source_target_pairs={{2,3},{3,2},{4,5},{5,4},{10,11},{11,10},{12,13},{13,12},{18,19},{1... | collective-permute-start | bytes 2457608 | tf_op jit(solution)/shard_map/swap_rows/ppermute | solution.py:209
  47.8 4.0 %collective-permute-start.6 = (bf16[160,2560]{1,0:T(8,128)(2,1)}, bf16[160,2560]{1,0:T(8,128)(2,1)}, u32[]{:S(2)}, u32[]{:S(2)}) collective-permute-start(bf16[160,2560]{1,0:T(8,128)(2,1)} %collective-permute-done.1.refs_2_), channel_id=1, source_target_pairs={{2,3},{3,2},{4,5},{5,4},{10,11},{11,10},{12,13},{13,12},{18,19},{1... | collective-permute-start | bytes 2457608 | tf_op jit(solution)/shard_map/swap_rows/ppermute | solution.py:209
  50.2 1.6 collective-permute-start.8
  51.8 1.1 copy-start.1
  53.0 1.1 copy-start.3
  57.0 1.4 copy-start.4
  80.0 0.8 collective-permute-start.10
  80.7 1.2 copy-start.6
  82.1 73.7 %collective-permute-start.14 = (bf16[320,1280]{1,0:T(8,128)(2,1)S(1)}, bf16[320,1280]{1,0:T(8,128)(2,1)S(1)}, u32[]{:S(2)}, u32[]{:S(2)}) collective-permute-start(bf16[320,1280]{1,0:T(8,128)(2,1)S(1)} %get-tuple-element.35), channel_id=1, source_target_pairs={{2,0},{3,1},{4,6},{5,7},{10,8},{11,9},{12,14},{13,15},{18,16},{19,... | collective-permute-start | bytes 2457608 | tf_op jit(solution)/shard_map/rows_out/ppermute | solution.py:209
  83.4 89.7 %collective-permute-start.11 = (bf16[320,1280]{1,0:T(8,128)(2,1)S(1)}, bf16[320,1280]{1,0:T(8,128)(2,1)S(1)}, u32[]{:S(2)}, u32[]{:S(2)}) collective-permute-start(bf16[320,1280]{1,0:T(8,128)(2,1)S(1)} %get-tuple-element.31), channel_id=1, source_target_pairs={{2,0},{3,1},{4,6},{5,7},{10,8},{11,9},{12,14},{13,15},{18,16},{19,... | collective-permute-start | bytes 2457608 | tf_op jit(solution)/shard_map/rows_out/ppermute | solution.py:209
  155.9 20.9 %collective-permute-start.15 = (bf16[320,1280]{1,0:T(8,128)(2,1)S(1)}, bf16[320,1280]{1,0:T(8,128)(2,1)S(1)}, u32[]{:S(2)}, u32[]{:S(2)}) collective-permute-start(bf16[320,1280]{1,0:T(8,128)(2,1)S(1)} %broadcast_select_fusion), channel_id=1, source_target_pairs={{0,8},{8,0},{16,24},{24,16},{1,9},{9,1},{17,25},{25,17},{2,10},{10... | collective-permute-start | bytes 2457608 | tf_op jit(solution)/shard_map/along_x/ppermute | solution.py:209
  157.4 19.4 %collective-permute-start.16 = (bf16[320,1280]{1,0:T(8,128)(2,1)S(1)}, bf16[320,1280]{1,0:T(8,128)(2,1)S(1)}, u32[]{:S(2)}, u32[]{:S(2)}) collective-permute-start(bf16[320,1280]{1,0:T(8,128)(2,1)S(1)} %broadcast_select_fusion), channel_id=1, source_target_pairs={{0,16},{8,24},{16,0},{24,8},{1,17},{9,25},{17,1},{25,9},{2,18},{10... | collective-permute-start | bytes 2457608 | tf_op jit(solution)/shard_map/along_y/ppermute | solution.py:209
  173.1 20.1 %collective-permute-start.12 = (bf16[320,1280]{1,0:T(8,128)(2,1)S(1)}, bf16[320,1280]{1,0:T(8,128)(2,1)}, u32[]{:S(2)}, u32[]{:S(2)}) collective-permute-start(bf16[320,1280]{1,0:T(8,128)(2,1)S(1)} %broadcast_select_fusion.1), channel_id=1, source_target_pairs={{0,8},{8,0},{16,24},{24,16},{1,9},{9,1},{17,25},{25,17},{2,10},{10... | collective-permute-start | bytes 2457608 | tf_op jit(solution)/shard_map/along_x/ppermute | solution.py:209
  174.7 19.8 %collective-permute-start.13 = (bf16[320,1280]{1,0:T(8,128)(2,1)S(1)}, bf16[320,1280]{1,0:T(8,128)(2,1)}, u32[]{:S(2)}, u32[]{:S(2)}) collective-permute-start(bf16[320,1280]{1,0:T(8,128)(2,1)S(1)} %broadcast_select_fusion.1), channel_id=1, source_target_pairs={{0,16},{8,24},{16,0},{24,8},{1,17},{9,25},{17,1},{25,9},{2,18},{10... | collective-permute-start | bytes 2457608 | tf_op jit(solution)/shard_map/along_y/ppermute | solution.py:209
  194.4 22.6 %collective-permute-start.17 = (bf16[320,1280]{1,0:T(8,128)(2,1)}, bf16[320,1280]{1,0:T(8,128)(2,1)S(1)}, u32[]{:S(2)}, u32[]{:S(2)}) collective-permute-start(bf16[320,1280]{1,0:T(8,128)(2,1)} %collective-permute-done.12), channel_id=1, source_target_pairs={{0,16},{8,24},{16,0},{24,8},{1,17},{9,25},{17,1},{25,9},{2,18},{10... | collective-permute-start | bytes 2457608 | tf_op jit(solution)/shard_map/across_y/ppermute | solution.py:209
  198.5 18.5 %collective-permute-start.18 = (bf16[320,1280]{1,0:T(8,128)(2,1)S(1)}, bf16[320,1280]{1,0:T(8,128)(2,1)S(1)}, u32[]{:S(2)}, u32[]{:S(2)}) collective-permute-start(bf16[320,1280]{1,0:T(8,128)(2,1)S(1)} %collective-permute-done.16), channel_id=1, source_target_pairs={{0,8},{8,0},{16,24},{24,16},{1,9},{9,1},{17,25},{25,17},{2,10},{10... | collective-permute-start | bytes 2457608 | tf_op jit(solution)/shard_map/across_x/ppermute | solution.py:209
  199.2 17.8 %copy-start.5 = (bf16[4,320,2560]{2,1,0:T(8,128)(2,1)}, bf16[4,320,2560]{2,1,0:T(8,128)(2,1)S(1)}, u32[]{:S(2)}) copy-start(bf16[4,320,2560]{2,1,0:T(8,128)(2,1)S(1)} %bitcast_dynamic-update-slice_fusion) | copy-start | bytes 19660804
  (2 other events, 1.8 us)

commit v10 on v9

--- a/solution.py
+++ b/solution.py
@@ -12,7 +12,7 @@
 coef_c = 2.0315
 
 TILE = 1024
-VMEM_LIMIT = 40 * 1024 * 1024
+VMEM_LIMIT = 30 * 1024 * 1024
 
 
 def dot_t(left, right):
@@ -213,15 +213,14 @@
 
     cut = rows // 2
     halves = [own[:cut], own[cut:]]
+    inner_rows = move("middle", own, "shard", middle)
     outer_rows = [move("rows_in", half, "shard", inwards) for half in halves]
-    first_rows = move("middle", halves[0], "shard", middle)
-    second_half, first_rows = tie((halves[1], first_rows))
-    inner_rows = [first_rows, move("middle", second_half, "shard", middle)]
-    outer_rows[1], inner_rows[1] = tie((outer_rows[1], inner_rows[1]))
+    own_swapped = swap("own", own)
+    outer_rows[0], own_swapped = tie((outer_rows[0], own_swapped))
     far_rows = move("rows_far", own, "shard", across_middle)
 
-    early = outer_rows + halves + [swap("own", own)] + inner_rows
-    early += [swap("rows", half) for half in outer_rows + inner_rows]
+    early = outer_rows + halves + [own_swapped, inner_rows]
+    early += [swap("rows", block) for block in outer_rows + [inner_rows]]
     gram, cubic = early_products(inner, rows, early)
     far_rows, gram, cubic = tie((far_rows, gram, cubic))
     late = [far_rows, swap("far", far_rows)]
@@ -240,13 +239,14 @@
         by_x = move("along_x", mine, "mat", along_x)
         by_y = move("along_y", mine, "mat", along_y)
         by_x, by_y = tie((by_x, by_y))
-        if k % 2 == 0:
-            corner.append(move("across_y", by_x, "mat", along_y))
-        else:
-            corner.append(move("across_x", by_y, "mat", along_x))
+        corner.append((by_x, by_y)[k % 2])
         for flip, part in enumerate((mine, by_x, by_y)):
             result = place_in(result, flip, begin, part)
         begin += width
+    corner = tie(corner)
+    for k, part in enumerate(corner):
+        name, pairs = ("across_y", along_y) if k % 2 == 0 else ("across_x", along_x)
+        corner[k] = move(name, part, "mat", pairs)
     result = place_in(result, 3, 0, jnp.concatenate(corner, axis=1))
     return result
 

time: 219 us -> 186 us (0.85)
  waiting for transfers between devices: 161 us -> 114 us
  starting transfers between devices: 40.4 us -> 61.8 us
  local copies, waits for them, and re-layouts: 11.4 us -> 7.28 us
  Pallas kernels: 3.39 us -> 0.74 us
    ppermute x19 -> x17, waiting for transfers between devices: 161 us -> 114 us  [move(): return lax.ppermute(block, axis, pairs)]
    ppermute x19 -> x17, starting transfers between devices: 40.4 us -> 61.8 us  [move(): return lax.ppermute(block, axis, pairs)]
    unnamed x14 -> x6, local copies, waits for them, and re-layouts: 6.71 us -> 2.6 us
    pallas_call x1, Pallas kernels: 2.89 us -> 0.08 us  [early_products(): pl.pallas_call(functools.partial(early_kernel, count), out_shape=(jax.Sha...]
  transfers between devices with their start and end apart: 19 -> 17, of which waited for: 8 -> 7; matrix products, arithmetic and copies ran while one was open for 2% -> 3% of each run, Pallas kernels for 1% -> 0%
where the time goes in v10:
time: 186 us
  waiting for transfers between devices  114 us (61%)
  starting transfers between devices  61.8 us (33%)
  local copies, waits for them, and re-layouts  7.28 us (4%)
    ppermute x17, waiting for transfers between devices, move(): return lax.ppermute(block, axis, pairs)  114 us
    ppermute x17, starting transfers between devices, move(): return lax.ppermute(block, axis, pairs)  61.8 us
  transfers between devices with their start and end apart: 17, of which 7 were waited for; matrix products, arithmetic and copies ran while one was open for 3% of the time, Pallas kernels for 0%

profile of v10, /device:TPU:0, one launch (start us, length us, event | category | flops | bytes accessed | tf_op | source)
XLA Modules:
  0.0 185.9 jit_solution(15150985688482491084)
XLA Ops:
  1.5 1.5 slice_bitcast_fusion
  3.0 9.7 %collective-permute-start.2 = (bf16[160,2560]{1,0:T(8,128)(2,1)S(1)}, bf16[160,2560]{1,0:T(8,128)(2,1)}, u32[]{:S(2)}, u32[]{:S(2)}) collective-permute-start(bf16[160,2560]{1,0:T(8,128)(2,1)S(1)} %get-tuple-element.39.refs_4_), channel_id=1, source_target_pairs={{0,2},{1,3},{6,4},{7,5},{8,10},{9,11},{14,12},{15,13},{16,18},{17,... | collective-permute-start | bytes 2457608 | tf_op jit(solution)/shard_map/rows_in/ppermute | solution.py:209
  12.8 2.2 %collective-permute-start = (bf16[160,2560]{1,0:T(8,128)(2,1)S(1)}, bf16[160,2560]{1,0:T(8,128)(2,1)}, u32[]{:S(2)}, u32[]{:S(2)}) collective-permute-start(bf16[160,2560]{1,0:T(8,128)(2,1)S(1)} %get-tuple-element.40.refs_3_), channel_id=1, source_target_pairs={{0,2},{1,3},{6,4},{7,5},{8,10},{9,11},{14,12},{15,13},{16,18},{17,... | collective-permute-start | bytes 2457608 | tf_op jit(solution)/shard_map/rows_in/ppermute | solution.py:209
  15.0 1.9 collective-permute-start.6
  16.8 31.9 %collective-permute-start.7 = (bf16[320,2560]{1,0:T(8,128)(2,1)}, bf16[320,2560]{1,0:T(8,128)(2,1)}, u32[]{:S(2)}, u32[]{:S(2)}) collective-permute-start(bf16[320,2560]{1,0:T(8,128)(2,1)} %bitcast.24), channel_id=1, source_target_pairs={{0,4},{1,5},{6,2},{7,3},{8,12},{9,13},{14,10},{15,11},{16,20},{17,... | collective-permute-start | bytes 4915208 | tf_op jit(solution)/shard_map/rows_far/ppermute | solution.py:209
  48.7 1.6 collective-permute-start.5
  51.4 1.6 collective-permute-start.4
  53.0 1.4 copy-done.1
  54.5 29.0 %collective-permute-done.7.refs_10_ = bf16[320,2560]{1,0:T(8,128)(2,1)} collective-permute-done((bf16[320,2560]{1,0:T(8,128)(2,1)}, bf16[320,2560]{1,0:T(8,128)(2,1)}, u32[]{:S(2)}, u32[]{:S(2)}) %collective-permute-start.7) | collective-permute-done | bytes 1638432 | tf_op jit(solution)/shard_map/rows_far/ppermute | solution.py:209
  84.6 1.3 collective-permute-start.12
  85.9 1.3 collective-permute-start.9
  87.6 38.9 %collective-permute-done.12 = bf16[320,1280]{1,0:T(8,128)(2,1)S(1)} collective-permute-done((bf16[320,1280]{1,0:T(8,128)(2,1)S(1)}, bf16[320,1280]{1,0:T(8,128)(2,1)S(1)}, u32[]{:S(2)}, u32[]{:S(2)}) %collective-permute-start.12) | collective-permute-done | bytes 819232 | tf_op jit(solution)/shard_map/rows_out/ppermute | solution.py:209
  126.6 1.6 collective-permute-start.13
  128.1 1.5 collective-permute-start.14
  129.7 13.9 %collective-permute-done.9 = bf16[320,1280]{1,0:T(8,128)(2,1)S(1)} collective-permute-done((bf16[320,1280]{1,0:T(8,128)(2,1)S(1)}, bf16[320,1280]{1,0:T(8,128)(2,1)S(1)}, u32[]{:S(2)}, u32[]{:S(2)}) %collective-permute-start.9) | collective-permute-done | bytes 819232 | tf_op jit(solution)/shard_map/rows_out/ppermute | solution.py:209
  143.7 1.5 collective-permute-start.10
  145.2 1.5 collective-permute-start.11
  147.3 16.3 %collective-permute-done.10 = bf16[320,1280]{1,0:T(8,128)(2,1)} collective-permute-done((bf16[320,1280]{1,0:T(8,128)(2,1)S(1)}, bf16[320,1280]{1,0:T(8,128)(2,1)}, u32[]{:S(2)}, u32[]{:S(2)}) %collective-permute-start.10) | collective-permute-done | bytes 819232 | tf_op jit(solution)/shard_map/along_x/ppermute | solution.py:209
  163.6 1.2 collective-permute-done.11
  164.8 1.5 collective-permute-start.15
  166.9 1.2 bitcast_dynamic-update-slice_fusion.4
  168.1 1.2 bitcast_dynamic-update-slice_fusion.3
  169.6 14.1 %collective-permute-done.15 = bf16[320,1280]{1,0:T(8,128)(2,1)S(1)} collective-permute-done((bf16[320,1280]{1,0:T(8,128)(2,1)}, bf16[320,1280]{1,0:T(8,128)(2,1)S(1)}, u32[]{:S(2)}, u32[]{:S(2)}) %collective-permute-start.15) | collective-permute-done | bytes 819232 | tf_op jit(solution)/shard_map/across_y/ppermute | solution.py:209
  184.6 1.3 fusion
  (30 shorter events, 6.7 us)
Async XLA Ops:
  0.0 15.0 %collective-permute-start.3 = (bf16[320,2560]{1,0:T(8,128)(2,1)}, bf16[320,2560]{1,0:T(8,128)(2,1)S(1)}, u32[]{:S(2)}, u32[]{:S(2)}) collective-permute-start(bf16[320,2560]{1,0:T(8,128)(2,1)} %bitcast.22), channel_id=1, source_target_pairs={{2,4},{3,5},{4,2},{5,3},{10,12},{11,13},{12,10},{13,11},{18,20},{1... | collective-permute-start | bytes 4915208 | tf_op jit(solution)/shard_map/middle/ppermute | solution.py:209
  0.8 49.5 %collective-permute-start.1 = (bf16[320,2560]{1,0:T(8,128)(2,1)}, bf16[320,2560]{1,0:T(8,128)(2,1)S(1)}, u32[]{:S(2)}, u32[]{:S(2)}) collective-permute-start(bf16[320,2560]{1,0:T(8,128)(2,1)} %bitcast.23), channel_id=1, source_target_pairs={{2,3},{3,2},{4,5},{5,4},{10,11},{11,10},{12,13},{13,12},{18,19},{1... | collective-permute-start | bytes 4915208 | tf_op jit(solution)/shard_map/swap_own/ppermute | solution.py:209
  3.0 45.6 %collective-permute-start.2 = (bf16[160,2560]{1,0:T(8,128)(2,1)S(1)}, bf16[160,2560]{1,0:T(8,128)(2,1)}, u32[]{:S(2)}, u32[]{:S(2)}) collective-permute-start(bf16[160,2560]{1,0:T(8,128)(2,1)S(1)} %get-tuple-element.39.refs_4_), channel_id=1, source_target_pairs={{0,2},{1,3},{6,4},{7,5},{8,10},{9,11},{14,12},{15,13},{16,18},{17,... | collective-permute-start | bytes 2457608 | tf_op jit(solution)/shard_map/rows_in/ppermute | solution.py:209
  12.8 37.5 %collective-permute-start = (bf16[160,2560]{1,0:T(8,128)(2,1)S(1)}, bf16[160,2560]{1,0:T(8,128)(2,1)}, u32[]{:S(2)}, u32[]{:S(2)}) collective-permute-start(bf16[160,2560]{1,0:T(8,128)(2,1)S(1)} %get-tuple-element.40.refs_3_), channel_id=1, source_target_pairs={{0,2},{1,3},{6,4},{7,5},{8,10},{9,11},{14,12},{15,13},{16,18},{17,... | collective-permute-start | bytes 2457608 | tf_op jit(solution)/shard_map/rows_in/ppermute | solution.py:209
  15.0 38.1 %collective-permute-start.6 = (bf16[320,2560]{1,0:T(8,128)(2,1)S(1)}, bf16[320,2560]{1,0:T(8,128)(2,1)}, u32[]{:S(2)}, u32[]{:S(2)}) collective-permute-start(bf16[320,2560]{1,0:T(8,128)(2,1)S(1)} %collective-permute-done.3.refs_6_), channel_id=1, source_target_pairs={{2,3},{3,2},{4,5},{5,4},{10,11},{11,10},{12,13},{13,12},{18,19},{1... | collective-permute-start | bytes 4915208 | tf_op jit(solution)/shard_map/swap_rows/ppermute | solution.py:209
  16.8 66.7 %collective-permute-start.7 = (bf16[320,2560]{1,0:T(8,128)(2,1)}, bf16[320,2560]{1,0:T(8,128)(2,1)}, u32[]{:S(2)}, u32[]{:S(2)}) collective-permute-start(bf16[320,2560]{1,0:T(8,128)(2,1)} %bitcast.24), channel_id=1, source_target_pairs={{0,4},{1,5},{6,2},{7,3},{8,12},{9,13},{14,10},{15,11},{16,20},{17,... | collective-permute-start | bytes 4915208 | tf_op jit(solution)/shard_map/rows_far/ppermute | solution.py:209
  48.7 4.3 %collective-permute-start.5 = (bf16[160,2560]{1,0:T(8,128)(2,1)}, bf16[160,2560]{1,0:T(8,128)(2,1)}, u32[]{:S(2)}, u32[]{:S(2)}) collective-permute-start(bf16[160,2560]{1,0:T(8,128)(2,1)} %collective-permute-done.2.refs_2_), channel_id=1, source_target_pairs={{2,3},{3,2},{4,5},{5,4},{10,11},{11,10},{12,13},{13,12},{18,19},{1... | collective-permute-start | bytes 2457608 | tf_op jit(solution)/shard_map/swap_rows/ppermute | solution.py:209
  50.3 1.2 copy-start
  51.4 1.6 collective-permute-start.4
  53.0 1.4 copy-start.1
  83.5 0.8 collective-permute-start.8
  84.6 41.9 %collective-permute-start.12 = (bf16[320,1280]{1,0:T(8,128)(2,1)S(1)}, bf16[320,1280]{1,0:T(8,128)(2,1)S(1)}, u32[]{:S(2)}, u32[]{:S(2)}) collective-permute-start(bf16[320,1280]{1,0:T(8,128)(2,1)S(1)} %get-tuple-element.33), channel_id=1, source_target_pairs={{2,0},{3,1},{4,6},{5,7},{10,8},{11,9},{12,14},{13,15},{18,16},{19,... | collective-permute-start | bytes 2457608 | tf_op jit(solution)/shard_map/rows_out/ppermute | solution.py:209
  85.9 57.7 %collective-permute-start.9 = (bf16[320,1280]{1,0:T(8,128)(2,1)S(1)}, bf16[320,1280]{1,0:T(8,128)(2,1)S(1)}, u32[]{:S(2)}, u32[]{:S(2)}) collective-permute-start(bf16[320,1280]{1,0:T(8,128)(2,1)S(1)} %get-tuple-element.29), channel_id=1, source_target_pairs={{2,0},{3,1},{4,6},{5,7},{10,8},{11,9},{12,14},{13,15},{18,16},{19,... | collective-permute-start | bytes 2457608 | tf_op jit(solution)/shard_map/rows_out/ppermute | solution.py:209
  126.6 20.7 %collective-permute-start.13 = (bf16[320,1280]{1,0:T(8,128)(2,1)S(1)}, bf16[320,1280]{1,0:T(8,128)(2,1)S(1)}, u32[]{:S(2)}, u32[]{:S(2)}) collective-permute-start(bf16[320,1280]{1,0:T(8,128)(2,1)S(1)} %broadcast_select_fusion), channel_id=1, source_target_pairs={{0,8},{8,0},{16,24},{24,16},{1,9},{9,1},{17,25},{25,17},{2,10},{10... | collective-permute-start | bytes 2457608 | tf_op jit(solution)/shard_map/along_x/ppermute | solution.py:209
  128.1 19.2 %collective-permute-start.14 = (bf16[320,1280]{1,0:T(8,128)(2,1)S(1)}, bf16[320,1280]{1,0:T(8,128)(2,1)S(1)}, u32[]{:S(2)}, u32[]{:S(2)}) collective-permute-start(bf16[320,1280]{1,0:T(8,128)(2,1)S(1)} %broadcast_select_fusion), channel_id=1, source_target_pairs={{0,16},{8,24},{16,0},{24,8},{1,17},{9,25},{17,1},{25,9},{2,18},{10... | collective-permute-start | bytes 2457608 | tf_op jit(solution)/shard_map/along_y/ppermute | solution.py:209
  143.7 20.0 %collective-permute-start.10 = (bf16[320,1280]{1,0:T(8,128)(2,1)S(1)}, bf16[320,1280]{1,0:T(8,128)(2,1)}, u32[]{:S(2)}, u32[]{:S(2)}) collective-permute-start(bf16[320,1280]{1,0:T(8,128)(2,1)S(1)} %broadcast_select_fusion.1), channel_id=1, source_target_pairs={{0,8},{8,0},{16,24},{24,16},{1,9},{9,1},{17,25},{25,17},{2,10},{10... | collective-permute-start | bytes 2457608 | tf_op jit(solution)/shard_map/along_x/ppermute | solution.py:209
  145.2 19.6 %collective-permute-start.11 = (bf16[320,1280]{1,0:T(8,128)(2,1)S(1)}, bf16[320,1280]{1,0:T(8,128)(2,1)}, u32[]{:S(2)}, u32[]{:S(2)}) collective-permute-start(bf16[320,1280]{1,0:T(8,128)(2,1)S(1)} %broadcast_select_fusion.1), channel_id=1, source_target_pairs={{0,16},{8,24},{16,0},{24,8},{1,17},{9,25},{17,1},{25,9},{2,18},{10... | collective-permute-start | bytes 2457608 | tf_op jit(solution)/shard_map/along_y/ppermute | solution.py:209
  164.8 18.8 %collective-permute-start.15 = (bf16[320,1280]{1,0:T(8,128)(2,1)}, bf16[320,1280]{1,0:T(8,128)(2,1)S(1)}, u32[]{:S(2)}, u32[]{:S(2)}) collective-permute-start(bf16[320,1280]{1,0:T(8,128)(2,1)} %collective-permute-done.10), channel_id=1, source_target_pairs={{0,16},{8,24},{16,0},{24,8},{1,17},{9,25},{17,1},{25,9},{2,18},{10... | collective-permute-start | bytes 2457608 | tf_op jit(solution)/shard_map/across_y/ppermute | solution.py:209
  166.3 18.3 %collective-permute-start.16 = (bf16[320,1280]{1,0:T(8,128)(2,1)S(1)}, bf16[320,1280]{1,0:T(8,128)(2,1)S(1)}, u32[]{:S(2)}, u32[]{:S(2)}) collective-permute-start(bf16[320,1280]{1,0:T(8,128)(2,1)S(1)} %collective-permute-done.14), channel_id=1, source_target_pairs={{0,8},{8,0},{16,24},{24,16},{1,9},{9,1},{17,25},{25,17},{2,10},{10... | collective-permute-start | bytes 2457608 | tf_op jit(solution)/shard_map/across_x/ppermute | solution.py:209
  169.5 15.1 %copy-start.2 = (bf16[4,320,2560]{2,1,0:T(8,128)(2,1)}, bf16[4,320,2560]{2,1,0:T(8,128)(2,1)S(1)}, u32[]{:S(2)}) copy-start(bf16[4,320,2560]{2,1,0:T(8,128)(2,1)S(1)} %bitcast_dynamic-update-slice_fusion) | copy-start | bytes 19660804

commit v11 on v10

--- a/solution.py
+++ b/solution.py
@@ -213,14 +213,17 @@
 
     cut = rows // 2
     halves = [own[:cut], own[cut:]]
-    inner_rows = move("middle", own, "shard", middle)
     outer_rows = [move("rows_in", half, "shard", inwards) for half in halves]
+    inner_rows = [move("middle", half, "shard", middle) for half in halves]
+    far_rows = move("rows_far", own, "shard", across_middle)
     own_swapped = swap("own", own)
     outer_rows[0], own_swapped = tie((outer_rows[0], own_swapped))
-    far_rows = move("rows_far", own, "shard", across_middle)
-
-    early = outer_rows + halves + [own_swapped, inner_rows]
-    early += [swap("rows", block) for block in outer_rows + [inner_rows]]
+    swapped = swap("rows", outer_rows[0])
+    outer_rows[1], inner_rows[0], inner_rows[1], swapped = tie(
+        (outer_rows[1], inner_rows[0], inner_rows[1], swapped)
+    )
+    early = outer_rows + halves + [own_swapped] + inner_rows
+    early += [swapped] + [swap("rows", half) for half in outer_rows[1:] + inner_rows]
     gram, cubic = early_products(inner, rows, early)
     far_rows, gram, cubic = tie((far_rows, gram, cubic))
     late = [far_rows, swap("far", far_rows)]

time: 186 us -> 212 us (1.14)
  waiting for transfers between devices: 114 us -> 162 us
  starting transfers between devices: 61.8 us -> 38.8 us
    ppermute x17 -> x19, waiting for transfers between devices: 114 us -> 162 us  [move(): return lax.ppermute(block, axis, pairs)]
    ppermute x17 -> x19, starting transfers between devices: 61.8 us -> 38.8 us  [move(): return lax.ppermute(block, axis, pairs)]
  transfers between devices with their start and end apart: 17 -> 19, of which waited for: 7 -> 9; matrix products, arithmetic and copies ran while one was open for 3% -> 2% of each run, Pallas kernels for 0% -> 0%
where the time goes in v11:
time: 212 us
  waiting for transfers between devices  162 us (76%)
  starting transfers between devices  38.8 us (18%)
  local copies, waits for them, and re-layouts  8.74 us (4%)
    ppermute x19, waiting for transfers between devices, move(): return lax.ppermute(block, axis, pairs)  162 us
    ppermute x19, starting transfers between devices, move(): return lax.ppermute(block, axis, pairs)  38.8 us
  transfers between devices with their start and end apart: 19, of which 9 were waited for; matrix products, arithmetic and copies ran while one was open for 2% of the time, Pallas kernels for 0%

profile of v11, /device:TPU:0, one launch (start us, length us, event | category | flops | bytes accessed | tf_op | source)
XLA Modules:
  0.0 211.6 jit_solution(3439453237776833515)
XLA Ops:
  0.8 1.5 slice_bitcast_fusion
  2.3 6.1 %collective-permute-start = (bf16[160,2560]{1,0:T(8,128)(2,1)S(1)}, bf16[160,2560]{1,0:T(8,128)(2,1)S(1)}, u32[]{:S(2)}, u32[]{:S(2)}) collective-permute-start(bf16[160,2560]{1,0:T(8,128)(2,1)S(1)} %get-tuple-element.48.refs_3_), channel_id=1, source_target_pairs={{0,2},{1,3},{6,4},{7,5},{8,10},{9,11},{14,12},{15,13},{16,18},{17,... | collective-permute-start | bytes 2457608 | tf_op jit(solution)/shard_map/rows_in/ppermute | solution.py:209
  8.4 1.6 collective-permute-start.3
  10.0 4.1 %collective-permute-start.2 = (bf16[160,2560]{1,0:T(8,128)(2,1)S(1)}, bf16[160,2560]{1,0:T(8,128)(2,1)}, u32[]{:S(2)}, u32[]{:S(2)}) collective-permute-start(bf16[160,2560]{1,0:T(8,128)(2,1)S(1)} %get-tuple-element.47.refs_4_), channel_id=1, source_target_pairs={{0,2},{1,3},{6,4},{7,5},{8,10},{9,11},{14,12},{15,13},{16,18},{17,... | collective-permute-start | bytes 2457608 | tf_op jit(solution)/shard_map/rows_in/ppermute | solution.py:209
  14.1 1.5 collective-permute-start.4
  15.6 11.3 %collective-permute-done.refs_1_ = bf16[160,2560]{1,0:T(8,128)(2,1)S(1)} collective-permute-done((bf16[160,2560]{1,0:T(8,128)(2,1)S(1)}, bf16[160,2560]{1,0:T(8,128)(2,1)S(1)}, u32[]{:S(2)}, u32[]{:S(2)}) %collective-permute-start) | collective-permute-done | bytes 819232 | tf_op jit(solution)/shard_map/rows_in/ppermute | solution.py:209
  28.5 7.8 %collective-permute-start.9 = (bf16[320,2560]{1,0:T(8,128)(2,1)}, bf16[320,2560]{1,0:T(8,128)(2,1)}, u32[]{:S(2)}, u32[]{:S(2)}) collective-permute-start(bf16[320,2560]{1,0:T(8,128)(2,1)} %bitcast.23), channel_id=1, source_target_pairs={{0,4},{1,5},{6,2},{7,3},{8,12},{9,13},{14,10},{15,11},{16,20},{17,... | collective-permute-start | bytes 4915208 | tf_op jit(solution)/shard_map/rows_far/ppermute | solution.py:209
  36.3 8.1 %collective-permute-done.2.refs_2_ = bf16[160,2560]{1,0:T(8,128)(2,1)} collective-permute-done((bf16[160,2560]{1,0:T(8,128)(2,1)S(1)}, bf16[160,2560]{1,0:T(8,128)(2,1)}, u32[]{:S(2)}, u32[]{:S(2)}) %collective-permute-start.2) | collective-permute-done | bytes 819232 | tf_op jit(solution)/shard_map/rows_in/ppermute | solution.py:209
  45.4 1.5 collective-permute-start.6
  46.9 1.6 collective-permute-start.7
  48.5 1.6 collective-permute-start.8
  52.5 26.9 %collective-permute-done.9.refs_12_ = bf16[320,2560]{1,0:T(8,128)(2,1)} collective-permute-done((bf16[320,2560]{1,0:T(8,128)(2,1)}, bf16[320,2560]{1,0:T(8,128)(2,1)}, u32[]{:S(2)}, u32[]{:S(2)}) %collective-permute-start.9) | collective-permute-done | bytes 1638432 | tf_op jit(solution)/shard_map/rows_far/ppermute | solution.py:209
  80.4 1.3 collective-permute-start.14
  81.7 1.3 collective-permute-start.11
  83.4 68.8 %collective-permute-done.14 = bf16[320,1280]{1,0:T(8,128)(2,1)S(1)} collective-permute-done((bf16[320,1280]{1,0:T(8,128)(2,1)S(1)}, bf16[320,1280]{1,0:T(8,128)(2,1)S(1)}, u32[]{:S(2)}, u32[]{:S(2)}) %collective-permute-start.14) | collective-permute-done | bytes 819232 | tf_op jit(solution)/shard_map/rows_out/ppermute | solution.py:209
  152.3 1.5 collective-permute-start.15
  153.8 1.5 collective-permute-start.16
  155.4 13.9 %collective-permute-done.11 = bf16[320,1280]{1,0:T(8,128)(2,1)S(1)} collective-permute-done((bf16[320,1280]{1,0:T(8,128)(2,1)S(1)}, bf16[320,1280]{1,0:T(8,128)(2,1)S(1)}, u32[]{:S(2)}, u32[]{:S(2)}) %collective-permute-start.11) | collective-permute-done | bytes 819232 | tf_op jit(solution)/shard_map/rows_out/ppermute | solution.py:209
  169.4 1.6 collective-permute-start.12
  171.0 1.5 collective-permute-start.13
  173.1 16.3 %collective-permute-done.12 = bf16[320,1280]{1,0:T(8,128)(2,1)} collective-permute-done((bf16[320,1280]{1,0:T(8,128)(2,1)S(1)}, bf16[320,1280]{1,0:T(8,128)(2,1)}, u32[]{:S(2)}, u32[]{:S(2)}) %collective-permute-start.12) | collective-permute-done | bytes 819232 | tf_op jit(solution)/shard_map/along_x/ppermute | solution.py:209
  190.6 1.5 collective-permute-start.17
  195.2 14.2 %collective-permute-done.17 = bf16[320,1280]{1,0:T(8,128)(2,1)S(1)} collective-permute-done((bf16[320,1280]{1,0:T(8,128)(2,1)}, bf16[320,1280]{1,0:T(8,128)(2,1)S(1)}, u32[]{:S(2)}, u32[]{:S(2)}) %collective-permute-start.17) | collective-permute-done | bytes 819232 | tf_op jit(solution)/shard_map/across_y/ppermute | solution.py:209
  210.3 1.3 fusion
  (38 shorter events, 13.2 us)
Async XLA Ops:
  0.0 26.9 %collective-permute-start.1 = (bf16[320,2560]{1,0:T(8,128)(2,1)}, bf16[320,2560]{1,0:T(8,128)(2,1)S(1)}, u32[]{:S(2)}, u32[]{:S(2)}) collective-permute-start(bf16[320,2560]{1,0:T(8,128)(2,1)} %bitcast.22), channel_id=1, source_target_pairs={{2,3},{3,2},{4,5},{5,4},{10,11},{11,10},{12,13},{13,12},{18,19},{1... | collective-permute-start | bytes 4915208 | tf_op jit(solution)/shard_map/swap_own/ppermute | solution.py:209
  2.3 24.6 %collective-permute-start = (bf16[160,2560]{1,0:T(8,128)(2,1)S(1)}, bf16[160,2560]{1,0:T(8,128)(2,1)S(1)}, u32[]{:S(2)}, u32[]{:S(2)}) collective-permute-start(bf16[160,2560]{1,0:T(8,128)(2,1)S(1)} %get-tuple-element.48.refs_3_), channel_id=1, source_target_pairs={{0,2},{1,3},{6,4},{7,5},{8,10},{9,11},{14,12},{15,13},{16,18},{17,... | collective-permute-start | bytes 2457608 | tf_op jit(solution)/shard_map/rows_in/ppermute | solution.py:209
  8.4 36.0 %collective-permute-start.3 = (bf16[160,2560]{1,0:T(8,128)(2,1)S(1)}, bf16[160,2560]{1,0:T(8,128)(2,1)}, u32[]{:S(2)}, u32[]{:S(2)}) collective-permute-start(bf16[160,2560]{1,0:T(8,128)(2,1)S(1)} %get-tuple-element.48.refs_3_), channel_id=1, source_target_pairs={{2,4},{3,5},{4,2},{5,3},{10,12},{11,13},{12,10},{13,11},{18,20},{1... | collective-permute-start | bytes 2457608 | tf_op jit(solution)/shard_map/middle/ppermute | solution.py:209
  10.0 34.5 %collective-permute-start.2 = (bf16[160,2560]{1,0:T(8,128)(2,1)S(1)}, bf16[160,2560]{1,0:T(8,128)(2,1)}, u32[]{:S(2)}, u32[]{:S(2)}) collective-permute-start(bf16[160,2560]{1,0:T(8,128)(2,1)S(1)} %get-tuple-element.47.refs_4_), channel_id=1, source_target_pairs={{0,2},{1,3},{6,4},{7,5},{8,10},{9,11},{14,12},{15,13},{16,18},{17,... | collective-permute-start | bytes 2457608 | tf_op jit(solution)/shard_map/rows_in/ppermute | solution.py:209
  14.1 30.4 %collective-permute-start.4 = (bf16[160,2560]{1,0:T(8,128)(2,1)S(1)}, bf16[160,2560]{1,0:T(8,128)(2,1)}, u32[]{:S(2)}, u32[]{:S(2)}) collective-permute-start(bf16[160,2560]{1,0:T(8,128)(2,1)S(1)} %get-tuple-element.47.refs_4_), channel_id=1, source_target_pairs={{2,4},{3,5},{4,2},{5,3},{10,12},{11,13},{12,10},{13,11},{18,20},{1... | collective-permute-start | bytes 2457608 | tf_op jit(solution)/shard_map/middle/ppermute | solution.py:209
  26.9 17.6 %collective-permute-start.5 = (bf16[160,2560]{1,0:T(8,128)(2,1)S(1)}, bf16[160,2560]{1,0:T(8,128)(2,1)S(1)}, u32[]{:S(2)}, u32[]{:S(2)}) collective-permute-start(bf16[160,2560]{1,0:T(8,128)(2,1)S(1)} %collective-permute-done.refs_1_), channel_id=1, source_target_pairs={{2,3},{3,2},{4,5},{5,4},{10,11},{11,10},{12,13},{13,12},{18,19},{1... | collective-permute-start | bytes 2457608 | tf_op jit(solution)/shard_map/swap_rows/ppermute | solution.py:209
  27.6 0.9 copy-start
  28.5 50.8 %collective-permute-start.9 = (bf16[320,2560]{1,0:T(8,128)(2,1)}, bf16[320,2560]{1,0:T(8,128)(2,1)}, u32[]{:S(2)}, u32[]{:S(2)}) collective-permute-start(bf16[320,2560]{1,0:T(8,128)(2,1)} %bitcast.23), channel_id=1, source_target_pairs={{0,4},{1,5},{6,2},{7,3},{8,12},{9,13},{14,10},{15,11},{16,20},{17,... | collective-permute-start | bytes 4915208 | tf_op jit(solution)/shard_map/rows_far/ppermute | solution.py:209
  44.5 0.9 copy-start.2
  45.4 4.7 %collective-permute-start.6 = (bf16[160,2560]{1,0:T(8,128)(2,1)}, bf16[160,2560]{1,0:T(8,128)(2,1)}, u32[]{:S(2)}, u32[]{:S(2)}) collective-permute-start(bf16[160,2560]{1,0:T(8,128)(2,1)} %collective-permute-done.2.refs_2_), channel_id=1, source_target_pairs={{2,3},{3,2},{4,5},{5,4},{10,11},{11,10},{12,13},{13,12},{18,19},{1... | collective-permute-start | bytes 2457608 | tf_op jit(solution)/shard_map/swap_rows/ppermute | solution.py:209
  46.9 3.1 %collective-permute-start.7 = (bf16[160,2560]{1,0:T(8,128)(2,1)}, bf16[160,2560]{1,0:T(8,128)(2,1)}, u32[]{:S(2)}, u32[]{:S(2)}) collective-permute-start(bf16[160,2560]{1,0:T(8,128)(2,1)} %collective-permute-done.3.refs_6_), channel_id=1, source_target_pairs={{2,3},{3,2},{4,5},{5,4},{10,11},{11,10},{12,13},{13,12},{18,19},{1... | collective-permute-start | bytes 2457608 | tf_op jit(solution)/shard_map/swap_rows/ppermute | solution.py:209
  48.5 1.6 collective-permute-start.8
  50.1 1.1 copy-start.1
  51.2 1.1 copy-start.3
  79.3 0.8 collective-permute-start.10
  80.4 71.8 %collective-permute-start.14 = (bf16[320,1280]{1,0:T(8,128)(2,1)S(1)}, bf16[320,1280]{1,0:T(8,128)(2,1)S(1)}, u32[]{:S(2)}, u32[]{:S(2)}) collective-permute-start(bf16[320,1280]{1,0:T(8,128)(2,1)S(1)} %get-tuple-element.41), channel_id=1, source_target_pairs={{2,0},{3,1},{4,6},{5,7},{10,8},{11,9},{12,14},{13,15},{18,16},{19,... | collective-permute-start | bytes 2457608 | tf_op jit(solution)/shard_map/rows_out/ppermute | solution.py:209
  81.7 87.6 %collective-permute-start.11 = (bf16[320,1280]{1,0:T(8,128)(2,1)S(1)}, bf16[320,1280]{1,0:T(8,128)(2,1)S(1)}, u32[]{:S(2)}, u32[]{:S(2)}) collective-permute-start(bf16[320,1280]{1,0:T(8,128)(2,1)S(1)} %get-tuple-element.37), channel_id=1, source_target_pairs={{2,0},{3,1},{4,6},{5,7},{10,8},{11,9},{12,14},{13,15},{18,16},{19,... | collective-permute-start | bytes 2457608 | tf_op jit(solution)/shard_map/rows_out/ppermute | solution.py:209
  152.3 20.7 %collective-permute-start.15 = (bf16[320,1280]{1,0:T(8,128)(2,1)S(1)}, bf16[320,1280]{1,0:T(8,128)(2,1)S(1)}, u32[]{:S(2)}, u32[]{:S(2)}) collective-permute-start(bf16[320,1280]{1,0:T(8,128)(2,1)S(1)} %broadcast_select_fusion), channel_id=1, source_target_pairs={{0,8},{8,0},{16,24},{24,16},{1,9},{9,1},{17,25},{25,17},{2,10},{10... | collective-permute-start | bytes 2457608 | tf_op jit(solution)/shard_map/along_x/ppermute | solution.py:209
  153.8 19.2 %collective-permute-start.16 = (bf16[320,1280]{1,0:T(8,128)(2,1)S(1)}, bf16[320,1280]{1,0:T(8,128)(2,1)S(1)}, u32[]{:S(2)}, u32[]{:S(2)}) collective-permute-start(bf16[320,1280]{1,0:T(8,128)(2,1)S(1)} %broadcast_select_fusion), channel_id=1, source_target_pairs={{0,16},{8,24},{16,0},{24,8},{1,17},{9,25},{17,1},{25,9},{2,18},{10... | collective-permute-start | bytes 2457608 | tf_op jit(solution)/shard_map/along_y/ppermute | solution.py:209
  169.4 19.9 %collective-permute-start.12 = (bf16[320,1280]{1,0:T(8,128)(2,1)S(1)}, bf16[320,1280]{1,0:T(8,128)(2,1)}, u32[]{:S(2)}, u32[]{:S(2)}) collective-permute-start(bf16[320,1280]{1,0:T(8,128)(2,1)S(1)} %broadcast_select_fusion.1), channel_id=1, source_target_pairs={{0,8},{8,0},{16,24},{24,16},{1,9},{9,1},{17,25},{25,17},{2,10},{10... | collective-permute-start | bytes 2457608 | tf_op jit(solution)/shard_map/along_x/ppermute | solution.py:209
  171.0 19.6 %collective-permute-start.13 = (bf16[320,1280]{1,0:T(8,128)(2,1)S(1)}, bf16[320,1280]{1,0:T(8,128)(2,1)}, u32[]{:S(2)}, u32[]{:S(2)}) collective-permute-start(bf16[320,1280]{1,0:T(8,128)(2,1)S(1)} %broadcast_select_fusion.1), channel_id=1, source_target_pairs={{0,16},{8,24},{16,0},{24,8},{1,17},{9,25},{17,1},{25,9},{2,18},{10... | collective-permute-start | bytes 2457608 | tf_op jit(solution)/shard_map/along_y/ppermute | solution.py:209
  190.6 18.8 %collective-permute-start.17 = (bf16[320,1280]{1,0:T(8,128)(2,1)}, bf16[320,1280]{1,0:T(8,128)(2,1)S(1)}, u32[]{:S(2)}, u32[]{:S(2)}) collective-permute-start(bf16[320,1280]{1,0:T(8,128)(2,1)} %collective-permute-done.12), channel_id=1, source_target_pairs={{0,16},{8,24},{16,0},{24,8},{1,17},{9,25},{17,1},{25,9},{2,18},{10... | collective-permute-start | bytes 2457608 | tf_op jit(solution)/shard_map/across_y/ppermute | solution.py:209
  192.0 18.3 %collective-permute-start.18 = (bf16[320,1280]{1,0:T(8,128)(2,1)S(1)}, bf16[320,1280]{1,0:T(8,128)(2,1)S(1)}, u32[]{:S(2)}, u32[]{:S(2)}) collective-permute-start(bf16[320,1280]{1,0:T(8,128)(2,1)S(1)} %collective-permute-done.16), channel_id=1, source_target_pairs={{0,8},{8,0},{16,24},{24,16},{1,9},{9,1},{17,25},{25,17},{2,10},{10... | collective-permute-start | bytes 2457608 | tf_op jit(solution)/shard_map/across_x/ppermute | solution.py:209
  195.2 15.1 %copy-start.4 = (bf16[4,320,2560]{2,1,0:T(8,128)(2,1)}, bf16[4,320,2560]{2,1,0:T(8,128)(2,1)S(1)}, u32[]{:S(2)}) copy-start(bf16[4,320,2560]{2,1,0:T(8,128)(2,1)S(1)} %bitcast_dynamic-update-slice_fusion) | copy-start | bytes 19660804

commit v12 on v9

--- a/solution.py
+++ b/solution.py
@@ -12,7 +12,7 @@
 coef_c = 2.0315
 
 TILE = 1024
-VMEM_LIMIT = 40 * 1024 * 1024
+VMEM_LIMIT = 30 * 1024 * 1024
 
 
 def dot_t(left, right):
@@ -186,7 +186,7 @@
     )(inner, *blocks, *grams, cubic)
 
 
-def line_shards(iterate, widths):
+def line_shards(iterate, widths, own_widths):
     own = iterate[0]
     rows, columns = own.shape
     place = lax.axis_index("shard") // 2
@@ -211,32 +211,30 @@
     def swap(name, block):
         return move("swap_" + name, block, "shard", other_core)
 
-    cut = rows // 2
-    halves = [own[:cut], own[cut:]]
-    outer_rows = [move("rows_in", half, "shard", inwards) for half in halves]
-    first_rows = move("middle", halves[0], "shard", middle)
-    second_half, first_rows = tie((halves[1], first_rows))
-    inner_rows = [first_rows, move("middle", second_half, "shard", middle)]
-    outer_rows[1], inner_rows[1] = tie((outer_rows[1], inner_rows[1]))
+    outer_rows = move("rows_in", own, "shard", inwards)
+    inner_rows = move("middle", own, "shard", middle)
+    outer_rows = move("rows_in", own, "shard", inwards)
+    inner_rows = move("middle", own, "shard", middle)
     far_rows = move("rows_far", own, "shard", across_middle)
-
-    early = outer_rows + halves + [swap("own", own)] + inner_rows
-    early += [swap("rows", half) for half in outer_rows + inner_rows]
+    early = [outer_rows, own, swap("own", own), inner_rows]
+    early += [swap("rows", outer_rows), swap("rows", inner_rows)]
     gram, cubic = early_products(inner, rows, early)
     far_rows, gram, cubic = tie((far_rows, gram, cubic))
     late = [far_rows, swap("far", far_rows)]
     for_outer = late_products(inner, 0, rows, early, late, [gram], cubic, widths)
-    for_own = late_products(inner, rows, rows, early, late, [gram], cubic, widths)
+    for_own = late_products(inner, rows, rows, early, late, [gram], cubic, own_widths)
 
     result = jnp.zeros((4, rows, columns), jnp.bfloat16)
 
     def place_in(result, flip, at, part):
         return lax.dynamic_update_slice(result, part[None], (mat ^ flip, 0, at))
 
+    returned = [move("rows_out", part, "shard", outwards) for part in for_outer]
     begin, corner = 0, []
-    for k, width in enumerate(widths):
-        returned = move("rows_out", for_outer[k], "shard", outwards)
-        mine = tie(jnp.where(outer, returned, for_own[k]))
+    for k, width in enumerate(own_widths):
+        n = min(k, len(widths) - 1)
+        at = begin - sum(widths[:n])
+        mine = tie(jnp.where(outer, returned[n][:, at : at + width], for_own[k]))
         by_x = move("along_x", mine, "mat", along_x)
         by_y = move("along_y", mine, "mat", along_y)
         by_x, by_y = tie((by_x, by_y))
@@ -254,7 +252,7 @@
 def solution(mesh):
     if (mesh.shape["mat"], mesh.shape["shard"]) == (4, 8):
         def shards(iterate):
-            return line_shards(iterate, widths=(1280, 1280))
+            return line_shards(iterate, widths=(640, 640, 1280), own_widths=(640,) * 4)
     else:
         shards = general_shards
     return jax.shard_map(

time: 219 us -> 202 us (0.922)
  waiting for transfers between devices: 161 us -> 144 us
  local copies, waits for them, and re-layouts: 11.4 us -> 15.4 us
  Pallas kernels: 3.39 us -> 0.47 us
    ppermute x19 -> x22, waiting for transfers between devices: 161 us -> 144 us  [move(): return lax.ppermute(block, axis, pairs)]
    unnamed x14 -> x20, local copies, waits for them, and re-layouts: 6.71 us -> 14.3 us
    pallas_call x1, Pallas kernels: 2.89 us -> 0.05 us  [early_products(): pl.pallas_call(functools.partial(early_kernel, count), out_shape=(jax.Sha...]
    ppermute x19 -> x22, starting transfers between devices: 40.4 us -> 39.7 us  [move(): return lax.ppermute(block, axis, pairs)]
  transfers between devices with their start and end apart: 19 -> 22, of which waited for: 8 -> 12; matrix products, arithmetic and copies ran while one was open for 2% -> 1% of each run, Pallas kernels for 1% -> 0%
where the time goes in v12:
time: 202 us
  waiting for transfers between devices  144 us (71%)
  starting transfers between devices  39.7 us (20%)
  local copies, waits for them, and re-layouts  15.4 us (8%)
    ppermute x22, waiting for transfers between devices, move(): return lax.ppermute(block, axis, pairs)  144 us
    ppermute x22, starting transfers between devices, move(): return lax.ppermute(block, axis, pairs)  39.7 us
    unnamed x20, local copies, waits for them, and re-layouts  14.3 us
  transfers between devices with their start and end apart: 22, of which 12 were waited for; matrix products, arithmetic and copies ran while one was open for 1% of the time, Pallas kernels for 0%

profile of v12, /device:TPU:0, one launch (start us, length us, event | category | flops | bytes accessed | tf_op | source)
XLA Modules:
  0.0 201.7 jit_solution(2076449707097402509)
XLA Ops:
  0.0 5.0 %collective-permute-start = (bf16[320,2560]{1,0:T(8,128)(2,1)}, bf16[320,2560]{1,0:T(8,128)(2,1)S(1)}, u32[]{:S(2)}, u32[]{:S(2)}) collective-permute-start(bf16[320,2560]{1,0:T(8,128)(2,1)} %bitcast.30), channel_id=1, source_target_pairs={{0,2},{1,3},{6,4},{7,5},{8,10},{9,11},{14,12},{15,13},{16,18},{17,... | collective-permute-start | bytes 4915208 | tf_op jit(solution)/shard_map/rows_in/ppermute | solution.py:209
  5.8 1.8 collective-permute-start.1
  7.6 32.6 %collective-permute-done.refs_1_ = bf16[320,2560]{1,0:T(8,128)(2,1)S(1)} collective-permute-done((bf16[320,2560]{1,0:T(8,128)(2,1)}, bf16[320,2560]{1,0:T(8,128)(2,1)S(1)}, u32[]{:S(2)}, u32[]{:S(2)}) %collective-permute-start) | collective-permute-done | bytes 1638432 | tf_op jit(solution)/shard_map/rows_in/ppermute | solution.py:209
  40.3 1.8 collective-permute-start.3
  42.1 1.8 collective-permute-start.4
  45.1 7.2 %collective-permute-start.5 = (bf16[320,2560]{1,0:T(8,128)(2,1)}, bf16[320,2560]{1,0:T(8,128)(2,1)}, u32[]{:S(2)}, u32[]{:S(2)}) collective-permute-start(bf16[320,2560]{1,0:T(8,128)(2,1)} %bitcast.33), channel_id=1, source_target_pairs={{0,4},{1,5},{6,2},{7,3},{8,12},{9,13},{14,10},{15,11},{16,20},{17,... | collective-permute-start | bytes 4915208 | tf_op jit(solution)/shard_map/rows_far/ppermute | solution.py:209
  55.3 2.8 %copy-done.5 = f32[640,2560]{1,0:T(8,128)} copy-done((f32[640,2560]{1,0:T(8,128)}, f32[640,2560]{1,0:T(8,128)S(1)}, u32[]{:S(2)}) %copy-start.5) | copy-done | bytes 6553624
  59.5 27.1 %collective-permute-done.5.refs_7_ = bf16[320,2560]{1,0:T(8,128)(2,1)} collective-permute-done((bf16[320,2560]{1,0:T(8,128)(2,1)}, bf16[320,2560]{1,0:T(8,128)(2,1)}, u32[]{:S(2)}, u32[]{:S(2)}) %collective-permute-start.5) | collective-permute-done | bytes 1638432 | tf_op jit(solution)/shard_map/rows_far/ppermute | solution.py:209
  86.6 1.8 collective-permute-start.6
  89.9 2.9 %copy-done.6 = f32[640,2560]{1,0:T(8,128)S(1)} copy-done((f32[640,2560]{1,0:T(8,128)S(1)}, f32[640,2560]{1,0:T(8,128)}, u32[]{:S(2)}) %copy-start.6) | copy-done | bytes 6553624
  92.8 1.7 copy-done.8
  98.8 45.9 %collective-permute-done.10 = bf16[320,640]{1,0:T(8,128)(2,1)S(1)} collective-permute-done((bf16[320,640]{1,0:T(8,128)(2,1)S(1)}, bf16[320,640]{1,0:T(8,128)(2,1)S(1)}, u32[]{:S(2)}, u32[]{:S(2)}) %collective-permute-start.10) | collective-permute-done | bytes 409632 | tf_op jit(solution)/shard_map/rows_out/ppermute | solution.py:209
  144.7 1.6 collective-permute-start.11
  147.8 5.2 %collective-permute-done.7 = bf16[320,640]{1,0:T(8,128)(2,1)S(1)} collective-permute-done((bf16[320,640]{1,0:T(8,128)(2,1)S(1)}, bf16[320,640]{1,0:T(8,128)(2,1)S(1)}, u32[]{:S(2)}, u32[]{:S(2)}) %collective-permute-start.7) | collective-permute-done | bytes 409632 | tf_op jit(solution)/shard_map/rows_out/ppermute | solution.py:209
  153.0 1.6 collective-permute-start.8
  154.6 1.5 collective-permute-start.9
  159.4 6.1 %collective-permute-done.8 = bf16[320,640]{1,0:T(8,128)(2,1)S(1)} collective-permute-done((bf16[320,640]{1,0:T(8,128)(2,1)S(1)}, bf16[320,640]{1,0:T(8,128)(2,1)S(1)}, u32[]{:S(2)}, u32[]{:S(2)}) %collective-permute-start.8) | collective-permute-done | bytes 409632 | tf_op jit(solution)/shard_map/along_x/ppermute | solution.py:209
  165.5 1.5 collective-permute-start.15
  167.2 1.6 collective-permute-start.19
  168.9 5.3 %collective-permute-done.16 = bf16[320,640]{1,0:T(8,128)(2,1)S(1)} collective-permute-done((bf16[320,640]{1,0:T(8,128)(2,1)S(1)}, bf16[320,640]{1,0:T(8,128)(2,1)S(1)}, u32[]{:S(2)}, u32[]{:S(2)}) %collective-permute-start.16) | collective-permute-done | bytes 409632 | tf_op jit(solution)/shard_map/along_x/ppermute | solution.py:209
  174.2 1.5 collective-permute-start.18
  175.8 7.3 %collective-permute-done.14 = bf16[320,640]{1,0:T(8,128)(2,1)S(1)} collective-permute-done((bf16[320,640]{1,0:T(8,128)(2,1)S(1)}, bf16[320,640]{1,0:T(8,128)(2,1)S(1)}, u32[]{:S(2)}, u32[]{:S(2)}) %collective-permute-start.14) | collective-permute-done | bytes 409632 | tf_op jit(solution)/shard_map/along_x/ppermute | solution.py:209
  186.9 4.8 %collective-permute-done.19 = bf16[320,640]{1,0:T(8,128)(2,1)S(1)} collective-permute-done((bf16[320,640]{1,0:T(8,128)(2,1)S(1)}, bf16[320,640]{1,0:T(8,128)(2,1)S(1)}, u32[]{:S(2)}, u32[]{:S(2)}) %collective-permute-start.19) | collective-permute-done | bytes 409632 | tf_op jit(solution)/shard_map/across_x/ppermute | solution.py:209
  193.3 5.9 %collective-permute-done.21 = bf16[320,640]{1,0:T(8,128)(2,1)S(1)} collective-permute-done((bf16[320,640]{1,0:T(8,128)(2,1)S(1)}, bf16[320,640]{1,0:T(8,128)(2,1)S(1)}, u32[]{:S(2)}, u32[]{:S(2)}) %collective-permute-start.21) | collective-permute-done | bytes 409632 | tf_op jit(solution)/shard_map/across_x/ppermute | solution.py:209
  (60 shorter events, 25.1 us)
Async XLA Ops:
  0.0 40.3 %collective-permute-start = (bf16[320,2560]{1,0:T(8,128)(2,1)}, bf16[320,2560]{1,0:T(8,128)(2,1)S(1)}, u32[]{:S(2)}, u32[]{:S(2)}) collective-permute-start(bf16[320,2560]{1,0:T(8,128)(2,1)} %bitcast.30), channel_id=1, source_target_pairs={{0,2},{1,3},{6,4},{7,5},{8,10},{9,11},{14,12},{15,13},{16,18},{17,... | collective-permute-start | bytes 4915208 | tf_op jit(solution)/shard_map/rows_in/ppermute | solution.py:209
  5.0 37.1 %collective-permute-start.2 = (bf16[320,2560]{1,0:T(8,128)(2,1)}, bf16[320,2560]{1,0:T(8,128)(2,1)S(1)}, u32[]{:S(2)}, u32[]{:S(2)}) collective-permute-start(bf16[320,2560]{1,0:T(8,128)(2,1)} %bitcast.31), channel_id=1, source_target_pairs={{2,4},{3,5},{4,2},{5,3},{10,12},{11,13},{12,10},{13,11},{18,20},{1... | collective-permute-start | bytes 4915208 | tf_op jit(solution)/shard_map/middle/ppermute | solution.py:209
  5.8 46.6 %collective-permute-start.1 = (bf16[320,2560]{1,0:T(8,128)(2,1)}, bf16[320,2560]{1,0:T(8,128)(2,1)}, u32[]{:S(2)}, u32[]{:S(2)}) collective-permute-start(bf16[320,2560]{1,0:T(8,128)(2,1)} %bitcast.32), channel_id=1, source_target_pairs={{2,3},{3,2},{4,5},{5,4},{10,11},{11,10},{12,13},{13,12},{18,19},{1... | collective-permute-start | bytes 4915208 | tf_op jit(solution)/shard_map/swap_own/ppermute | solution.py:209
  40.3 12.1 %collective-permute-start.3 = (bf16[320,2560]{1,0:T(8,128)(2,1)S(1)}, bf16[320,2560]{1,0:T(8,128)(2,1)}, u32[]{:S(2)}, u32[]{:S(2)}) collective-permute-start(bf16[320,2560]{1,0:T(8,128)(2,1)S(1)} %collective-permute-done.refs_1_), channel_id=1, source_target_pairs={{2,3},{3,2},{4,5},{5,4},{10,11},{11,10},{12,13},{13,12},{18,19},{1... | collective-permute-start | bytes 4915208 | tf_op jit(solution)/shard_map/swap_rows/ppermute | solution.py:209
  42.1 10.2 %collective-permute-start.4 = (bf16[320,2560]{1,0:T(8,128)(2,1)S(1)}, bf16[320,2560]{1,0:T(8,128)(2,1)}, u32[]{:S(2)}, u32[]{:S(2)}) collective-permute-start(bf16[320,2560]{1,0:T(8,128)(2,1)S(1)} %collective-permute-done.2.refs_4_), channel_id=1, source_target_pairs={{2,3},{3,2},{4,5},{5,4},{10,11},{11,10},{12,13},{13,12},{18,19},{1... | collective-permute-start | bytes 4915208 | tf_op jit(solution)/shard_map/swap_rows/ppermute | solution.py:209
  45.1 41.5 %collective-permute-start.5 = (bf16[320,2560]{1,0:T(8,128)(2,1)}, bf16[320,2560]{1,0:T(8,128)(2,1)}, u32[]{:S(2)}, u32[]{:S(2)}) collective-permute-start(bf16[320,2560]{1,0:T(8,128)(2,1)} %bitcast.33), channel_id=1, source_target_pairs={{0,4},{1,5},{6,2},{7,3},{8,12},{9,13},{14,10},{15,11},{16,20},{17,... | collective-permute-start | bytes 4915208 | tf_op jit(solution)/shard_map/rows_far/ppermute | solution.py:209
  55.2 33.2 %copy-start.1 = (bf16[1,320,2560]{2,1,0:T(8,128)(2,1)S(1)}, bf16[1,320,2560]{2,1,0:T(8,128)(2,1)}, u32[]{:S(2)}) copy-start(bf16[1,320,2560]{2,1,0:T(8,128)(2,1)} %param.1) | copy-start | bytes 4915204
  86.6 1.8 collective-permute-start.6
  94.6 62.1 %collective-permute-start.13 = (bf16[320,1280]{1,0:T(8,128)(2,1)S(1)}, bf16[320,1280]{1,0:T(8,128)(2,1)S(1)}, u32[]{:S(2)}, u32[]{:S(2)}) collective-permute-start(bf16[320,1280]{1,0:T(8,128)(2,1)S(1)} %get-tuple-element.38), channel_id=1, source_target_pairs={{2,0},{3,1},{4,6},{5,7},{10,8},{11,9},{12,14},{13,15},{18,16},{19,... | collective-permute-start | bytes 2457608 | tf_op jit(solution)/shard_map/rows_out/ppermute | solution.py:209
  95.9 48.8 %collective-permute-start.10 = (bf16[320,640]{1,0:T(8,128)(2,1)S(1)}, bf16[320,640]{1,0:T(8,128)(2,1)S(1)}, u32[]{:S(2)}, u32[]{:S(2)}) collective-permute-start(bf16[320,640]{1,0:T(8,128)(2,1)S(1)} %get-tuple-element.34), channel_id=1, source_target_pairs={{2,0},{3,1},{4,6},{5,7},{10,8},{11,9},{12,14},{13,15},{18,16},{19,... | collective-permute-start | bytes 1228808 | tf_op jit(solution)/shard_map/rows_out/ppermute | solution.py:209
  97.2 55.8 %collective-permute-start.7 = (bf16[320,640]{1,0:T(8,128)(2,1)S(1)}, bf16[320,640]{1,0:T(8,128)(2,1)S(1)}, u32[]{:S(2)}, u32[]{:S(2)}) collective-permute-start(bf16[320,640]{1,0:T(8,128)(2,1)S(1)} %get-tuple-element.30), channel_id=1, source_target_pairs={{2,0},{3,1},{4,6},{5,7},{10,8},{11,9},{12,14},{13,15},{18,16},{19,... | collective-permute-start | bytes 1228808 | tf_op jit(solution)/shard_map/rows_out/ppermute | solution.py:209
  144.7 12.7 %collective-permute-start.11 = (bf16[320,640]{1,0:T(8,128)(2,1)S(1)}, bf16[320,640]{1,0:T(8,128)(2,1)S(1)}, u32[]{:S(2)}, u32[]{:S(2)}) collective-permute-start(bf16[320,640]{1,0:T(8,128)(2,1)S(1)} %broadcast_select_fusion), channel_id=1, source_target_pairs={{0,8},{8,0},{16,24},{24,16},{1,9},{9,1},{17,25},{25,17},{2,10},{10... | collective-permute-start | bytes 1228808 | tf_op jit(solution)/shard_map/along_x/ppermute | solution.py:209
  146.3 11.6 %collective-permute-start.12 = (bf16[320,640]{1,0:T(8,128)(2,1)S(1)}, bf16[320,640]{1,0:T(8,128)(2,1)S(1)}, u32[]{:S(2)}, u32[]{:S(2)}) collective-permute-start(bf16[320,640]{1,0:T(8,128)(2,1)S(1)} %broadcast_select_fusion), channel_id=1, source_target_pairs={{0,16},{8,24},{16,0},{24,8},{1,17},{9,25},{17,1},{25,9},{2,18},{10... | collective-permute-start | bytes 1228808 | tf_op jit(solution)/shard_map/along_y/ppermute | solution.py:209
  153.0 12.4 %collective-permute-start.8 = (bf16[320,640]{1,0:T(8,128)(2,1)S(1)}, bf16[320,640]{1,0:T(8,128)(2,1)S(1)}, u32[]{:S(2)}, u32[]{:S(2)}) collective-permute-start(bf16[320,640]{1,0:T(8,128)(2,1)S(1)} %broadcast_select_fusion.1), channel_id=1, source_target_pairs={{0,8},{8,0},{16,24},{24,16},{1,9},{9,1},{17,25},{25,17},{2,10},{10... | collective-permute-start | bytes 1228808 | tf_op jit(solution)/shard_map/along_x/ppermute | solution.py:209
  154.6 12.4 %collective-permute-start.9 = (bf16[320,640]{1,0:T(8,128)(2,1)S(1)}, bf16[320,640]{1,0:T(8,128)(2,1)S(1)}, u32[]{:S(2)}, u32[]{:S(2)}) collective-permute-start(bf16[320,640]{1,0:T(8,128)(2,1)S(1)} %broadcast_select_fusion.1), channel_id=1, source_target_pairs={{0,16},{8,24},{16,0},{24,8},{1,17},{9,25},{17,1},{25,9},{2,18},{10... | collective-permute-start | bytes 1228808 | tf_op jit(solution)/shard_map/along_y/ppermute | solution.py:209
  156.8 17.5 %collective-permute-start.16 = (bf16[320,640]{1,0:T(8,128)(2,1)S(1)}, bf16[320,640]{1,0:T(8,128)(2,1)S(1)}, u32[]{:S(2)}, u32[]{:S(2)}) collective-permute-start(bf16[320,640]{1,0:T(8,128)(2,1)S(1)} %get-tuple-element.45), channel_id=1, source_target_pairs={{0,8},{8,0},{16,24},{24,16},{1,9},{9,1},{17,25},{25,17},{2,10},{10... | collective-permute-start | bytes 1228808 | tf_op jit(solution)/shard_map/along_x/ppermute | solution.py:209
  157.4 18.4 %collective-permute-start.17 = (bf16[320,640]{1,0:T(8,128)(2,1)S(1)}, bf16[320,640]{1,0:T(8,128)(2,1)S(1)}, u32[]{:S(2)}, u32[]{:S(2)}) collective-permute-start(bf16[320,640]{1,0:T(8,128)(2,1)S(1)} %get-tuple-element.45), channel_id=1, source_target_pairs={{0,16},{8,24},{16,0},{24,8},{1,17},{9,25},{17,1},{25,9},{2,18},{10... | collective-permute-start | bytes 1228808 | tf_op jit(solution)/shard_map/along_y/ppermute | solution.py:209
  157.9 25.1 %collective-permute-start.14 = (bf16[320,640]{1,0:T(8,128)(2,1)S(1)}, bf16[320,640]{1,0:T(8,128)(2,1)S(1)}, u32[]{:S(2)}, u32[]{:S(2)}) collective-permute-start(bf16[320,640]{1,0:T(8,128)(2,1)S(1)} %get-tuple-element.46), channel_id=1, source_target_pairs={{0,8},{8,0},{16,24},{24,16},{1,9},{9,1},{17,25},{25,17},{2,10},{10... | collective-permute-start | bytes 1228808 | tf_op jit(solution)/shard_map/along_x/ppermute | solution.py:209
  165.5 19.1 %collective-permute-start.15 = (bf16[320,640]{1,0:T(8,128)(2,1)S(1)}, bf16[320,640]{1,0:T(8,128)(2,1)S(1)}, u32[]{:S(2)}, u32[]{:S(2)}) collective-permute-start(bf16[320,640]{1,0:T(8,128)(2,1)S(1)} %get-tuple-element.46), channel_id=1, source_target_pairs={{0,16},{8,24},{16,0},{24,8},{1,17},{9,25},{17,1},{25,9},{2,18},{10... | collective-permute-start | bytes 1228808 | tf_op jit(solution)/shard_map/along_y/ppermute | solution.py:209
  167.2 24.6 %collective-permute-start.19 = (bf16[320,640]{1,0:T(8,128)(2,1)S(1)}, bf16[320,640]{1,0:T(8,128)(2,1)S(1)}, u32[]{:S(2)}, u32[]{:S(2)}) collective-permute-start(bf16[320,640]{1,0:T(8,128)(2,1)S(1)} %collective-permute-done.12), channel_id=1, source_target_pairs={{0,8},{8,0},{16,24},{24,16},{1,9},{9,1},{17,25},{25,17},{2,10},{10... | collective-permute-start | bytes 1228808 | tf_op jit(solution)/shard_map/across_x/ppermute | solution.py:209
  174.2 19.1 %collective-permute-start.18 = (bf16[320,640]{1,0:T(8,128)(2,1)S(1)}, bf16[320,640]{1,0:T(8,128)(2,1)S(1)}, u32[]{:S(2)}, u32[]{:S(2)}) collective-permute-start(bf16[320,640]{1,0:T(8,128)(2,1)S(1)} %collective-permute-done.8), channel_id=1, source_target_pairs={{0,16},{8,24},{16,0},{24,8},{1,17},{9,25},{17,1},{25,9},{2,18},{10... | collective-permute-start | bytes 1228808 | tf_op jit(solution)/shard_map/across_y/ppermute | solution.py:209
  184.5 15.8 %collective-permute-start.20 = (bf16[320,640]{1,0:T(8,128)(2,1)S(1)}, bf16[320,640]{1,0:T(8,128)(2,1)S(1)}, u32[]{:S(2)}, u32[]{:S(2)}) collective-permute-start(bf16[320,640]{1,0:T(8,128)(2,1)S(1)} %collective-permute-done.14), channel_id=1, source_target_pairs={{0,16},{8,24},{16,0},{24,8},{1,17},{9,25},{17,1},{25,9},{2,18},{10... | collective-permute-start | bytes 1228808 | tf_op jit(solution)/shard_map/across_y/ppermute | solution.py:209
  186.2 13.0 %collective-permute-start.21 = (bf16[320,640]{1,0:T(8,128)(2,1)S(1)}, bf16[320,640]{1,0:T(8,128)(2,1)S(1)}, u32[]{:S(2)}, u32[]{:S(2)}) collective-permute-start(bf16[320,640]{1,0:T(8,128)(2,1)S(1)} %collective-permute-done.17), channel_id=1, source_target_pairs={{0,8},{8,0},{16,24},{24,16},{1,9},{9,1},{17,25},{25,17},{2,10},{10... | collective-permute-start | bytes 1228808 | tf_op jit(solution)/shard_map/across_x/ppermute | solution.py:209
  186.9 13.4 %copy-start.9 = (bf16[4,320,2560]{2,1,0:T(8,128)(2,1)}, bf16[4,320,2560]{2,1,0:T(8,128)(2,1)S(1)}, u32[]{:S(2)}) copy-start(bf16[4,320,2560]{2,1,0:T(8,128)(2,1)S(1)} %bitcast_dynamic-update-slice_fusion) | copy-start | bytes 19660804
  (8 other events, 14.3 us)

commit v13 on v10

--- a/solution.py
+++ b/solution.py
@@ -213,14 +213,14 @@
 
     cut = rows // 2
     halves = [own[:cut], own[cut:]]
-    inner_rows = move("middle", own, "shard", middle)
-    outer_rows = [move("rows_in", half, "shard", inwards) for half in halves]
-    own_swapped = swap("own", own)
-    outer_rows[0], own_swapped = tie((outer_rows[0], own_swapped))
+    first_rows = move("rows_in", halves[0], "shard", inwards)
+    second_half, first_rows = tie((halves[1], first_rows))
+    outer_rows = [first_rows, move("rows_in", second_half, "shard", inwards)]
+    inner_rows = [move("middle", half, "shard", middle) for half in halves]
     far_rows = move("rows_far", own, "shard", across_middle)
 
-    early = outer_rows + halves + [own_swapped, inner_rows]
-    early += [swap("rows", block) for block in outer_rows + [inner_rows]]
+    early = outer_rows + [own, swap("own", own)] + inner_rows
+    early += [swap("rows", half) for half in outer_rows + inner_rows]
     gram, cubic = early_products(inner, rows, early)
     far_rows, gram, cubic = tie((far_rows, gram, cubic))
     late = [far_rows, swap("far", far_rows)]

time: 186 us -> 184 us (0.989)
  starting transfers between devices: 61.8 us -> 34.9 us
  waiting for transfers between devices: 114 us -> 136 us
  local copies, waits for them, and re-layouts: 7.28 us -> 10.3 us
    ppermute x17 -> x19, starting transfers between devices: 61.8 us -> 34.9 us  [move(): return lax.ppermute(block, axis, pairs)]
    ppermute x17 -> x19, waiting for transfers between devices: 114 us -> 136 us  [move(): return lax.ppermute(block, axis, pairs)]
    unnamed x6 -> x16, local copies, waits for them, and re-layouts: 2.6 us -> 5.5 us
  transfers between devices with their start and end apart: 17 -> 19, of which waited for: 7 -> 9; matrix products, arithmetic and copies ran while one was open for 3% -> 2% of each run, Pallas kernels for 0% -> 0%
where the time goes in v13:
time: 184 us
  waiting for transfers between devices  136 us (74%)
  starting transfers between devices  34.9 us (19%)
  local copies, waits for them, and re-layouts  10.3 us (6%)
    ppermute x19, waiting for transfers between devices, move(): return lax.ppermute(block, axis, pairs)  136 us
    ppermute x19, starting transfers between devices, move(): return lax.ppermute(block, axis, pairs)  34.9 us
    unnamed x16, local copies, waits for them, and re-layouts  5.5 us
  transfers between devices with their start and end apart: 19, of which 9 were waited for; matrix products, arithmetic and copies ran while one was open for 2% of the time, Pallas kernels for 0%

profile of v13, /device:TPU:0, one launch (start us, length us, event | category | flops | bytes accessed | tf_op | source)
XLA Modules:
  0.0 183.7 jit_solution(7421723882777264075)
XLA Ops:
  0.0 1.6 slice_bitcast_fusion
  1.6 5.0 %collective-permute-start = (bf16[160,2560]{1,0:T(8,128)(2,1)S(1)}, bf16[160,2560]{1,0:T(8,128)(2,1)S(1)}, u32[]{:S(2)}, u32[]{:S(2)}) collective-permute-start(bf16[160,2560]{1,0:T(8,128)(2,1)S(1)} %get-tuple-element.39), channel_id=1, source_target_pairs={{0,2},{1,3},{6,4},{7,5},{8,10},{9,11},{14,12},{15,13},{16,18},{17,... | collective-permute-start | bytes 2457608 | tf_op jit(solution)/shard_map/rows_in/ppermute | solution.py:209
  6.6 1.6 collective-permute-start.3
  8.2 1.5 collective-permute-start.4
  10.5 13.6 %collective-permute-done.refs_1_ = bf16[160,2560]{1,0:T(8,128)(2,1)S(1)} collective-permute-done((bf16[160,2560]{1,0:T(8,128)(2,1)S(1)}, bf16[160,2560]{1,0:T(8,128)(2,1)S(1)}, u32[]{:S(2)}, u32[]{:S(2)}) %collective-permute-start) | collective-permute-done | bytes 819232 | tf_op jit(solution)/shard_map/rows_in/ppermute | solution.py:209
  24.0 5.3 %collective-permute-start.1 = (bf16[160,2560]{1,0:T(8,128)(2,1)S(1)}, bf16[160,2560]{1,0:T(8,128)(2,1)}, u32[]{:S(2)}, u32[]{:S(2)}) collective-permute-start(bf16[160,2560]{1,0:T(8,128)(2,1)S(1)} %get-tuple-element.23), channel_id=1, source_target_pairs={{0,2},{1,3},{6,4},{7,5},{8,10},{9,11},{14,12},{15,13},{16,18},{17,... | collective-permute-start | bytes 2457608 | tf_op jit(solution)/shard_map/rows_in/ppermute | solution.py:209
  30.9 3.8 %collective-permute-start.9 = (bf16[320,2560]{1,0:T(8,128)(2,1)}, bf16[320,2560]{1,0:T(8,128)(2,1)}, u32[]{:S(2)}, u32[]{:S(2)}) collective-permute-start(bf16[320,2560]{1,0:T(8,128)(2,1)} %bitcast.23), channel_id=1, source_target_pairs={{0,4},{1,5},{6,2},{7,3},{8,12},{9,13},{14,10},{15,11},{16,20},{17,... | collective-permute-start | bytes 4915208 | tf_op jit(solution)/shard_map/rows_far/ppermute | solution.py:209
  34.8 1.5 collective-permute-start.7
  36.3 10.8 %collective-permute-done.1.refs_2_ = bf16[160,2560]{1,0:T(8,128)(2,1)} collective-permute-done((bf16[160,2560]{1,0:T(8,128)(2,1)S(1)}, bf16[160,2560]{1,0:T(8,128)(2,1)}, u32[]{:S(2)}, u32[]{:S(2)}) %collective-permute-start.1) | collective-permute-done | bytes 819232 | tf_op jit(solution)/shard_map/rows_in/ppermute | solution.py:209
  47.1 1.6 collective-permute-start.8
  49.6 1.5 collective-permute-start.6
  51.2 1.4 copy-done
  55.0 25.4 %collective-permute-done.9.refs_11_ = bf16[320,2560]{1,0:T(8,128)(2,1)} collective-permute-done((bf16[320,2560]{1,0:T(8,128)(2,1)}, bf16[320,2560]{1,0:T(8,128)(2,1)}, u32[]{:S(2)}, u32[]{:S(2)}) %collective-permute-start.9) | collective-permute-done | bytes 1638432 | tf_op jit(solution)/shard_map/rows_far/ppermute | solution.py:209
  81.5 1.3 collective-permute-start.14
  82.8 1.3 collective-permute-start.11
  84.5 39.9 %collective-permute-done.14 = bf16[320,1280]{1,0:T(8,128)(2,1)S(1)} collective-permute-done((bf16[320,1280]{1,0:T(8,128)(2,1)S(1)}, bf16[320,1280]{1,0:T(8,128)(2,1)S(1)}, u32[]{:S(2)}, u32[]{:S(2)}) %collective-permute-start.14) | collective-permute-done | bytes 819232 | tf_op jit(solution)/shard_map/rows_out/ppermute | solution.py:209
  124.4 1.6 collective-permute-start.15
  126.0 1.5 collective-permute-start.16
  127.5 13.9 %collective-permute-done.11 = bf16[320,1280]{1,0:T(8,128)(2,1)S(1)} collective-permute-done((bf16[320,1280]{1,0:T(8,128)(2,1)S(1)}, bf16[320,1280]{1,0:T(8,128)(2,1)S(1)}, u32[]{:S(2)}, u32[]{:S(2)}) %collective-permute-start.11) | collective-permute-done | bytes 819232 | tf_op jit(solution)/shard_map/rows_out/ppermute | solution.py:209
  141.5 1.6 collective-permute-start.12
  143.1 1.5 collective-permute-start.13
  145.2 16.3 %collective-permute-done.12 = bf16[320,1280]{1,0:T(8,128)(2,1)} collective-permute-done((bf16[320,1280]{1,0:T(8,128)(2,1)S(1)}, bf16[320,1280]{1,0:T(8,128)(2,1)}, u32[]{:S(2)}, u32[]{:S(2)}) %collective-permute-start.12) | collective-permute-done | bytes 819232 | tf_op jit(solution)/shard_map/along_x/ppermute | solution.py:209
  162.7 1.5 collective-permute-start.17
  167.4 14.1 %collective-permute-done.17 = bf16[320,1280]{1,0:T(8,128)(2,1)S(1)} collective-permute-done((bf16[320,1280]{1,0:T(8,128)(2,1)}, bf16[320,1280]{1,0:T(8,128)(2,1)S(1)}, u32[]{:S(2)}, u32[]{:S(2)}) %collective-permute-start.17) | collective-permute-done | bytes 819232 | tf_op jit(solution)/shard_map/across_y/ppermute | solution.py:209
  (44 shorter events, 14.5 us)
Async XLA Ops:
  0.0 81.1 %copy-start.1 = (bf16[1,320,2560]{2,1,0:T(8,128)(2,1)S(1)}, bf16[1,320,2560]{2,1,0:T(8,128)(2,1)}, u32[]{:S(2)}) copy-start(bf16[1,320,2560]{2,1,0:T(8,128)(2,1)} %param.1) | copy-start | bytes 4915204
  1.6 22.4 %collective-permute-start = (bf16[160,2560]{1,0:T(8,128)(2,1)S(1)}, bf16[160,2560]{1,0:T(8,128)(2,1)S(1)}, u32[]{:S(2)}, u32[]{:S(2)}) collective-permute-start(bf16[160,2560]{1,0:T(8,128)(2,1)S(1)} %get-tuple-element.39), channel_id=1, source_target_pairs={{0,2},{1,3},{6,4},{7,5},{8,10},{9,11},{14,12},{15,13},{16,18},{17,... | collective-permute-start | bytes 2457608 | tf_op jit(solution)/shard_map/rows_in/ppermute | solution.py:209
  6.6 24.3 %collective-permute-start.3 = (bf16[160,2560]{1,0:T(8,128)(2,1)S(1)}, bf16[160,2560]{1,0:T(8,128)(2,1)}, u32[]{:S(2)}, u32[]{:S(2)}) collective-permute-start(bf16[160,2560]{1,0:T(8,128)(2,1)S(1)} %get-tuple-element.39), channel_id=1, source_target_pairs={{2,4},{3,5},{4,2},{5,3},{10,12},{11,13},{12,10},{13,11},{18,20},{1... | collective-permute-start | bytes 2457608 | tf_op jit(solution)/shard_map/middle/ppermute | solution.py:209
  8.2 26.6 %collective-permute-start.4 = (bf16[160,2560]{1,0:T(8,128)(2,1)S(1)}, bf16[160,2560]{1,0:T(8,128)(2,1)}, u32[]{:S(2)}, u32[]{:S(2)}) collective-permute-start(bf16[160,2560]{1,0:T(8,128)(2,1)S(1)} %get-tuple-element.23), channel_id=1, source_target_pairs={{2,4},{3,5},{4,2},{5,3},{10,12},{11,13},{12,10},{13,11},{18,20},{1... | collective-permute-start | bytes 2457608 | tf_op jit(solution)/shard_map/middle/ppermute | solution.py:209
  9.7 41.4 %collective-permute-start.2 = (bf16[320,2560]{1,0:T(8,128)(2,1)}, bf16[320,2560]{1,0:T(8,128)(2,1)S(1)}, u32[]{:S(2)}, u32[]{:S(2)}) collective-permute-start(bf16[320,2560]{1,0:T(8,128)(2,1)} %bitcast.22), channel_id=1, source_target_pairs={{2,3},{3,2},{4,5},{5,4},{10,11},{11,10},{12,13},{13,12},{18,19},{1... | collective-permute-start | bytes 4915208 | tf_op jit(solution)/shard_map/swap_own/ppermute | solution.py:209
  24.0 23.1 %collective-permute-start.1 = (bf16[160,2560]{1,0:T(8,128)(2,1)S(1)}, bf16[160,2560]{1,0:T(8,128)(2,1)}, u32[]{:S(2)}, u32[]{:S(2)}) collective-permute-start(bf16[160,2560]{1,0:T(8,128)(2,1)S(1)} %get-tuple-element.23), channel_id=1, source_target_pairs={{0,2},{1,3},{6,4},{7,5},{8,10},{9,11},{14,12},{15,13},{16,18},{17,... | collective-permute-start | bytes 2457608 | tf_op jit(solution)/shard_map/rows_in/ppermute | solution.py:209
  29.3 19.4 %collective-permute-start.5 = (bf16[160,2560]{1,0:T(8,128)(2,1)S(1)}, bf16[160,2560]{1,0:T(8,128)(2,1)S(1)}, u32[]{:S(2)}, u32[]{:S(2)}) collective-permute-start(bf16[160,2560]{1,0:T(8,128)(2,1)S(1)} %collective-permute-done.refs_1_), channel_id=1, source_target_pairs={{2,3},{3,2},{4,5},{5,4},{10,11},{11,10},{12,13},{13,12},{18,19},{1... | collective-permute-start | bytes 2457608 | tf_op jit(solution)/shard_map/swap_rows/ppermute | solution.py:209
  30.9 49.4 %collective-permute-start.9 = (bf16[320,2560]{1,0:T(8,128)(2,1)}, bf16[320,2560]{1,0:T(8,128)(2,1)}, u32[]{:S(2)}, u32[]{:S(2)}) collective-permute-start(bf16[320,2560]{1,0:T(8,128)(2,1)} %bitcast.23), channel_id=1, source_target_pairs={{0,4},{1,5},{6,2},{7,3},{8,12},{9,13},{14,10},{15,11},{16,20},{17,... | collective-permute-start | bytes 4915208 | tf_op jit(solution)/shard_map/rows_far/ppermute | solution.py:209
  34.8 16.4 %collective-permute-start.7 = (bf16[160,2560]{1,0:T(8,128)(2,1)}, bf16[160,2560]{1,0:T(8,128)(2,1)}, u32[]{:S(2)}, u32[]{:S(2)}) collective-permute-start(bf16[160,2560]{1,0:T(8,128)(2,1)} %collective-permute-done.3.refs_5_), channel_id=1, source_target_pairs={{2,3},{3,2},{4,5},{5,4},{10,11},{11,10},{12,13},{13,12},{18,19},{1... | collective-permute-start | bytes 2457608 | tf_op jit(solution)/shard_map/swap_rows/ppermute | solution.py:209
  47.1 4.0 %collective-permute-start.8 = (bf16[160,2560]{1,0:T(8,128)(2,1)}, bf16[160,2560]{1,0:T(8,128)(2,1)}, u32[]{:S(2)}, u32[]{:S(2)}) collective-permute-start(bf16[160,2560]{1,0:T(8,128)(2,1)} %collective-permute-done.4.refs_6_), channel_id=1, source_target_pairs={{2,3},{3,2},{4,5},{5,4},{10,11},{11,10},{12,13},{13,12},{18,19},{1... | collective-permute-start | bytes 2457608 | tf_op jit(solution)/shard_map/swap_rows/ppermute | solution.py:209
  49.6 1.6 collective-permute-start.6
  51.2 1.4 copy-start
  52.6 1.1 copy-start.3
  54.9 26.2 %copy-start.4 = (bf16[160,2560]{1,0:T(8,128)(2,1)S(1)}, bf16[160,2560]{1,0:T(8,128)(2,1)}, u32[]{:S(2)}) copy-start(bf16[160,2560]{1,0:T(8,128)(2,1)} %copy-done.2) | copy-start | bytes 2457604
  80.4 0.8 collective-permute-start.10
  81.5 42.8 %collective-permute-start.14 = (bf16[320,1280]{1,0:T(8,128)(2,1)S(1)}, bf16[320,1280]{1,0:T(8,128)(2,1)S(1)}, u32[]{:S(2)}, u32[]{:S(2)}) collective-permute-start(bf16[320,1280]{1,0:T(8,128)(2,1)S(1)} %get-tuple-element.33), channel_id=1, source_target_pairs={{2,0},{3,1},{4,6},{5,7},{10,8},{11,9},{12,14},{13,15},{18,16},{19,... | collective-permute-start | bytes 2457608 | tf_op jit(solution)/shard_map/rows_out/ppermute | solution.py:209
  82.8 58.6 %collective-permute-start.11 = (bf16[320,1280]{1,0:T(8,128)(2,1)S(1)}, bf16[320,1280]{1,0:T(8,128)(2,1)S(1)}, u32[]{:S(2)}, u32[]{:S(2)}) collective-permute-start(bf16[320,1280]{1,0:T(8,128)(2,1)S(1)} %get-tuple-element.29), channel_id=1, source_target_pairs={{2,0},{3,1},{4,6},{5,7},{10,8},{11,9},{12,14},{13,15},{18,16},{19,... | collective-permute-start | bytes 2457608 | tf_op jit(solution)/shard_map/rows_out/ppermute | solution.py:209
  124.4 20.7 %collective-permute-start.15 = (bf16[320,1280]{1,0:T(8,128)(2,1)S(1)}, bf16[320,1280]{1,0:T(8,128)(2,1)S(1)}, u32[]{:S(2)}, u32[]{:S(2)}) collective-permute-start(bf16[320,1280]{1,0:T(8,128)(2,1)S(1)} %broadcast_select_fusion), channel_id=1, source_target_pairs={{0,8},{8,0},{16,24},{24,16},{1,9},{9,1},{17,25},{25,17},{2,10},{10... | collective-permute-start | bytes 2457608 | tf_op jit(solution)/shard_map/along_x/ppermute | solution.py:209
  126.0 19.2 %collective-permute-start.16 = (bf16[320,1280]{1,0:T(8,128)(2,1)S(1)}, bf16[320,1280]{1,0:T(8,128)(2,1)S(1)}, u32[]{:S(2)}, u32[]{:S(2)}) collective-permute-start(bf16[320,1280]{1,0:T(8,128)(2,1)S(1)} %broadcast_select_fusion), channel_id=1, source_target_pairs={{0,16},{8,24},{16,0},{24,8},{1,17},{9,25},{17,1},{25,9},{2,18},{10... | collective-permute-start | bytes 2457608 | tf_op jit(solution)/shard_map/along_y/ppermute | solution.py:209
  141.5 20.0 %collective-permute-start.12 = (bf16[320,1280]{1,0:T(8,128)(2,1)S(1)}, bf16[320,1280]{1,0:T(8,128)(2,1)}, u32[]{:S(2)}, u32[]{:S(2)}) collective-permute-start(bf16[320,1280]{1,0:T(8,128)(2,1)S(1)} %broadcast_select_fusion.1), channel_id=1, source_target_pairs={{0,8},{8,0},{16,24},{24,16},{1,9},{9,1},{17,25},{25,17},{2,10},{10... | collective-permute-start | bytes 2457608 | tf_op jit(solution)/shard_map/along_x/ppermute | solution.py:209
  143.1 19.6 %collective-permute-start.13 = (bf16[320,1280]{1,0:T(8,128)(2,1)S(1)}, bf16[320,1280]{1,0:T(8,128)(2,1)}, u32[]{:S(2)}, u32[]{:S(2)}) collective-permute-start(bf16[320,1280]{1,0:T(8,128)(2,1)S(1)} %broadcast_select_fusion.1), channel_id=1, source_target_pairs={{0,16},{8,24},{16,0},{24,8},{1,17},{9,25},{17,1},{25,9},{2,18},{10... | collective-permute-start | bytes 2457608 | tf_op jit(solution)/shard_map/along_y/ppermute | solution.py:209
  162.7 18.8 %collective-permute-start.17 = (bf16[320,1280]{1,0:T(8,128)(2,1)}, bf16[320,1280]{1,0:T(8,128)(2,1)S(1)}, u32[]{:S(2)}, u32[]{:S(2)}) collective-permute-start(bf16[320,1280]{1,0:T(8,128)(2,1)} %collective-permute-done.12), channel_id=1, source_target_pairs={{0,16},{8,24},{16,0},{24,8},{1,17},{9,25},{17,1},{25,9},{2,18},{10... | collective-permute-start | bytes 2457608 | tf_op jit(solution)/shard_map/across_y/ppermute | solution.py:209
  164.1 18.3 %collective-permute-start.18 = (bf16[320,1280]{1,0:T(8,128)(2,1)S(1)}, bf16[320,1280]{1,0:T(8,128)(2,1)S(1)}, u32[]{:S(2)}, u32[]{:S(2)}) collective-permute-start(bf16[320,1280]{1,0:T(8,128)(2,1)S(1)} %collective-permute-done.16), channel_id=1, source_target_pairs={{0,8},{8,0},{16,24},{24,16},{1,9},{9,1},{17,25},{25,17},{2,10},{10... | collective-permute-start | bytes 2457608 | tf_op jit(solution)/shard_map/across_x/ppermute | solution.py:209
  167.4 15.0 %copy-start.7 = (bf16[4,320,2560]{2,1,0:T(8,128)(2,1)}, bf16[4,320,2560]{2,1,0:T(8,128)(2,1)S(1)}, u32[]{:S(2)}) copy-start(bf16[4,320,2560]{2,1,0:T(8,128)(2,1)S(1)} %bitcast_dynamic-update-slice_fusion) | copy-start | bytes 19660804
  (3 other events, 2.9 us)

commit v14 on v13

--- a/solution.py
+++ b/solution.py
@@ -11,7 +11,7 @@
 coef_b = -4.775
 coef_c = 2.0315
 
-TILE = 1024
+TILE = 512
 VMEM_LIMIT = 30 * 1024 * 1024
 
 
@@ -118,7 +118,9 @@
 
         own = [k for k in range(early_count) if first <= begin[k] < first + rows]
         others = [k for k in range(early_count) if k not in own]
-        for k in own + list(range(early_count, count)):
+        for k in own + [early_count]:
+            fetch_block(k)
+        for k in range(early_count + 1, count):
             fetch_block(k)
         at = 0
         for k, gram_in in enumerate(grams_in):
@@ -129,11 +131,14 @@
         for k in others:
             fetch_block(k)
 
-        for k in own + list(range(early_count, count)):
+        for k in own:
             copies[k].wait()
+        for k in range(early_count, count):
+            copies[k].wait()
+            at = pl.ds(begin[k], blocks[k].shape[0])
+            gram[:, at] = dot_t(whole[mine, :], whole[at, :]).astype(jnp.bfloat16)
         for k in range(gram_count):
             copies["gram%d" % k].wait()
-        gram[:, late] = dot_t(whole[mine, :], whole[late, :]).astype(jnp.bfloat16)
         copies["cubic"].wait()
         for at in tiles(0, columns):
             add = dot(gram[:, late], whole[late, at])

time: 184 us -> 184 us (level)
  no operation moved by 1% of the time
where the time goes in v14:
time: 184 us; the launch traced here: 183 us
  waiting for transfers between devices  136 us (74%)
  starting transfers between devices  34.9 us (19%)
  local copies, waits for them, and re-layouts  10.3 us (6%)
    ppermute x19, waiting for transfers between devices, move(): return lax.ppermute(block, axis, pairs)  136 us
    ppermute x19, starting transfers between devices, move(): return lax.ppermute(block, axis, pairs)  34.9 us
    unnamed x16, local copies, waits for them, and re-layouts  5.5 us
  transfers between devices with their start and end apart: 19, of which 9 were waited for; matrix products, arithmetic and copies ran while one was open for 2% of the time, Pallas kernels for 0%

profile of v14, /device:TPU:0, one launch (start us, length us, event | category | flops | bytes accessed | tf_op | source)
XLA Modules:
  0.0 183.4 jit_solution(8705087218058488937)
XLA Ops:
  0.0 1.6 slice_bitcast_fusion
  1.6 5.0 %collective-permute-start = (bf16[160,2560]{1,0:T(8,128)(2,1)S(1)}, bf16[160,2560]{1,0:T(8,128)(2,1)S(1)}, u32[]{:S(2)}, u32[]{:S(2)}) collective-permute-start(bf16[160,2560]{1,0:T(8,128)(2,1)S(1)} %get-tuple-element.39), channel_id=1, source_target_pairs={{0,2},{1,3},{6,4},{7,5},{8,10},{9,11},{14,12},{15,13},{16,18},{17,... | collective-permute-start | bytes 2457608 | tf_op jit(solution)/shard_map/rows_in/ppermute | solution.py:214
  6.6 1.6 collective-permute-start.3
  8.2 1.5 collective-permute-start.4
  10.5 13.6 %collective-permute-done.refs_1_ = bf16[160,2560]{1,0:T(8,128)(2,1)S(1)} collective-permute-done((bf16[160,2560]{1,0:T(8,128)(2,1)S(1)}, bf16[160,2560]{1,0:T(8,128)(2,1)S(1)}, u32[]{:S(2)}, u32[]{:S(2)}) %collective-permute-start) | collective-permute-done | bytes 819232 | tf_op jit(solution)/shard_map/rows_in/ppermute | solution.py:214
  24.0 5.3 %collective-permute-start.1 = (bf16[160,2560]{1,0:T(8,128)(2,1)S(1)}, bf16[160,2560]{1,0:T(8,128)(2,1)}, u32[]{:S(2)}, u32[]{:S(2)}) collective-permute-start(bf16[160,2560]{1,0:T(8,128)(2,1)S(1)} %get-tuple-element.23), channel_id=1, source_target_pairs={{0,2},{1,3},{6,4},{7,5},{8,10},{9,11},{14,12},{15,13},{16,18},{17,... | collective-permute-start | bytes 2457608 | tf_op jit(solution)/shard_map/rows_in/ppermute | solution.py:214
  30.9 3.8 %collective-permute-start.9 = (bf16[320,2560]{1,0:T(8,128)(2,1)}, bf16[320,2560]{1,0:T(8,128)(2,1)}, u32[]{:S(2)}, u32[]{:S(2)}) collective-permute-start(bf16[320,2560]{1,0:T(8,128)(2,1)} %bitcast.23), channel_id=1, source_target_pairs={{0,4},{1,5},{6,2},{7,3},{8,12},{9,13},{14,10},{15,11},{16,20},{17,... | collective-permute-start | bytes 4915208 | tf_op jit(solution)/shard_map/rows_far/ppermute | solution.py:214
  34.8 1.5 collective-permute-start.7
  36.3 10.8 %collective-permute-done.1.refs_2_ = bf16[160,2560]{1,0:T(8,128)(2,1)} collective-permute-done((bf16[160,2560]{1,0:T(8,128)(2,1)S(1)}, bf16[160,2560]{1,0:T(8,128)(2,1)}, u32[]{:S(2)}, u32[]{:S(2)}) %collective-permute-start.1) | collective-permute-done | bytes 819232 | tf_op jit(solution)/shard_map/rows_in/ppermute | solution.py:214
  47.1 1.6 collective-permute-start.8
  49.6 1.5 collective-permute-start.6
  51.2 1.4 copy-done
  55.0 25.4 %collective-permute-done.9.refs_11_ = bf16[320,2560]{1,0:T(8,128)(2,1)} collective-permute-done((bf16[320,2560]{1,0:T(8,128)(2,1)}, bf16[320,2560]{1,0:T(8,128)(2,1)}, u32[]{:S(2)}, u32[]{:S(2)}) %collective-permute-start.9) | collective-permute-done | bytes 1638432 | tf_op jit(solution)/shard_map/rows_far/ppermute | solution.py:214
  81.5 1.3 collective-permute-start.14
  82.8 1.3 collective-permute-start.11
  84.5 39.6 %collective-permute-done.14 = bf16[320,1280]{1,0:T(8,128)(2,1)S(1)} collective-permute-done((bf16[320,1280]{1,0:T(8,128)(2,1)S(1)}, bf16[320,1280]{1,0:T(8,128)(2,1)S(1)}, u32[]{:S(2)}, u32[]{:S(2)}) %collective-permute-start.14) | collective-permute-done | bytes 819232 | tf_op jit(solution)/shard_map/rows_out/ppermute | solution.py:214
  124.1 1.6 collective-permute-start.15
  125.7 1.5 collective-permute-start.16
  127.2 13.9 %collective-permute-done.11 = bf16[320,1280]{1,0:T(8,128)(2,1)S(1)} collective-permute-done((bf16[320,1280]{1,0:T(8,128)(2,1)S(1)}, bf16[320,1280]{1,0:T(8,128)(2,1)S(1)}, u32[]{:S(2)}, u32[]{:S(2)}) %collective-permute-start.11) | collective-permute-done | bytes 819232 | tf_op jit(solution)/shard_map/rows_out/ppermute | solution.py:214
  141.2 1.6 collective-permute-start.12
  142.8 1.5 collective-permute-start.13
  144.9 16.3 %collective-permute-done.12 = bf16[320,1280]{1,0:T(8,128)(2,1)} collective-permute-done((bf16[320,1280]{1,0:T(8,128)(2,1)S(1)}, bf16[320,1280]{1,0:T(8,128)(2,1)}, u32[]{:S(2)}, u32[]{:S(2)}) %collective-permute-start.12) | collective-permute-done | bytes 819232 | tf_op jit(solution)/shard_map/along_x/ppermute | solution.py:214
  162.3 1.5 collective-permute-start.17
  167.1 14.1 %collective-permute-done.17 = bf16[320,1280]{1,0:T(8,128)(2,1)S(1)} collective-permute-done((bf16[320,1280]{1,0:T(8,128)(2,1)}, bf16[320,1280]{1,0:T(8,128)(2,1)S(1)}, u32[]{:S(2)}, u32[]{:S(2)}) %collective-permute-start.17) | collective-permute-done | bytes 819232 | tf_op jit(solution)/shard_map/across_y/ppermute | solution.py:214
  (44 shorter events, 14.5 us)
Async XLA Ops:
  0.0 81.1 %copy-start.1 = (bf16[1,320,2560]{2,1,0:T(8,128)(2,1)S(1)}, bf16[1,320,2560]{2,1,0:T(8,128)(2,1)}, u32[]{:S(2)}) copy-start(bf16[1,320,2560]{2,1,0:T(8,128)(2,1)} %param.1) | copy-start | bytes 4915204
  1.6 22.4 %collective-permute-start = (bf16[160,2560]{1,0:T(8,128)(2,1)S(1)}, bf16[160,2560]{1,0:T(8,128)(2,1)S(1)}, u32[]{:S(2)}, u32[]{:S(2)}) collective-permute-start(bf16[160,2560]{1,0:T(8,128)(2,1)S(1)} %get-tuple-element.39), channel_id=1, source_target_pairs={{0,2},{1,3},{6,4},{7,5},{8,10},{9,11},{14,12},{15,13},{16,18},{17,... | collective-permute-start | bytes 2457608 | tf_op jit(solution)/shard_map/rows_in/ppermute | solution.py:214
  6.6 24.3 %collective-permute-start.3 = (bf16[160,2560]{1,0:T(8,128)(2,1)S(1)}, bf16[160,2560]{1,0:T(8,128)(2,1)}, u32[]{:S(2)}, u32[]{:S(2)}) collective-permute-start(bf16[160,2560]{1,0:T(8,128)(2,1)S(1)} %get-tuple-element.39), channel_id=1, source_target_pairs={{2,4},{3,5},{4,2},{5,3},{10,12},{11,13},{12,10},{13,11},{18,20},{1... | collective-permute-start | bytes 2457608 | tf_op jit(solution)/shard_map/middle/ppermute | solution.py:214
  8.2 26.6 %collective-permute-start.4 = (bf16[160,2560]{1,0:T(8,128)(2,1)S(1)}, bf16[160,2560]{1,0:T(8,128)(2,1)}, u32[]{:S(2)}, u32[]{:S(2)}) collective-permute-start(bf16[160,2560]{1,0:T(8,128)(2,1)S(1)} %get-tuple-element.23), channel_id=1, source_target_pairs={{2,4},{3,5},{4,2},{5,3},{10,12},{11,13},{12,10},{13,11},{18,20},{1... | collective-permute-start | bytes 2457608 | tf_op jit(solution)/shard_map/middle/ppermute | solution.py:214
  9.7 41.4 %collective-permute-start.2 = (bf16[320,2560]{1,0:T(8,128)(2,1)}, bf16[320,2560]{1,0:T(8,128)(2,1)S(1)}, u32[]{:S(2)}, u32[]{:S(2)}) collective-permute-start(bf16[320,2560]{1,0:T(8,128)(2,1)} %bitcast.22), channel_id=1, source_target_pairs={{2,3},{3,2},{4,5},{5,4},{10,11},{11,10},{12,13},{13,12},{18,19},{1... | collective-permute-start | bytes 4915208 | tf_op jit(solution)/shard_map/swap_own/ppermute | solution.py:214
  24.0 23.1 %collective-permute-start.1 = (bf16[160,2560]{1,0:T(8,128)(2,1)S(1)}, bf16[160,2560]{1,0:T(8,128)(2,1)}, u32[]{:S(2)}, u32[]{:S(2)}) collective-permute-start(bf16[160,2560]{1,0:T(8,128)(2,1)S(1)} %get-tuple-element.23), channel_id=1, source_target_pairs={{0,2},{1,3},{6,4},{7,5},{8,10},{9,11},{14,12},{15,13},{16,18},{17,... | collective-permute-start | bytes 2457608 | tf_op jit(solution)/shard_map/rows_in/ppermute | solution.py:214
  29.3 19.4 %collective-permute-start.5 = (bf16[160,2560]{1,0:T(8,128)(2,1)S(1)}, bf16[160,2560]{1,0:T(8,128)(2,1)S(1)}, u32[]{:S(2)}, u32[]{:S(2)}) collective-permute-start(bf16[160,2560]{1,0:T(8,128)(2,1)S(1)} %collective-permute-done.refs_1_), channel_id=1, source_target_pairs={{2,3},{3,2},{4,5},{5,4},{10,11},{11,10},{12,13},{13,12},{18,19},{1... | collective-permute-start | bytes 2457608 | tf_op jit(solution)/shard_map/swap_rows/ppermute | solution.py:214
  30.9 49.4 %collective-permute-start.9 = (bf16[320,2560]{1,0:T(8,128)(2,1)}, bf16[320,2560]{1,0:T(8,128)(2,1)}, u32[]{:S(2)}, u32[]{:S(2)}) collective-permute-start(bf16[320,2560]{1,0:T(8,128)(2,1)} %bitcast.23), channel_id=1, source_target_pairs={{0,4},{1,5},{6,2},{7,3},{8,12},{9,13},{14,10},{15,11},{16,20},{17,... | collective-permute-start | bytes 4915208 | tf_op jit(solution)/shard_map/rows_far/ppermute | solution.py:214
  34.8 16.4 %collective-permute-start.7 = (bf16[160,2560]{1,0:T(8,128)(2,1)}, bf16[160,2560]{1,0:T(8,128)(2,1)}, u32[]{:S(2)}, u32[]{:S(2)}) collective-permute-start(bf16[160,2560]{1,0:T(8,128)(2,1)} %collective-permute-done.3.refs_5_), channel_id=1, source_target_pairs={{2,3},{3,2},{4,5},{5,4},{10,11},{11,10},{12,13},{13,12},{18,19},{1... | collective-permute-start | bytes 2457608 | tf_op jit(solution)/shard_map/swap_rows/ppermute | solution.py:214
  47.1 4.0 %collective-permute-start.8 = (bf16[160,2560]{1,0:T(8,128)(2,1)}, bf16[160,2560]{1,0:T(8,128)(2,1)}, u32[]{:S(2)}, u32[]{:S(2)}) collective-permute-start(bf16[160,2560]{1,0:T(8,128)(2,1)} %collective-permute-done.4.refs_6_), channel_id=1, source_target_pairs={{2,3},{3,2},{4,5},{5,4},{10,11},{11,10},{12,13},{13,12},{18,19},{1... | collective-permute-start | bytes 2457608 | tf_op jit(solution)/shard_map/swap_rows/ppermute | solution.py:214
  49.6 1.6 collective-permute-start.6
  51.2 1.4 copy-start
  52.6 1.1 copy-start.3
  54.9 26.2 %copy-start.4 = (bf16[160,2560]{1,0:T(8,128)(2,1)S(1)}, bf16[160,2560]{1,0:T(8,128)(2,1)}, u32[]{:S(2)}) copy-start(bf16[160,2560]{1,0:T(8,128)(2,1)} %copy-done.2) | copy-start | bytes 2457604
  80.4 0.8 collective-permute-start.10
  81.5 42.5 %collective-permute-start.14 = (bf16[320,1280]{1,0:T(8,128)(2,1)S(1)}, bf16[320,1280]{1,0:T(8,128)(2,1)S(1)}, u32[]{:S(2)}, u32[]{:S(2)}) collective-permute-start(bf16[320,1280]{1,0:T(8,128)(2,1)S(1)} %get-tuple-element.33), channel_id=1, source_target_pairs={{2,0},{3,1},{4,6},{5,7},{10,8},{11,9},{12,14},{13,15},{18,16},{19,... | collective-permute-start | bytes 2457608 | tf_op jit(solution)/shard_map/rows_out/ppermute | solution.py:214
  82.8 58.3 %collective-permute-start.11 = (bf16[320,1280]{1,0:T(8,128)(2,1)S(1)}, bf16[320,1280]{1,0:T(8,128)(2,1)S(1)}, u32[]{:S(2)}, u32[]{:S(2)}) collective-permute-start(bf16[320,1280]{1,0:T(8,128)(2,1)S(1)} %get-tuple-element.29), channel_id=1, source_target_pairs={{2,0},{3,1},{4,6},{5,7},{10,8},{11,9},{12,14},{13,15},{18,16},{19,... | collective-permute-start | bytes 2457608 | tf_op jit(solution)/shard_map/rows_out/ppermute | solution.py:214
  124.1 20.7 %collective-permute-start.15 = (bf16[320,1280]{1,0:T(8,128)(2,1)S(1)}, bf16[320,1280]{1,0:T(8,128)(2,1)S(1)}, u32[]{:S(2)}, u32[]{:S(2)}) collective-permute-start(bf16[320,1280]{1,0:T(8,128)(2,1)S(1)} %broadcast_select_fusion), channel_id=1, source_target_pairs={{0,8},{8,0},{16,24},{24,16},{1,9},{9,1},{17,25},{25,17},{2,10},{10... | collective-permute-start | bytes 2457608 | tf_op jit(solution)/shard_map/along_x/ppermute | solution.py:214
  125.7 19.2 %collective-permute-start.16 = (bf16[320,1280]{1,0:T(8,128)(2,1)S(1)}, bf16[320,1280]{1,0:T(8,128)(2,1)S(1)}, u32[]{:S(2)}, u32[]{:S(2)}) collective-permute-start(bf16[320,1280]{1,0:T(8,128)(2,1)S(1)} %broadcast_select_fusion), channel_id=1, source_target_pairs={{0,16},{8,24},{16,0},{24,8},{1,17},{9,25},{17,1},{25,9},{2,18},{10... | collective-permute-start | bytes 2457608 | tf_op jit(solution)/shard_map/along_y/ppermute | solution.py:214
  141.2 19.9 %collective-permute-start.12 = (bf16[320,1280]{1,0:T(8,128)(2,1)S(1)}, bf16[320,1280]{1,0:T(8,128)(2,1)}, u32[]{:S(2)}, u32[]{:S(2)}) collective-permute-start(bf16[320,1280]{1,0:T(8,128)(2,1)S(1)} %broadcast_select_fusion.1), channel_id=1, source_target_pairs={{0,8},{8,0},{16,24},{24,16},{1,9},{9,1},{17,25},{25,17},{2,10},{10... | collective-permute-start | bytes 2457608 | tf_op jit(solution)/shard_map/along_x/ppermute | solution.py:214
  142.8 19.6 %collective-permute-start.13 = (bf16[320,1280]{1,0:T(8,128)(2,1)S(1)}, bf16[320,1280]{1,0:T(8,128)(2,1)}, u32[]{:S(2)}, u32[]{:S(2)}) collective-permute-start(bf16[320,1280]{1,0:T(8,128)(2,1)S(1)} %broadcast_select_fusion.1), channel_id=1, source_target_pairs={{0,16},{8,24},{16,0},{24,8},{1,17},{9,25},{17,1},{25,9},{2,18},{10... | collective-permute-start | bytes 2457608 | tf_op jit(solution)/shard_map/along_y/ppermute | solution.py:214
  162.3 18.8 %collective-permute-start.17 = (bf16[320,1280]{1,0:T(8,128)(2,1)}, bf16[320,1280]{1,0:T(8,128)(2,1)S(1)}, u32[]{:S(2)}, u32[]{:S(2)}) collective-permute-start(bf16[320,1280]{1,0:T(8,128)(2,1)} %collective-permute-done.12), channel_id=1, source_target_pairs={{0,16},{8,24},{16,0},{24,8},{1,17},{9,25},{17,1},{25,9},{2,18},{10... | collective-permute-start | bytes 2457608 | tf_op jit(solution)/shard_map/across_y/ppermute | solution.py:214
  163.9 18.3 %collective-permute-start.18 = (bf16[320,1280]{1,0:T(8,128)(2,1)S(1)}, bf16[320,1280]{1,0:T(8,128)(2,1)S(1)}, u32[]{:S(2)}, u32[]{:S(2)}) collective-permute-start(bf16[320,1280]{1,0:T(8,128)(2,1)S(1)} %collective-permute-done.16), channel_id=1, source_target_pairs={{0,8},{8,0},{16,24},{24,16},{1,9},{9,1},{17,25},{25,17},{2,10},{10... | collective-permute-start | bytes 2457608 | tf_op jit(solution)/shard_map/across_x/ppermute | solution.py:214
  167.1 15.1 %copy-start.7 = (bf16[4,320,2560]{2,1,0:T(8,128)(2,1)}, bf16[4,320,2560]{2,1,0:T(8,128)(2,1)S(1)}, u32[]{:S(2)}) copy-start(bf16[4,320,2560]{2,1,0:T(8,128)(2,1)S(1)} %bitcast_dynamic-update-slice_fusion) | copy-start | bytes 19660804
  (3 other events, 2.9 us)

commit v15 on v10

--- a/solution.py
+++ b/solution.py
@@ -211,16 +211,13 @@
     def swap(name, block):
         return move("swap_" + name, block, "shard", other_core)
 
-    cut = rows // 2
-    halves = [own[:cut], own[cut:]]
     inner_rows = move("middle", own, "shard", middle)
-    outer_rows = [move("rows_in", half, "shard", inwards) for half in halves]
-    own_swapped = swap("own", own)
-    outer_rows[0], own_swapped = tie((outer_rows[0], own_swapped))
+    outer_rows = move("rows_in", own, "shard", inwards)
     far_rows = move("rows_far", own, "shard", across_middle)
 
-    early = outer_rows + halves + [own_swapped, inner_rows]
-    early += [swap("rows", block) for block in outer_rows + [inner_rows]]
+    early = [outer_rows, own, swap("own", own), inner_rows]
+    for block, cut in ((outer_rows, rows // 2), (inner_rows, rows * 13 // 20)):
+        early += [swap("rows", part) for part in (block[:cut], block[cut:])]
     gram, cubic = early_products(inner, rows, early)
     far_rows, gram, cubic = tie((far_rows, gram, cubic))
     late = [far_rows, swap("far", far_rows)]

time: 186 us -> 181 us (0.973)
  starting transfers between devices: 61.8 us -> 30.5 us
  waiting for transfers between devices: 114 us -> 137 us
  local copies, waits for them, and re-layouts: 7.28 us -> 10.5 us
    ppermute x17, starting transfers between devices: 61.8 us -> 30.5 us  [move(): return lax.ppermute(block, axis, pairs)]
    ppermute x17, waiting for transfers between devices: 114 us -> 137 us  [move(): return lax.ppermute(block, axis, pairs)]
    unnamed x6 -> x8, local copies, waits for them, and re-layouts: 2.6 us -> 4.03 us
  transfers between devices with their start and end apart: 17 -> 17, of which waited for: 7 -> 8; matrix products, arithmetic and copies ran while one was open for 3% -> 4% of each run, Pallas kernels for 0% -> 0%
where the time goes in v15:
time: 181 us
  waiting for transfers between devices  137 us (76%)
  starting transfers between devices  30.5 us (17%)
  local copies, waits for them, and re-layouts  10.5 us (6%)
    ppermute x17, waiting for transfers between devices, move(): return lax.ppermute(block, axis, pairs)  137 us
    ppermute x17, starting transfers between devices, move(): return lax.ppermute(block, axis, pairs)  30.5 us
    unnamed x8, local copies, waits for them, and re-layouts  4.03 us
  transfers between devices with their start and end apart: 17, of which 8 were waited for; matrix products, arithmetic and copies ran while one was open for 4% of the time, Pallas kernels for 0%

profile of v15, /device:TPU:0, one launch (start us, length us, event | category | flops | bytes accessed | tf_op | source)
XLA Modules:
  0.0 180.7 jit_solution(2243481411973414841)
XLA Ops:
  0.8 7.8 %collective-permute-start = (bf16[320,2560]{1,0:T(8,128)(2,1)}, bf16[320,2560]{1,0:T(8,128)(2,1)S(1)}, u32[]{:S(2)}, u32[]{:S(2)}) collective-permute-start(bf16[320,2560]{1,0:T(8,128)(2,1)} %bitcast.19), channel_id=1, source_target_pairs={{0,2},{1,3},{6,4},{7,5},{8,10},{9,11},{14,12},{15,13},{16,18},{17,... | collective-permute-start | bytes 4915208 | tf_op jit(solution)/shard_map/rows_in/ppermute | solution.py:209
  9.3 3.4 %collective-permute-start.7 = (bf16[320,2560]{1,0:T(8,128)(2,1)}, bf16[320,2560]{1,0:T(8,128)(2,1)}, u32[]{:S(2)}, u32[]{:S(2)}) collective-permute-start(bf16[320,2560]{1,0:T(8,128)(2,1)} %bitcast.21), channel_id=1, source_target_pairs={{0,4},{1,5},{6,2},{7,3},{8,12},{9,13},{14,10},{15,11},{16,20},{17,... | collective-permute-start | bytes 4915208 | tf_op jit(solution)/shard_map/rows_far/ppermute | solution.py:209
  13.8 1.7 collective-permute-start.5
  15.4 29.5 %collective-permute-done.refs_1_ = bf16[320,2560]{1,0:T(8,128)(2,1)S(1)} collective-permute-done((bf16[320,2560]{1,0:T(8,128)(2,1)}, bf16[320,2560]{1,0:T(8,128)(2,1)S(1)}, u32[]{:S(2)}, u32[]{:S(2)}) %collective-permute-start) | collective-permute-done | bytes 1638432 | tf_op jit(solution)/shard_map/rows_in/ppermute | solution.py:209
  45.0 1.3 fusion.1
  46.3 1.6 collective-permute-start.3
  47.8 1.6 collective-permute-start.4
  51.5 1.5 collective-permute-start.6
  53.0 1.4 copy-done
  54.4 1.4 copy-done.2
  55.9 22.7 %collective-permute-done.7.refs_9_ = bf16[320,2560]{1,0:T(8,128)(2,1)} collective-permute-done((bf16[320,2560]{1,0:T(8,128)(2,1)}, bf16[320,2560]{1,0:T(8,128)(2,1)}, u32[]{:S(2)}, u32[]{:S(2)}) %collective-permute-start.7) | collective-permute-done | bytes 1638432 | tf_op jit(solution)/shard_map/rows_far/ppermute | solution.py:209
  79.7 1.3 collective-permute-start.12
  81.0 1.3 collective-permute-start.9
  82.6 38.6 %collective-permute-done.12 = bf16[320,1280]{1,0:T(8,128)(2,1)S(1)} collective-permute-done((bf16[320,1280]{1,0:T(8,128)(2,1)S(1)}, bf16[320,1280]{1,0:T(8,128)(2,1)S(1)}, u32[]{:S(2)}, u32[]{:S(2)}) %collective-permute-start.12) | collective-permute-done | bytes 819232 | tf_op jit(solution)/shard_map/rows_out/ppermute | solution.py:209
  121.4 1.5 collective-permute-start.13
  122.9 1.5 collective-permute-start.14
  124.4 13.9 %collective-permute-done.9 = bf16[320,1280]{1,0:T(8,128)(2,1)S(1)} collective-permute-done((bf16[320,1280]{1,0:T(8,128)(2,1)S(1)}, bf16[320,1280]{1,0:T(8,128)(2,1)S(1)}, u32[]{:S(2)}, u32[]{:S(2)}) %collective-permute-start.9) | collective-permute-done | bytes 819232 | tf_op jit(solution)/shard_map/rows_out/ppermute | solution.py:209
  138.4 1.6 collective-permute-start.10
  140.0 1.5 collective-permute-start.11
  142.1 16.3 %collective-permute-done.10 = bf16[320,1280]{1,0:T(8,128)(2,1)} collective-permute-done((bf16[320,1280]{1,0:T(8,128)(2,1)S(1)}, bf16[320,1280]{1,0:T(8,128)(2,1)}, u32[]{:S(2)}, u32[]{:S(2)}) %collective-permute-start.10) | collective-permute-done | bytes 819232 | tf_op jit(solution)/shard_map/along_x/ppermute | solution.py:209
  158.4 1.2 collective-permute-done.11
  159.6 1.5 collective-permute-start.15
  164.3 14.1 %collective-permute-done.15 = bf16[320,1280]{1,0:T(8,128)(2,1)S(1)} collective-permute-done((bf16[320,1280]{1,0:T(8,128)(2,1)}, bf16[320,1280]{1,0:T(8,128)(2,1)S(1)}, u32[]{:S(2)}, u32[]{:S(2)}) %collective-permute-start.15) | collective-permute-done | bytes 819232 | tf_op jit(solution)/shard_map/across_y/ppermute | solution.py:209
  179.4 1.3 fusion
  (34 shorter events, 11.0 us)
Async XLA Ops:
  0.0 12.7 %collective-permute-start.2 = (bf16[320,2560]{1,0:T(8,128)(2,1)}, bf16[320,2560]{1,0:T(8,128)(2,1)S(1)}, u32[]{:S(2)}, u32[]{:S(2)}) collective-permute-start(bf16[320,2560]{1,0:T(8,128)(2,1)} %bitcast.18), channel_id=1, source_target_pairs={{2,4},{3,5},{4,2},{5,3},{10,12},{11,13},{12,10},{13,11},{18,20},{1... | collective-permute-start | bytes 4915208 | tf_op jit(solution)/shard_map/middle/ppermute | solution.py:209
  0.8 44.2 %collective-permute-start = (bf16[320,2560]{1,0:T(8,128)(2,1)}, bf16[320,2560]{1,0:T(8,128)(2,1)S(1)}, u32[]{:S(2)}, u32[]{:S(2)}) collective-permute-start(bf16[320,2560]{1,0:T(8,128)(2,1)} %bitcast.19), channel_id=1, source_target_pairs={{0,2},{1,3},{6,4},{7,5},{8,10},{9,11},{14,12},{15,13},{16,18},{17,... | collective-permute-start | bytes 4915208 | tf_op jit(solution)/shard_map/rows_in/ppermute | solution.py:209
  8.5 41.8 %collective-permute-start.1 = (bf16[320,2560]{1,0:T(8,128)(2,1)}, bf16[320,2560]{1,0:T(8,128)(2,1)S(1)}, u32[]{:S(2)}, u32[]{:S(2)}) collective-permute-start(bf16[320,2560]{1,0:T(8,128)(2,1)} %bitcast.20), channel_id=1, source_target_pairs={{2,3},{3,2},{4,5},{5,4},{10,11},{11,10},{12,13},{13,12},{18,19},{1... | collective-permute-start | bytes 4915208 | tf_op jit(solution)/shard_map/swap_own/ppermute | solution.py:209
  9.3 69.3 %collective-permute-start.7 = (bf16[320,2560]{1,0:T(8,128)(2,1)}, bf16[320,2560]{1,0:T(8,128)(2,1)}, u32[]{:S(2)}, u32[]{:S(2)}) collective-permute-start(bf16[320,2560]{1,0:T(8,128)(2,1)} %bitcast.21), channel_id=1, source_target_pairs={{0,4},{1,5},{6,2},{7,3},{8,12},{9,13},{14,10},{15,11},{16,20},{17,... | collective-permute-start | bytes 4915208 | tf_op jit(solution)/shard_map/rows_far/ppermute | solution.py:209
  13.8 39.2 %collective-permute-start.5 = (bf16[208,2560]{1,0:T(8,128)(2,1)}, bf16[208,2560]{1,0:T(8,128)(2,1)}, u32[]{:S(2)}, u32[]{:S(2)}) collective-permute-start(bf16[208,2560]{1,0:T(8,128)(2,1)} %slice.18), channel_id=1, source_target_pairs={{2,3},{3,2},{4,5},{5,4},{10,11},{11,10},{12,13},{13,12},{18,19},{1... | collective-permute-start | bytes 3194888 | tf_op jit(solution)/shard_map/swap_rows/ppermute | solution.py:209
  46.3 6.7 %collective-permute-start.3 = (bf16[160,2560]{1,0:T(8,128)(2,1)}, bf16[160,2560]{1,0:T(8,128)(2,1)}, u32[]{:S(2)}, u32[]{:S(2)}) collective-permute-start(bf16[160,2560]{1,0:T(8,128)(2,1)} %get-tuple-element.36), channel_id=1, source_target_pairs={{2,3},{3,2},{4,5},{5,4},{10,11},{11,10},{12,13},{13,12},{18,19},{1... | collective-permute-start | bytes 2457608 | tf_op jit(solution)/shard_map/swap_rows/ppermute | solution.py:209
  47.8 5.1 %collective-permute-start.4 = (bf16[160,2560]{1,0:T(8,128)(2,1)}, bf16[160,2560]{1,0:T(8,128)(2,1)}, u32[]{:S(2)}, u32[]{:S(2)}) collective-permute-start(bf16[160,2560]{1,0:T(8,128)(2,1)} %get-tuple-element.35), channel_id=1, source_target_pairs={{2,3},{3,2},{4,5},{5,4},{10,11},{11,10},{12,13},{13,12},{18,19},{1... | collective-permute-start | bytes 2457608 | tf_op jit(solution)/shard_map/swap_rows/ppermute | solution.py:209
  50.3 1.2 copy-start.1
  51.5 1.5 collective-permute-start.6
  53.0 1.4 copy-start
  54.4 1.4 copy-start.2
  78.6 0.8 collective-permute-start.8
  79.7 41.6 %collective-permute-start.12 = (bf16[320,1280]{1,0:T(8,128)(2,1)S(1)}, bf16[320,1280]{1,0:T(8,128)(2,1)S(1)}, u32[]{:S(2)}, u32[]{:S(2)}) collective-permute-start(bf16[320,1280]{1,0:T(8,128)(2,1)S(1)} %get-tuple-element.29), channel_id=1, source_target_pairs={{2,0},{3,1},{4,6},{5,7},{10,8},{11,9},{12,14},{13,15},{18,16},{19,... | collective-permute-start | bytes 2457608 | tf_op jit(solution)/shard_map/rows_out/ppermute | solution.py:209
  81.0 57.3 %collective-permute-start.9 = (bf16[320,1280]{1,0:T(8,128)(2,1)S(1)}, bf16[320,1280]{1,0:T(8,128)(2,1)S(1)}, u32[]{:S(2)}, u32[]{:S(2)}) collective-permute-start(bf16[320,1280]{1,0:T(8,128)(2,1)S(1)} %get-tuple-element.25), channel_id=1, source_target_pairs={{2,0},{3,1},{4,6},{5,7},{10,8},{11,9},{12,14},{13,15},{18,16},{19,... | collective-permute-start | bytes 2457608 | tf_op jit(solution)/shard_map/rows_out/ppermute | solution.py:209
  121.4 20.7 %collective-permute-start.13 = (bf16[320,1280]{1,0:T(8,128)(2,1)S(1)}, bf16[320,1280]{1,0:T(8,128)(2,1)S(1)}, u32[]{:S(2)}, u32[]{:S(2)}) collective-permute-start(bf16[320,1280]{1,0:T(8,128)(2,1)S(1)} %broadcast_select_fusion), channel_id=1, source_target_pairs={{0,8},{8,0},{16,24},{24,16},{1,9},{9,1},{17,25},{25,17},{2,10},{10... | collective-permute-start | bytes 2457608 | tf_op jit(solution)/shard_map/along_x/ppermute | solution.py:209
  122.9 19.2 %collective-permute-start.14 = (bf16[320,1280]{1,0:T(8,128)(2,1)S(1)}, bf16[320,1280]{1,0:T(8,128)(2,1)S(1)}, u32[]{:S(2)}, u32[]{:S(2)}) collective-permute-start(bf16[320,1280]{1,0:T(8,128)(2,1)S(1)} %broadcast_select_fusion), channel_id=1, source_target_pairs={{0,16},{8,24},{16,0},{24,8},{1,17},{9,25},{17,1},{25,9},{2,18},{10... | collective-permute-start | bytes 2457608 | tf_op jit(solution)/shard_map/along_y/ppermute | solution.py:209
  138.4 19.9 %collective-permute-start.10 = (bf16[320,1280]{1,0:T(8,128)(2,1)S(1)}, bf16[320,1280]{1,0:T(8,128)(2,1)}, u32[]{:S(2)}, u32[]{:S(2)}) collective-permute-start(bf16[320,1280]{1,0:T(8,128)(2,1)S(1)} %broadcast_select_fusion.1), channel_id=1, source_target_pairs={{0,8},{8,0},{16,24},{24,16},{1,9},{9,1},{17,25},{25,17},{2,10},{10... | collective-permute-start | bytes 2457608 | tf_op jit(solution)/shard_map/along_x/ppermute | solution.py:209
  140.0 19.6 %collective-permute-start.11 = (bf16[320,1280]{1,0:T(8,128)(2,1)S(1)}, bf16[320,1280]{1,0:T(8,128)(2,1)}, u32[]{:S(2)}, u32[]{:S(2)}) collective-permute-start(bf16[320,1280]{1,0:T(8,128)(2,1)S(1)} %broadcast_select_fusion.1), channel_id=1, source_target_pairs={{0,16},{8,24},{16,0},{24,8},{1,17},{9,25},{17,1},{25,9},{2,18},{10... | collective-permute-start | bytes 2457608 | tf_op jit(solution)/shard_map/along_y/ppermute | solution.py:209
  159.6 18.8 %collective-permute-start.15 = (bf16[320,1280]{1,0:T(8,128)(2,1)}, bf16[320,1280]{1,0:T(8,128)(2,1)S(1)}, u32[]{:S(2)}, u32[]{:S(2)}) collective-permute-start(bf16[320,1280]{1,0:T(8,128)(2,1)} %collective-permute-done.10), channel_id=1, source_target_pairs={{0,16},{8,24},{16,0},{24,8},{1,17},{9,25},{17,1},{25,9},{2,18},{10... | collective-permute-start | bytes 2457608 | tf_op jit(solution)/shard_map/across_y/ppermute | solution.py:209
  161.1 18.3 %collective-permute-start.16 = (bf16[320,1280]{1,0:T(8,128)(2,1)S(1)}, bf16[320,1280]{1,0:T(8,128)(2,1)S(1)}, u32[]{:S(2)}, u32[]{:S(2)}) collective-permute-start(bf16[320,1280]{1,0:T(8,128)(2,1)S(1)} %collective-permute-done.14), channel_id=1, source_target_pairs={{0,8},{8,0},{16,24},{24,16},{1,9},{9,1},{17,25},{25,17},{2,10},{10... | collective-permute-start | bytes 2457608 | tf_op jit(solution)/shard_map/across_x/ppermute | solution.py:209
  164.3 15.1 %copy-start.3 = (bf16[4,320,2560]{2,1,0:T(8,128)(2,1)}, bf16[4,320,2560]{2,1,0:T(8,128)(2,1)S(1)}, u32[]{:S(2)}) copy-start(bf16[4,320,2560]{2,1,0:T(8,128)(2,1)S(1)} %bitcast_dynamic-update-slice_fusion) | copy-start | bytes 19660804

commit v16 on v15

--- a/solution.py
+++ b/solution.py
@@ -92,18 +92,21 @@
     )(inner, *blocks)
 
 
-def late_kernel(first, early_count, count, gram_count, widths, *refs):
+def late_kernel(early_count, count, own, *refs):
     inner, refs = refs[0], refs[1:]
-    blocks, grams_in = refs[:count], refs[count : count + gram_count]
-    cubic_in, refs = refs[count + gram_count], refs[count + gram_count + 1 :]
-    outs = refs[: len(widths)]
-    whole, gram, cubic_sum, cubic, poly, sems = refs[len(widths) :]
+    blocks, gram_in, cubic_in, refs = refs[:count], refs[count], refs[count + 1], refs[count + 2 :]
+    if own:
+        outer_poly, out, out_more, outer_more, whole, gram, cubic_sum, cubic, poly, sems = refs
+    else:
+        out, poly, whole, gram, cubic_sum, cubic, sems = refs
     rows, total = gram.shape
     columns = blocks[0].shape[1]
     begin = starts(blocks)
     known = begin[early_count]
+    first = rows if own else 0
     mine = pl.ds(first, rows)
     late = pl.ds(known, total - known)
+    mine_poly = pl.ds(first, rows)
 
     @pl.when(inner[0] != 0)
     def _():
@@ -116,23 +119,20 @@
         def fetch_block(k):
             fetch(k, blocks[k], whole.at[pl.ds(begin[k], blocks[k].shape[0]), :])
 
-        own = [k for k in range(early_count) if first <= begin[k] < first + rows]
-        others = [k for k in range(early_count) if k not in own]
-        for k in own + list(range(early_count, count)):
+        needed = [k for k in range(early_count) if first <= begin[k] < first + rows]
+        others = [k for k in range(early_count) if k not in needed]
+        for k in needed + list(range(early_count, count)):
             fetch_block(k)
-        at = 0
-        for k, gram_in in enumerate(grams_in):
-            width = gram_in.shape[1]
-            fetch("gram%d" % k, gram_in.at[mine, :], gram.at[:, pl.ds(at, width)])
-            at += width
+        fetch("gram", gram_in.at[mine, :], gram.at[:, pl.ds(0, known)])
         fetch("cubic", cubic_in.at[mine, :], cubic_sum)
         for k in others:
             fetch_block(k)
-
-        for k in own + list(range(early_count, count)):
+        if own:
+            fetch("poly", outer_poly, poly.at[pl.ds(0, rows), :])
+
+        for k in needed + list(range(early_count, count)):
             copies[k].wait()
-        for k in range(gram_count):
-            copies["gram%d" % k].wait()
+        copies["gram"].wait()
         gram[:, late] = dot_t(whole[mine, :], whole[late, :]).astype(jnp.bfloat16)
         copies["cubic"].wait()
         for at in tiles(0, columns):
@@ -143,50 +143,58 @@
             copies[k].wait()
         for at in tiles(0, total):
             squared = dot_t(cubic[...], whole[at, :])
-            poly[:, at] = (coef_b * gram[:, at].astype(jnp.float32) + coef_c * squared).astype(
-                jnp.bfloat16
-            )
-
-        for at in tiles(0, columns):
-            product = dot(poly[...], whole[:, at])
-            base = whole[mine, at].astype(jnp.float32)
-            new = (coef_a * base + product).astype(jnp.bfloat16)
-            left = 0
-            for out, width in zip(outs, widths):
-                low, high = max(at.start, left), min(at.start + at.size, left + width)
-                if low < high:
-                    out[:, low - left : high - left] = new[:, low - at.start : high - at.start]
-                left += width
-
-
-def late_products(inner, first, rows, early, late, grams, cubic, widths):
+            poly[mine_poly, at] = (
+                coef_b * gram[:, at].astype(jnp.float32) + coef_c * squared
+            ).astype(jnp.bfloat16)
+
+        def new(which, at):
+            product = dot(poly[which, :], whole[:, at])
+            base = whole[which, at].astype(jnp.float32)
+            return (coef_a * base + product).astype(jnp.bfloat16)
+
+        half = out.shape[1]
+        out[...] = new(mine, pl.ds(0, half))
+        if own:
+            copies["poly"].wait()
+            both = new(pl.ds(0, 2 * rows), pl.ds(half, columns - half))
+            outer_more[...] = both[:rows]
+            out_more[...] = both[rows:]
+
+
+def late_products(inner, rows, early, late, gram, cubic, outer_poly=None):
     blocks = early + late
     count = len(blocks)
     columns = blocks[0].shape[1]
     total = starts(blocks)[-1]
+    own = outer_poly is not None
+    half = jax.ShapeDtypeStruct((rows, columns // 2), jnp.bfloat16)
+    poly = jax.ShapeDtypeStruct((rows, total), jnp.bfloat16)
+    out_shape = (half,) * 3 if own else (half, poly)
+    more = [gram, cubic] + ([outer_poly] if own else [])
+    scratch = [
+        pltpu.VMEM((total, columns), jnp.bfloat16),
+        pltpu.VMEM((rows, total), jnp.bfloat16),
+        pltpu.VMEM((rows, columns), jnp.float32),
+        pltpu.VMEM((rows, columns), jnp.bfloat16),
+    ]
+    if own:
+        scratch.append(pltpu.VMEM((2 * rows, total), jnp.bfloat16))
     return pl.pallas_call(
-        functools.partial(late_kernel, first, len(early), count, len(grams), widths),
-        out_shape=tuple(jax.ShapeDtypeStruct((rows, w), jnp.bfloat16) for w in widths),
+        functools.partial(late_kernel, len(early), count, own),
+        out_shape=out_shape,
         in_specs=[pl.BlockSpec(memory_space=pltpu.SMEM)]
         + [pl.BlockSpec(memory_space=pltpu.HBM)] * count
-        + [pl.BlockSpec(memory_space=pl.ANY)] * (len(grams) + 1),
-        out_specs=tuple(pl.BlockSpec(memory_space=pltpu.VMEM) for _ in widths),
-        scratch_shapes=[
-            pltpu.VMEM((total, columns), jnp.bfloat16),
-            pltpu.VMEM((rows, total), jnp.bfloat16),
-            pltpu.VMEM((rows, columns), jnp.float32),
-            pltpu.VMEM((rows, columns), jnp.bfloat16),
-            pltpu.VMEM((rows, total), jnp.bfloat16),
-            pltpu.SemaphoreType.DMA((count + len(grams) + 1,)),
-        ],
+        + [pl.BlockSpec(memory_space=pl.ANY)] * len(more),
+        out_specs=tuple(pl.BlockSpec(memory_space=pltpu.VMEM) for _ in out_shape),
+        scratch_shapes=scratch + [pltpu.SemaphoreType.DMA((count + len(more),))],
         compiler_params=pltpu.CompilerParams(vmem_limit_bytes=VMEM_LIMIT),
         cost_estimate=pl.CostEstimate(
             flops=5 * rows * total * columns, bytes_accessed=2 * total * columns, transcendentals=0
         ),
-    )(inner, *blocks, *grams, cubic)
-
-
-def line_shards(iterate, widths):
+    )(inner, *blocks, *more)
+
+
+def line_shards(iterate):
     own = iterate[0]
     rows, columns = own.shape
     place = lax.axis_index("shard") // 2
@@ -221,37 +229,37 @@
     gram, cubic = early_products(inner, rows, early)
     far_rows, gram, cubic = tie((far_rows, gram, cubic))
     late = [far_rows, swap("far", far_rows)]
-    for_outer = late_products(inner, 0, rows, early, late, [gram], cubic, widths)
-    for_own = late_products(inner, rows, rows, early, late, [gram], cubic, widths)
+    outer_first, outer_poly = late_products(inner, rows, early, late, gram, cubic)
+    own_first, own_second, outer_second = late_products(
+        inner, rows, early, late, gram, cubic, outer_poly
+    )
+    for_outer, for_own = (outer_first, outer_second), (own_first, own_second)
 
     result = jnp.zeros((4, rows, columns), jnp.bfloat16)
 
     def place_in(result, flip, at, part):
         return lax.dynamic_update_slice(result, part[None], (mat ^ flip, 0, at))
 
-    begin, corner = 0, []
-    for k, width in enumerate(widths):
+    width, corner = columns // 2, [None, None]
+    for k in (1, 0):
         returned = move("rows_out", for_outer[k], "shard", outwards)
         mine = tie(jnp.where(outer, returned, for_own[k]))
         by_x = move("along_x", mine, "mat", along_x)
         by_y = move("along_y", mine, "mat", along_y)
         by_x, by_y = tie((by_x, by_y))
-        corner.append((by_x, by_y)[k % 2])
+        corner[k] = (by_x, by_y)[k]
         for flip, part in enumerate((mine, by_x, by_y)):
-            result = place_in(result, flip, begin, part)
-        begin += width
+            result = place_in(result, flip, k * width, part)
     corner = tie(corner)
-    for k, part in enumerate(corner):
-        name, pairs = ("across_y", along_y) if k % 2 == 0 else ("across_x", along_x)
-        corner[k] = move(name, part, "mat", pairs)
+    corner[0] = move("across_y", corner[0], "mat", along_y)
+    corner[1] = move("across_x", corner[1], "mat", along_x)
     result = place_in(result, 3, 0, jnp.concatenate(corner, axis=1))
     return result
 
 
 def solution(mesh):
     if (mesh.shape["mat"], mesh.shape["shard"]) == (4, 8):
-        def shards(iterate):
-            return line_shards(iterate, widths=(1280, 1280))
+        shards = line_shards
     else:
         shards = general_shards
     return jax.shard_map(

time: 181 us -> 181 us (level)
    unnamed x8 -> x10, local copies, waits for them, and re-layouts: 4.03 us -> 4.03 us
where the time goes in v16:
time: 181 us; the launch traced here: 180 us
  waiting for transfers between devices  137 us (76%)
  starting transfers between devices  30.5 us (17%)
  local copies, waits for them, and re-layouts  10.5 us (6%)
    ppermute x17, waiting for transfers between devices, move(): return lax.ppermute(block, axis, pairs)  137 us
    ppermute x17, starting transfers between devices, move(): return lax.ppermute(block, axis, pairs)  30.5 us
    unnamed x10, local copies, waits for them, and re-layouts  4.03 us
  transfers between devices with their start and end apart: 17, of which 8 were waited for; matrix products, arithmetic and copies ran while one was open for 4% of the time, Pallas kernels for 0%

profile of v16, /device:TPU:0, one launch (start us, length us, event | category | flops | bytes accessed | tf_op | source)
XLA Modules:
  0.0 180.3 jit_solution(18284595792758198500)
XLA Ops:
  0.8 7.8 %collective-permute-start = (bf16[320,2560]{1,0:T(8,128)(2,1)}, bf16[320,2560]{1,0:T(8,128)(2,1)S(1)}, u32[]{:S(2)}, u32[]{:S(2)}) collective-permute-start(bf16[320,2560]{1,0:T(8,128)(2,1)} %bitcast.19), channel_id=1, source_target_pairs={{0,2},{1,3},{6,4},{7,5},{8,10},{9,11},{14,12},{15,13},{16,18},{17,... | collective-permute-start | bytes 4915208 | tf_op jit(solution)/shard_map/rows_in/ppermute | solution.py:217
  9.3 3.4 %collective-permute-start.7 = (bf16[320,2560]{1,0:T(8,128)(2,1)}, bf16[320,2560]{1,0:T(8,128)(2,1)}, u32[]{:S(2)}, u32[]{:S(2)}) collective-permute-start(bf16[320,2560]{1,0:T(8,128)(2,1)} %bitcast.21), channel_id=1, source_target_pairs={{0,4},{1,5},{6,2},{7,3},{8,12},{9,13},{14,10},{15,11},{16,20},{17,... | collective-permute-start | bytes 4915208 | tf_op jit(solution)/shard_map/rows_far/ppermute | solution.py:217
  13.8 1.7 collective-permute-start.5
  15.5 29.5 %collective-permute-done.refs_1_ = bf16[320,2560]{1,0:T(8,128)(2,1)S(1)} collective-permute-done((bf16[320,2560]{1,0:T(8,128)(2,1)}, bf16[320,2560]{1,0:T(8,128)(2,1)S(1)}, u32[]{:S(2)}, u32[]{:S(2)}) %collective-permute-start) | collective-permute-done | bytes 1638432 | tf_op jit(solution)/shard_map/rows_in/ppermute | solution.py:217
  45.0 1.3 fusion.1
  46.3 1.6 collective-permute-start.3
  47.8 1.6 collective-permute-start.4
  51.5 1.5 collective-permute-start.6
  53.0 1.4 copy-done
  54.4 1.4 copy-done.2
  55.9 22.7 %collective-permute-done.7.refs_9_ = bf16[320,2560]{1,0:T(8,128)(2,1)} collective-permute-done((bf16[320,2560]{1,0:T(8,128)(2,1)}, bf16[320,2560]{1,0:T(8,128)(2,1)}, u32[]{:S(2)}, u32[]{:S(2)}) %collective-permute-start.7) | collective-permute-done | bytes 1638432 | tf_op jit(solution)/shard_map/rows_far/ppermute | solution.py:217
  79.7 1.3 collective-permute-start.12
  81.4 1.3 collective-permute-start.9
  82.7 36.1 %collective-permute-done.12 = bf16[320,1280]{1,0:T(8,128)(2,1)S(1)} collective-permute-done((bf16[320,1280]{1,0:T(8,128)(2,1)S(1)}, bf16[320,1280]{1,0:T(8,128)(2,1)S(1)}, u32[]{:S(2)}, u32[]{:S(2)}) %collective-permute-start.12) | collective-permute-done | bytes 819232 | tf_op jit(solution)/shard_map/rows_out/ppermute | solution.py:217
  118.8 1.6 collective-permute-start.13
  120.4 1.5 collective-permute-start.14
  121.9 15.8 %collective-permute-done.9 = bf16[320,1280]{1,0:T(8,128)(2,1)S(1)} collective-permute-done((bf16[320,1280]{1,0:T(8,128)(2,1)S(1)}, bf16[320,1280]{1,0:T(8,128)(2,1)S(1)}, u32[]{:S(2)}, u32[]{:S(2)}) %collective-permute-start.9) | collective-permute-done | bytes 819232 | tf_op jit(solution)/shard_map/rows_out/ppermute | solution.py:217
  137.8 1.6 collective-permute-start.10
  139.4 1.5 collective-permute-start.11
  141.5 16.2 %collective-permute-done.10 = bf16[320,1280]{1,0:T(8,128)(2,1)} collective-permute-done((bf16[320,1280]{1,0:T(8,128)(2,1)S(1)}, bf16[320,1280]{1,0:T(8,128)(2,1)}, u32[]{:S(2)}, u32[]{:S(2)}) %collective-permute-start.10) | collective-permute-done | bytes 819232 | tf_op jit(solution)/shard_map/along_x/ppermute | solution.py:217
  159.0 1.5 collective-permute-start.15
  163.7 13.9 %collective-permute-done.15 = bf16[320,1280]{1,0:T(8,128)(2,1)S(1)} collective-permute-done((bf16[320,1280]{1,0:T(8,128)(2,1)S(1)}, bf16[320,1280]{1,0:T(8,128)(2,1)S(1)}, u32[]{:S(2)}, u32[]{:S(2)}) %collective-permute-start.15) | collective-permute-done | bytes 819232 | tf_op jit(solution)/shard_map/across_y/ppermute | solution.py:217
  177.5 1.5 collective-permute-done.16
  179.0 1.3 fusion
  (36 shorter events, 11.3 us)
Async XLA Ops:
  0.0 12.7 %collective-permute-start.2 = (bf16[320,2560]{1,0:T(8,128)(2,1)}, bf16[320,2560]{1,0:T(8,128)(2,1)S(1)}, u32[]{:S(2)}, u32[]{:S(2)}) collective-permute-start(bf16[320,2560]{1,0:T(8,128)(2,1)} %bitcast.18), channel_id=1, source_target_pairs={{2,4},{3,5},{4,2},{5,3},{10,12},{11,13},{12,10},{13,11},{18,20},{1... | collective-permute-start | bytes 4915208 | tf_op jit(solution)/shard_map/middle/ppermute | solution.py:217
  0.8 44.2 %collective-permute-start = (bf16[320,2560]{1,0:T(8,128)(2,1)}, bf16[320,2560]{1,0:T(8,128)(2,1)S(1)}, u32[]{:S(2)}, u32[]{:S(2)}) collective-permute-start(bf16[320,2560]{1,0:T(8,128)(2,1)} %bitcast.19), channel_id=1, source_target_pairs={{0,2},{1,3},{6,4},{7,5},{8,10},{9,11},{14,12},{15,13},{16,18},{17,... | collective-permute-start | bytes 4915208 | tf_op jit(solution)/shard_map/rows_in/ppermute | solution.py:217
  8.5 41.8 %collective-permute-start.1 = (bf16[320,2560]{1,0:T(8,128)(2,1)}, bf16[320,2560]{1,0:T(8,128)(2,1)S(1)}, u32[]{:S(2)}, u32[]{:S(2)}) collective-permute-start(bf16[320,2560]{1,0:T(8,128)(2,1)} %bitcast.20), channel_id=1, source_target_pairs={{2,3},{3,2},{4,5},{5,4},{10,11},{11,10},{12,13},{13,12},{18,19},{1... | collective-permute-start | bytes 4915208 | tf_op jit(solution)/shard_map/swap_own/ppermute | solution.py:217
  9.3 69.3 %collective-permute-start.7 = (bf16[320,2560]{1,0:T(8,128)(2,1)}, bf16[320,2560]{1,0:T(8,128)(2,1)}, u32[]{:S(2)}, u32[]{:S(2)}) collective-permute-start(bf16[320,2560]{1,0:T(8,128)(2,1)} %bitcast.21), channel_id=1, source_target_pairs={{0,4},{1,5},{6,2},{7,3},{8,12},{9,13},{14,10},{15,11},{16,20},{17,... | collective-permute-start | bytes 4915208 | tf_op jit(solution)/shard_map/rows_far/ppermute | solution.py:217
  13.8 39.1 %collective-permute-start.5 = (bf16[208,2560]{1,0:T(8,128)(2,1)}, bf16[208,2560]{1,0:T(8,128)(2,1)}, u32[]{:S(2)}, u32[]{:S(2)}) collective-permute-start(bf16[208,2560]{1,0:T(8,128)(2,1)} %slice.18), channel_id=1, source_target_pairs={{2,3},{3,2},{4,5},{5,4},{10,11},{11,10},{12,13},{13,12},{18,19},{1... | collective-permute-start | bytes 3194888 | tf_op jit(solution)/shard_map/swap_rows/ppermute | solution.py:217
  46.3 6.7 %collective-permute-start.3 = (bf16[160,2560]{1,0:T(8,128)(2,1)}, bf16[160,2560]{1,0:T(8,128)(2,1)}, u32[]{:S(2)}, u32[]{:S(2)}) collective-permute-start(bf16[160,2560]{1,0:T(8,128)(2,1)} %get-tuple-element.38), channel_id=1, source_target_pairs={{2,3},{3,2},{4,5},{5,4},{10,11},{11,10},{12,13},{13,12},{18,19},{1... | collective-permute-start | bytes 2457608 | tf_op jit(solution)/shard_map/swap_rows/ppermute | solution.py:217
  47.8 5.1 %collective-permute-start.4 = (bf16[160,2560]{1,0:T(8,128)(2,1)}, bf16[160,2560]{1,0:T(8,128)(2,1)}, u32[]{:S(2)}, u32[]{:S(2)}) collective-permute-start(bf16[160,2560]{1,0:T(8,128)(2,1)} %get-tuple-element.37), channel_id=1, source_target_pairs={{2,3},{3,2},{4,5},{5,4},{10,11},{11,10},{12,13},{13,12},{18,19},{1... | collective-permute-start | bytes 2457608 | tf_op jit(solution)/shard_map/swap_rows/ppermute | solution.py:217
  50.3 1.2 copy-start.1
  51.5 1.5 collective-permute-start.6
  53.0 1.4 copy-start
  54.4 1.4 copy-start.2
  55.9 23.8 %copy-start.3 = (f32[640,2560]{1,0:T(8,128)}, f32[640,2560]{1,0:T(8,128)S(1)}, u32[]{:S(2)}) copy-start(f32[640,2560]{1,0:T(8,128)S(1)} %get-tuple-element.25.refs_12_) | copy-start | bytes 19660804
  78.6 0.8 collective-permute-start.8
  79.7 39.0 %collective-permute-start.12 = (bf16[320,1280]{1,0:T(8,128)(2,1)S(1)}, bf16[320,1280]{1,0:T(8,128)(2,1)S(1)}, u32[]{:S(2)}, u32[]{:S(2)}) collective-permute-start(bf16[320,1280]{1,0:T(8,128)(2,1)S(1)} %get-tuple-element.31), channel_id=1, source_target_pairs={{2,0},{3,1},{4,6},{5,7},{10,8},{11,9},{12,14},{13,15},{18,16},{19,... | collective-permute-start | bytes 2457608 | tf_op jit(solution)/shard_map/rows_out/ppermute | solution.py:217
  81.4 56.3 %collective-permute-start.9 = (bf16[320,1280]{1,0:T(8,128)(2,1)S(1)}, bf16[320,1280]{1,0:T(8,128)(2,1)S(1)}, u32[]{:S(2)}, u32[]{:S(2)}) collective-permute-start(bf16[320,1280]{1,0:T(8,128)(2,1)S(1)} %get-tuple-element.27), channel_id=1, source_target_pairs={{2,0},{3,1},{4,6},{5,7},{10,8},{11,9},{12,14},{13,15},{18,16},{19,... | collective-permute-start | bytes 2457608 | tf_op jit(solution)/shard_map/rows_out/ppermute | solution.py:217
  118.8 22.7 %collective-permute-start.13 = (bf16[320,1280]{1,0:T(8,128)(2,1)S(1)}, bf16[320,1280]{1,0:T(8,128)(2,1)S(1)}, u32[]{:S(2)}, u32[]{:S(2)}) collective-permute-start(bf16[320,1280]{1,0:T(8,128)(2,1)S(1)} %broadcast_select_fusion), channel_id=1, source_target_pairs={{0,8},{8,0},{16,24},{24,16},{1,9},{9,1},{17,25},{25,17},{2,10},{10... | collective-permute-start | bytes 2457608 | tf_op jit(solution)/shard_map/along_x/ppermute | solution.py:217
  120.4 21.1 %collective-permute-start.14 = (bf16[320,1280]{1,0:T(8,128)(2,1)S(1)}, bf16[320,1280]{1,0:T(8,128)(2,1)S(1)}, u32[]{:S(2)}, u32[]{:S(2)}) collective-permute-start(bf16[320,1280]{1,0:T(8,128)(2,1)S(1)} %broadcast_select_fusion), channel_id=1, source_target_pairs={{0,16},{8,24},{16,0},{24,8},{1,17},{9,25},{17,1},{25,9},{2,18},{10... | collective-permute-start | bytes 2457608 | tf_op jit(solution)/shard_map/along_y/ppermute | solution.py:217
  137.8 19.9 %collective-permute-start.10 = (bf16[320,1280]{1,0:T(8,128)(2,1)S(1)}, bf16[320,1280]{1,0:T(8,128)(2,1)}, u32[]{:S(2)}, u32[]{:S(2)}) collective-permute-start(bf16[320,1280]{1,0:T(8,128)(2,1)S(1)} %broadcast_select_fusion.1), channel_id=1, source_target_pairs={{0,8},{8,0},{16,24},{24,16},{1,9},{9,1},{17,25},{25,17},{2,10},{10... | collective-permute-start | bytes 2457608 | tf_op jit(solution)/shard_map/along_x/ppermute | solution.py:217
  139.4 19.6 %collective-permute-start.11 = (bf16[320,1280]{1,0:T(8,128)(2,1)S(1)}, bf16[320,1280]{1,0:T(8,128)(2,1)}, u32[]{:S(2)}, u32[]{:S(2)}) collective-permute-start(bf16[320,1280]{1,0:T(8,128)(2,1)S(1)} %broadcast_select_fusion.1), channel_id=1, source_target_pairs={{0,16},{8,24},{16,0},{24,8},{1,17},{9,25},{17,1},{25,9},{2,18},{10... | collective-permute-start | bytes 2457608 | tf_op jit(solution)/shard_map/along_y/ppermute | solution.py:217
  159.0 18.6 %collective-permute-start.15 = (bf16[320,1280]{1,0:T(8,128)(2,1)S(1)}, bf16[320,1280]{1,0:T(8,128)(2,1)S(1)}, u32[]{:S(2)}, u32[]{:S(2)}) collective-permute-start(bf16[320,1280]{1,0:T(8,128)(2,1)S(1)} %collective-permute-done.13), channel_id=1, source_target_pairs={{0,16},{8,24},{16,0},{24,8},{1,17},{9,25},{17,1},{25,9},{2,18},{10... | collective-permute-start | bytes 2457608 | tf_op jit(solution)/shard_map/across_y/ppermute | solution.py:217
  160.5 18.5 %collective-permute-start.16 = (bf16[320,1280]{1,0:T(8,128)(2,1)}, bf16[320,1280]{1,0:T(8,128)(2,1)S(1)}, u32[]{:S(2)}, u32[]{:S(2)}) collective-permute-start(bf16[320,1280]{1,0:T(8,128)(2,1)} %collective-permute-done.11), channel_id=1, source_target_pairs={{0,8},{8,0},{16,24},{24,16},{1,9},{9,1},{17,25},{25,17},{2,10},{10... | collective-permute-start | bytes 2457608 | tf_op jit(solution)/shard_map/across_x/ppermute | solution.py:217
  163.6 15.4 %copy-start.4 = (bf16[4,320,2560]{2,1,0:T(8,128)(2,1)}, bf16[4,320,2560]{2,1,0:T(8,128)(2,1)S(1)}, u32[]{:S(2)}) copy-start(bf16[4,320,2560]{2,1,0:T(8,128)(2,1)S(1)} %bitcast_dynamic-update-slice_fusion) | copy-start | bytes 19660804

commit v17 on v16

--- a/solution.py
+++ b/solution.py
@@ -221,14 +221,19 @@
 
     inner_rows = move("middle", own, "shard", middle)
     outer_rows = move("rows_in", own, "shard", inwards)
-    far_rows = move("rows_far", own, "shard", across_middle)
-
-    early = [outer_rows, own, swap("own", own), inner_rows]
-    for block, cut in ((outer_rows, rows // 2), (inner_rows, rows * 13 // 20)):
-        early += [swap("rows", part) for part in (block[:cut], block[cut:])]
+    cut = rows * 13 // 20
+    far_rows = [
+        move("rows_far", part, "shard", across_middle) for part in (own[:cut], own[cut:])
+    ]
+
+    own_kept = pltpu.with_memory_space_constraint(own, pltpu.HBM)
+    early = [outer_rows, own_kept, swap("own", own), inner_rows]
+    for block, at in ((outer_rows, rows // 2), (inner_rows, rows * 11 // 20)):
+        early += [swap("rows", part) for part in (block[:at], block[at:])]
     gram, cubic = early_products(inner, rows, early)
-    far_rows, gram, cubic = tie((far_rows, gram, cubic))
-    late = [far_rows, swap("far", far_rows)]
+    far_rows[0], gram, cubic = tie((far_rows[0], gram, cubic))
+    swapped = swap("far", far_rows[0])
+    late = far_rows + [swapped, swap("far_last", far_rows[1])]
     outer_first, outer_poly = late_products(inner, rows, early, late, gram, cubic)
     own_first, own_second, outer_second = late_products(
         inner, rows, early, late, gram, cubic, outer_poly

time: 181 us -> 181 us (level)
  waiting for transfers between devices: 137 us -> 125 us
  starting transfers between devices: 30.5 us -> 37.8 us
  local copies, waits for them, and re-layouts: 10.5 us -> 14.4 us
    ppermute x17 -> x19, waiting for transfers between devices: 137 us -> 125 us  [move(): return lax.ppermute(block, axis, pairs)]
    ppermute x17 -> x19, starting transfers between devices: 30.5 us -> 37.8 us  [move(): return lax.ppermute(block, axis, pairs)]
    slice x3 -> x5, local copies, waits for them, and re-layouts: 3.24 us -> 6.6 us  [the longest x3 2.37 us: line_shards(): early += [swap('rows', part) for part in (block[:at], block[at:])]]
  transfers between devices with their start and end apart: 17 -> 19, of which waited for: 8 -> 9; matrix products, arithmetic and copies ran while one was open for 4% -> 6% of each run, Pallas kernels for 0% -> 0%
where the time goes in v17:
time: 181 us; the launch traced here: 180 us
  waiting for transfers between devices  125 us (69%)
  starting transfers between devices  37.8 us (21%)
  local copies, waits for them, and re-layouts  14.4 us (8%)
    ppermute x19, waiting for transfers between devices, move(): return lax.ppermute(block, axis, pairs)  125 us
    ppermute x19, starting transfers between devices, move(): return lax.ppermute(block, axis, pairs)  37.8 us
    unnamed x10, local copies, waits for them, and re-layouts  4.59 us
  transfers between devices with their start and end apart: 19, of which 9 were waited for; matrix products, arithmetic and copies ran while one was open for 6% of the time, Pallas kernels for 0%

profile of v17, /device:TPU:0, one launch (start us, length us, event | category | flops | bytes accessed | tf_op | source)
XLA Modules:
  0.0 179.9 jit_solution(16965993353791543545)
XLA Ops:
  0.8 7.8 %collective-permute-start = (bf16[320,2560]{1,0:T(8,128)(2,1)}, bf16[320,2560]{1,0:T(8,128)(2,1)S(1)}, u32[]{:S(2)}, u32[]{:S(2)}) collective-permute-start(bf16[320,2560]{1,0:T(8,128)(2,1)} %bitcast.23), channel_id=1, source_target_pairs={{0,2},{1,3},{6,4},{7,5},{8,10},{9,11},{14,12},{15,13},{16,18},{17,... | collective-permute-start | bytes 4915208 | tf_op jit(solution)/shard_map/rows_in/ppermute | solution.py:217
  9.3 2.3 %slice_bitcast_fusion = bf16[208,2560]{1,0:T(8,128)(2,1)} fusion(bf16[1,320,2560]{2,1,0:T(8,128)(2,1)} %param.1), kind=kLoop, calls=%fused_computation.2 | loop fusion | bytes 2129920 | tf_op jit(solution)/shard_map/slice | solution.py:226
  11.6 3.2 %collective-permute-start.7 = (bf16[208,2560]{1,0:T(8,128)(2,1)}, bf16[208,2560]{1,0:T(8,128)(2,1)}, u32[]{:S(2)}, u32[]{:S(2)}) collective-permute-start(bf16[208,2560]{1,0:T(8,128)(2,1)} %slice_bitcast_fusion), channel_id=1, source_target_pairs={{0,4},{1,5},{6,2},{7,3},{8,12},{9,13},{14,10},{15,11},{16,20},{17,... | collective-permute-start | bytes 3194888 | tf_op jit(solution)/shard_map/rows_far/ppermute | solution.py:217
  15.8 1.6 collective-permute-start.5
  17.4 27.6 %collective-permute-done.refs_1_ = bf16[320,2560]{1,0:T(8,128)(2,1)S(1)} collective-permute-done((bf16[320,2560]{1,0:T(8,128)(2,1)}, bf16[320,2560]{1,0:T(8,128)(2,1)S(1)}, u32[]{:S(2)}, u32[]{:S(2)}) %collective-permute-start) | collective-permute-done | bytes 1638432 | tf_op jit(solution)/shard_map/rows_in/ppermute | solution.py:217
  45.0 1.3 fusion.1
  46.3 1.6 collective-permute-start.3
  47.8 1.6 collective-permute-start.4
  51.3 2.0 %slice_bitcast_fusion.1 = bf16[112,2560]{1,0:T(8,128)(2,1)} fusion(bf16[1,320,2560]{2,1,0:T(8,128)(2,1)} %param.1), kind=kLoop, calls=%fused_computation.11 | loop fusion | bytes 1146880 | tf_op jit(solution)/shard_map/slice | solution.py:226
  54.2 7.7 %collective-permute-start.8 = (bf16[112,2560]{1,0:T(8,128)(2,1)}, bf16[112,2560]{1,0:T(8,128)(2,1)}, u32[]{:S(2)}, u32[]{:S(2)}) collective-permute-start(bf16[112,2560]{1,0:T(8,128)(2,1)} %slice_bitcast_fusion.1), channel_id=1, source_target_pairs={{0,4},{1,5},{6,2},{7,3},{8,12},{9,13},{14,10},{15,11},{16,20},{17,... | collective-permute-start | bytes 1720328 | tf_op jit(solution)/shard_map/rows_far/ppermute | solution.py:217
  61.9 1.4 copy-done.1
  64.5 3.3 %collective-permute-done.7.refs_9_ = bf16[208,2560]{1,0:T(8,128)(2,1)} collective-permute-done((bf16[208,2560]{1,0:T(8,128)(2,1)}, bf16[208,2560]{1,0:T(8,128)(2,1)}, u32[]{:S(2)}, u32[]{:S(2)}) %collective-permute-start.7) | collective-permute-done | bytes 1064992 | tf_op jit(solution)/shard_map/rows_far/ppermute | solution.py:217
  68.5 10.1 %collective-permute-done.8.refs_10_ = bf16[112,2560]{1,0:T(8,128)(2,1)} collective-permute-done((bf16[112,2560]{1,0:T(8,128)(2,1)}, bf16[112,2560]{1,0:T(8,128)(2,1)}, u32[]{:S(2)}, u32[]{:S(2)}) %collective-permute-start.8) | collective-permute-done | bytes 573472 | tf_op jit(solution)/shard_map/rows_far/ppermute | solution.py:217
  79.7 1.3 collective-permute-start.14
  82.6 35.3 %collective-permute-done.14 = bf16[320,1280]{1,0:T(8,128)(2,1)S(1)} collective-permute-done((bf16[320,1280]{1,0:T(8,128)(2,1)S(1)}, bf16[320,1280]{1,0:T(8,128)(2,1)S(1)}, u32[]{:S(2)}, u32[]{:S(2)}) %collective-permute-start.14) | collective-permute-done | bytes 819232 | tf_op jit(solution)/shard_map/rows_out/ppermute | solution.py:217
  118.0 1.5 collective-permute-start.15
  119.5 1.5 collective-permute-start.16
  121.1 16.1 %collective-permute-done.11 = bf16[320,1280]{1,0:T(8,128)(2,1)S(1)} collective-permute-done((bf16[320,1280]{1,0:T(8,128)(2,1)S(1)}, bf16[320,1280]{1,0:T(8,128)(2,1)S(1)}, u32[]{:S(2)}, u32[]{:S(2)}) %collective-permute-start.11) | collective-permute-done | bytes 819232 | tf_op jit(solution)/shard_map/rows_out/ppermute | solution.py:217
  137.2 1.5 collective-permute-start.12
  138.8 1.5 collective-permute-start.13
  140.9 16.4 %collective-permute-done.12 = bf16[320,1280]{1,0:T(8,128)(2,1)} collective-permute-done((bf16[320,1280]{1,0:T(8,128)(2,1)S(1)}, bf16[320,1280]{1,0:T(8,128)(2,1)}, u32[]{:S(2)}, u32[]{:S(2)}) %collective-permute-start.12) | collective-permute-done | bytes 819232 | tf_op jit(solution)/shard_map/along_x/ppermute | solution.py:217
  158.5 1.5 collective-permute-start.17
  163.2 13.9 %collective-permute-done.17 = bf16[320,1280]{1,0:T(8,128)(2,1)S(1)} collective-permute-done((bf16[320,1280]{1,0:T(8,128)(2,1)S(1)}, bf16[320,1280]{1,0:T(8,128)(2,1)S(1)}, u32[]{:S(2)}, u32[]{:S(2)}) %collective-permute-start.17) | collective-permute-done | bytes 819232 | tf_op jit(solution)/shard_map/across_y/ppermute | solution.py:217
  177.1 1.5 collective-permute-done.18
  (42 shorter events, 16.3 us)
Async XLA Ops:
  0.0 14.8 %collective-permute-start.2 = (bf16[320,2560]{1,0:T(8,128)(2,1)}, bf16[320,2560]{1,0:T(8,128)(2,1)S(1)}, u32[]{:S(2)}, u32[]{:S(2)}) collective-permute-start(bf16[320,2560]{1,0:T(8,128)(2,1)} %bitcast.22), channel_id=1, source_target_pairs={{2,4},{3,5},{4,2},{5,3},{10,12},{11,13},{12,10},{13,11},{18,20},{1... | collective-permute-start | bytes 4915208 | tf_op jit(solution)/shard_map/middle/ppermute | solution.py:217
  0.8 44.2 %collective-permute-start = (bf16[320,2560]{1,0:T(8,128)(2,1)}, bf16[320,2560]{1,0:T(8,128)(2,1)S(1)}, u32[]{:S(2)}, u32[]{:S(2)}) collective-permute-start(bf16[320,2560]{1,0:T(8,128)(2,1)} %bitcast.23), channel_id=1, source_target_pairs={{0,2},{1,3},{6,4},{7,5},{8,10},{9,11},{14,12},{15,13},{16,18},{17,... | collective-permute-start | bytes 4915208 | tf_op jit(solution)/shard_map/rows_in/ppermute | solution.py:217
  8.5 40.9 %collective-permute-start.1 = (bf16[320,2560]{1,0:T(8,128)(2,1)}, bf16[320,2560]{1,0:T(8,128)(2,1)S(1)}, u32[]{:S(2)}, u32[]{:S(2)}) collective-permute-start(bf16[320,2560]{1,0:T(8,128)(2,1)} %bitcast.24), channel_id=1, source_target_pairs={{2,3},{3,2},{4,5},{5,4},{10,11},{11,10},{12,13},{13,12},{18,19},{1... | collective-permute-start | bytes 4915208 | tf_op jit(solution)/shard_map/swap_own/ppermute | solution.py:217
  11.6 56.2 %collective-permute-start.7 = (bf16[208,2560]{1,0:T(8,128)(2,1)}, bf16[208,2560]{1,0:T(8,128)(2,1)}, u32[]{:S(2)}, u32[]{:S(2)}) collective-permute-start(bf16[208,2560]{1,0:T(8,128)(2,1)} %slice_bitcast_fusion), channel_id=1, source_target_pairs={{0,4},{1,5},{6,2},{7,3},{8,12},{9,13},{14,10},{15,11},{16,20},{17,... | collective-permute-start | bytes 3194888 | tf_op jit(solution)/shard_map/rows_far/ppermute | solution.py:217
  15.8 46.0 %collective-permute-start.5 = (bf16[176,2560]{1,0:T(8,128)(2,1)}, bf16[176,2560]{1,0:T(8,128)(2,1)}, u32[]{:S(2)}, u32[]{:S(2)}) collective-permute-start(bf16[176,2560]{1,0:T(8,128)(2,1)} %slice.34), channel_id=1, source_target_pairs={{2,3},{3,2},{4,5},{5,4},{10,11},{11,10},{12,13},{13,12},{18,19},{1... | collective-permute-start | bytes 2703368 | tf_op jit(solution)/shard_map/swap_rows/ppermute | solution.py:217
  46.3 15.6 %collective-permute-start.3 = (bf16[160,2560]{1,0:T(8,128)(2,1)}, bf16[160,2560]{1,0:T(8,128)(2,1)}, u32[]{:S(2)}, u32[]{:S(2)}) collective-permute-start(bf16[160,2560]{1,0:T(8,128)(2,1)} %get-tuple-element.38), channel_id=1, source_target_pairs={{2,3},{3,2},{4,5},{5,4},{10,11},{11,10},{12,13},{13,12},{18,19},{1... | collective-permute-start | bytes 2457608 | tf_op jit(solution)/shard_map/swap_rows/ppermute | solution.py:217
  47.8 14.0 %collective-permute-start.4 = (bf16[160,2560]{1,0:T(8,128)(2,1)}, bf16[160,2560]{1,0:T(8,128)(2,1)}, u32[]{:S(2)}, u32[]{:S(2)}) collective-permute-start(bf16[160,2560]{1,0:T(8,128)(2,1)} %get-tuple-element.37), channel_id=1, source_target_pairs={{2,3},{3,2},{4,5},{5,4},{10,11},{11,10},{12,13},{13,12},{18,19},{1... | collective-permute-start | bytes 2457608 | tf_op jit(solution)/shard_map/swap_rows/ppermute | solution.py:217
  49.5 1.2 copy-start
  50.6 2.7 %collective-permute-start.6 = (bf16[144,2560]{1,0:T(8,128)(2,1)S(1)}, bf16[144,2560]{1,0:T(8,128)(2,1)S(1)}, u32[]{:S(2)}, u32[]{:S(2)}) collective-permute-start(bf16[144,2560]{1,0:T(8,128)(2,1)S(1)} %slice.35), channel_id=1, source_target_pairs={{2,3},{3,2},{4,5},{5,4},{10,11},{11,10},{12,13},{13,12},{18,19},{1... | collective-permute-start | bytes 2211848 | tf_op jit(solution)/shard_map/swap_rows/ppermute | solution.py:217
  53.3 0.9 copy-start.2
  54.2 24.4 %collective-permute-start.8 = (bf16[112,2560]{1,0:T(8,128)(2,1)}, bf16[112,2560]{1,0:T(8,128)(2,1)}, u32[]{:S(2)}, u32[]{:S(2)}) collective-permute-start(bf16[112,2560]{1,0:T(8,128)(2,1)} %slice_bitcast_fusion.1), channel_id=1, source_target_pairs={{0,4},{1,5},{6,2},{7,3},{8,12},{9,13},{14,10},{15,11},{16,20},{17,... | collective-permute-start | bytes 1720328 | tf_op jit(solution)/shard_map/rows_far/ppermute | solution.py:217
  61.9 1.4 copy-start.1
  63.3 1.1 copy-start.3
  67.8 11.5 %collective-permute-start.9 = (bf16[208,2560]{1,0:T(8,128)(2,1)}, bf16[208,2560]{1,0:T(8,128)(2,1)S(1)}, u32[]{:S(2)}, u32[]{:S(2)}) collective-permute-start(bf16[208,2560]{1,0:T(8,128)(2,1)} %collective-permute-done.7.refs_9_), channel_id=1, source_target_pairs={{2,3},{3,2},{4,5},{5,4},{10,11},{11,10},{12,13},{13,12},{18,19},{1... | collective-permute-start | bytes 3194888 | tf_op jit(solution)/shard_map/swap_far/ppermute | solution.py:217
  78.6 0.7 collective-permute-start.10
  79.7 38.2 %collective-permute-start.14 = (bf16[320,1280]{1,0:T(8,128)(2,1)S(1)}, bf16[320,1280]{1,0:T(8,128)(2,1)S(1)}, u32[]{:S(2)}, u32[]{:S(2)}) collective-permute-start(bf16[320,1280]{1,0:T(8,128)(2,1)S(1)} %get-tuple-element.31), channel_id=1, source_target_pairs={{2,0},{3,1},{4,6},{5,7},{10,8},{11,9},{12,14},{13,15},{18,16},{19,... | collective-permute-start | bytes 2457608 | tf_op jit(solution)/shard_map/rows_out/ppermute | solution.py:217
  81.3 55.8 %collective-permute-start.11 = (bf16[320,1280]{1,0:T(8,128)(2,1)S(1)}, bf16[320,1280]{1,0:T(8,128)(2,1)S(1)}, u32[]{:S(2)}, u32[]{:S(2)}) collective-permute-start(bf16[320,1280]{1,0:T(8,128)(2,1)S(1)} %get-tuple-element.27), channel_id=1, source_target_pairs={{2,0},{3,1},{4,6},{5,7},{10,8},{11,9},{12,14},{13,15},{18,16},{19,... | collective-permute-start | bytes 2457608 | tf_op jit(solution)/shard_map/rows_out/ppermute | solution.py:217
  118.0 22.9 %collective-permute-start.15 = (bf16[320,1280]{1,0:T(8,128)(2,1)S(1)}, bf16[320,1280]{1,0:T(8,128)(2,1)S(1)}, u32[]{:S(2)}, u32[]{:S(2)}) collective-permute-start(bf16[320,1280]{1,0:T(8,128)(2,1)S(1)} %broadcast_select_fusion), channel_id=1, source_target_pairs={{0,8},{8,0},{16,24},{24,16},{1,9},{9,1},{17,25},{25,17},{2,10},{10... | collective-permute-start | bytes 2457608 | tf_op jit(solution)/shard_map/along_x/ppermute | solution.py:217
  119.5 21.4 %collective-permute-start.16 = (bf16[320,1280]{1,0:T(8,128)(2,1)S(1)}, bf16[320,1280]{1,0:T(8,128)(2,1)S(1)}, u32[]{:S(2)}, u32[]{:S(2)}) collective-permute-start(bf16[320,1280]{1,0:T(8,128)(2,1)S(1)} %broadcast_select_fusion), channel_id=1, source_target_pairs={{0,16},{8,24},{16,0},{24,8},{1,17},{9,25},{17,1},{25,9},{2,18},{10... | collective-permute-start | bytes 2457608 | tf_op jit(solution)/shard_map/along_y/ppermute | solution.py:217
  137.2 20.0 %collective-permute-start.12 = (bf16[320,1280]{1,0:T(8,128)(2,1)S(1)}, bf16[320,1280]{1,0:T(8,128)(2,1)}, u32[]{:S(2)}, u32[]{:S(2)}) collective-permute-start(bf16[320,1280]{1,0:T(8,128)(2,1)S(1)} %broadcast_select_fusion.1), channel_id=1, source_target_pairs={{0,8},{8,0},{16,24},{24,16},{1,9},{9,1},{17,25},{25,17},{2,10},{10... | collective-permute-start | bytes 2457608 | tf_op jit(solution)/shard_map/along_x/ppermute | solution.py:217
  138.8 19.7 %collective-permute-start.13 = (bf16[320,1280]{1,0:T(8,128)(2,1)S(1)}, bf16[320,1280]{1,0:T(8,128)(2,1)}, u32[]{:S(2)}, u32[]{:S(2)}) collective-permute-start(bf16[320,1280]{1,0:T(8,128)(2,1)S(1)} %broadcast_select_fusion.1), channel_id=1, source_target_pairs={{0,16},{8,24},{16,0},{24,8},{1,17},{9,25},{17,1},{25,9},{2,18},{10... | collective-permute-start | bytes 2457608 | tf_op jit(solution)/shard_map/along_y/ppermute | solution.py:217
  158.5 18.7 %collective-permute-start.17 = (bf16[320,1280]{1,0:T(8,128)(2,1)S(1)}, bf16[320,1280]{1,0:T(8,128)(2,1)S(1)}, u32[]{:S(2)}, u32[]{:S(2)}) collective-permute-start(bf16[320,1280]{1,0:T(8,128)(2,1)S(1)} %collective-permute-done.15), channel_id=1, source_target_pairs={{0,16},{8,24},{16,0},{24,8},{1,17},{9,25},{17,1},{25,9},{2,18},{10... | collective-permute-start | bytes 2457608 | tf_op jit(solution)/shard_map/across_y/ppermute | solution.py:217
  160.0 18.6 %collective-permute-start.18 = (bf16[320,1280]{1,0:T(8,128)(2,1)}, bf16[320,1280]{1,0:T(8,128)(2,1)S(1)}, u32[]{:S(2)}, u32[]{:S(2)}) collective-permute-start(bf16[320,1280]{1,0:T(8,128)(2,1)} %collective-permute-done.13), channel_id=1, source_target_pairs={{0,8},{8,0},{16,24},{24,16},{1,9},{9,1},{17,25},{25,17},{2,10},{10... | collective-permute-start | bytes 2457608 | tf_op jit(solution)/shard_map/across_x/ppermute | solution.py:217
  163.2 15.4 %copy-start.4 = (bf16[4,320,2560]{2,1,0:T(8,128)(2,1)}, bf16[4,320,2560]{2,1,0:T(8,128)(2,1)S(1)}, u32[]{:S(2)}) copy-start(bf16[4,320,2560]{2,1,0:T(8,128)(2,1)S(1)} %bitcast_dynamic-update-slice_fusion) | copy-start | bytes 19660804

commit v18 on v17

--- a/solution.py
+++ b/solution.py
@@ -161,15 +161,17 @@
             out_more[...] = both[rows:]
 
 
-def late_products(inner, rows, early, late, gram, cubic, outer_poly=None):
+def late_products(inner, rows, first, early, late, gram, cubic, outer_poly=None):
     blocks = early + late
     count = len(blocks)
     columns = blocks[0].shape[1]
     total = starts(blocks)[-1]
     own = outer_poly is not None
-    half = jax.ShapeDtypeStruct((rows, columns // 2), jnp.bfloat16)
+    part, rest = (
+        jax.ShapeDtypeStruct((rows, width), jnp.bfloat16) for width in (first, columns - first)
+    )
     poly = jax.ShapeDtypeStruct((rows, total), jnp.bfloat16)
-    out_shape = (half,) * 3 if own else (half, poly)
+    out_shape = (part, rest, rest) if own else (part, poly)
     more = [gram, cubic] + ([outer_poly] if own else [])
     scratch = [
         pltpu.VMEM((total, columns), jnp.bfloat16),
@@ -234,9 +236,10 @@
     far_rows[0], gram, cubic = tie((far_rows[0], gram, cubic))
     swapped = swap("far", far_rows[0])
     late = far_rows + [swapped, swap("far_last", far_rows[1])]
-    outer_first, outer_poly = late_products(inner, rows, early, late, gram, cubic)
+    first = columns * 11 // 20
+    outer_first, outer_poly = late_products(inner, rows, first, early, late, gram, cubic)
     own_first, own_second, outer_second = late_products(
-        inner, rows, early, late, gram, cubic, outer_poly
+        inner, rows, first, early, late, gram, cubic, outer_poly
     )
     for_outer, for_own = (outer_first, outer_second), (own_first, own_second)
 
@@ -245,8 +248,8 @@
     def place_in(result, flip, at, part):
         return lax.dynamic_update_slice(result, part[None], (mat ^ flip, 0, at))
 
-    width, corner = columns // 2, [None, None]
-    for k in (1, 0):
+    corner = [None, None]
+    for k in (0, 1):
         returned = move("rows_out", for_outer[k], "shard", outwards)
         mine = tie(jnp.where(outer, returned, for_own[k]))
         by_x = move("along_x", mine, "mat", along_x)
@@ -254,7 +257,7 @@
         by_x, by_y = tie((by_x, by_y))
         corner[k] = (by_x, by_y)[k]
         for flip, part in enumerate((mine, by_x, by_y)):
-            result = place_in(result, flip, k * width, part)
+            result = place_in(result, flip, k * first, part)
     corner = tie(corner)
     corner[0] = move("across_y", corner[0], "mat", along_y)
     corner[1] = move("across_x", corner[1], "mat", along_x)

time: 181 us -> 181 us (level)
  no operation moved by 1% of the time
where the time goes in v18:
time: 181 us; the launch traced here: 180 us
  waiting for transfers between devices  126 us (70%)
  starting transfers between devices  37.7 us (21%)
  local copies, waits for them, and re-layouts  14.6 us (8%)
    ppermute x19, waiting for transfers between devices, move(): return lax.ppermute(block, axis, pairs)  126 us
    ppermute x19, starting transfers between devices, move(): return lax.ppermute(block, axis, pairs)  37.7 us
    unnamed x10, local copies, waits for them, and re-layouts  4.59 us
  transfers between devices with their start and end apart: 19, of which 9 were waited for; matrix products, arithmetic and copies ran while one was open for 6% of the time, Pallas kernels for 0%

profile of v18, /device:TPU:0, one launch (start us, length us, event | category | flops | bytes accessed | tf_op | source)
XLA Modules:
  0.0 180.5 jit_solution(5927536814531257588)
XLA Ops:
  0.8 7.8 %collective-permute-start = (bf16[320,2560]{1,0:T(8,128)(2,1)}, bf16[320,2560]{1,0:T(8,128)(2,1)S(1)}, u32[]{:S(2)}, u32[]{:S(2)}) collective-permute-start(bf16[320,2560]{1,0:T(8,128)(2,1)} %bitcast.23), channel_id=1, source_target_pairs={{0,2},{1,3},{6,4},{7,5},{8,10},{9,11},{14,12},{15,13},{16,18},{17,... | collective-permute-start | bytes 4915208 | tf_op jit(solution)/shard_map/rows_in/ppermute | solution.py:219
  9.3 2.3 %slice_bitcast_fusion = bf16[208,2560]{1,0:T(8,128)(2,1)} fusion(bf16[1,320,2560]{2,1,0:T(8,128)(2,1)} %param.1), kind=kLoop, calls=%fused_computation.2 | loop fusion | bytes 2129920 | tf_op jit(solution)/shard_map/slice | solution.py:228
  11.6 3.2 %collective-permute-start.7 = (bf16[208,2560]{1,0:T(8,128)(2,1)}, bf16[208,2560]{1,0:T(8,128)(2,1)}, u32[]{:S(2)}, u32[]{:S(2)}) collective-permute-start(bf16[208,2560]{1,0:T(8,128)(2,1)} %slice_bitcast_fusion), channel_id=1, source_target_pairs={{0,4},{1,5},{6,2},{7,3},{8,12},{9,13},{14,10},{15,11},{16,20},{17,... | collective-permute-start | bytes 3194888 | tf_op jit(solution)/shard_map/rows_far/ppermute | solution.py:219
  15.8 1.6 collective-permute-start.5
  17.4 27.6 %collective-permute-done.refs_1_ = bf16[320,2560]{1,0:T(8,128)(2,1)S(1)} collective-permute-done((bf16[320,2560]{1,0:T(8,128)(2,1)}, bf16[320,2560]{1,0:T(8,128)(2,1)S(1)}, u32[]{:S(2)}, u32[]{:S(2)}) %collective-permute-start) | collective-permute-done | bytes 1638432 | tf_op jit(solution)/shard_map/rows_in/ppermute | solution.py:219
  45.0 1.3 fusion.1
  46.3 1.6 collective-permute-start.3
  47.8 1.6 collective-permute-start.4
  51.3 2.0 %slice_bitcast_fusion.1 = bf16[112,2560]{1,0:T(8,128)(2,1)} fusion(bf16[1,320,2560]{2,1,0:T(8,128)(2,1)} %param.1), kind=kLoop, calls=%fused_computation.11 | loop fusion | bytes 1146880 | tf_op jit(solution)/shard_map/slice | solution.py:228
  54.2 7.7 %collective-permute-start.8 = (bf16[112,2560]{1,0:T(8,128)(2,1)}, bf16[112,2560]{1,0:T(8,128)(2,1)}, u32[]{:S(2)}, u32[]{:S(2)}) collective-permute-start(bf16[112,2560]{1,0:T(8,128)(2,1)} %slice_bitcast_fusion.1), channel_id=1, source_target_pairs={{0,4},{1,5},{6,2},{7,3},{8,12},{9,13},{14,10},{15,11},{16,20},{17,... | collective-permute-start | bytes 1720328 | tf_op jit(solution)/shard_map/rows_far/ppermute | solution.py:219
  61.9 1.4 copy-done.1
  64.5 3.3 %collective-permute-done.7.refs_9_ = bf16[208,2560]{1,0:T(8,128)(2,1)} collective-permute-done((bf16[208,2560]{1,0:T(8,128)(2,1)}, bf16[208,2560]{1,0:T(8,128)(2,1)}, u32[]{:S(2)}, u32[]{:S(2)}) %collective-permute-start.7) | collective-permute-done | bytes 1064992 | tf_op jit(solution)/shard_map/rows_far/ppermute | solution.py:219
  68.5 10.1 %collective-permute-done.8.refs_10_ = bf16[112,2560]{1,0:T(8,128)(2,1)} collective-permute-done((bf16[112,2560]{1,0:T(8,128)(2,1)}, bf16[112,2560]{1,0:T(8,128)(2,1)}, u32[]{:S(2)}, u32[]{:S(2)}) %collective-permute-start.8) | collective-permute-done | bytes 573472 | tf_op jit(solution)/shard_map/rows_far/ppermute | solution.py:219
  79.7 1.3 collective-permute-start.11
  82.6 37.7 %collective-permute-done.11 = bf16[320,1408]{1,0:T(8,128)(2,1)S(1)} collective-permute-done((bf16[320,1408]{1,0:T(8,128)(2,1)S(1)}, bf16[320,1408]{1,0:T(8,128)(2,1)S(1)}, u32[]{:S(2)}, u32[]{:S(2)}) %collective-permute-start.11) | collective-permute-done | bytes 901152 | tf_op jit(solution)/shard_map/rows_out/ppermute | solution.py:219
  120.4 1.5 collective-permute-start.12
  122.0 1.5 collective-permute-start.13
  123.5 12.4 %collective-permute-done.14 = bf16[320,1152]{1,0:T(8,128)(2,1)S(1)} collective-permute-done((bf16[320,1152]{1,0:T(8,128)(2,1)S(1)}, bf16[320,1152]{1,0:T(8,128)(2,1)S(1)}, u32[]{:S(2)}, u32[]{:S(2)}) %collective-permute-start.14) | collective-permute-done | bytes 737312 | tf_op jit(solution)/shard_map/rows_out/ppermute | solution.py:219
  136.0 1.5 collective-permute-start.15
  137.5 1.5 collective-permute-start.16
  139.7 18.1 %collective-permute-done.15 = bf16[320,1152]{1,0:T(8,128)(2,1)} collective-permute-done((bf16[320,1152]{1,0:T(8,128)(2,1)S(1)}, bf16[320,1152]{1,0:T(8,128)(2,1)}, u32[]{:S(2)}, u32[]{:S(2)}) %collective-permute-start.15) | collective-permute-done | bytes 737312 | tf_op jit(solution)/shard_map/along_x/ppermute | solution.py:219
  159.0 1.5 collective-permute-start.17
  163.9 13.3 %collective-permute-done.18 = bf16[320,1152]{1,0:T(8,128)(2,1)S(1)} collective-permute-done((bf16[320,1152]{1,0:T(8,128)(2,1)}, bf16[320,1152]{1,0:T(8,128)(2,1)S(1)}, u32[]{:S(2)}, u32[]{:S(2)}) %collective-permute-start.18) | collective-permute-done | bytes 737312 | tf_op jit(solution)/shard_map/across_x/ppermute | solution.py:219
  177.1 2.1 %collective-permute-done.17 = bf16[320,1408]{1,0:T(8,128)(2,1)S(1)} collective-permute-done((bf16[320,1408]{1,0:T(8,128)(2,1)S(1)}, bf16[320,1408]{1,0:T(8,128)(2,1)S(1)}, u32[]{:S(2)}, u32[]{:S(2)}) %collective-permute-start.17) | collective-permute-done | bytes 901152 | tf_op jit(solution)/shard_map/across_y/ppermute | solution.py:219
  (42 shorter events, 16.5 us)
Async XLA Ops:
  0.0 14.8 %collective-permute-start.2 = (bf16[320,2560]{1,0:T(8,128)(2,1)}, bf16[320,2560]{1,0:T(8,128)(2,1)S(1)}, u32[]{:S(2)}, u32[]{:S(2)}) collective-permute-start(bf16[320,2560]{1,0:T(8,128)(2,1)} %bitcast.22), channel_id=1, source_target_pairs={{2,4},{3,5},{4,2},{5,3},{10,12},{11,13},{12,10},{13,11},{18,20},{1... | collective-permute-start | bytes 4915208 | tf_op jit(solution)/shard_map/middle/ppermute | solution.py:219
  0.8 44.2 %collective-permute-start = (bf16[320,2560]{1,0:T(8,128)(2,1)}, bf16[320,2560]{1,0:T(8,128)(2,1)S(1)}, u32[]{:S(2)}, u32[]{:S(2)}) collective-permute-start(bf16[320,2560]{1,0:T(8,128)(2,1)} %bitcast.23), channel_id=1, source_target_pairs={{0,2},{1,3},{6,4},{7,5},{8,10},{9,11},{14,12},{15,13},{16,18},{17,... | collective-permute-start | bytes 4915208 | tf_op jit(solution)/shard_map/rows_in/ppermute | solution.py:219
  8.5 40.9 %collective-permute-start.1 = (bf16[320,2560]{1,0:T(8,128)(2,1)}, bf16[320,2560]{1,0:T(8,128)(2,1)S(1)}, u32[]{:S(2)}, u32[]{:S(2)}) collective-permute-start(bf16[320,2560]{1,0:T(8,128)(2,1)} %bitcast.24), channel_id=1, source_target_pairs={{2,3},{3,2},{4,5},{5,4},{10,11},{11,10},{12,13},{13,12},{18,19},{1... | collective-permute-start | bytes 4915208 | tf_op jit(solution)/shard_map/swap_own/ppermute | solution.py:219
  11.6 56.2 %collective-permute-start.7 = (bf16[208,2560]{1,0:T(8,128)(2,1)}, bf16[208,2560]{1,0:T(8,128)(2,1)}, u32[]{:S(2)}, u32[]{:S(2)}) collective-permute-start(bf16[208,2560]{1,0:T(8,128)(2,1)} %slice_bitcast_fusion), channel_id=1, source_target_pairs={{0,4},{1,5},{6,2},{7,3},{8,12},{9,13},{14,10},{15,11},{16,20},{17,... | collective-permute-start | bytes 3194888 | tf_op jit(solution)/shard_map/rows_far/ppermute | solution.py:219
  15.8 46.0 %collective-permute-start.5 = (bf16[176,2560]{1,0:T(8,128)(2,1)}, bf16[176,2560]{1,0:T(8,128)(2,1)}, u32[]{:S(2)}, u32[]{:S(2)}) collective-permute-start(bf16[176,2560]{1,0:T(8,128)(2,1)} %slice.34), channel_id=1, source_target_pairs={{2,3},{3,2},{4,5},{5,4},{10,11},{11,10},{12,13},{13,12},{18,19},{1... | collective-permute-start | bytes 2703368 | tf_op jit(solution)/shard_map/swap_rows/ppermute | solution.py:219
  46.3 15.6 %collective-permute-start.3 = (bf16[160,2560]{1,0:T(8,128)(2,1)}, bf16[160,2560]{1,0:T(8,128)(2,1)}, u32[]{:S(2)}, u32[]{:S(2)}) collective-permute-start(bf16[160,2560]{1,0:T(8,128)(2,1)} %get-tuple-element.38), channel_id=1, source_target_pairs={{2,3},{3,2},{4,5},{5,4},{10,11},{11,10},{12,13},{13,12},{18,19},{1... | collective-permute-start | bytes 2457608 | tf_op jit(solution)/shard_map/swap_rows/ppermute | solution.py:219
  47.8 14.0 %collective-permute-start.4 = (bf16[160,2560]{1,0:T(8,128)(2,1)}, bf16[160,2560]{1,0:T(8,128)(2,1)}, u32[]{:S(2)}, u32[]{:S(2)}) collective-permute-start(bf16[160,2560]{1,0:T(8,128)(2,1)} %get-tuple-element.37), channel_id=1, source_target_pairs={{2,3},{3,2},{4,5},{5,4},{10,11},{11,10},{12,13},{13,12},{18,19},{1... | collective-permute-start | bytes 2457608 | tf_op jit(solution)/shard_map/swap_rows/ppermute | solution.py:219
  49.5 1.2 copy-start
  50.6 2.7 %collective-permute-start.6 = (bf16[144,2560]{1,0:T(8,128)(2,1)S(1)}, bf16[144,2560]{1,0:T(8,128)(2,1)S(1)}, u32[]{:S(2)}, u32[]{:S(2)}) collective-permute-start(bf16[144,2560]{1,0:T(8,128)(2,1)S(1)} %slice.35), channel_id=1, source_target_pairs={{2,3},{3,2},{4,5},{5,4},{10,11},{11,10},{12,13},{13,12},{18,19},{1... | collective-permute-start | bytes 2211848 | tf_op jit(solution)/shard_map/swap_rows/ppermute | solution.py:219
  53.3 0.9 copy-start.2
  54.2 24.4 %collective-permute-start.8 = (bf16[112,2560]{1,0:T(8,128)(2,1)}, bf16[112,2560]{1,0:T(8,128)(2,1)}, u32[]{:S(2)}, u32[]{:S(2)}) collective-permute-start(bf16[112,2560]{1,0:T(8,128)(2,1)} %slice_bitcast_fusion.1), channel_id=1, source_target_pairs={{0,4},{1,5},{6,2},{7,3},{8,12},{9,13},{14,10},{15,11},{16,20},{17,... | collective-permute-start | bytes 1720328 | tf_op jit(solution)/shard_map/rows_far/ppermute | solution.py:219
  61.9 1.4 copy-start.1
  63.3 1.1 copy-start.3
  67.8 11.5 %collective-permute-start.9 = (bf16[208,2560]{1,0:T(8,128)(2,1)}, bf16[208,2560]{1,0:T(8,128)(2,1)S(1)}, u32[]{:S(2)}, u32[]{:S(2)}) collective-permute-start(bf16[208,2560]{1,0:T(8,128)(2,1)} %collective-permute-done.7.refs_9_), channel_id=1, source_target_pairs={{2,3},{3,2},{4,5},{5,4},{10,11},{11,10},{12,13},{13,12},{18,19},{1... | collective-permute-start | bytes 3194888 | tf_op jit(solution)/shard_map/swap_far/ppermute | solution.py:219
  78.6 0.7 collective-permute-start.10
  79.7 40.7 %collective-permute-start.11 = (bf16[320,1408]{1,0:T(8,128)(2,1)S(1)}, bf16[320,1408]{1,0:T(8,128)(2,1)S(1)}, u32[]{:S(2)}, u32[]{:S(2)}) collective-permute-start(bf16[320,1408]{1,0:T(8,128)(2,1)S(1)} %get-tuple-element.26), channel_id=1, source_target_pairs={{2,0},{3,1},{4,6},{5,7},{10,8},{11,9},{12,14},{13,15},{18,16},{19,... | collective-permute-start | bytes 2703368 | tf_op jit(solution)/shard_map/rows_out/ppermute | solution.py:219
  81.3 54.6 %collective-permute-start.14 = (bf16[320,1152]{1,0:T(8,128)(2,1)S(1)}, bf16[320,1152]{1,0:T(8,128)(2,1)S(1)}, u32[]{:S(2)}, u32[]{:S(2)}) collective-permute-start(bf16[320,1152]{1,0:T(8,128)(2,1)S(1)} %get-tuple-element.31), channel_id=1, source_target_pairs={{2,0},{3,1},{4,6},{5,7},{10,8},{11,9},{12,14},{13,15},{18,16},{19,... | collective-permute-start | bytes 2211848 | tf_op jit(solution)/shard_map/rows_out/ppermute | solution.py:219
  120.4 38.6 %collective-permute-start.12 = (bf16[320,1408]{1,0:T(8,128)(2,1)S(1)}, bf16[320,1408]{1,0:T(8,128)(2,1)S(1)}, u32[]{:S(2)}, u32[]{:S(2)}) collective-permute-start(bf16[320,1408]{1,0:T(8,128)(2,1)S(1)} %broadcast_select_fusion), channel_id=1, source_target_pairs={{0,8},{8,0},{16,24},{24,16},{1,9},{9,1},{17,25},{25,17},{2,10},{10... | collective-permute-start | bytes 2703368 | tf_op jit(solution)/shard_map/along_x/ppermute | solution.py:219
  122.0 37.0 %collective-permute-start.13 = (bf16[320,1408]{1,0:T(8,128)(2,1)S(1)}, bf16[320,1408]{1,0:T(8,128)(2,1)S(1)}, u32[]{:S(2)}, u32[]{:S(2)}) collective-permute-start(bf16[320,1408]{1,0:T(8,128)(2,1)S(1)} %broadcast_select_fusion), channel_id=1, source_target_pairs={{0,16},{8,24},{16,0},{24,8},{1,17},{9,25},{17,1},{25,9},{2,18},{10... | collective-permute-start | bytes 2703368 | tf_op jit(solution)/shard_map/along_y/ppermute | solution.py:219
  136.0 21.8 %collective-permute-start.15 = (bf16[320,1152]{1,0:T(8,128)(2,1)S(1)}, bf16[320,1152]{1,0:T(8,128)(2,1)}, u32[]{:S(2)}, u32[]{:S(2)}) collective-permute-start(bf16[320,1152]{1,0:T(8,128)(2,1)S(1)} %broadcast_select_fusion.1), channel_id=1, source_target_pairs={{0,8},{8,0},{16,24},{24,16},{1,9},{9,1},{17,25},{25,17},{2,10},{10... | collective-permute-start | bytes 2211848 | tf_op jit(solution)/shard_map/along_x/ppermute | solution.py:219
  137.5 21.5 %collective-permute-start.16 = (bf16[320,1152]{1,0:T(8,128)(2,1)S(1)}, bf16[320,1152]{1,0:T(8,128)(2,1)}, u32[]{:S(2)}, u32[]{:S(2)}) collective-permute-start(bf16[320,1152]{1,0:T(8,128)(2,1)S(1)} %broadcast_select_fusion.1), channel_id=1, source_target_pairs={{0,16},{8,24},{16,0},{24,8},{1,17},{9,25},{17,1},{25,9},{2,18},{10... | collective-permute-start | bytes 2211848 | tf_op jit(solution)/shard_map/along_y/ppermute | solution.py:219
  159.0 20.2 %collective-permute-start.17 = (bf16[320,1408]{1,0:T(8,128)(2,1)S(1)}, bf16[320,1408]{1,0:T(8,128)(2,1)S(1)}, u32[]{:S(2)}, u32[]{:S(2)}) collective-permute-start(bf16[320,1408]{1,0:T(8,128)(2,1)S(1)} %collective-permute-done.12), channel_id=1, source_target_pairs={{0,16},{8,24},{16,0},{24,8},{1,17},{9,25},{17,1},{25,9},{2,18},{10... | collective-permute-start | bytes 2703368 | tf_op jit(solution)/shard_map/across_y/ppermute | solution.py:219
  160.5 16.6 %collective-permute-start.18 = (bf16[320,1152]{1,0:T(8,128)(2,1)}, bf16[320,1152]{1,0:T(8,128)(2,1)S(1)}, u32[]{:S(2)}, u32[]{:S(2)}) collective-permute-start(bf16[320,1152]{1,0:T(8,128)(2,1)} %collective-permute-done.16), channel_id=1, source_target_pairs={{0,8},{8,0},{16,24},{24,16},{1,9},{9,1},{17,25},{25,17},{2,10},{10... | collective-permute-start | bytes 2211848 | tf_op jit(solution)/shard_map/across_x/ppermute | solution.py:219
  163.9 15.3 %copy-start.4 = (bf16[4,320,2560]{2,1,0:T(8,128)(2,1)}, bf16[4,320,2560]{2,1,0:T(8,128)(2,1)S(1)}, u32[]{:S(2)}) copy-start(bf16[4,320,2560]{2,1,0:T(8,128)(2,1)S(1)} %bitcast_dynamic-update-slice_fusion.3) | copy-start | bytes 19660804

commit v19 on v17

--- a/solution.py
+++ b/solution.py
@@ -11,7 +11,7 @@
 coef_b = -4.775
 coef_c = 2.0315
 
-TILE = 1024
+TILE = 512
 VMEM_LIMIT = 30 * 1024 * 1024
 
 
@@ -60,9 +60,10 @@
 
     @pl.when(inner[0] != 0)
     def _():
-        for copy in fetch_blocks(blocks, whole, sems):
-            copy.wait()
+        copies = fetch_blocks(blocks, whole, sems)
         for at in tiles(0, whole.shape[0]):
+            while copies and starts(blocks)[count - len(copies)] < at.start + at.size:
+                copies.pop(0).wait()
             gram[:, at] = dot_t(whole[left, :], whole[at, :]).astype(jnp.bfloat16)
         for at in tiles(0, whole.shape[1]):
             cubic[:, at] = dot(gram[...], whole[:, at])
@@ -226,10 +227,13 @@
         move("rows_far", part, "shard", across_middle) for part in (own[:cut], own[cut:])
     ]
 
-    own_kept = pltpu.with_memory_space_constraint(own, pltpu.HBM)
-    early = [outer_rows, own_kept, swap("own", own), inner_rows]
+    def kept(block):
+        return pltpu.with_memory_space_constraint(block, pltpu.HBM)
+
+    early = [outer_rows, kept(own), kept(swap("own", own)), inner_rows]
     for block, at in ((outer_rows, rows // 2), (inner_rows, rows * 11 // 20)):
         early += [swap("rows", part) for part in (block[:at], block[at:])]
+    early[-1] = kept(early[-1])
     gram, cubic = early_products(inner, rows, early)
     far_rows[0], gram, cubic = tie((far_rows[0], gram, cubic))
     swapped = swap("far", far_rows[0])
@@ -255,7 +259,6 @@
         corner[k] = (by_x, by_y)[k]
         for flip, part in enumerate((mine, by_x, by_y)):
             result = place_in(result, flip, k * width, part)
-    corner = tie(corner)
     corner[0] = move("across_y", corner[0], "mat", along_y)
     corner[1] = move("across_x", corner[1], "mat", along_x)
     result = place_in(result, 3, 0, jnp.concatenate(corner, axis=1))

time: 181 us -> 181 us (level)
  waiting for transfers between devices: 125 us -> 130 us
  local copies, waits for them, and re-layouts: 14.4 us -> 9.68 us
    ppermute x19, waiting for transfers between devices: 125 us -> 130 us  [move(): return lax.ppermute(block, axis, pairs)]
    unnamed x10 -> x2, local copies, waits for them, and re-layouts: 4.59 us -> 0.01 us
  transfers between devices with their start and end apart: 19 -> 19, of which waited for: 9 -> 8; matrix products, arithmetic and copies ran while one was open for 6% -> 5% of each run, Pallas kernels for 0% -> 0%
where the time goes in v19:
time: 181 us; the launch traced here: 180 us
  waiting for transfers between devices  130 us (72%)
  starting transfers between devices  38.2 us (21%)
  local copies, waits for them, and re-layouts  9.68 us (5%)
    ppermute x19, waiting for transfers between devices, move(): return lax.ppermute(block, axis, pairs)  130 us
    ppermute x19, starting transfers between devices, move(): return lax.ppermute(block, axis, pairs)  38.2 us
  transfers between devices with their start and end apart: 19, of which 8 were waited for; matrix products, arithmetic and copies ran while one was open for 5% of the time, Pallas kernels for 0%

profile of v19, /device:TPU:0, one launch (start us, length us, event | category | flops | bytes accessed | tf_op | source)
XLA Modules:
  0.0 180.4 jit_solution(6354405576679390078)
XLA Ops:
  0.8 7.8 %collective-permute-start = (bf16[320,2560]{1,0:T(8,128)(2,1)}, bf16[320,2560]{1,0:T(8,128)(2,1)S(1)}, u32[]{:S(2)}, u32[]{:S(2)}) collective-permute-start(bf16[320,2560]{1,0:T(8,128)(2,1)} %bitcast.23), channel_id=1, source_target_pairs={{0,2},{1,3},{6,4},{7,5},{8,10},{9,11},{14,12},{15,13},{16,18},{17,... | collective-permute-start | bytes 4915208 | tf_op jit(solution)/shard_map/rows_in/ppermute | solution.py:218
  8.5 1.9 %collective-permute-start.1 = (bf16[320,2560]{1,0:T(8,128)(2,1)}, bf16[320,2560]{1,0:T(8,128)(2,1)}, u32[]{:S(2)}, u32[]{:S(2)}) collective-permute-start(bf16[320,2560]{1,0:T(8,128)(2,1)} %bitcast.24), channel_id=1, source_target_pairs={{2,3},{3,2},{4,5},{5,4},{10,11},{11,10},{12,13},{13,12},{18,19},{1... | collective-permute-start | bytes 4915208 | tf_op jit(solution)/shard_map/swap_own/ppermute | solution.py:218
  10.4 2.3 %slice_bitcast_fusion = bf16[208,2560]{1,0:T(8,128)(2,1)} fusion(bf16[1,320,2560]{2,1,0:T(8,128)(2,1)} %param.1), kind=kLoop, calls=%fused_computation.2 | loop fusion | bytes 2129920 | tf_op jit(solution)/shard_map/slice | solution.py:227
  12.7 2.3 %collective-permute-start.7 = (bf16[208,2560]{1,0:T(8,128)(2,1)}, bf16[208,2560]{1,0:T(8,128)(2,1)}, u32[]{:S(2)}, u32[]{:S(2)}) collective-permute-start(bf16[208,2560]{1,0:T(8,128)(2,1)} %slice_bitcast_fusion), channel_id=1, source_target_pairs={{0,4},{1,5},{6,2},{7,3},{8,12},{9,13},{14,10},{15,11},{16,20},{17,... | collective-permute-start | bytes 3194888 | tf_op jit(solution)/shard_map/rows_far/ppermute | solution.py:218
  15.9 1.6 collective-permute-start.5
  17.5 27.4 %collective-permute-done.refs_1_ = bf16[320,2560]{1,0:T(8,128)(2,1)S(1)} collective-permute-done((bf16[320,2560]{1,0:T(8,128)(2,1)}, bf16[320,2560]{1,0:T(8,128)(2,1)S(1)}, u32[]{:S(2)}, u32[]{:S(2)}) %collective-permute-start) | collective-permute-done | bytes 1638432 | tf_op jit(solution)/shard_map/rows_in/ppermute | solution.py:218
  46.2 1.6 collective-permute-start.3
  47.8 1.6 collective-permute-start.4
  49.5 1.6 collective-permute-start.6
  51.1 1.9 %slice_bitcast_fusion.1 = bf16[112,2560]{1,0:T(8,128)(2,1)} fusion(bf16[1,320,2560]{2,1,0:T(8,128)(2,1)} %param.1), kind=kLoop, calls=%fused_computation.11 | loop fusion | bytes 1146880 | tf_op jit(solution)/shard_map/slice | solution.py:227
  53.0 7.0 %collective-permute-start.8 = (bf16[112,2560]{1,0:T(8,128)(2,1)}, bf16[112,2560]{1,0:T(8,128)(2,1)}, u32[]{:S(2)}, u32[]{:S(2)}) collective-permute-start(bf16[112,2560]{1,0:T(8,128)(2,1)} %slice_bitcast_fusion.1), channel_id=1, source_target_pairs={{0,4},{1,5},{6,2},{7,3},{8,12},{9,13},{14,10},{15,11},{16,20},{17,... | collective-permute-start | bytes 1720328 | tf_op jit(solution)/shard_map/rows_far/ppermute | solution.py:218
  60.0 7.7 %collective-permute-done.7.refs_9_ = bf16[208,2560]{1,0:T(8,128)(2,1)} collective-permute-done((bf16[208,2560]{1,0:T(8,128)(2,1)}, bf16[208,2560]{1,0:T(8,128)(2,1)}, u32[]{:S(2)}, u32[]{:S(2)}) %collective-permute-start.7) | collective-permute-done | bytes 1064992 | tf_op jit(solution)/shard_map/rows_far/ppermute | solution.py:218
  68.5 10.1 %collective-permute-done.8.refs_10_ = bf16[112,2560]{1,0:T(8,128)(2,1)} collective-permute-done((bf16[112,2560]{1,0:T(8,128)(2,1)}, bf16[112,2560]{1,0:T(8,128)(2,1)}, u32[]{:S(2)}, u32[]{:S(2)}) %collective-permute-start.8) | collective-permute-done | bytes 573472 | tf_op jit(solution)/shard_map/rows_far/ppermute | solution.py:218
  79.7 1.3 collective-permute-start.14
  81.3 1.3 collective-permute-start.11
  82.6 34.5 %collective-permute-done.14 = bf16[320,1280]{1,0:T(8,128)(2,1)S(1)} collective-permute-done((bf16[320,1280]{1,0:T(8,128)(2,1)S(1)}, bf16[320,1280]{1,0:T(8,128)(2,1)S(1)}, u32[]{:S(2)}, u32[]{:S(2)}) %collective-permute-start.14) | collective-permute-done | bytes 819232 | tf_op jit(solution)/shard_map/rows_out/ppermute | solution.py:218
  117.3 1.5 collective-permute-start.15
  118.8 1.5 collective-permute-start.16
  120.3 16.1 %collective-permute-done.11 = bf16[320,1280]{1,0:T(8,128)(2,1)S(1)} collective-permute-done((bf16[320,1280]{1,0:T(8,128)(2,1)S(1)}, bf16[320,1280]{1,0:T(8,128)(2,1)S(1)}, u32[]{:S(2)}, u32[]{:S(2)}) %collective-permute-start.11) | collective-permute-done | bytes 819232 | tf_op jit(solution)/shard_map/rows_out/ppermute | solution.py:218
  136.5 1.5 collective-permute-start.12
  138.1 1.5 collective-permute-start.13
  140.2 16.3 %collective-permute-done.12 = bf16[320,1280]{1,0:T(8,128)(2,1)} collective-permute-done((bf16[320,1280]{1,0:T(8,128)(2,1)S(1)}, bf16[320,1280]{1,0:T(8,128)(2,1)}, u32[]{:S(2)}, u32[]{:S(2)}) %collective-permute-start.12) | collective-permute-done | bytes 819232 | tf_op jit(solution)/shard_map/along_x/ppermute | solution.py:218
  160.7 1.6 collective-permute-start.17
  162.4 16.7 %collective-permute-done.17 = bf16[320,1280]{1,0:T(8,128)(2,1)S(1)} collective-permute-done((bf16[320,1280]{1,0:T(8,128)(2,1)S(1)}, bf16[320,1280]{1,0:T(8,128)(2,1)S(1)}, u32[]{:S(2)}, u32[]{:S(2)}) %collective-permute-start.17) | collective-permute-done | bytes 819232 | tf_op jit(solution)/shard_map/across_y/ppermute | solution.py:218
  (34 shorter events, 11.7 us)
Async XLA Ops:
  0.0 14.9 %collective-permute-start.2 = (bf16[320,2560]{1,0:T(8,128)(2,1)}, bf16[320,2560]{1,0:T(8,128)(2,1)S(1)}, u32[]{:S(2)}, u32[]{:S(2)}) collective-permute-start(bf16[320,2560]{1,0:T(8,128)(2,1)} %bitcast.22), channel_id=1, source_target_pairs={{2,4},{3,5},{4,2},{5,3},{10,12},{11,13},{12,10},{13,11},{18,20},{1... | collective-permute-start | bytes 4915208 | tf_op jit(solution)/shard_map/middle/ppermute | solution.py:218
  0.8 44.2 %collective-permute-start = (bf16[320,2560]{1,0:T(8,128)(2,1)}, bf16[320,2560]{1,0:T(8,128)(2,1)S(1)}, u32[]{:S(2)}, u32[]{:S(2)}) collective-permute-start(bf16[320,2560]{1,0:T(8,128)(2,1)} %bitcast.23), channel_id=1, source_target_pairs={{0,2},{1,3},{6,4},{7,5},{8,10},{9,11},{14,12},{15,13},{16,18},{17,... | collective-permute-start | bytes 4915208 | tf_op jit(solution)/shard_map/rows_in/ppermute | solution.py:218
  8.5 40.9 %collective-permute-start.1 = (bf16[320,2560]{1,0:T(8,128)(2,1)}, bf16[320,2560]{1,0:T(8,128)(2,1)}, u32[]{:S(2)}, u32[]{:S(2)}) collective-permute-start(bf16[320,2560]{1,0:T(8,128)(2,1)} %bitcast.24), channel_id=1, source_target_pairs={{2,3},{3,2},{4,5},{5,4},{10,11},{11,10},{12,13},{13,12},{18,19},{1... | collective-permute-start | bytes 4915208 | tf_op jit(solution)/shard_map/swap_own/ppermute | solution.py:218
  12.7 55.1 %collective-permute-start.7 = (bf16[208,2560]{1,0:T(8,128)(2,1)}, bf16[208,2560]{1,0:T(8,128)(2,1)}, u32[]{:S(2)}, u32[]{:S(2)}) collective-permute-start(bf16[208,2560]{1,0:T(8,128)(2,1)} %slice_bitcast_fusion), channel_id=1, source_target_pairs={{0,4},{1,5},{6,2},{7,3},{8,12},{9,13},{14,10},{15,11},{16,20},{17,... | collective-permute-start | bytes 3194888 | tf_op jit(solution)/shard_map/rows_far/ppermute | solution.py:218
  15.9 44.0 %collective-permute-start.5 = (bf16[176,2560]{1,0:T(8,128)(2,1)}, bf16[176,2560]{1,0:T(8,128)(2,1)}, u32[]{:S(2)}, u32[]{:S(2)}) collective-permute-start(bf16[176,2560]{1,0:T(8,128)(2,1)} %slice.34), channel_id=1, source_target_pairs={{2,3},{3,2},{4,5},{5,4},{10,11},{11,10},{12,13},{13,12},{18,19},{1... | collective-permute-start | bytes 2703368 | tf_op jit(solution)/shard_map/swap_rows/ppermute | solution.py:218
  46.2 13.7 %collective-permute-start.3 = (bf16[160,2560]{1,0:T(8,128)(2,1)}, bf16[160,2560]{1,0:T(8,128)(2,1)}, u32[]{:S(2)}, u32[]{:S(2)}) collective-permute-start(bf16[160,2560]{1,0:T(8,128)(2,1)} %get-tuple-element.34), channel_id=1, source_target_pairs={{2,3},{3,2},{4,5},{5,4},{10,11},{11,10},{12,13},{13,12},{18,19},{1... | collective-permute-start | bytes 2457608 | tf_op jit(solution)/shard_map/swap_rows/ppermute | solution.py:218
  47.8 12.1 %collective-permute-start.4 = (bf16[160,2560]{1,0:T(8,128)(2,1)}, bf16[160,2560]{1,0:T(8,128)(2,1)}, u32[]{:S(2)}, u32[]{:S(2)}) collective-permute-start(bf16[160,2560]{1,0:T(8,128)(2,1)} %get-tuple-element.33), channel_id=1, source_target_pairs={{2,3},{3,2},{4,5},{5,4},{10,11},{11,10},{12,13},{13,12},{18,19},{1... | collective-permute-start | bytes 2457608 | tf_op jit(solution)/shard_map/swap_rows/ppermute | solution.py:218
  49.5 3.5 %collective-permute-start.6 = (bf16[144,2560]{1,0:T(8,128)(2,1)S(1)}, bf16[144,2560]{1,0:T(8,128)(2,1)}, u32[]{:S(2)}, u32[]{:S(2)}) collective-permute-start(bf16[144,2560]{1,0:T(8,128)(2,1)S(1)} %slice.35), channel_id=1, source_target_pairs={{2,3},{3,2},{4,5},{5,4},{10,11},{11,10},{12,13},{13,12},{18,19},{1... | collective-permute-start | bytes 2211848 | tf_op jit(solution)/shard_map/swap_rows/ppermute | solution.py:218
  53.0 25.6 %collective-permute-start.8 = (bf16[112,2560]{1,0:T(8,128)(2,1)}, bf16[112,2560]{1,0:T(8,128)(2,1)}, u32[]{:S(2)}, u32[]{:S(2)}) collective-permute-start(bf16[112,2560]{1,0:T(8,128)(2,1)} %slice_bitcast_fusion.1), channel_id=1, source_target_pairs={{0,4},{1,5},{6,2},{7,3},{8,12},{9,13},{14,10},{15,11},{16,20},{17,... | collective-permute-start | bytes 1720328 | tf_op jit(solution)/shard_map/rows_far/ppermute | solution.py:218
  67.8 11.5 %collective-permute-start.9 = (bf16[208,2560]{1,0:T(8,128)(2,1)}, bf16[208,2560]{1,0:T(8,128)(2,1)S(1)}, u32[]{:S(2)}, u32[]{:S(2)}) collective-permute-start(bf16[208,2560]{1,0:T(8,128)(2,1)} %collective-permute-done.7.refs_9_), channel_id=1, source_target_pairs={{2,3},{3,2},{4,5},{5,4},{10,11},{11,10},{12,13},{13,12},{18,19},{1... | collective-permute-start | bytes 3194888 | tf_op jit(solution)/shard_map/swap_far/ppermute | solution.py:218
  78.6 0.7 collective-permute-start.10
  79.7 37.5 %collective-permute-start.14 = (bf16[320,1280]{1,0:T(8,128)(2,1)S(1)}, bf16[320,1280]{1,0:T(8,128)(2,1)S(1)}, u32[]{:S(2)}, u32[]{:S(2)}) collective-permute-start(bf16[320,1280]{1,0:T(8,128)(2,1)S(1)} %get-tuple-element.29), channel_id=1, source_target_pairs={{2,0},{3,1},{4,6},{5,7},{10,8},{11,9},{12,14},{13,15},{18,16},{19,... | collective-permute-start | bytes 2457608 | tf_op jit(solution)/shard_map/rows_out/ppermute | solution.py:218
  81.3 55.1 %collective-permute-start.11 = (bf16[320,1280]{1,0:T(8,128)(2,1)S(1)}, bf16[320,1280]{1,0:T(8,128)(2,1)S(1)}, u32[]{:S(2)}, u32[]{:S(2)}) collective-permute-start(bf16[320,1280]{1,0:T(8,128)(2,1)S(1)} %get-tuple-element.25), channel_id=1, source_target_pairs={{2,0},{3,1},{4,6},{5,7},{10,8},{11,9},{12,14},{13,15},{18,16},{19,... | collective-permute-start | bytes 2457608 | tf_op jit(solution)/shard_map/rows_out/ppermute | solution.py:218
  117.3 22.9 %collective-permute-start.15 = (bf16[320,1280]{1,0:T(8,128)(2,1)S(1)}, bf16[320,1280]{1,0:T(8,128)(2,1)S(1)}, u32[]{:S(2)}, u32[]{:S(2)}) collective-permute-start(bf16[320,1280]{1,0:T(8,128)(2,1)S(1)} %broadcast_select_fusion), channel_id=1, source_target_pairs={{0,8},{8,0},{16,24},{24,16},{1,9},{9,1},{17,25},{25,17},{2,10},{10... | collective-permute-start | bytes 2457608 | tf_op jit(solution)/shard_map/along_x/ppermute | solution.py:218
  118.8 21.4 %collective-permute-start.16 = (bf16[320,1280]{1,0:T(8,128)(2,1)S(1)}, bf16[320,1280]{1,0:T(8,128)(2,1)S(1)}, u32[]{:S(2)}, u32[]{:S(2)}) collective-permute-start(bf16[320,1280]{1,0:T(8,128)(2,1)S(1)} %broadcast_select_fusion), channel_id=1, source_target_pairs={{0,16},{8,24},{16,0},{24,8},{1,17},{9,25},{17,1},{25,9},{2,18},{10... | collective-permute-start | bytes 2457608 | tf_op jit(solution)/shard_map/along_y/ppermute | solution.py:218
  136.5 19.9 %collective-permute-start.12 = (bf16[320,1280]{1,0:T(8,128)(2,1)S(1)}, bf16[320,1280]{1,0:T(8,128)(2,1)}, u32[]{:S(2)}, u32[]{:S(2)}) collective-permute-start(bf16[320,1280]{1,0:T(8,128)(2,1)S(1)} %broadcast_select_fusion.1), channel_id=1, source_target_pairs={{0,8},{8,0},{16,24},{24,16},{1,9},{9,1},{17,25},{25,17},{2,10},{10... | collective-permute-start | bytes 2457608 | tf_op jit(solution)/shard_map/along_x/ppermute | solution.py:218
  138.1 19.6 %collective-permute-start.13 = (bf16[320,1280]{1,0:T(8,128)(2,1)S(1)}, bf16[320,1280]{1,0:T(8,128)(2,1)}, u32[]{:S(2)}, u32[]{:S(2)}) collective-permute-start(bf16[320,1280]{1,0:T(8,128)(2,1)S(1)} %broadcast_select_fusion.1), channel_id=1, source_target_pairs={{0,16},{8,24},{16,0},{24,8},{1,17},{9,25},{17,1},{25,9},{2,18},{10... | collective-permute-start | bytes 2457608 | tf_op jit(solution)/shard_map/along_y/ppermute | solution.py:218
  157.6 21.4 %collective-permute-start.18 = (bf16[320,1280]{1,0:T(8,128)(2,1)}, bf16[320,1280]{1,0:T(8,128)(2,1)S(1)}, u32[]{:S(2)}, u32[]{:S(2)}) collective-permute-start(bf16[320,1280]{1,0:T(8,128)(2,1)} %collective-permute-done.13), channel_id=1, source_target_pairs={{0,8},{8,0},{16,24},{24,16},{1,9},{9,1},{17,25},{25,17},{2,10},{10... | collective-permute-start | bytes 2457608 | tf_op jit(solution)/shard_map/across_x/ppermute | solution.py:218
  160.7 18.4 %collective-permute-start.17 = (bf16[320,1280]{1,0:T(8,128)(2,1)S(1)}, bf16[320,1280]{1,0:T(8,128)(2,1)S(1)}, u32[]{:S(2)}, u32[]{:S(2)}) collective-permute-start(bf16[320,1280]{1,0:T(8,128)(2,1)S(1)} %collective-permute-done.15), channel_id=1, source_target_pairs={{0,16},{8,24},{16,0},{24,8},{1,17},{9,25},{17,1},{25,9},{2,18},{10... | collective-permute-start | bytes 2457608 | tf_op jit(solution)/shard_map/across_y/ppermute | solution.py:218
  162.4 16.7 %copy-start = (bf16[4,320,2560]{2,1,0:T(8,128)(2,1)}, bf16[4,320,2560]{2,1,0:T(8,128)(2,1)S(1)}, u32[]{:S(2)}) copy-start(bf16[4,320,2560]{2,1,0:T(8,128)(2,1)S(1)} %bitcast_dynamic-update-slice_fusion) | copy-start | bytes 19660804

commit v20 on v19

--- a/solution.py
+++ b/solution.py
@@ -259,6 +259,7 @@
         corner[k] = (by_x, by_y)[k]
         for flip, part in enumerate((mine, by_x, by_y)):
             result = place_in(result, flip, k * width, part)
+    corner = tie(corner)
     corner[0] = move("across_y", corner[0], "mat", along_y)
     corner[1] = move("across_x", corner[1], "mat", along_x)
     result = place_in(result, 3, 0, jnp.concatenate(corner, axis=1))

time: 181 us -> 180 us (level)
  transfers between devices with their start and end apart: 19 -> 19, of which waited for: 8 -> 9; matrix products, arithmetic and copies ran while one was open for 5% -> 6% of each run, Pallas kernels for 0% -> 0%
where the time goes in v20:
time: 180 us; the launch traced here: 179 us
  waiting for transfers between devices  129 us (72%)
  starting transfers between devices  38.2 us (21%)
  local copies, waits for them, and re-layouts  9.68 us (5%)
    ppermute x19, waiting for transfers between devices, move(): return lax.ppermute(block, axis, pairs)  129 us
    ppermute x19, starting transfers between devices, move(): return lax.ppermute(block, axis, pairs)  38.2 us
  transfers between devices with their start and end apart: 19, of which 9 were waited for; matrix products, arithmetic and copies ran while one was open for 6% of the time, Pallas kernels for 0%

profile of v20, /device:TPU:0, one launch (start us, length us, event | category | flops | bytes accessed | tf_op | source)
XLA Modules:
  0.0 179.0 jit_solution(9529007359112691112)
XLA Ops:
  0.8 7.8 %collective-permute-start = (bf16[320,2560]{1,0:T(8,128)(2,1)}, bf16[320,2560]{1,0:T(8,128)(2,1)S(1)}, u32[]{:S(2)}, u32[]{:S(2)}) collective-permute-start(bf16[320,2560]{1,0:T(8,128)(2,1)} %bitcast.23), channel_id=1, source_target_pairs={{0,2},{1,3},{6,4},{7,5},{8,10},{9,11},{14,12},{15,13},{16,18},{17,... | collective-permute-start | bytes 4915208 | tf_op jit(solution)/shard_map/rows_in/ppermute | solution.py:218
  8.5 1.9 %collective-permute-start.1 = (bf16[320,2560]{1,0:T(8,128)(2,1)}, bf16[320,2560]{1,0:T(8,128)(2,1)}, u32[]{:S(2)}, u32[]{:S(2)}) collective-permute-start(bf16[320,2560]{1,0:T(8,128)(2,1)} %bitcast.24), channel_id=1, source_target_pairs={{2,3},{3,2},{4,5},{5,4},{10,11},{11,10},{12,13},{13,12},{18,19},{1... | collective-permute-start | bytes 4915208 | tf_op jit(solution)/shard_map/swap_own/ppermute | solution.py:218
  10.4 2.3 %slice_bitcast_fusion = bf16[208,2560]{1,0:T(8,128)(2,1)} fusion(bf16[1,320,2560]{2,1,0:T(8,128)(2,1)} %param.1), kind=kLoop, calls=%fused_computation.2 | loop fusion | bytes 2129920 | tf_op jit(solution)/shard_map/slice | solution.py:227
  12.7 2.3 %collective-permute-start.7 = (bf16[208,2560]{1,0:T(8,128)(2,1)}, bf16[208,2560]{1,0:T(8,128)(2,1)}, u32[]{:S(2)}, u32[]{:S(2)}) collective-permute-start(bf16[208,2560]{1,0:T(8,128)(2,1)} %slice_bitcast_fusion), channel_id=1, source_target_pairs={{0,4},{1,5},{6,2},{7,3},{8,12},{9,13},{14,10},{15,11},{16,20},{17,... | collective-permute-start | bytes 3194888 | tf_op jit(solution)/shard_map/rows_far/ppermute | solution.py:218
  15.9 1.6 collective-permute-start.5
  17.5 27.4 %collective-permute-done.refs_1_ = bf16[320,2560]{1,0:T(8,128)(2,1)S(1)} collective-permute-done((bf16[320,2560]{1,0:T(8,128)(2,1)}, bf16[320,2560]{1,0:T(8,128)(2,1)S(1)}, u32[]{:S(2)}, u32[]{:S(2)}) %collective-permute-start) | collective-permute-done | bytes 1638432 | tf_op jit(solution)/shard_map/rows_in/ppermute | solution.py:218
  46.2 1.6 collective-permute-start.3
  47.8 1.6 collective-permute-start.4
  49.5 1.6 collective-permute-start.6
  51.1 1.9 %slice_bitcast_fusion.1 = bf16[112,2560]{1,0:T(8,128)(2,1)} fusion(bf16[1,320,2560]{2,1,0:T(8,128)(2,1)} %param.1), kind=kLoop, calls=%fused_computation.11 | loop fusion | bytes 1146880 | tf_op jit(solution)/shard_map/slice | solution.py:227
  53.0 7.0 %collective-permute-start.8 = (bf16[112,2560]{1,0:T(8,128)(2,1)}, bf16[112,2560]{1,0:T(8,128)(2,1)}, u32[]{:S(2)}, u32[]{:S(2)}) collective-permute-start(bf16[112,2560]{1,0:T(8,128)(2,1)} %slice_bitcast_fusion.1), channel_id=1, source_target_pairs={{0,4},{1,5},{6,2},{7,3},{8,12},{9,13},{14,10},{15,11},{16,20},{17,... | collective-permute-start | bytes 1720328 | tf_op jit(solution)/shard_map/rows_far/ppermute | solution.py:218
  60.0 7.7 %collective-permute-done.7.refs_9_ = bf16[208,2560]{1,0:T(8,128)(2,1)} collective-permute-done((bf16[208,2560]{1,0:T(8,128)(2,1)}, bf16[208,2560]{1,0:T(8,128)(2,1)}, u32[]{:S(2)}, u32[]{:S(2)}) %collective-permute-start.7) | collective-permute-done | bytes 1064992 | tf_op jit(solution)/shard_map/rows_far/ppermute | solution.py:218
  68.5 10.1 %collective-permute-done.8.refs_10_ = bf16[112,2560]{1,0:T(8,128)(2,1)} collective-permute-done((bf16[112,2560]{1,0:T(8,128)(2,1)}, bf16[112,2560]{1,0:T(8,128)(2,1)}, u32[]{:S(2)}, u32[]{:S(2)}) %collective-permute-start.8) | collective-permute-done | bytes 573472 | tf_op jit(solution)/shard_map/rows_far/ppermute | solution.py:218
  79.7 1.3 collective-permute-start.14
  82.6 34.5 %collective-permute-done.14 = bf16[320,1280]{1,0:T(8,128)(2,1)S(1)} collective-permute-done((bf16[320,1280]{1,0:T(8,128)(2,1)S(1)}, bf16[320,1280]{1,0:T(8,128)(2,1)S(1)}, u32[]{:S(2)}, u32[]{:S(2)}) %collective-permute-start.14) | collective-permute-done | bytes 819232 | tf_op jit(solution)/shard_map/rows_out/ppermute | solution.py:218
  117.3 1.5 collective-permute-start.15
  118.8 1.5 collective-permute-start.16
  120.3 16.1 %collective-permute-done.11 = bf16[320,1280]{1,0:T(8,128)(2,1)S(1)} collective-permute-done((bf16[320,1280]{1,0:T(8,128)(2,1)S(1)}, bf16[320,1280]{1,0:T(8,128)(2,1)S(1)}, u32[]{:S(2)}, u32[]{:S(2)}) %collective-permute-start.11) | collective-permute-done | bytes 819232 | tf_op jit(solution)/shard_map/rows_out/ppermute | solution.py:218
  136.5 1.5 collective-permute-start.12
  138.1 1.5 collective-permute-start.13
  140.2 16.3 %collective-permute-done.12 = bf16[320,1280]{1,0:T(8,128)(2,1)} collective-permute-done((bf16[320,1280]{1,0:T(8,128)(2,1)S(1)}, bf16[320,1280]{1,0:T(8,128)(2,1)}, u32[]{:S(2)}, u32[]{:S(2)}) %collective-permute-start.12) | collective-permute-done | bytes 819232 | tf_op jit(solution)/shard_map/along_x/ppermute | solution.py:218
  157.6 1.5 collective-permute-start.17
  162.4 13.8 %collective-permute-done.17 = bf16[320,1280]{1,0:T(8,128)(2,1)S(1)} collective-permute-done((bf16[320,1280]{1,0:T(8,128)(2,1)S(1)}, bf16[320,1280]{1,0:T(8,128)(2,1)S(1)}, u32[]{:S(2)}, u32[]{:S(2)}) %collective-permute-start.17) | collective-permute-done | bytes 819232 | tf_op jit(solution)/shard_map/across_y/ppermute | solution.py:218
  176.2 1.5 collective-permute-done.18
  (34 shorter events, 13.0 us)
Async XLA Ops:
  0.0 14.9 %collective-permute-start.2 = (bf16[320,2560]{1,0:T(8,128)(2,1)}, bf16[320,2560]{1,0:T(8,128)(2,1)S(1)}, u32[]{:S(2)}, u32[]{:S(2)}) collective-permute-start(bf16[320,2560]{1,0:T(8,128)(2,1)} %bitcast.22), channel_id=1, source_target_pairs={{2,4},{3,5},{4,2},{5,3},{10,12},{11,13},{12,10},{13,11},{18,20},{1... | collective-permute-start | bytes 4915208 | tf_op jit(solution)/shard_map/middle/ppermute | solution.py:218
  0.8 44.2 %collective-permute-start = (bf16[320,2560]{1,0:T(8,128)(2,1)}, bf16[320,2560]{1,0:T(8,128)(2,1)S(1)}, u32[]{:S(2)}, u32[]{:S(2)}) collective-permute-start(bf16[320,2560]{1,0:T(8,128)(2,1)} %bitcast.23), channel_id=1, source_target_pairs={{0,2},{1,3},{6,4},{7,5},{8,10},{9,11},{14,12},{15,13},{16,18},{17,... | collective-permute-start | bytes 4915208 | tf_op jit(solution)/shard_map/rows_in/ppermute | solution.py:218
  8.5 40.9 %collective-permute-start.1 = (bf16[320,2560]{1,0:T(8,128)(2,1)}, bf16[320,2560]{1,0:T(8,128)(2,1)}, u32[]{:S(2)}, u32[]{:S(2)}) collective-permute-start(bf16[320,2560]{1,0:T(8,128)(2,1)} %bitcast.24), channel_id=1, source_target_pairs={{2,3},{3,2},{4,5},{5,4},{10,11},{11,10},{12,13},{13,12},{18,19},{1... | collective-permute-start | bytes 4915208 | tf_op jit(solution)/shard_map/swap_own/ppermute | solution.py:218
  12.7 55.1 %collective-permute-start.7 = (bf16[208,2560]{1,0:T(8,128)(2,1)}, bf16[208,2560]{1,0:T(8,128)(2,1)}, u32[]{:S(2)}, u32[]{:S(2)}) collective-permute-start(bf16[208,2560]{1,0:T(8,128)(2,1)} %slice_bitcast_fusion), channel_id=1, source_target_pairs={{0,4},{1,5},{6,2},{7,3},{8,12},{9,13},{14,10},{15,11},{16,20},{17,... | collective-permute-start | bytes 3194888 | tf_op jit(solution)/shard_map/rows_far/ppermute | solution.py:218
  15.9 44.0 %collective-permute-start.5 = (bf16[176,2560]{1,0:T(8,128)(2,1)}, bf16[176,2560]{1,0:T(8,128)(2,1)}, u32[]{:S(2)}, u32[]{:S(2)}) collective-permute-start(bf16[176,2560]{1,0:T(8,128)(2,1)} %slice.34), channel_id=1, source_target_pairs={{2,3},{3,2},{4,5},{5,4},{10,11},{11,10},{12,13},{13,12},{18,19},{1... | collective-permute-start | bytes 2703368 | tf_op jit(solution)/shard_map/swap_rows/ppermute | solution.py:218
  46.2 13.7 %collective-permute-start.3 = (bf16[160,2560]{1,0:T(8,128)(2,1)}, bf16[160,2560]{1,0:T(8,128)(2,1)}, u32[]{:S(2)}, u32[]{:S(2)}) collective-permute-start(bf16[160,2560]{1,0:T(8,128)(2,1)} %get-tuple-element.38), channel_id=1, source_target_pairs={{2,3},{3,2},{4,5},{5,4},{10,11},{11,10},{12,13},{13,12},{18,19},{1... | collective-permute-start | bytes 2457608 | tf_op jit(solution)/shard_map/swap_rows/ppermute | solution.py:218
  47.8 12.1 %collective-permute-start.4 = (bf16[160,2560]{1,0:T(8,128)(2,1)}, bf16[160,2560]{1,0:T(8,128)(2,1)}, u32[]{:S(2)}, u32[]{:S(2)}) collective-permute-start(bf16[160,2560]{1,0:T(8,128)(2,1)} %get-tuple-element.37), channel_id=1, source_target_pairs={{2,3},{3,2},{4,5},{5,4},{10,11},{11,10},{12,13},{13,12},{18,19},{1... | collective-permute-start | bytes 2457608 | tf_op jit(solution)/shard_map/swap_rows/ppermute | solution.py:218
  49.5 3.5 %collective-permute-start.6 = (bf16[144,2560]{1,0:T(8,128)(2,1)S(1)}, bf16[144,2560]{1,0:T(8,128)(2,1)}, u32[]{:S(2)}, u32[]{:S(2)}) collective-permute-start(bf16[144,2560]{1,0:T(8,128)(2,1)S(1)} %slice.35), channel_id=1, source_target_pairs={{2,3},{3,2},{4,5},{5,4},{10,11},{11,10},{12,13},{13,12},{18,19},{1... | collective-permute-start | bytes 2211848 | tf_op jit(solution)/shard_map/swap_rows/ppermute | solution.py:218
  53.0 25.6 %collective-permute-start.8 = (bf16[112,2560]{1,0:T(8,128)(2,1)}, bf16[112,2560]{1,0:T(8,128)(2,1)}, u32[]{:S(2)}, u32[]{:S(2)}) collective-permute-start(bf16[112,2560]{1,0:T(8,128)(2,1)} %slice_bitcast_fusion.1), channel_id=1, source_target_pairs={{0,4},{1,5},{6,2},{7,3},{8,12},{9,13},{14,10},{15,11},{16,20},{17,... | collective-permute-start | bytes 1720328 | tf_op jit(solution)/shard_map/rows_far/ppermute | solution.py:218
  67.8 11.5 %collective-permute-start.9 = (bf16[208,2560]{1,0:T(8,128)(2,1)}, bf16[208,2560]{1,0:T(8,128)(2,1)S(1)}, u32[]{:S(2)}, u32[]{:S(2)}) collective-permute-start(bf16[208,2560]{1,0:T(8,128)(2,1)} %collective-permute-done.7.refs_9_), channel_id=1, source_target_pairs={{2,3},{3,2},{4,5},{5,4},{10,11},{11,10},{12,13},{13,12},{18,19},{1... | collective-permute-start | bytes 3194888 | tf_op jit(solution)/shard_map/swap_far/ppermute | solution.py:218
  78.6 0.7 collective-permute-start.10
  79.7 37.5 %collective-permute-start.14 = (bf16[320,1280]{1,0:T(8,128)(2,1)S(1)}, bf16[320,1280]{1,0:T(8,128)(2,1)S(1)}, u32[]{:S(2)}, u32[]{:S(2)}) collective-permute-start(bf16[320,1280]{1,0:T(8,128)(2,1)S(1)} %get-tuple-element.31), channel_id=1, source_target_pairs={{2,0},{3,1},{4,6},{5,7},{10,8},{11,9},{12,14},{13,15},{18,16},{19,... | collective-permute-start | bytes 2457608 | tf_op jit(solution)/shard_map/rows_out/ppermute | solution.py:218
  81.3 55.1 %collective-permute-start.11 = (bf16[320,1280]{1,0:T(8,128)(2,1)S(1)}, bf16[320,1280]{1,0:T(8,128)(2,1)S(1)}, u32[]{:S(2)}, u32[]{:S(2)}) collective-permute-start(bf16[320,1280]{1,0:T(8,128)(2,1)S(1)} %get-tuple-element.27), channel_id=1, source_target_pairs={{2,0},{3,1},{4,6},{5,7},{10,8},{11,9},{12,14},{13,15},{18,16},{19,... | collective-permute-start | bytes 2457608 | tf_op jit(solution)/shard_map/rows_out/ppermute | solution.py:218
  117.3 22.9 %collective-permute-start.15 = (bf16[320,1280]{1,0:T(8,128)(2,1)S(1)}, bf16[320,1280]{1,0:T(8,128)(2,1)S(1)}, u32[]{:S(2)}, u32[]{:S(2)}) collective-permute-start(bf16[320,1280]{1,0:T(8,128)(2,1)S(1)} %broadcast_select_fusion), channel_id=1, source_target_pairs={{0,8},{8,0},{16,24},{24,16},{1,9},{9,1},{17,25},{25,17},{2,10},{10... | collective-permute-start | bytes 2457608 | tf_op jit(solution)/shard_map/along_x/ppermute | solution.py:218
  118.8 21.4 %collective-permute-start.16 = (bf16[320,1280]{1,0:T(8,128)(2,1)S(1)}, bf16[320,1280]{1,0:T(8,128)(2,1)S(1)}, u32[]{:S(2)}, u32[]{:S(2)}) collective-permute-start(bf16[320,1280]{1,0:T(8,128)(2,1)S(1)} %broadcast_select_fusion), channel_id=1, source_target_pairs={{0,16},{8,24},{16,0},{24,8},{1,17},{9,25},{17,1},{25,9},{2,18},{10... | collective-permute-start | bytes 2457608 | tf_op jit(solution)/shard_map/along_y/ppermute | solution.py:218
  136.5 19.9 %collective-permute-start.12 = (bf16[320,1280]{1,0:T(8,128)(2,1)S(1)}, bf16[320,1280]{1,0:T(8,128)(2,1)}, u32[]{:S(2)}, u32[]{:S(2)}) collective-permute-start(bf16[320,1280]{1,0:T(8,128)(2,1)S(1)} %broadcast_select_fusion.1), channel_id=1, source_target_pairs={{0,8},{8,0},{16,24},{24,16},{1,9},{9,1},{17,25},{25,17},{2,10},{10... | collective-permute-start | bytes 2457608 | tf_op jit(solution)/shard_map/along_x/ppermute | solution.py:218
  138.1 19.6 %collective-permute-start.13 = (bf16[320,1280]{1,0:T(8,128)(2,1)S(1)}, bf16[320,1280]{1,0:T(8,128)(2,1)}, u32[]{:S(2)}, u32[]{:S(2)}) collective-permute-start(bf16[320,1280]{1,0:T(8,128)(2,1)S(1)} %broadcast_select_fusion.1), channel_id=1, source_target_pairs={{0,16},{8,24},{16,0},{24,8},{1,17},{9,25},{17,1},{25,9},{2,18},{10... | collective-permute-start | bytes 2457608 | tf_op jit(solution)/shard_map/along_y/ppermute | solution.py:218
  157.6 18.6 %collective-permute-start.17 = (bf16[320,1280]{1,0:T(8,128)(2,1)S(1)}, bf16[320,1280]{1,0:T(8,128)(2,1)S(1)}, u32[]{:S(2)}, u32[]{:S(2)}) collective-permute-start(bf16[320,1280]{1,0:T(8,128)(2,1)S(1)} %collective-permute-done.15), channel_id=1, source_target_pairs={{0,16},{8,24},{16,0},{24,8},{1,17},{9,25},{17,1},{25,9},{2,18},{10... | collective-permute-start | bytes 2457608 | tf_op jit(solution)/shard_map/across_y/ppermute | solution.py:218
  159.2 18.5 %collective-permute-start.18 = (bf16[320,1280]{1,0:T(8,128)(2,1)}, bf16[320,1280]{1,0:T(8,128)(2,1)S(1)}, u32[]{:S(2)}, u32[]{:S(2)}) collective-permute-start(bf16[320,1280]{1,0:T(8,128)(2,1)} %collective-permute-done.13), channel_id=1, source_target_pairs={{0,8},{8,0},{16,24},{24,16},{1,9},{9,1},{17,25},{25,17},{2,10},{10... | collective-permute-start | bytes 2457608 | tf_op jit(solution)/shard_map/across_x/ppermute | solution.py:218
  162.4 15.3 %copy-start = (bf16[4,320,2560]{2,1,0:T(8,128)(2,1)}, bf16[4,320,2560]{2,1,0:T(8,128)(2,1)S(1)}, u32[]{:S(2)}) copy-start(bf16[4,320,2560]{2,1,0:T(8,128)(2,1)S(1)} %bitcast_dynamic-update-slice_fusion) | copy-start | bytes 19660804

commit v21 on v20

--- a/solution.py
+++ b/solution.py
@@ -256,12 +256,12 @@
         by_x = move("along_x", mine, "mat", along_x)
         by_y = move("along_y", mine, "mat", along_y)
         by_x, by_y = tie((by_x, by_y))
-        corner[k] = (by_x, by_y)[k]
+        corner[k] = (by_y, by_x)[k]
         for flip, part in enumerate((mine, by_x, by_y)):
             result = place_in(result, flip, k * width, part)
     corner = tie(corner)
-    corner[0] = move("across_y", corner[0], "mat", along_y)
-    corner[1] = move("across_x", corner[1], "mat", along_x)
+    corner[0] = move("across_x", corner[0], "mat", along_x)
+    corner[1] = move("across_y", corner[1], "mat", along_y)
     result = place_in(result, 3, 0, jnp.concatenate(corner, axis=1))
     return result
 

time: 180 us -> 179 us (level)
  no operation moved by 1% of the time
where the time goes in v21:
time: 179 us; the launch traced here: 178 us
  waiting for transfers between devices  128 us (72%)
  starting transfers between devices  38.2 us (21%)
  local copies, waits for them, and re-layouts  9.72 us (5%)
    ppermute x19, waiting for transfers between devices, move(): return lax.ppermute(block, axis, pairs)  128 us
    ppermute x19, starting transfers between devices, move(): return lax.ppermute(block, axis, pairs)  38.2 us
  transfers between devices with their start and end apart: 19, of which 9 were waited for; matrix products, arithmetic and copies ran while one was open for 6% of the time, Pallas kernels for 0%

profile of v21, /device:TPU:0, one launch (start us, length us, event | category | flops | bytes accessed | tf_op | source)
XLA Modules:
  0.0 178.0 jit_solution(15236192018435586371)
XLA Ops:
  0.8 7.8 %collective-permute-start = (bf16[320,2560]{1,0:T(8,128)(2,1)}, bf16[320,2560]{1,0:T(8,128)(2,1)S(1)}, u32[]{:S(2)}, u32[]{:S(2)}) collective-permute-start(bf16[320,2560]{1,0:T(8,128)(2,1)} %bitcast.23), channel_id=1, source_target_pairs={{0,2},{1,3},{6,4},{7,5},{8,10},{9,11},{14,12},{15,13},{16,18},{17,... | collective-permute-start | bytes 4915208 | tf_op jit(solution)/shard_map/rows_in/ppermute | solution.py:218
  8.5 1.9 %collective-permute-start.1 = (bf16[320,2560]{1,0:T(8,128)(2,1)}, bf16[320,2560]{1,0:T(8,128)(2,1)}, u32[]{:S(2)}, u32[]{:S(2)}) collective-permute-start(bf16[320,2560]{1,0:T(8,128)(2,1)} %bitcast.24), channel_id=1, source_target_pairs={{2,3},{3,2},{4,5},{5,4},{10,11},{11,10},{12,13},{13,12},{18,19},{1... | collective-permute-start | bytes 4915208 | tf_op jit(solution)/shard_map/swap_own/ppermute | solution.py:218
  10.4 2.3 %slice_bitcast_fusion = bf16[208,2560]{1,0:T(8,128)(2,1)} fusion(bf16[1,320,2560]{2,1,0:T(8,128)(2,1)} %param.1), kind=kLoop, calls=%fused_computation.2 | loop fusion | bytes 2129920 | tf_op jit(solution)/shard_map/slice | solution.py:227
  12.7 2.3 %collective-permute-start.7 = (bf16[208,2560]{1,0:T(8,128)(2,1)}, bf16[208,2560]{1,0:T(8,128)(2,1)}, u32[]{:S(2)}, u32[]{:S(2)}) collective-permute-start(bf16[208,2560]{1,0:T(8,128)(2,1)} %slice_bitcast_fusion), channel_id=1, source_target_pairs={{0,4},{1,5},{6,2},{7,3},{8,12},{9,13},{14,10},{15,11},{16,20},{17,... | collective-permute-start | bytes 3194888 | tf_op jit(solution)/shard_map/rows_far/ppermute | solution.py:218
  15.9 1.6 collective-permute-start.5
  17.5 27.4 %collective-permute-done.refs_1_ = bf16[320,2560]{1,0:T(8,128)(2,1)S(1)} collective-permute-done((bf16[320,2560]{1,0:T(8,128)(2,1)}, bf16[320,2560]{1,0:T(8,128)(2,1)S(1)}, u32[]{:S(2)}, u32[]{:S(2)}) %collective-permute-start) | collective-permute-done | bytes 1638432 | tf_op jit(solution)/shard_map/rows_in/ppermute | solution.py:218
  46.2 1.6 collective-permute-start.3
  47.8 1.6 collective-permute-start.4
  49.5 1.6 collective-permute-start.6
  51.1 1.9 %slice_bitcast_fusion.1 = bf16[112,2560]{1,0:T(8,128)(2,1)} fusion(bf16[1,320,2560]{2,1,0:T(8,128)(2,1)} %param.1), kind=kLoop, calls=%fused_computation.11 | loop fusion | bytes 1146880 | tf_op jit(solution)/shard_map/slice | solution.py:227
  53.0 7.0 %collective-permute-start.8 = (bf16[112,2560]{1,0:T(8,128)(2,1)}, bf16[112,2560]{1,0:T(8,128)(2,1)}, u32[]{:S(2)}, u32[]{:S(2)}) collective-permute-start(bf16[112,2560]{1,0:T(8,128)(2,1)} %slice_bitcast_fusion.1), channel_id=1, source_target_pairs={{0,4},{1,5},{6,2},{7,3},{8,12},{9,13},{14,10},{15,11},{16,20},{17,... | collective-permute-start | bytes 1720328 | tf_op jit(solution)/shard_map/rows_far/ppermute | solution.py:218
  60.0 7.7 %collective-permute-done.7.refs_9_ = bf16[208,2560]{1,0:T(8,128)(2,1)} collective-permute-done((bf16[208,2560]{1,0:T(8,128)(2,1)}, bf16[208,2560]{1,0:T(8,128)(2,1)}, u32[]{:S(2)}, u32[]{:S(2)}) %collective-permute-start.7) | collective-permute-done | bytes 1064992 | tf_op jit(solution)/shard_map/rows_far/ppermute | solution.py:218
  68.5 10.1 %collective-permute-done.8.refs_10_ = bf16[112,2560]{1,0:T(8,128)(2,1)} collective-permute-done((bf16[112,2560]{1,0:T(8,128)(2,1)}, bf16[112,2560]{1,0:T(8,128)(2,1)}, u32[]{:S(2)}, u32[]{:S(2)}) %collective-permute-start.8) | collective-permute-done | bytes 573472 | tf_op jit(solution)/shard_map/rows_far/ppermute | solution.py:218
  79.7 1.3 collective-permute-start.14
  81.3 1.3 collective-permute-start.11
  82.6 34.5 %collective-permute-done.14 = bf16[320,1280]{1,0:T(8,128)(2,1)S(1)} collective-permute-done((bf16[320,1280]{1,0:T(8,128)(2,1)S(1)}, bf16[320,1280]{1,0:T(8,128)(2,1)S(1)}, u32[]{:S(2)}, u32[]{:S(2)}) %collective-permute-start.14) | collective-permute-done | bytes 819232 | tf_op jit(solution)/shard_map/rows_out/ppermute | solution.py:218
  117.3 1.5 collective-permute-start.15
  118.8 1.5 collective-permute-start.16
  120.3 16.1 %collective-permute-done.11 = bf16[320,1280]{1,0:T(8,128)(2,1)S(1)} collective-permute-done((bf16[320,1280]{1,0:T(8,128)(2,1)S(1)}, bf16[320,1280]{1,0:T(8,128)(2,1)S(1)}, u32[]{:S(2)}, u32[]{:S(2)}) %collective-permute-start.11) | collective-permute-done | bytes 819232 | tf_op jit(solution)/shard_map/rows_out/ppermute | solution.py:218
  136.5 1.5 collective-permute-start.12
  138.1 1.5 collective-permute-start.13
  140.2 16.3 %collective-permute-done.12 = bf16[320,1280]{1,0:T(8,128)(2,1)} collective-permute-done((bf16[320,1280]{1,0:T(8,128)(2,1)S(1)}, bf16[320,1280]{1,0:T(8,128)(2,1)}, u32[]{:S(2)}, u32[]{:S(2)}) %collective-permute-start.12) | collective-permute-done | bytes 819232 | tf_op jit(solution)/shard_map/along_x/ppermute | solution.py:218
  158.2 1.5 collective-permute-start.18
  162.4 13.8 %collective-permute-done.17 = bf16[320,1280]{1,0:T(8,128)(2,1)S(1)} collective-permute-done((bf16[320,1280]{1,0:T(8,128)(2,1)S(1)}, bf16[320,1280]{1,0:T(8,128)(2,1)S(1)}, u32[]{:S(2)}, u32[]{:S(2)}) %collective-permute-start.17) | collective-permute-done | bytes 819232 | tf_op jit(solution)/shard_map/across_x/ppermute | solution.py:218
  (34 shorter events, 12.2 us)
Async XLA Ops:
  0.0 14.9 %collective-permute-start.2 = (bf16[320,2560]{1,0:T(8,128)(2,1)}, bf16[320,2560]{1,0:T(8,128)(2,1)S(1)}, u32[]{:S(2)}, u32[]{:S(2)}) collective-permute-start(bf16[320,2560]{1,0:T(8,128)(2,1)} %bitcast.22), channel_id=1, source_target_pairs={{2,4},{3,5},{4,2},{5,3},{10,12},{11,13},{12,10},{13,11},{18,20},{1... | collective-permute-start | bytes 4915208 | tf_op jit(solution)/shard_map/middle/ppermute | solution.py:218
  0.8 44.2 %collective-permute-start = (bf16[320,2560]{1,0:T(8,128)(2,1)}, bf16[320,2560]{1,0:T(8,128)(2,1)S(1)}, u32[]{:S(2)}, u32[]{:S(2)}) collective-permute-start(bf16[320,2560]{1,0:T(8,128)(2,1)} %bitcast.23), channel_id=1, source_target_pairs={{0,2},{1,3},{6,4},{7,5},{8,10},{9,11},{14,12},{15,13},{16,18},{17,... | collective-permute-start | bytes 4915208 | tf_op jit(solution)/shard_map/rows_in/ppermute | solution.py:218
  8.5 40.9 %collective-permute-start.1 = (bf16[320,2560]{1,0:T(8,128)(2,1)}, bf16[320,2560]{1,0:T(8,128)(2,1)}, u32[]{:S(2)}, u32[]{:S(2)}) collective-permute-start(bf16[320,2560]{1,0:T(8,128)(2,1)} %bitcast.24), channel_id=1, source_target_pairs={{2,3},{3,2},{4,5},{5,4},{10,11},{11,10},{12,13},{13,12},{18,19},{1... | collective-permute-start | bytes 4915208 | tf_op jit(solution)/shard_map/swap_own/ppermute | solution.py:218
  12.7 55.1 %collective-permute-start.7 = (bf16[208,2560]{1,0:T(8,128)(2,1)}, bf16[208,2560]{1,0:T(8,128)(2,1)}, u32[]{:S(2)}, u32[]{:S(2)}) collective-permute-start(bf16[208,2560]{1,0:T(8,128)(2,1)} %slice_bitcast_fusion), channel_id=1, source_target_pairs={{0,4},{1,5},{6,2},{7,3},{8,12},{9,13},{14,10},{15,11},{16,20},{17,... | collective-permute-start | bytes 3194888 | tf_op jit(solution)/shard_map/rows_far/ppermute | solution.py:218
  15.9 44.0 %collective-permute-start.5 = (bf16[176,2560]{1,0:T(8,128)(2,1)}, bf16[176,2560]{1,0:T(8,128)(2,1)}, u32[]{:S(2)}, u32[]{:S(2)}) collective-permute-start(bf16[176,2560]{1,0:T(8,128)(2,1)} %slice.34), channel_id=1, source_target_pairs={{2,3},{3,2},{4,5},{5,4},{10,11},{11,10},{12,13},{13,12},{18,19},{1... | collective-permute-start | bytes 2703368 | tf_op jit(solution)/shard_map/swap_rows/ppermute | solution.py:218
  46.2 13.7 %collective-permute-start.3 = (bf16[160,2560]{1,0:T(8,128)(2,1)}, bf16[160,2560]{1,0:T(8,128)(2,1)}, u32[]{:S(2)}, u32[]{:S(2)}) collective-permute-start(bf16[160,2560]{1,0:T(8,128)(2,1)} %get-tuple-element.38), channel_id=1, source_target_pairs={{2,3},{3,2},{4,5},{5,4},{10,11},{11,10},{12,13},{13,12},{18,19},{1... | collective-permute-start | bytes 2457608 | tf_op jit(solution)/shard_map/swap_rows/ppermute | solution.py:218
  47.8 12.1 %collective-permute-start.4 = (bf16[160,2560]{1,0:T(8,128)(2,1)}, bf16[160,2560]{1,0:T(8,128)(2,1)}, u32[]{:S(2)}, u32[]{:S(2)}) collective-permute-start(bf16[160,2560]{1,0:T(8,128)(2,1)} %get-tuple-element.37), channel_id=1, source_target_pairs={{2,3},{3,2},{4,5},{5,4},{10,11},{11,10},{12,13},{13,12},{18,19},{1... | collective-permute-start | bytes 2457608 | tf_op jit(solution)/shard_map/swap_rows/ppermute | solution.py:218
  49.5 3.5 %collective-permute-start.6 = (bf16[144,2560]{1,0:T(8,128)(2,1)S(1)}, bf16[144,2560]{1,0:T(8,128)(2,1)}, u32[]{:S(2)}, u32[]{:S(2)}) collective-permute-start(bf16[144,2560]{1,0:T(8,128)(2,1)S(1)} %slice.35), channel_id=1, source_target_pairs={{2,3},{3,2},{4,5},{5,4},{10,11},{11,10},{12,13},{13,12},{18,19},{1... | collective-permute-start | bytes 2211848 | tf_op jit(solution)/shard_map/swap_rows/ppermute | solution.py:218
  53.0 25.6 %collective-permute-start.8 = (bf16[112,2560]{1,0:T(8,128)(2,1)}, bf16[112,2560]{1,0:T(8,128)(2,1)}, u32[]{:S(2)}, u32[]{:S(2)}) collective-permute-start(bf16[112,2560]{1,0:T(8,128)(2,1)} %slice_bitcast_fusion.1), channel_id=1, source_target_pairs={{0,4},{1,5},{6,2},{7,3},{8,12},{9,13},{14,10},{15,11},{16,20},{17,... | collective-permute-start | bytes 1720328 | tf_op jit(solution)/shard_map/rows_far/ppermute | solution.py:218
  67.8 11.5 %collective-permute-start.9 = (bf16[208,2560]{1,0:T(8,128)(2,1)}, bf16[208,2560]{1,0:T(8,128)(2,1)S(1)}, u32[]{:S(2)}, u32[]{:S(2)}) collective-permute-start(bf16[208,2560]{1,0:T(8,128)(2,1)} %collective-permute-done.7.refs_9_), channel_id=1, source_target_pairs={{2,3},{3,2},{4,5},{5,4},{10,11},{11,10},{12,13},{13,12},{18,19},{1... | collective-permute-start | bytes 3194888 | tf_op jit(solution)/shard_map/swap_far/ppermute | solution.py:218
  78.6 0.7 collective-permute-start.10
  79.7 37.5 %collective-permute-start.14 = (bf16[320,1280]{1,0:T(8,128)(2,1)S(1)}, bf16[320,1280]{1,0:T(8,128)(2,1)S(1)}, u32[]{:S(2)}, u32[]{:S(2)}) collective-permute-start(bf16[320,1280]{1,0:T(8,128)(2,1)S(1)} %get-tuple-element.31), channel_id=1, source_target_pairs={{2,0},{3,1},{4,6},{5,7},{10,8},{11,9},{12,14},{13,15},{18,16},{19,... | collective-permute-start | bytes 2457608 | tf_op jit(solution)/shard_map/rows_out/ppermute | solution.py:218
  81.3 55.1 %collective-permute-start.11 = (bf16[320,1280]{1,0:T(8,128)(2,1)S(1)}, bf16[320,1280]{1,0:T(8,128)(2,1)S(1)}, u32[]{:S(2)}, u32[]{:S(2)}) collective-permute-start(bf16[320,1280]{1,0:T(8,128)(2,1)S(1)} %get-tuple-element.27), channel_id=1, source_target_pairs={{2,0},{3,1},{4,6},{5,7},{10,8},{11,9},{12,14},{13,15},{18,16},{19,... | collective-permute-start | bytes 2457608 | tf_op jit(solution)/shard_map/rows_out/ppermute | solution.py:218
  117.3 22.9 %collective-permute-start.15 = (bf16[320,1280]{1,0:T(8,128)(2,1)S(1)}, bf16[320,1280]{1,0:T(8,128)(2,1)S(1)}, u32[]{:S(2)}, u32[]{:S(2)}) collective-permute-start(bf16[320,1280]{1,0:T(8,128)(2,1)S(1)} %broadcast_select_fusion), channel_id=1, source_target_pairs={{0,8},{8,0},{16,24},{24,16},{1,9},{9,1},{17,25},{25,17},{2,10},{10... | collective-permute-start | bytes 2457608 | tf_op jit(solution)/shard_map/along_x/ppermute | solution.py:218
  118.8 21.4 %collective-permute-start.16 = (bf16[320,1280]{1,0:T(8,128)(2,1)S(1)}, bf16[320,1280]{1,0:T(8,128)(2,1)S(1)}, u32[]{:S(2)}, u32[]{:S(2)}) collective-permute-start(bf16[320,1280]{1,0:T(8,128)(2,1)S(1)} %broadcast_select_fusion), channel_id=1, source_target_pairs={{0,16},{8,24},{16,0},{24,8},{1,17},{9,25},{17,1},{25,9},{2,18},{10... | collective-permute-start | bytes 2457608 | tf_op jit(solution)/shard_map/along_y/ppermute | solution.py:218
  136.5 19.9 %collective-permute-start.12 = (bf16[320,1280]{1,0:T(8,128)(2,1)S(1)}, bf16[320,1280]{1,0:T(8,128)(2,1)}, u32[]{:S(2)}, u32[]{:S(2)}) collective-permute-start(bf16[320,1280]{1,0:T(8,128)(2,1)S(1)} %broadcast_select_fusion.1), channel_id=1, source_target_pairs={{0,8},{8,0},{16,24},{24,16},{1,9},{9,1},{17,25},{25,17},{2,10},{10... | collective-permute-start | bytes 2457608 | tf_op jit(solution)/shard_map/along_x/ppermute | solution.py:218
  138.1 19.6 %collective-permute-start.13 = (bf16[320,1280]{1,0:T(8,128)(2,1)S(1)}, bf16[320,1280]{1,0:T(8,128)(2,1)}, u32[]{:S(2)}, u32[]{:S(2)}) collective-permute-start(bf16[320,1280]{1,0:T(8,128)(2,1)S(1)} %broadcast_select_fusion.1), channel_id=1, source_target_pairs={{0,16},{8,24},{16,0},{24,8},{1,17},{9,25},{17,1},{25,9},{2,18},{10... | collective-permute-start | bytes 2457608 | tf_op jit(solution)/shard_map/along_y/ppermute | solution.py:218
  157.6 18.6 %collective-permute-start.17 = (bf16[320,1280]{1,0:T(8,128)(2,1)S(1)}, bf16[320,1280]{1,0:T(8,128)(2,1)S(1)}, u32[]{:S(2)}, u32[]{:S(2)}) collective-permute-start(bf16[320,1280]{1,0:T(8,128)(2,1)S(1)} %collective-permute-done.16), channel_id=1, source_target_pairs={{0,8},{8,0},{16,24},{24,16},{1,9},{9,1},{17,25},{25,17},{2,10},{10... | collective-permute-start | bytes 2457608 | tf_op jit(solution)/shard_map/across_x/ppermute | solution.py:218
  158.2 18.5 %collective-permute-start.18 = (bf16[320,1280]{1,0:T(8,128)(2,1)}, bf16[320,1280]{1,0:T(8,128)(2,1)S(1)}, u32[]{:S(2)}, u32[]{:S(2)}) collective-permute-start(bf16[320,1280]{1,0:T(8,128)(2,1)} %collective-permute-done.12), channel_id=1, source_target_pairs={{0,16},{8,24},{16,0},{24,8},{1,17},{9,25},{17,1},{25,9},{2,18},{10... | collective-permute-start | bytes 2457608 | tf_op jit(solution)/shard_map/across_y/ppermute | solution.py:218
  162.4 14.3 %copy-start = (bf16[4,320,2560]{2,1,0:T(8,128)(2,1)}, bf16[4,320,2560]{2,1,0:T(8,128)(2,1)S(1)}, u32[]{:S(2)}) copy-start(bf16[4,320,2560]{2,1,0:T(8,128)(2,1)S(1)} %bitcast_dynamic-update-slice_fusion) | copy-start | bytes 19660804

commit v22 on v21

--- a/solution.py
+++ b/solution.py
@@ -157,9 +157,9 @@
         out[...] = new(mine, pl.ds(0, half))
         if own:
             copies["poly"].wait()
-            both = new(pl.ds(0, 2 * rows), pl.ds(half, columns - half))
-            outer_more[...] = both[:rows]
-            out_more[...] = both[rows:]
+            rest = pl.ds(half, columns - half)
+            outer_more[...] = new(pl.ds(0, rows), rest)
+            out_more[...] = new(mine, rest)
 
 
 def late_products(inner, rows, early, late, gram, cubic, outer_poly=None):

time: 179 us -> 178 us (level)
  no operation moved by 1% of the time
where the time goes in v22:
time: 178 us; the launch traced here: 177 us
  waiting for transfers between devices  127 us (71%)
  starting transfers between devices  38.2 us (21%)
  local copies, waits for them, and re-layouts  9.72 us (5%)
    ppermute x19, waiting for transfers between devices, move(): return lax.ppermute(block, axis, pairs)  127 us
    ppermute x19, starting transfers between devices, move(): return lax.ppermute(block, axis, pairs)  38.2 us
  transfers between devices with their start and end apart: 19, of which 9 were waited for; matrix products, arithmetic and copies ran while one was open for 6% of the time, Pallas kernels for 0%

profile of v22, /device:TPU:0, one launch (start us, length us, event | category | flops | bytes accessed | tf_op | source)
XLA Modules:
  0.0 177.3 jit_solution(6588920739561500474)
XLA Ops:
  0.8 7.8 %collective-permute-start = (bf16[320,2560]{1,0:T(8,128)(2,1)}, bf16[320,2560]{1,0:T(8,128)(2,1)S(1)}, u32[]{:S(2)}, u32[]{:S(2)}) collective-permute-start(bf16[320,2560]{1,0:T(8,128)(2,1)} %bitcast.23), channel_id=1, source_target_pairs={{0,2},{1,3},{6,4},{7,5},{8,10},{9,11},{14,12},{15,13},{16,18},{17,... | collective-permute-start | bytes 4915208 | tf_op jit(solution)/shard_map/rows_in/ppermute | solution.py:218
  8.5 1.9 %collective-permute-start.1 = (bf16[320,2560]{1,0:T(8,128)(2,1)}, bf16[320,2560]{1,0:T(8,128)(2,1)}, u32[]{:S(2)}, u32[]{:S(2)}) collective-permute-start(bf16[320,2560]{1,0:T(8,128)(2,1)} %bitcast.24), channel_id=1, source_target_pairs={{2,3},{3,2},{4,5},{5,4},{10,11},{11,10},{12,13},{13,12},{18,19},{1... | collective-permute-start | bytes 4915208 | tf_op jit(solution)/shard_map/swap_own/ppermute | solution.py:218
  10.4 2.3 %slice_bitcast_fusion = bf16[208,2560]{1,0:T(8,128)(2,1)} fusion(bf16[1,320,2560]{2,1,0:T(8,128)(2,1)} %param.1), kind=kLoop, calls=%fused_computation.2 | loop fusion | bytes 2129920 | tf_op jit(solution)/shard_map/slice | solution.py:227
  12.7 2.3 %collective-permute-start.7 = (bf16[208,2560]{1,0:T(8,128)(2,1)}, bf16[208,2560]{1,0:T(8,128)(2,1)}, u32[]{:S(2)}, u32[]{:S(2)}) collective-permute-start(bf16[208,2560]{1,0:T(8,128)(2,1)} %slice_bitcast_fusion), channel_id=1, source_target_pairs={{0,4},{1,5},{6,2},{7,3},{8,12},{9,13},{14,10},{15,11},{16,20},{17,... | collective-permute-start | bytes 3194888 | tf_op jit(solution)/shard_map/rows_far/ppermute | solution.py:218
  15.9 1.6 collective-permute-start.5
  17.5 27.4 %collective-permute-done.refs_1_ = bf16[320,2560]{1,0:T(8,128)(2,1)S(1)} collective-permute-done((bf16[320,2560]{1,0:T(8,128)(2,1)}, bf16[320,2560]{1,0:T(8,128)(2,1)S(1)}, u32[]{:S(2)}, u32[]{:S(2)}) %collective-permute-start) | collective-permute-done | bytes 1638432 | tf_op jit(solution)/shard_map/rows_in/ppermute | solution.py:218
  46.2 1.6 collective-permute-start.3
  47.8 1.6 collective-permute-start.4
  49.5 1.6 collective-permute-start.6
  51.1 1.9 %slice_bitcast_fusion.1 = bf16[112,2560]{1,0:T(8,128)(2,1)} fusion(bf16[1,320,2560]{2,1,0:T(8,128)(2,1)} %param.1), kind=kLoop, calls=%fused_computation.11 | loop fusion | bytes 1146880 | tf_op jit(solution)/shard_map/slice | solution.py:227
  53.0 7.0 %collective-permute-start.8 = (bf16[112,2560]{1,0:T(8,128)(2,1)}, bf16[112,2560]{1,0:T(8,128)(2,1)}, u32[]{:S(2)}, u32[]{:S(2)}) collective-permute-start(bf16[112,2560]{1,0:T(8,128)(2,1)} %slice_bitcast_fusion.1), channel_id=1, source_target_pairs={{0,4},{1,5},{6,2},{7,3},{8,12},{9,13},{14,10},{15,11},{16,20},{17,... | collective-permute-start | bytes 1720328 | tf_op jit(solution)/shard_map/rows_far/ppermute | solution.py:218
  60.0 7.7 %collective-permute-done.7.refs_9_ = bf16[208,2560]{1,0:T(8,128)(2,1)} collective-permute-done((bf16[208,2560]{1,0:T(8,128)(2,1)}, bf16[208,2560]{1,0:T(8,128)(2,1)}, u32[]{:S(2)}, u32[]{:S(2)}) %collective-permute-start.7) | collective-permute-done | bytes 1064992 | tf_op jit(solution)/shard_map/rows_far/ppermute | solution.py:218
  68.5 10.1 %collective-permute-done.8.refs_10_ = bf16[112,2560]{1,0:T(8,128)(2,1)} collective-permute-done((bf16[112,2560]{1,0:T(8,128)(2,1)}, bf16[112,2560]{1,0:T(8,128)(2,1)}, u32[]{:S(2)}, u32[]{:S(2)}) %collective-permute-start.8) | collective-permute-done | bytes 573472 | tf_op jit(solution)/shard_map/rows_far/ppermute | solution.py:218
  79.7 1.3 collective-permute-start.14
  81.3 1.3 collective-permute-start.11
  82.6 34.5 %collective-permute-done.14 = bf16[320,1280]{1,0:T(8,128)(2,1)S(1)} collective-permute-done((bf16[320,1280]{1,0:T(8,128)(2,1)S(1)}, bf16[320,1280]{1,0:T(8,128)(2,1)S(1)}, u32[]{:S(2)}, u32[]{:S(2)}) %collective-permute-start.14) | collective-permute-done | bytes 819232 | tf_op jit(solution)/shard_map/rows_out/ppermute | solution.py:218
  117.3 1.5 collective-permute-start.15
  118.8 1.5 collective-permute-start.16
  120.3 15.4 %collective-permute-done.11 = bf16[320,1280]{1,0:T(8,128)(2,1)S(1)} collective-permute-done((bf16[320,1280]{1,0:T(8,128)(2,1)S(1)}, bf16[320,1280]{1,0:T(8,128)(2,1)S(1)}, u32[]{:S(2)}, u32[]{:S(2)}) %collective-permute-start.11) | collective-permute-done | bytes 819232 | tf_op jit(solution)/shard_map/rows_out/ppermute | solution.py:218
  135.8 1.6 collective-permute-start.12
  137.4 1.5 collective-permute-start.13
  139.5 16.3 %collective-permute-done.12 = bf16[320,1280]{1,0:T(8,128)(2,1)} collective-permute-done((bf16[320,1280]{1,0:T(8,128)(2,1)S(1)}, bf16[320,1280]{1,0:T(8,128)(2,1)}, u32[]{:S(2)}, u32[]{:S(2)}) %collective-permute-start.12) | collective-permute-done | bytes 819232 | tf_op jit(solution)/shard_map/along_x/ppermute | solution.py:218
  157.5 1.5 collective-permute-start.18
  161.7 13.8 %collective-permute-done.17 = bf16[320,1280]{1,0:T(8,128)(2,1)S(1)} collective-permute-done((bf16[320,1280]{1,0:T(8,128)(2,1)S(1)}, bf16[320,1280]{1,0:T(8,128)(2,1)S(1)}, u32[]{:S(2)}, u32[]{:S(2)}) %collective-permute-start.17) | collective-permute-done | bytes 819232 | tf_op jit(solution)/shard_map/across_x/ppermute | solution.py:218
  (34 shorter events, 12.2 us)
Async XLA Ops:
  0.0 14.9 %collective-permute-start.2 = (bf16[320,2560]{1,0:T(8,128)(2,1)}, bf16[320,2560]{1,0:T(8,128)(2,1)S(1)}, u32[]{:S(2)}, u32[]{:S(2)}) collective-permute-start(bf16[320,2560]{1,0:T(8,128)(2,1)} %bitcast.22), channel_id=1, source_target_pairs={{2,4},{3,5},{4,2},{5,3},{10,12},{11,13},{12,10},{13,11},{18,20},{1... | collective-permute-start | bytes 4915208 | tf_op jit(solution)/shard_map/middle/ppermute | solution.py:218
  0.8 44.2 %collective-permute-start = (bf16[320,2560]{1,0:T(8,128)(2,1)}, bf16[320,2560]{1,0:T(8,128)(2,1)S(1)}, u32[]{:S(2)}, u32[]{:S(2)}) collective-permute-start(bf16[320,2560]{1,0:T(8,128)(2,1)} %bitcast.23), channel_id=1, source_target_pairs={{0,2},{1,3},{6,4},{7,5},{8,10},{9,11},{14,12},{15,13},{16,18},{17,... | collective-permute-start | bytes 4915208 | tf_op jit(solution)/shard_map/rows_in/ppermute | solution.py:218
  8.5 40.9 %collective-permute-start.1 = (bf16[320,2560]{1,0:T(8,128)(2,1)}, bf16[320,2560]{1,0:T(8,128)(2,1)}, u32[]{:S(2)}, u32[]{:S(2)}) collective-permute-start(bf16[320,2560]{1,0:T(8,128)(2,1)} %bitcast.24), channel_id=1, source_target_pairs={{2,3},{3,2},{4,5},{5,4},{10,11},{11,10},{12,13},{13,12},{18,19},{1... | collective-permute-start | bytes 4915208 | tf_op jit(solution)/shard_map/swap_own/ppermute | solution.py:218
  12.7 55.1 %collective-permute-start.7 = (bf16[208,2560]{1,0:T(8,128)(2,1)}, bf16[208,2560]{1,0:T(8,128)(2,1)}, u32[]{:S(2)}, u32[]{:S(2)}) collective-permute-start(bf16[208,2560]{1,0:T(8,128)(2,1)} %slice_bitcast_fusion), channel_id=1, source_target_pairs={{0,4},{1,5},{6,2},{7,3},{8,12},{9,13},{14,10},{15,11},{16,20},{17,... | collective-permute-start | bytes 3194888 | tf_op jit(solution)/shard_map/rows_far/ppermute | solution.py:218
  15.9 44.0 %collective-permute-start.5 = (bf16[176,2560]{1,0:T(8,128)(2,1)}, bf16[176,2560]{1,0:T(8,128)(2,1)}, u32[]{:S(2)}, u32[]{:S(2)}) collective-permute-start(bf16[176,2560]{1,0:T(8,128)(2,1)} %slice.34), channel_id=1, source_target_pairs={{2,3},{3,2},{4,5},{5,4},{10,11},{11,10},{12,13},{13,12},{18,19},{1... | collective-permute-start | bytes 2703368 | tf_op jit(solution)/shard_map/swap_rows/ppermute | solution.py:218
  46.2 13.7 %collective-permute-start.3 = (bf16[160,2560]{1,0:T(8,128)(2,1)}, bf16[160,2560]{1,0:T(8,128)(2,1)}, u32[]{:S(2)}, u32[]{:S(2)}) collective-permute-start(bf16[160,2560]{1,0:T(8,128)(2,1)} %get-tuple-element.38), channel_id=1, source_target_pairs={{2,3},{3,2},{4,5},{5,4},{10,11},{11,10},{12,13},{13,12},{18,19},{1... | collective-permute-start | bytes 2457608 | tf_op jit(solution)/shard_map/swap_rows/ppermute | solution.py:218
  47.8 12.1 %collective-permute-start.4 = (bf16[160,2560]{1,0:T(8,128)(2,1)}, bf16[160,2560]{1,0:T(8,128)(2,1)}, u32[]{:S(2)}, u32[]{:S(2)}) collective-permute-start(bf16[160,2560]{1,0:T(8,128)(2,1)} %get-tuple-element.37), channel_id=1, source_target_pairs={{2,3},{3,2},{4,5},{5,4},{10,11},{11,10},{12,13},{13,12},{18,19},{1... | collective-permute-start | bytes 2457608 | tf_op jit(solution)/shard_map/swap_rows/ppermute | solution.py:218
  49.5 3.5 %collective-permute-start.6 = (bf16[144,2560]{1,0:T(8,128)(2,1)S(1)}, bf16[144,2560]{1,0:T(8,128)(2,1)}, u32[]{:S(2)}, u32[]{:S(2)}) collective-permute-start(bf16[144,2560]{1,0:T(8,128)(2,1)S(1)} %slice.35), channel_id=1, source_target_pairs={{2,3},{3,2},{4,5},{5,4},{10,11},{11,10},{12,13},{13,12},{18,19},{1... | collective-permute-start | bytes 2211848 | tf_op jit(solution)/shard_map/swap_rows/ppermute | solution.py:218
  53.0 25.6 %collective-permute-start.8 = (bf16[112,2560]{1,0:T(8,128)(2,1)}, bf16[112,2560]{1,0:T(8,128)(2,1)}, u32[]{:S(2)}, u32[]{:S(2)}) collective-permute-start(bf16[112,2560]{1,0:T(8,128)(2,1)} %slice_bitcast_fusion.1), channel_id=1, source_target_pairs={{0,4},{1,5},{6,2},{7,3},{8,12},{9,13},{14,10},{15,11},{16,20},{17,... | collective-permute-start | bytes 1720328 | tf_op jit(solution)/shard_map/rows_far/ppermute | solution.py:218
  67.8 11.5 %collective-permute-start.9 = (bf16[208,2560]{1,0:T(8,128)(2,1)}, bf16[208,2560]{1,0:T(8,128)(2,1)S(1)}, u32[]{:S(2)}, u32[]{:S(2)}) collective-permute-start(bf16[208,2560]{1,0:T(8,128)(2,1)} %collective-permute-done.7.refs_9_), channel_id=1, source_target_pairs={{2,3},{3,2},{4,5},{5,4},{10,11},{11,10},{12,13},{13,12},{18,19},{1... | collective-permute-start | bytes 3194888 | tf_op jit(solution)/shard_map/swap_far/ppermute | solution.py:218
  78.6 0.7 collective-permute-start.10
  79.7 37.5 %collective-permute-start.14 = (bf16[320,1280]{1,0:T(8,128)(2,1)S(1)}, bf16[320,1280]{1,0:T(8,128)(2,1)S(1)}, u32[]{:S(2)}, u32[]{:S(2)}) collective-permute-start(bf16[320,1280]{1,0:T(8,128)(2,1)S(1)} %get-tuple-element.31), channel_id=1, source_target_pairs={{2,0},{3,1},{4,6},{5,7},{10,8},{11,9},{12,14},{13,15},{18,16},{19,... | collective-permute-start | bytes 2457608 | tf_op jit(solution)/shard_map/rows_out/ppermute | solution.py:218
  81.3 54.4 %collective-permute-start.11 = (bf16[320,1280]{1,0:T(8,128)(2,1)S(1)}, bf16[320,1280]{1,0:T(8,128)(2,1)S(1)}, u32[]{:S(2)}, u32[]{:S(2)}) collective-permute-start(bf16[320,1280]{1,0:T(8,128)(2,1)S(1)} %get-tuple-element.27), channel_id=1, source_target_pairs={{2,0},{3,1},{4,6},{5,7},{10,8},{11,9},{12,14},{13,15},{18,16},{19,... | collective-permute-start | bytes 2457608 | tf_op jit(solution)/shard_map/rows_out/ppermute | solution.py:218
  117.3 22.2 %collective-permute-start.15 = (bf16[320,1280]{1,0:T(8,128)(2,1)S(1)}, bf16[320,1280]{1,0:T(8,128)(2,1)S(1)}, u32[]{:S(2)}, u32[]{:S(2)}) collective-permute-start(bf16[320,1280]{1,0:T(8,128)(2,1)S(1)} %broadcast_select_fusion), channel_id=1, source_target_pairs={{0,8},{8,0},{16,24},{24,16},{1,9},{9,1},{17,25},{25,17},{2,10},{10... | collective-permute-start | bytes 2457608 | tf_op jit(solution)/shard_map/along_x/ppermute | solution.py:218
  118.8 20.7 %collective-permute-start.16 = (bf16[320,1280]{1,0:T(8,128)(2,1)S(1)}, bf16[320,1280]{1,0:T(8,128)(2,1)S(1)}, u32[]{:S(2)}, u32[]{:S(2)}) collective-permute-start(bf16[320,1280]{1,0:T(8,128)(2,1)S(1)} %broadcast_select_fusion), channel_id=1, source_target_pairs={{0,16},{8,24},{16,0},{24,8},{1,17},{9,25},{17,1},{25,9},{2,18},{10... | collective-permute-start | bytes 2457608 | tf_op jit(solution)/shard_map/along_y/ppermute | solution.py:218
  135.8 19.9 %collective-permute-start.12 = (bf16[320,1280]{1,0:T(8,128)(2,1)S(1)}, bf16[320,1280]{1,0:T(8,128)(2,1)}, u32[]{:S(2)}, u32[]{:S(2)}) collective-permute-start(bf16[320,1280]{1,0:T(8,128)(2,1)S(1)} %broadcast_select_fusion.1), channel_id=1, source_target_pairs={{0,8},{8,0},{16,24},{24,16},{1,9},{9,1},{17,25},{25,17},{2,10},{10... | collective-permute-start | bytes 2457608 | tf_op jit(solution)/shard_map/along_x/ppermute | solution.py:218
  137.4 19.6 %collective-permute-start.13 = (bf16[320,1280]{1,0:T(8,128)(2,1)S(1)}, bf16[320,1280]{1,0:T(8,128)(2,1)}, u32[]{:S(2)}, u32[]{:S(2)}) collective-permute-start(bf16[320,1280]{1,0:T(8,128)(2,1)S(1)} %broadcast_select_fusion.1), channel_id=1, source_target_pairs={{0,16},{8,24},{16,0},{24,8},{1,17},{9,25},{17,1},{25,9},{2,18},{10... | collective-permute-start | bytes 2457608 | tf_op jit(solution)/shard_map/along_y/ppermute | solution.py:218
  157.0 18.6 %collective-permute-start.17 = (bf16[320,1280]{1,0:T(8,128)(2,1)S(1)}, bf16[320,1280]{1,0:T(8,128)(2,1)S(1)}, u32[]{:S(2)}, u32[]{:S(2)}) collective-permute-start(bf16[320,1280]{1,0:T(8,128)(2,1)S(1)} %collective-permute-done.16), channel_id=1, source_target_pairs={{0,8},{8,0},{16,24},{24,16},{1,9},{9,1},{17,25},{25,17},{2,10},{10... | collective-permute-start | bytes 2457608 | tf_op jit(solution)/shard_map/across_x/ppermute | solution.py:218
  157.5 18.5 %collective-permute-start.18 = (bf16[320,1280]{1,0:T(8,128)(2,1)}, bf16[320,1280]{1,0:T(8,128)(2,1)S(1)}, u32[]{:S(2)}, u32[]{:S(2)}) collective-permute-start(bf16[320,1280]{1,0:T(8,128)(2,1)} %collective-permute-done.12), channel_id=1, source_target_pairs={{0,16},{8,24},{16,0},{24,8},{1,17},{9,25},{17,1},{25,9},{2,18},{10... | collective-permute-start | bytes 2457608 | tf_op jit(solution)/shard_map/across_y/ppermute | solution.py:218
  161.7 14.3 %copy-start = (bf16[4,320,2560]{2,1,0:T(8,128)(2,1)}, bf16[4,320,2560]{2,1,0:T(8,128)(2,1)S(1)}, u32[]{:S(2)}) copy-start(bf16[4,320,2560]{2,1,0:T(8,128)(2,1)S(1)} %bitcast_dynamic-update-slice_fusion) | copy-start | bytes 19660804

commit v23 on v22

--- a/solution.py
+++ b/solution.py
@@ -231,7 +231,7 @@
         return pltpu.with_memory_space_constraint(block, pltpu.HBM)
 
     early = [outer_rows, kept(own), kept(swap("own", own)), inner_rows]
-    for block, at in ((outer_rows, rows // 2), (inner_rows, rows * 11 // 20)):
+    for block, at in ((outer_rows, rows * 11 // 20), (inner_rows, rows // 2)):
         early += [swap("rows", part) for part in (block[:at], block[at:])]
     early[-1] = kept(early[-1])
     gram, cubic = early_products(inner, rows, early)

time: 178 us -> 195 us (1.096)
  starting transfers between devices: 38.2 us -> 59.3 us
  waiting for transfers between devices: 127 us -> 121 us
  local copies, waits for them, and re-layouts: 9.72 us -> 11.8 us
    ppermute x19, starting transfers between devices: 38.2 us -> 59.3 us  [move(): return lax.ppermute(block, axis, pairs)]
    ppermute x19, waiting for transfers between devices: 127 us -> 121 us  [move(): return lax.ppermute(block, axis, pairs)]
    unnamed x2 -> x8, local copies, waits for them, and re-layouts: 0.01 us -> 1.99 us
  transfers between devices with their start and end apart: 19 -> 19, of which waited for: 9 -> 8; matrix products, arithmetic and copies ran while one was open for 6% -> 5% of each run, Pallas kernels for 0% -> 0%
where the time goes in v23:
time: 195 us
  waiting for transfers between devices  121 us (62%)
  starting transfers between devices  59.3 us (30%)
  local copies, waits for them, and re-layouts  11.8 us (6%)
    ppermute x19, waiting for transfers between devices, move(): return lax.ppermute(block, axis, pairs)  121 us
    ppermute x19, starting transfers between devices, move(): return lax.ppermute(block, axis, pairs)  59.3 us
  transfers between devices with their start and end apart: 19, of which 8 were waited for; matrix products, arithmetic and copies ran while one was open for 5% of the time, Pallas kernels for 0%

profile of v23, /device:TPU:0, one launch (start us, length us, event | category | flops | bytes accessed | tf_op | source)
XLA Modules:
  0.0 194.9 jit_solution(6342154137598297293)
XLA Ops:
  0.0 5.0 %collective-permute-start = (bf16[320,2560]{1,0:T(8,128)(2,1)}, bf16[320,2560]{1,0:T(8,128)(2,1)S(1)}, u32[]{:S(2)}, u32[]{:S(2)}) collective-permute-start(bf16[320,2560]{1,0:T(8,128)(2,1)} %bitcast.22), channel_id=1, source_target_pairs={{0,2},{1,3},{6,4},{7,5},{8,10},{9,11},{14,12},{15,13},{16,18},{17,... | collective-permute-start | bytes 4915208 | tf_op jit(solution)/shard_map/rows_in/ppermute | solution.py:218
  6.6 2.3 %slice_bitcast_fusion = bf16[208,2560]{1,0:T(8,128)(2,1)} fusion(bf16[1,320,2560]{2,1,0:T(8,128)(2,1)} %param.1), kind=kLoop, calls=%fused_computation.2 | loop fusion | bytes 2129920 | tf_op jit(solution)/shard_map/slice | solution.py:227
  8.8 6.0 %collective-permute-start.7 = (bf16[208,2560]{1,0:T(8,128)(2,1)}, bf16[208,2560]{1,0:T(8,128)(2,1)}, u32[]{:S(2)}, u32[]{:S(2)}) collective-permute-start(bf16[208,2560]{1,0:T(8,128)(2,1)} %slice_bitcast_fusion), channel_id=1, source_target_pairs={{0,4},{1,5},{6,2},{7,3},{8,12},{9,13},{14,10},{15,11},{16,20},{17,... | collective-permute-start | bytes 3194888 | tf_op jit(solution)/shard_map/rows_far/ppermute | solution.py:218
  14.8 26.6 %collective-permute-done.refs_1_ = bf16[320,2560]{1,0:T(8,128)(2,1)S(1)} collective-permute-done((bf16[320,2560]{1,0:T(8,128)(2,1)}, bf16[320,2560]{1,0:T(8,128)(2,1)S(1)}, u32[]{:S(2)}, u32[]{:S(2)}) %collective-permute-start) | collective-permute-done | bytes 1638432 | tf_op jit(solution)/shard_map/rows_in/ppermute | solution.py:218
  42.4 1.6 collective-permute-start.3
  44.0 1.3 fusion.1
  45.3 1.6 collective-permute-start.5
  46.9 1.6 collective-permute-start.6
  49.2 1.9 slice_bitcast_fusion.1
  52.1 29.2 %collective-permute-start.8 = (bf16[112,2560]{1,0:T(8,128)(2,1)}, bf16[112,2560]{1,0:T(8,128)(2,1)}, u32[]{:S(2)}, u32[]{:S(2)}) collective-permute-start(bf16[112,2560]{1,0:T(8,128)(2,1)} %slice_bitcast_fusion.1), channel_id=1, source_target_pairs={{0,4},{1,5},{6,2},{7,3},{8,12},{9,13},{14,10},{15,11},{16,20},{17,... | collective-permute-start | bytes 1720328 | tf_op jit(solution)/shard_map/rows_far/ppermute | solution.py:218
  83.2 10.1 %collective-permute-done.8.refs_10_ = bf16[112,2560]{1,0:T(8,128)(2,1)} collective-permute-done((bf16[112,2560]{1,0:T(8,128)(2,1)}, bf16[112,2560]{1,0:T(8,128)(2,1)}, u32[]{:S(2)}, u32[]{:S(2)}) %collective-permute-start.8) | collective-permute-done | bytes 573472 | tf_op jit(solution)/shard_map/rows_far/ppermute | solution.py:218
  94.4 1.3 collective-permute-start.14
  96.1 1.3 collective-permute-start.11
  97.4 37.1 %collective-permute-done.14 = bf16[320,1280]{1,0:T(8,128)(2,1)S(1)} collective-permute-done((bf16[320,1280]{1,0:T(8,128)(2,1)S(1)}, bf16[320,1280]{1,0:T(8,128)(2,1)S(1)}, u32[]{:S(2)}, u32[]{:S(2)}) %collective-permute-start.14) | collective-permute-done | bytes 819232 | tf_op jit(solution)/shard_map/rows_out/ppermute | solution.py:218
  134.5 1.5 collective-permute-start.15
  136.1 1.5 collective-permute-start.16
  137.6 15.4 %collective-permute-done.11 = bf16[320,1280]{1,0:T(8,128)(2,1)S(1)} collective-permute-done((bf16[320,1280]{1,0:T(8,128)(2,1)S(1)}, bf16[320,1280]{1,0:T(8,128)(2,1)S(1)}, u32[]{:S(2)}, u32[]{:S(2)}) %collective-permute-start.11) | collective-permute-done | bytes 819232 | tf_op jit(solution)/shard_map/rows_out/ppermute | solution.py:218
  153.1 1.5 collective-permute-start.12
  154.7 1.5 collective-permute-start.13
  156.8 16.4 %collective-permute-done.12 = bf16[320,1280]{1,0:T(8,128)(2,1)} collective-permute-done((bf16[320,1280]{1,0:T(8,128)(2,1)S(1)}, bf16[320,1280]{1,0:T(8,128)(2,1)}, u32[]{:S(2)}, u32[]{:S(2)}) %collective-permute-start.12) | collective-permute-done | bytes 819232 | tf_op jit(solution)/shard_map/along_x/ppermute | solution.py:218
  174.9 1.5 collective-permute-start.18
  176.4 1.2 bitcast_dynamic-update-slice_fusion.4
  179.1 13.9 %collective-permute-done.17 = bf16[320,1280]{1,0:T(8,128)(2,1)S(1)} collective-permute-done((bf16[320,1280]{1,0:T(8,128)(2,1)S(1)}, bf16[320,1280]{1,0:T(8,128)(2,1)S(1)}, u32[]{:S(2)}, u32[]{:S(2)}) %collective-permute-start.17) | collective-permute-done | bytes 819232 | tf_op jit(solution)/shard_map/across_x/ppermute | solution.py:218
  193.6 1.3 fusion
  (40 shorter events, 11.9 us)
Async XLA Ops:
  0.0 41.4 %collective-permute-start = (bf16[320,2560]{1,0:T(8,128)(2,1)}, bf16[320,2560]{1,0:T(8,128)(2,1)S(1)}, u32[]{:S(2)}, u32[]{:S(2)}) collective-permute-start(bf16[320,2560]{1,0:T(8,128)(2,1)} %bitcast.22), channel_id=1, source_target_pairs={{0,2},{1,3},{6,4},{7,5},{8,10},{9,11},{14,12},{15,13},{16,18},{17,... | collective-permute-start | bytes 4915208 | tf_op jit(solution)/shard_map/rows_in/ppermute | solution.py:218
  5.0 39.0 %collective-permute-start.2 = (bf16[320,2560]{1,0:T(8,128)(2,1)}, bf16[320,2560]{1,0:T(8,128)(2,1)S(1)}, u32[]{:S(2)}, u32[]{:S(2)}) collective-permute-start(bf16[320,2560]{1,0:T(8,128)(2,1)} %bitcast.23), channel_id=1, source_target_pairs={{2,4},{3,5},{4,2},{5,3},{10,12},{11,13},{12,10},{13,11},{18,20},{1... | collective-permute-start | bytes 4915208 | tf_op jit(solution)/shard_map/middle/ppermute | solution.py:218
  5.8 42.7 %collective-permute-start.1 = (bf16[320,2560]{1,0:T(8,128)(2,1)}, bf16[320,2560]{1,0:T(8,128)(2,1)S(1)}, u32[]{:S(2)}, u32[]{:S(2)}) collective-permute-start(bf16[320,2560]{1,0:T(8,128)(2,1)} %bitcast.24), channel_id=1, source_target_pairs={{2,3},{3,2},{4,5},{5,4},{10,11},{11,10},{12,13},{13,12},{18,19},{1... | collective-permute-start | bytes 4915208 | tf_op jit(solution)/shard_map/swap_own/ppermute | solution.py:218
  8.8 73.6 %collective-permute-start.7 = (bf16[208,2560]{1,0:T(8,128)(2,1)}, bf16[208,2560]{1,0:T(8,128)(2,1)}, u32[]{:S(2)}, u32[]{:S(2)}) collective-permute-start(bf16[208,2560]{1,0:T(8,128)(2,1)} %slice_bitcast_fusion), channel_id=1, source_target_pairs={{0,4},{1,5},{6,2},{7,3},{8,12},{9,13},{14,10},{15,11},{16,20},{17,... | collective-permute-start | bytes 3194888 | tf_op jit(solution)/shard_map/rows_far/ppermute | solution.py:218
  42.4 38.8 %collective-permute-start.3 = (bf16[176,2560]{1,0:T(8,128)(2,1)}, bf16[176,2560]{1,0:T(8,128)(2,1)}, u32[]{:S(2)}, u32[]{:S(2)}) collective-permute-start(bf16[176,2560]{1,0:T(8,128)(2,1)} %slice.32), channel_id=1, source_target_pairs={{2,3},{3,2},{4,5},{5,4},{10,11},{11,10},{12,13},{13,12},{18,19},{1... | collective-permute-start | bytes 2703368 | tf_op jit(solution)/shard_map/swap_rows/ppermute | solution.py:218
  45.3 35.9 %collective-permute-start.5 = (bf16[160,2560]{1,0:T(8,128)(2,1)}, bf16[160,2560]{1,0:T(8,128)(2,1)}, u32[]{:S(2)}, u32[]{:S(2)}) collective-permute-start(bf16[160,2560]{1,0:T(8,128)(2,1)} %get-tuple-element.38), channel_id=1, source_target_pairs={{2,3},{3,2},{4,5},{5,4},{10,11},{11,10},{12,13},{13,12},{18,19},{1... | collective-permute-start | bytes 2457608 | tf_op jit(solution)/shard_map/swap_rows/ppermute | solution.py:218
  46.9 34.4 %collective-permute-start.6 = (bf16[160,2560]{1,0:T(8,128)(2,1)}, bf16[160,2560]{1,0:T(8,128)(2,1)}, u32[]{:S(2)}, u32[]{:S(2)}) collective-permute-start(bf16[160,2560]{1,0:T(8,128)(2,1)} %get-tuple-element.37), channel_id=1, source_target_pairs={{2,3},{3,2},{4,5},{5,4},{10,11},{11,10},{12,13},{13,12},{18,19},{1... | collective-permute-start | bytes 2457608 | tf_op jit(solution)/shard_map/swap_rows/ppermute | solution.py:218
  48.5 2.7 %copy-start.3 = (bf16[320,2560]{1,0:T(8,128)(2,1)}, bf16[320,2560]{1,0:T(8,128)(2,1)S(1)}, u32[]{:S(2)}) copy-start(bf16[320,2560]{1,0:T(8,128)(2,1)S(1)} %collective-permute-done.1.refs_3_) | copy-start | bytes 4915204
  48.5 2.7 %collective-permute-start.4 = (bf16[144,2560]{1,0:T(8,128)(2,1)S(1)}, bf16[144,2560]{1,0:T(8,128)(2,1)S(1)}, u32[]{:S(2)}, u32[]{:S(2)}) collective-permute-start(bf16[144,2560]{1,0:T(8,128)(2,1)S(1)} %slice.33), channel_id=1, source_target_pairs={{2,3},{3,2},{4,5},{5,4},{10,11},{11,10},{12,13},{13,12},{18,19},{1... | collective-permute-start | bytes 2211848 | tf_op jit(solution)/shard_map/swap_rows/ppermute | solution.py:218
  51.2 0.9 copy-start
  52.1 41.3 %collective-permute-start.8 = (bf16[112,2560]{1,0:T(8,128)(2,1)}, bf16[112,2560]{1,0:T(8,128)(2,1)}, u32[]{:S(2)}, u32[]{:S(2)}) collective-permute-start(bf16[112,2560]{1,0:T(8,128)(2,1)} %slice_bitcast_fusion.1), channel_id=1, source_target_pairs={{0,4},{1,5},{6,2},{7,3},{8,12},{9,13},{14,10},{15,11},{16,20},{17,... | collective-permute-start | bytes 1720328 | tf_op jit(solution)/shard_map/rows_far/ppermute | solution.py:218
  81.3 1.1 copy-start.1
  82.5 11.6 %collective-permute-start.9 = (bf16[208,2560]{1,0:T(8,128)(2,1)}, bf16[208,2560]{1,0:T(8,128)(2,1)S(1)}, u32[]{:S(2)}, u32[]{:S(2)}) collective-permute-start(bf16[208,2560]{1,0:T(8,128)(2,1)} %collective-permute-done.7.refs_9_), channel_id=1, source_target_pairs={{2,3},{3,2},{4,5},{5,4},{10,11},{11,10},{12,13},{13,12},{18,19},{1... | collective-permute-start | bytes 3194888 | tf_op jit(solution)/shard_map/swap_far/ppermute | solution.py:218
  93.4 0.7 collective-permute-start.10
  94.4 40.1 %collective-permute-start.14 = (bf16[320,1280]{1,0:T(8,128)(2,1)S(1)}, bf16[320,1280]{1,0:T(8,128)(2,1)S(1)}, u32[]{:S(2)}, u32[]{:S(2)}) collective-permute-start(bf16[320,1280]{1,0:T(8,128)(2,1)S(1)} %get-tuple-element.31), channel_id=1, source_target_pairs={{2,0},{3,1},{4,6},{5,7},{10,8},{11,9},{12,14},{13,15},{18,16},{19,... | collective-permute-start | bytes 2457608 | tf_op jit(solution)/shard_map/rows_out/ppermute | solution.py:218
  96.1 56.9 %collective-permute-start.11 = (bf16[320,1280]{1,0:T(8,128)(2,1)S(1)}, bf16[320,1280]{1,0:T(8,128)(2,1)S(1)}, u32[]{:S(2)}, u32[]{:S(2)}) collective-permute-start(bf16[320,1280]{1,0:T(8,128)(2,1)S(1)} %get-tuple-element.27), channel_id=1, source_target_pairs={{2,0},{3,1},{4,6},{5,7},{10,8},{11,9},{12,14},{13,15},{18,16},{19,... | collective-permute-start | bytes 2457608 | tf_op jit(solution)/shard_map/rows_out/ppermute | solution.py:218
  134.5 22.2 %collective-permute-start.15 = (bf16[320,1280]{1,0:T(8,128)(2,1)S(1)}, bf16[320,1280]{1,0:T(8,128)(2,1)S(1)}, u32[]{:S(2)}, u32[]{:S(2)}) collective-permute-start(bf16[320,1280]{1,0:T(8,128)(2,1)S(1)} %broadcast_select_fusion), channel_id=1, source_target_pairs={{0,8},{8,0},{16,24},{24,16},{1,9},{9,1},{17,25},{25,17},{2,10},{10... | collective-permute-start | bytes 2457608 | tf_op jit(solution)/shard_map/along_x/ppermute | solution.py:218
  136.1 20.7 %collective-permute-start.16 = (bf16[320,1280]{1,0:T(8,128)(2,1)S(1)}, bf16[320,1280]{1,0:T(8,128)(2,1)S(1)}, u32[]{:S(2)}, u32[]{:S(2)}) collective-permute-start(bf16[320,1280]{1,0:T(8,128)(2,1)S(1)} %broadcast_select_fusion), channel_id=1, source_target_pairs={{0,16},{8,24},{16,0},{24,8},{1,17},{9,25},{17,1},{25,9},{2,18},{10... | collective-permute-start | bytes 2457608 | tf_op jit(solution)/shard_map/along_y/ppermute | solution.py:218
  153.1 20.1 %collective-permute-start.12 = (bf16[320,1280]{1,0:T(8,128)(2,1)S(1)}, bf16[320,1280]{1,0:T(8,128)(2,1)}, u32[]{:S(2)}, u32[]{:S(2)}) collective-permute-start(bf16[320,1280]{1,0:T(8,128)(2,1)S(1)} %broadcast_select_fusion.1), channel_id=1, source_target_pairs={{0,8},{8,0},{16,24},{24,16},{1,9},{9,1},{17,25},{25,17},{2,10},{10... | collective-permute-start | bytes 2457608 | tf_op jit(solution)/shard_map/along_x/ppermute | solution.py:218
  154.7 19.7 %collective-permute-start.13 = (bf16[320,1280]{1,0:T(8,128)(2,1)S(1)}, bf16[320,1280]{1,0:T(8,128)(2,1)}, u32[]{:S(2)}, u32[]{:S(2)}) collective-permute-start(bf16[320,1280]{1,0:T(8,128)(2,1)S(1)} %broadcast_select_fusion.1), channel_id=1, source_target_pairs={{0,16},{8,24},{16,0},{24,8},{1,17},{9,25},{17,1},{25,9},{2,18},{10... | collective-permute-start | bytes 2457608 | tf_op jit(solution)/shard_map/along_y/ppermute | solution.py:218
  174.4 18.7 %collective-permute-start.17 = (bf16[320,1280]{1,0:T(8,128)(2,1)S(1)}, bf16[320,1280]{1,0:T(8,128)(2,1)S(1)}, u32[]{:S(2)}, u32[]{:S(2)}) collective-permute-start(bf16[320,1280]{1,0:T(8,128)(2,1)S(1)} %collective-permute-done.16), channel_id=1, source_target_pairs={{0,8},{8,0},{16,24},{24,16},{1,9},{9,1},{17,25},{25,17},{2,10},{10... | collective-permute-start | bytes 2457608 | tf_op jit(solution)/shard_map/across_x/ppermute | solution.py:218
  174.9 18.6 %collective-permute-start.18 = (bf16[320,1280]{1,0:T(8,128)(2,1)}, bf16[320,1280]{1,0:T(8,128)(2,1)S(1)}, u32[]{:S(2)}, u32[]{:S(2)}) collective-permute-start(bf16[320,1280]{1,0:T(8,128)(2,1)} %collective-permute-done.12), channel_id=1, source_target_pairs={{0,16},{8,24},{16,0},{24,8},{1,17},{9,25},{17,1},{25,9},{2,18},{10... | collective-permute-start | bytes 2457608 | tf_op jit(solution)/shard_map/across_y/ppermute | solution.py:218
  179.1 14.5 %copy-start.2 = (bf16[4,320,2560]{2,1,0:T(8,128)(2,1)}, bf16[4,320,2560]{2,1,0:T(8,128)(2,1)S(1)}, u32[]{:S(2)}) copy-start(bf16[4,320,2560]{2,1,0:T(8,128)(2,1)S(1)} %bitcast_dynamic-update-slice_fusion) | copy-start | bytes 19660804
